TPU v7x, 128 devices: a whole 4x4x4 slice. The times are simulated.
128 devices in a mesh: slide: 4 (over y), seq: 32 (over x, z, core).
Axes of the slice: x: 4, y: 4, z: 4, core: 2. Of those that a mesh axis runs over, the one named last changes fastest.
Arguments:
- query_tiles: bfloat16 [131072, 768], P(('slide', 'seq')), parts along dimension 0, may hold values from -160 to 160
- key_tiles: bfloat16 [131072, 768], P(('slide', 'seq')), parts along dimension 0, may hold values from -4.04 to 4.04
- value_tiles: bfloat16 [131072, 768], P(('slide', 'seq')), parts along dimension 0, may hold values from -6 to 6
- slide_length: int32 [4], P('slide'), parts along dimension 0, may hold values from 32256 to 32768
Outputs:
- attended: bfloat16 [131072, 768], P(('slide', 'seq')), parts along dimension 0
There are 4 independent parts, one for each index of `slide`. A program takes and returns all parts, laid end to end along the dimension named above; each array names one. Nothing has to cross between parts.
All inputs are finite; a program needn't handle non-finite values.
Results may differ from a plain program's by a relative error of at most 0.0045.
Values may be sent and summed in bfloat16 or wider, within the bound.
No kernel may reach another device: no remote copies, remote signals or barrier semaphores. Data moves between devices by JAX's collectives and lax.ppermute only.
A program may use at most 128 MiB of HBM per device.

v0:
```python
import functools

import jax
import jax.numpy as jnp
import numpy as np
from jax import lax
from jax.experimental import pallas as pl
from jax.experimental.pallas import tpu as pltpu
from jax.sharding import PartitionSpec as P

HEADS = 12
HEAD_DIM = 64
WIDTH = 768
ROWS = 1024
RES = 16
GROUPS = ROWS // RES
HALF = GROUPS // 2
PAIRS = HEADS // 2
NX, NZ, NC = 4, 4, 2
MASKED = -1e30

BF = jnp.bfloat16
F32 = jnp.float32

ODD = [1, 3, 5, 7, 9, 11, 13, 15]
EVEN = [2, 6, 10, 14, 4, 12, 8, 0]
SHARED = [0, 8, 4, 12]
CLASS_U = {"A": ODD, "B": [2, 6, 10, 14], "C": [4, 12], "D": [8, 0]}
PAIR_OF = [0, 2, 3, 5]
LONE_OF = [2, 3, 8, 9]


def level(u):
    return 4 if u == 0 else min((u & -u).bit_length() - 1, 4)


def tables():
    lane = np.arange(256)
    ints = np.zeros((8, 256), np.int32)
    ints[0] = np.array(ODD)[lane // 32]
    ints[1] = np.array(EVEN)[lane // 32]
    ints[2] = lane % 32 * 16
    ints[3] = np.array(SHARED)[lane // 64]
    ints[4] = lane % 64 * 16
    ints[5] = np.array([0, 8, 0, 8])[lane // 64]
    even = np.array([level(u) for u in EVEN])[lane // 32]
    shared = np.array([level(u) for u in SHARED])[lane // 64]
    floats = np.zeros((8, 256), np.float32)
    floats[1] = np.log(1.0 + np.minimum(even, 1))
    floats[2] = np.log(1.0 + np.minimum(even, 2))
    floats[3] = np.log(1.0 + np.minimum(even, 3))
    floats[4] = np.log(1.0 * np.minimum(even, 2))
    floats[5] = np.log(1.0 * np.minimum(even, 3))
    floats[6] = np.log(np.minimum(shared, 3) - 1.0)
    return ints, floats


def swap_matrix():
    row = lax.broadcasted_iota(jnp.int32, (256, 256), 0)
    col = lax.broadcasted_iota(jnp.int32, (256, 256), 1)
    return jnp.where(((row & 15) * 16 + (row >> 4)) == col, 1.0, 0.0).astype(BF)


def lane_low(rows):
    return lax.broadcasted_iota(jnp.int32, (rows, 128), 1) < 64


def split_kernel(meta, q_ref, k_ref, v_ref, qt, kt, vt, sel, sel8, z0, z1, z2, z3, stage):
    step = pl.program_id(0)
    zpos = meta[1] // 2 % NZ
    swap = swap_matrix()
    for source, target in ((q_ref, qt), (k_ref, kt), (v_ref, vt)):
        for block in range(4):
            moved = jnp.dot(
                swap, source[block * 256 : (block + 1) * 256, :], preferred_element_type=F32
            ).astype(BF)
            for res in range(RES):
                target[res, block * 16 : (block + 1) * 16, :] = moved[res * 16 : (res + 1) * 16, :]
    low = lane_low(GROUPS)

    def picked(ref, u):
        return jnp.where(low, ref[(u + 2 * step) & 15], ref[(u + 2 * step + 1) & 15])

    for at, u in enumerate(SHARED):
        for kv, ref in enumerate((kt, vt)):
            rows = picked(ref, u)
            sel[at, kv] = rows
            if at < 2:
                sel8[at, kv] = rows
    q0, k0, v0 = picked(qt, 0), sel[0, 0], sel[0, 1]
    zero = jnp.zeros_like(q0)

    for group in range(NZ):
        slot = (group - zpos) & 3

        @pl.when(step == PAIR_OF[group])
        def _():
            stage[slot, :, 0:128] = q0
            stage[slot, :, 256:384] = k0
            stage[slot, :, 384:512] = v0

        @pl.when(step == LONE_OF[group] // 2)
        def _():
            def other(rows):
                return pltpu.roll(rows.astype(F32), 64, 1).astype(BF)

            if LONE_OF[group] % 2 == 0:
                lone_q, lone_k, lone_v = q0, k0, other(v0)
            else:
                lone_q, lone_k, lone_v = other(q0), other(k0), v0
            stage[slot, :, 128:256] = jnp.where(low, lone_q, zero)
            stage[slot, :, 512:640] = jnp.where(low, lone_k, lone_v)

    @pl.when(step == PAIRS - 1)
    def _():
        for slot, out in enumerate((z0, z1, z2, z3)):
            out[...] = stage[slot]


def softmax_parts(query, keys, values, biases):
    scores = [
        lax.dot_general(query, key, (((1,), (1,)), ((), ())), preferred_element_type=F32) + bias
        for key, bias in zip(keys, biases)
    ]
    peak = functools.reduce(jnp.maximum, scores)
    peak = jnp.max(peak, axis=1, keepdims=True)
    total = None
    for score, value in zip(scores, values):
        weight = jnp.exp(score - peak).astype(BF)
        part = jnp.dot(weight, value, preferred_element_type=F32)
        total = part if total is None else total + part
    return total, peak


def local_kernel(classes, meta, ints, floats, q_ref, k_ref, v_ref, *rest):
    far = classes == "CD"
    if far:
        sel, near, cross, before, out, o0, lse0 = rest
        out[...] = before[...]
    else:
        (out,) = rest
    bound = meta[0]
    device = meta[1]
    low = lane_low(256)
    for parity in range(2):
        head = 2 * pl.program_id(0) + parity
        mine = low if parity == 0 else jnp.logical_not(low)

        def gathered(ref, order, half):
            return jnp.concatenate(
                [ref[(u + head) & 15, half * HALF : (half + 1) * HALF, :] for u in order], axis=0
            )

        def widened(value):
            return jnp.where(mine, value, jnp.ones_like(value))

        def bias(kind, place, device_of, offset, row):
            position = (
                device_of * ROWS
                + offset
                + ints[place : place + 1, :]
                + ((ints[kind : kind + 1, :] + head) & 15)
            )
            return jnp.where(position < bound, floats[row : row + 1, :], MASKED)

        odd_k = [gathered(k_ref, ODD, half) for half in range(2)]
        even_k = [gathered(k_ref, EVEN, half) for half in range(2)]
        odd_v = [widened(gathered(v_ref, ODD, half)) for half in range(2)]
        even_v = [widened(gathered(v_ref, EVEN, half)) for half in range(2)]
        if far:
            pair_k = sel[:, 0].reshape(256, 128)
            pair_v = widened(sel[:, 1].reshape(256, 128))
            next_k = jnp.concatenate([near[0, 0], near[1, 0], cross[0, 0], cross[1, 0]], axis=0)
            next_v = widened(
                jnp.concatenate([near[0, 1], near[1, 1], cross[0, 1], cross[1, 1]], axis=0)
            )
            lane = lax.broadcasted_iota(jnp.int32, (1, 256), 1)
            next_device = jnp.where(lane < 128, device ^ 2, device ^ 3)
        for half in range(2):
            own = half * 512
            away = 512 - own
            for name in classes:
                order = CLASS_U[name]
                query = gathered(q_ref, order, half)
                count = query.shape[0]
                query = jnp.where(mine[:count], query, jnp.zeros_like(query)) * 0.125
                query = query.astype(BF)
                keys = [odd_k[half], even_k[half]]
                values = [odd_v[half], even_v[half]]
                cap = "ABCD".index(name)
                biases = [bias(0, 2, device, own, 0), bias(1, 2, device, own, cap)]
                if cap >= 1:
                    keys.append(even_k[1 - half])
                    values.append(even_v[1 - half])
                    biases.append(bias(1, 2, device, away, (0, 0, 4, 5)[cap]))
                if cap >= 2:
                    keys.append(pair_k)
                    values.append(pair_v)
                    biases.append(bias(3, 4, device ^ 1, 0, (0, 0, 0, 6)[cap]))
                if cap >= 3:
                    keys.append(next_k)
                    values.append(next_v)
                    biases.append(bias(5, 4, next_device, 0, 0))
                total, peak = softmax_parts(query, keys, values, biases)
                sums = pltpu.roll(total, 64, 1)
                result = total / sums
                rounded = result.astype(BF)
                for at, u in enumerate(order):
                    spot = ((u + head) & 15, slice(half * HALF, (half + 1) * HALF), slice(None))
                    out[spot] = jnp.where(
                        mine[:HALF], rounded[at * HALF : (at + 1) * HALF, :], out[spot]
                    )
                if name == "D":
                    rows = slice(half * HALF, (half + 1) * HALF)
                    log_total = peak[HALF:] + jnp.log(sums[HALF:])
                    o0[rows, :] = jnp.where(mine[:HALF], result[HALF:], o0[rows, :])
                    lse0[rows, :] = jnp.where(mine[:HALF], log_total, lse0[rows, :])


def far_kernel(meta, a0, a1, a2, a3, *rest):
    blocks, outs = rest[:8], rest[8:]
    bound = meta[0]
    device = meta[1]
    xpos, zpos, core = device // 8, device // 2 % NZ, device % 2
    low256 = lane_low(256)
    group = zpos
    lane = lax.broadcasted_iota(jnp.int32, (1, 256), 1)
    part = lane >> 6
    pair = jnp.where(group == 0, 0, jnp.where(group == 1, 4, jnp.where(group == 2, 6, 10)))
    lone = jnp.where(group == 0, 2, jnp.where(group == 1, 3, jnp.where(group == 2, 8, 9)))
    results = []
    for which in range(3):
        head = (pair, pair + 1, lone)[which]
        if which < 2:
            mine = low256 if which == 0 else jnp.logical_not(low256)
        else:
            mine = jnp.logical_not(low256)
        keys, values, biases = [], [], []
        for at, block in enumerate(blocks):
            from_x = (xpos - at % 4) & 3
            from_c = core if at < 4 else 1 - core
            from_z = (zpos - part) & 3
            position = ((from_x * NZ + from_z) * NC + from_c) * ROWS + (lane & 63) * 16 + head
            biases.append(jnp.where(position < bound, 0.0, MASKED))
            if which < 2:
                keys.append(block[:, 0:128])
                value = block[:, 128:256]
            else:
                keys.append(block[:, 256:384])
                value = block[:, 256:384]
            values.append(jnp.where(mine, value, jnp.ones_like(value)))
        parts = []
        for source in (a0, a1, a2, a3):
            if which < 2:
                query = jnp.where(mine[:64], source[:, 0:128], jnp.zeros((64, 128), BF))
            else:
                query = source[:, 128:256]
            query = (query * 0.125).astype(BF)
            total, peak = softmax_parts(query, keys, values, biases)
            sums = pltpu.roll(total, 64, 1)
            parts.append((total / sums, peak + jnp.log(sums), peak + jnp.log(total)))
        results.append(parts)
    low = low256[:64]
    for at, out in enumerate(outs):
        first, second, third = (results[which][at] for which in range(3))
        out[:, 0:128] = jnp.where(low, first[0], second[0])
        out[:, 128:256] = jnp.where(low, third[2], third[0])
        out[:, 256:384] = jnp.where(low, first[1], second[1])


def merge_kernel(meta, mixed, o0, lse0, r0, r1, r2, r3, out, stage, grid_rows):
    bound = meta[0]
    device = meta[1]
    zpos = device // 2 % NZ
    for slot, ref in enumerate((r0, r1, r2, r3)):
        stage[slot] = ref[...]
    low = lane_low(GROUPS)
    for pair in range(PAIRS):
        lanes = slice(pair * 128, pair * 128 + 128)
        if pair in PAIR_OF:
            slot = (PAIR_OF.index(pair) - zpos) & 3
            away, away_lse = stage[slot, :, 0:128], stage[slot, :, 256:384]
        else:
            first = LONE_OF.index(2 * pair)
            left = stage[(first - zpos) & 3, :, 128:256]
            right = stage[(first + 1 - zpos) & 3, :, 128:256]
            away = jnp.where(low, pltpu.roll(left, 64, 1), right)
            away_lse = jnp.where(low, left, pltpu.roll(right, 64, 1))
        here, here_lse = o0[:, lanes], lse0[:, lanes]
        top = jnp.maximum(here_lse, away_lse)
        weight = jnp.exp(here_lse - top)
        away_weight = jnp.exp(away_lse - top)
        blended = (here * weight + away * away_weight) / (weight + away_weight)
        blended = blended.astype(BF)
        for res in range(RES):
            rows = mixed[res, :, lanes]
            if res == 2 * pair:
                rows = jnp.where(low, blended, rows)
            if res == 2 * pair + 1:
                rows = jnp.where(low, rows, blended)
            for block in range(4):
                grid_rows[block, res * 16 : (res + 1) * 16, lanes] = rows[
                    block * 16 : (block + 1) * 16, :
                ]
    swap = swap_matrix()
    index = lax.broadcasted_iota(jnp.int32, (256, WIDTH), 0)
    for block in range(4):
        rows = jnp.dot(swap, grid_rows[block], preferred_element_type=F32)
        position = device * ROWS + block * 256 + index
        out[block * 256 : (block + 1) * 256, :] = jnp.where(position < bound, rows, 0.0).astype(BF)


def smem():
    return pl.BlockSpec(memory_space=pltpu.SMEM)


def vmem():
    return pl.BlockSpec(memory_space=pltpu.VMEM)


def whole(shape):
    return pl.BlockSpec(shape, lambda i: (0,) * len(shape))


def params(mib):
    return pltpu.CompilerParams(vmem_limit_bytes=mib * 1024 * 1024)


def shape(dims, dtype=BF):
    return jax.ShapeDtypeStruct(dims, dtype)


def by_residue():
    return pl.BlockSpec((RES, GROUPS, 128), lambda i: (0, 0, i))


def by_part(parts):
    return pl.BlockSpec((parts, 2, GROUPS, 128), lambda i: (0, 0, 0, i))


def flat(block):
    return pl.BlockSpec((GROUPS, 128), lambda i: (0, i))


def split(meta, q, k, v):
    rows = pl.BlockSpec((ROWS, 128), lambda i: (0, i))
    return pl.pallas_call(
        split_kernel,
        grid=(PAIRS,),
        in_specs=[smem(), rows, rows, rows],
        out_specs=[by_residue()] * 3 + [by_part(4), by_part(2)] + [whole((GROUPS, 640))] * 4,
        out_shape=[shape((RES, GROUPS, WIDTH))] * 3
        + [shape((4, 2, GROUPS, WIDTH)), shape((2, 2, GROUPS, WIDTH))]
        + [shape((GROUPS, 640))] * 4,
        scratch_shapes=[pltpu.VMEM((4, GROUPS, 640), BF)],
        compiler_params=params(40),
        name="split_rows",
    )(meta, q, k, v)


def local_near(meta, ints, floats, q, k, v):
    return pl.pallas_call(
        functools.partial(local_kernel, "AB"),
        grid=(PAIRS,),
        in_specs=[smem(), whole((8, 256)), whole((8, 256))] + [by_residue()] * 3,
        out_specs=by_residue(),
        out_shape=shape((RES, GROUPS, WIDTH)),
        compiler_params=params(40),
        cost_estimate=pl.CostEstimate(flops=3000000000, bytes_accessed=6000000, transcendentals=6000000),
        name="near_queries",
    )(meta, ints, floats, q, k, v)


def local_far(meta, ints, floats, q, k, v, sel, near, cross, before):
    return pl.pallas_call(
        functools.partial(local_kernel, "CD"),
        grid=(PAIRS,),
        in_specs=[smem(), whole((8, 256)), whole((8, 256))]
        + [by_residue()] * 3
        + [by_part(4), by_part(2), by_part(2), by_residue()],
        out_specs=[by_residue(), flat(None), flat(None)],
        out_shape=[
            shape((RES, GROUPS, WIDTH)),
            shape((GROUPS, WIDTH), F32),
            shape((GROUPS, WIDTH), F32),
        ],
        compiler_params=params(40),
        cost_estimate=pl.CostEstimate(flops=2000000000, bytes_accessed=9000000, transcendentals=4000000),
        name="wide_queries",
    )(meta, ints, floats, q, k, v, sel, near, cross, before)


def slide_wide(meta, queries, blocks):
    return pl.pallas_call(
        far_kernel,
        in_specs=[smem()] + [vmem()] * 12,
        out_specs=[vmem()] * 4,
        out_shape=[shape((GROUPS, 384), F32)] * 4,
        compiler_params=params(40),
        cost_estimate=pl.CostEstimate(flops=800000000, bytes_accessed=2000000, transcendentals=1600000),
        name="slide_queries",
    )(meta, *queries, *blocks)


def merge(meta, mixed, o0, lse0, back):
    return pl.pallas_call(
        merge_kernel,
        in_specs=[smem()] + [vmem()] * 7,
        out_specs=vmem(),
        out_shape=shape((ROWS, WIDTH)),
        scratch_shapes=[
            pltpu.VMEM((4, GROUPS, 384), F32),
            pltpu.VMEM((4, 256, WIDTH), BF),
        ],
        compiler_params=params(40),
        name="merge_rows",
    )(meta, mixed, o0, lse0, *back)


def at(x, z, c):
    return (x % NX * NZ + z % NZ) * NC + c


def move(block, to):
    route = [
        (at(x, z, c), at(*to(x, z, c))) for x in range(NX) for z in range(NZ) for c in range(NC)
    ]
    return lax.ppermute(block, "seq", route)


def along_x(steps):
    return lambda x, z, c: (x + steps, z, c)


def along_z(steps):
    return lambda x, z, c: (x, z + steps, c)


def other_core(x, z, c):
    return (x, z, 1 - c)


def next_chip(x, z, c):
    return (x, z ^ 1, c)


def per_device(query_tiles, key_tiles, value_tiles, slide_length):
    device = lax.axis_index("seq").astype(jnp.int32)
    meta = jnp.stack([slide_length[0], device])
    ints, floats = (jnp.asarray(table) for table in tables())
    qt, kt, vt, sel, sel8, z0, z1, z2, z3 = split(meta, query_tiles, key_tiles, value_tiles)
    slabs = [z0] + [move(slab, along_z(step)) for step, slab in ((1, z1), (2, z2), (3, z3))]
    near = move(sel8, next_chip)
    pair = move(sel, other_core)
    mixed = local_near(meta, ints, floats, qt, kt, vt)
    own = jnp.concatenate([slab[:, 256:640] for slab in slabs], axis=0)
    blocks = [own] + [move(own, along_x(step)) for step in (1, 2, 3)]
    cross = move(near, other_core)
    blocks += [move(block, other_core) for block in blocks]
    mixed, o0, lse0 = local_far(meta, ints, floats, qt, kt, vt, pair, near, cross, mixed)
    back = slide_wide(meta, [slab[:, 0:256] for slab in slabs], blocks)
    back = [back[0]] + [move(back[step], along_z(-step)) for step in (1, 2, 3)]
    return merge(meta, mixed, o0, lse0, back)


def solution(mesh):
    placed = (
        P(("slide", "seq"), None),
        P(("slide", "seq"), None),
        P(("slide", "seq"), None),
        P("slide"),
    )
    return jax.shard_map(
        per_device, mesh=mesh, in_specs=placed, out_specs=P(("slide", "seq"), None), check_vma=False
    )
```

profile of v0, /device:TPU:1, one launch (start us, length us, event | category | flops | bytes accessed | tf_op | source)
XLA Modules:
  0.0 86.5 jit_solution(8687727608102789699)
XLA Ops:
  0.7 0.1 pad_add_fusion.meta
  0.7 1.4 %copy-done = bf16[1024,768]{1,0:T(8,128)(2,1)S(1)} copy-done((bf16[1024,768]{1,0:T(8,128)(2,1)S(1)}, bf16[1024,768]{1,0:T(8,128)(2,1)}, u32[]{:S(2)}) %copy-start) | copy-done | bytes 1572888
  2.1 1.4 %copy-done.1 = bf16[1024,768]{1,0:T(8,128)(2,1)S(1)} copy-done((bf16[1024,768]{1,0:T(8,128)(2,1)S(1)}, bf16[1024,768]{1,0:T(8,128)(2,1)}, u32[]{:S(2)}) %copy-start.1) | copy-done | bytes 1572888
  3.5 1.4 %copy-done.2 = bf16[1024,768]{1,0:T(8,128)(2,1)S(1)} copy-done((bf16[1024,768]{1,0:T(8,128)(2,1)S(1)}, bf16[1024,768]{1,0:T(8,128)(2,1)}, u32[]{:S(2)}) %copy-start.2) | copy-done | bytes 1572888
  5.0 6.5 %split_rows.1 = (bf16[16,64,768]{2,1,0:T(8,128)(2,1)S(1)}, bf16[16,64,768]{2,1,0:T(8,128)(2,1)S(1)}, bf16[16,64,768]{2,1,0:T(8,128)(2,1)S(1)}, bf16[4,2,64,768]{...) custom-call(s32[2]{0:T(128)S(1)} %pad_add_fusion.meta, ...), custom_call_target="tpu_custom_call" | custom-call | tf_op jit(solution)/shard_map/split_rows/pallas_call | solution.py:347
  11.5 4.7 %collective-permute-start.5 = (bf16[64,640]{1,0:T(8,128)(2,1)S(1)}, bf16[64,640]{1,0:T(8,128)(2,1)S(1)}, u32[]{:S(2)}, u32[]{:S(2)}) collective-permute-start(bf16[64,640]{1,0:T(8,128)(2,1)S(1)} %get-tuple-element.32), channel_id=1, source_target_pairs={{0,6},{1,7},{2,0},{3,1},{4,2},{5,3},{6,4},{7,5},{8,14},{9,15},{10,... | collective-permute-start | bytes 245768 | tf_op jit(solution)/shard_map/ppermute | solution.py:428
  16.1 0.7 collective-permute-start.3
  16.8 1.5 %collective-permute-start = (bf16[4,2,64,768]{3,2,1,0:T(8,128)(2,1)S(1)}, bf16[4,2,64,768]{3,2,1,0:T(8,128)(2,1)S(1)}, u32[]{:S(2)}, u32[]{:S(2)}) collective-permute-start(bf16[4,2,64,768]{3,2,1,0:T(8,128)(2,1)S(1)} %get-tuple-element.24), channel_id=1, source_target_pairs={{0,1},{1,0},{2,3},{3,2},{4,5},{5,4},{6,7},{7,6},{8,9},{9,8},{10,11... | collective-permute-start | bytes 2359304 | tf_op jit(solution)/shard_map/ppermute | solution.py:428
  18.4 1.9 %collective-permute-start.1 = (bf16[2,2,64,768]{3,2,1,0:T(8,128)(2,1)S(1)}, bf16[2,2,64,768]{3,2,1,0:T(8,128)(2,1)S(1)}, u32[]{:S(2)}, u32[]{:S(2)}) collective-permute-start(bf16[2,2,64,768]{3,2,1,0:T(8,128)(2,1)S(1)} %get-tuple-element.25), channel_id=1, source_target_pairs={{0,2},{1,3},{2,0},{3,1},{4,6},{5,7},{6,4},{7,5},{8,10},{9,11},{10,... | collective-permute-start | bytes 1179656 | tf_op jit(solution)/shard_map/ppermute | solution.py:428
  20.3 0.0 collective-permute-done.5
  20.3 0.7 collective-permute-done.4
  21.0 1.3 %collective-permute-done.3 = bf16[64,640]{1,0:T(8,128)(2,1)S(1)} collective-permute-done((bf16[64,640]{1,0:T(8,128)(2,1)S(1)}, bf16[64,640]{1,0:T(8,128)(2,1)S(1)}, u32[]{:S(2)}, u32[]{:S(2)}) %collective-permute-start.3) | collective-permute-done | bytes 81952 | tf_op jit(solution)/shard_map/ppermute | solution.py:428
  22.4 1.3 %collective-permute-start.6 = (bf16[256,384]{1,0:T(8,128)(2,1)S(1)}, bf16[256,384]{1,0:T(8,128)(2,1)S(1)}, u32[]{:S(2)}, u32[]{:S(2)}) collective-permute-start(bf16[256,384]{1,0:T(8,128)(2,1)S(1)} %pad_maximum_fusion.rest_0_), channel_id=1, source_target_pairs={{0,8},{1,9},{2,10},{3,11},{4,12},{5,13},{6,14},{7,15},{8,16},{9,17... | collective-permute-start | bytes 589832 | tf_op jit(solution)/shard_map/ppermute | solution.py:428
  23.7 2.4 %collective-permute-start.7 = (bf16[256,384]{1,0:T(8,128)(2,1)S(1)}, bf16[256,384]{1,0:T(8,128)(2,1)S(1)}, u32[]{:S(2)}, u32[]{:S(2)}) collective-permute-start(bf16[256,384]{1,0:T(8,128)(2,1)S(1)} %pad_maximum_fusion.rest_0_), channel_id=1, source_target_pairs={{0,16},{1,17},{2,18},{3,19},{4,20},{5,21},{6,22},{7,23},{8,24},{9,... | collective-permute-start | bytes 589832 | tf_op jit(solution)/shard_map/ppermute | solution.py:428
  26.1 1.2 %collective-permute-start.8 = (bf16[256,384]{1,0:T(8,128)(2,1)S(1)}, bf16[256,384]{1,0:T(8,128)(2,1)S(1)}, u32[]{:S(2)}, u32[]{:S(2)}) collective-permute-start(bf16[256,384]{1,0:T(8,128)(2,1)S(1)} %pad_maximum_fusion.rest_0_), channel_id=1, source_target_pairs={{0,24},{1,25},{2,26},{3,27},{4,28},{5,29},{6,30},{7,31},{8,0},{9,1... | collective-permute-start | bytes 589832 | tf_op jit(solution)/shard_map/ppermute | solution.py:428
  27.3 0.9 %collective-permute-done.6.rest_1_ = bf16[256,384]{1,0:T(8,128)(2,1)S(1)} collective-permute-done((bf16[256,384]{1,0:T(8,128)(2,1)S(1)}, bf16[256,384]{1,0:T(8,128)(2,1)S(1)}, u32[]{:S(2)}, u32[]{:S(2)}) %collective-permute-start.6) | collective-permute-done | bytes 196640 | tf_op jit(solution)/shard_map/ppermute | solution.py:428
  28.2 3.9 %collective-permute-start.9 = (bf16[256,384]{1,0:T(8,128)(2,1)S(1)}, bf16[256,384]{1,0:T(8,128)(2,1)S(1)}, u32[]{:S(2)}, u32[]{:S(2)}) collective-permute-start(bf16[256,384]{1,0:T(8,128)(2,1)S(1)} %pad_maximum_fusion.rest_0_), channel_id=1, source_target_pairs={{0,1},{1,0},{2,3},{3,2},{4,5},{5,4},{6,7},{7,6},{8,9},{9,8},{10,11... | collective-permute-start | bytes 589832 | tf_op jit(solution)/shard_map/ppermute | solution.py:428
  32.2 0.0 collective-permute-start.2
  32.2 1.2 %collective-permute-done.7.rest_2_ = bf16[256,384]{1,0:T(8,128)(2,1)S(1)} collective-permute-done((bf16[256,384]{1,0:T(8,128)(2,1)S(1)}, bf16[256,384]{1,0:T(8,128)(2,1)S(1)}, u32[]{:S(2)}, u32[]{:S(2)}) %collective-permute-start.7) | collective-permute-done | bytes 196640 | tf_op jit(solution)/shard_map/ppermute | solution.py:428
  33.4 2.8 %collective-permute-start.10 = (bf16[256,384]{1,0:T(8,128)(2,1)S(1)}, bf16[256,384]{1,0:T(8,128)(2,1)S(1)}, u32[]{:S(2)}, u32[]{:S(2)}) collective-permute-start(bf16[256,384]{1,0:T(8,128)(2,1)S(1)} %collective-permute-done.6.rest_1_), channel_id=1, source_target_pairs={{0,1},{1,0},{2,3},{3,2},{4,5},{5,4},{6,7},{7,6},{8,9},{9,8},{10,11... | collective-permute-start | bytes 589832 | tf_op jit(solution)/shard_map/ppermute | solution.py:428
  36.2 0.0 collective-permute-start.11
  36.2 0.5 collective-permute-start.12
  36.7 18.6 %near_queries.1.rest_3_ = bf16[16,64,768]{2,1,0:T(8,128)(2,1)S(1)} custom-call(s32[2]{0:T(128)S(1)} %pad_add_fusion.meta, s32[8,256]{1,0:T(8,128)S(1)} %copy-done.3, f32[8,256]{1,0:T(8,128)S(1)} %copy-done.4, bf16[16,64,768]{2,1,0:T(8,128)(2,1)S(1)} %get-tuple-element.21.q_ref, bf16[16,64,768]{2,1,0:T(8,128)(2,1)S(1)} %get-tuple-element.22.k_ref, ...), custom_call_target="tpu_custom_call" | custom-call | flops 3000000000 | bytes 6000000 | tf_op jit(solution)/shard_map/near_queries/pallas_call | solution.py:362
  55.4 0.0 collective-permute-done.11.rest_6_
  55.4 0.0 collective-permute-done.12.rest_7_
  55.4 6.4 %slide_queries.1 = (f32[64,384]{1,0:T(8,128)S(1)}, f32[64,384]{1,0:T(8,128)S(1)}, f32[64,384]{1,0:T(8,128)S(1)}, f32[64,384]{1,0:T(8,128)S(1)}) custom-call(s32[2]{0:T(128)S(1)} %pad_add_fusion.meta, bf16[64,256]{1,0:T(8,128)(2,1)S(1)} %slice.24.a0, bf16[64,256]{1,0:T(8,128)(2,1)S(1)} %slice.32.a1, bf16[64,256]{1,0:T(8,128)(2,1)S(1)} %slice.33.a2, ...), custom_call_target="tpu_custom_call" | custom-call | flops 800000000 | bytes 2000000 | tf_op jit(solution)/shard_map/slide_queries/pallas_call | solution.py:394
  61.8 0.8 collective-permute-start.13
  62.6 0.3 collective-permute-start.14
  62.9 0.6 collective-permute-start.15
  63.5 20.5 %wide_queries.1 = (bf16[16,64,768]{2,1,0:T(8,128)(2,1)S(1)}, f32[64,768]{1,0:T(8,128)S(1)}, f32[64,768]{1,0:T(8,128)S(1)}) custom-call(s32[2]{0:T(128)S(1)} %pad_add_fusion.meta, s32[8,256]{1,0:T(8,128)S(1)} %copy-done.3, f32[8,256]{1,0:T(8,128)S(1)} %copy-done.4, bf16[16,64,768]{2,1,0:T(8,128)(2,1)S(1)} %get-tuple-element.21.q_ref, ...), custom_call_target="tpu_custom_call" | custom-call | flops 2000000000 | bytes 9000000 | tf_op jit(solution)/shard_map/wide_queries/pallas_call | solution.py:375
  84.0 0.0 collective-permute-done.13.r1
  84.0 2.4 %merge_rows.1 = bf16[1024,768]{1,0:T(8,128)(2,1)} custom-call(s32[2]{0:T(128)S(1)} %pad_add_fusion.meta, bf16[16,64,768]{2,1,0:T(8,128)(2,1)S(1)} %get-tuple-element.26.mixed, f32[64,768]{1,0:T(8,128)S(1)} %get-tuple-element.27.o0, f32[64,768]{1,0:T(8,128)S(1)} %get-tuple-element.28.lse0, f32[64,384]{1,0:T(8,128)S(1)} %get-tuple-element.33.r0, ...), custom_call_target="tpu_custom_call" | custom-call | tf_op jit(solution)/shard_map/merge_rows/pallas_call | solution.py:406
  (25 shorter events, 0.1 us)
Async XLA Ops:
  0.7 1.4 %copy-start = (bf16[1024,768]{1,0:T(8,128)(2,1)S(1)}, bf16[1024,768]{1,0:T(8,128)(2,1)}, u32[]{:S(2)}) copy-start(bf16[1024,768]{1,0:T(8,128)(2,1)} %q_ref.1) | copy-start | bytes 4718596
  2.1 1.4 %copy-start.1 = (bf16[1024,768]{1,0:T(8,128)(2,1)S(1)}, bf16[1024,768]{1,0:T(8,128)(2,1)}, u32[]{:S(2)}) copy-start(bf16[1024,768]{1,0:T(8,128)(2,1)} %k_ref.1) | copy-start | bytes 4718596
  3.5 1.4 %copy-start.2 = (bf16[1024,768]{1,0:T(8,128)(2,1)S(1)}, bf16[1024,768]{1,0:T(8,128)(2,1)}, u32[]{:S(2)}) copy-start(bf16[1024,768]{1,0:T(8,128)(2,1)} %v_ref.1) | copy-start | bytes 4718596
  5.0 31.8 %copy-start.3 = (s32[8,256]{1,0:T(8,128)S(1)}, s32[8,256]{1,0:T(8,128)}, u32[]{:S(2)}) copy-start(s32[8,256]{1,0:T(8,128)} %constant.8.clone.ints) | copy-start | bytes 24580
  5.0 31.8 %copy-start.4 = (f32[8,256]{1,0:T(8,128)S(1)}, f32[8,256]{1,0:T(8,128)}, u32[]{:S(2)}) copy-start(f32[8,256]{1,0:T(8,128)} %constant.9.clone.floats) | copy-start | bytes 24580
  11.5 8.8 %collective-permute-start.5 = (bf16[64,640]{1,0:T(8,128)(2,1)S(1)}, bf16[64,640]{1,0:T(8,128)(2,1)S(1)}, u32[]{:S(2)}, u32[]{:S(2)}) collective-permute-start(bf16[64,640]{1,0:T(8,128)(2,1)S(1)} %get-tuple-element.32), channel_id=1, source_target_pairs={{0,6},{1,7},{2,0},{3,1},{4,2},{5,3},{6,4},{7,5},{8,14},{9,15},{10,... | collective-permute-start | bytes 245768 | tf_op jit(solution)/shard_map/ppermute | solution.py:428
  16.1 4.9 %collective-permute-start.4 = (bf16[64,640]{1,0:T(8,128)(2,1)S(1)}, bf16[64,640]{1,0:T(8,128)(2,1)S(1)}, u32[]{:S(2)}, u32[]{:S(2)}) collective-permute-start(bf16[64,640]{1,0:T(8,128)(2,1)S(1)} %get-tuple-element.31), channel_id=1, source_target_pairs={{0,4},{1,5},{2,6},{3,7},{4,0},{5,1},{6,2},{7,3},{8,12},{9,13},{10,... | collective-permute-start | bytes 245768 | tf_op jit(solution)/shard_map/ppermute | solution.py:428
  16.1 6.2 %collective-permute-start.3 = (bf16[64,640]{1,0:T(8,128)(2,1)S(1)}, bf16[64,640]{1,0:T(8,128)(2,1)S(1)}, u32[]{:S(2)}, u32[]{:S(2)}) collective-permute-start(bf16[64,640]{1,0:T(8,128)(2,1)S(1)} %get-tuple-element.30), channel_id=1, source_target_pairs={{0,2},{1,3},{2,4},{3,5},{4,6},{5,7},{6,0},{7,1},{8,10},{9,11},{10,... | collective-permute-start | bytes 245768 | tf_op jit(solution)/shard_map/ppermute | solution.py:428
  16.8 46.7 %collective-permute-start = (bf16[4,2,64,768]{3,2,1,0:T(8,128)(2,1)S(1)}, bf16[4,2,64,768]{3,2,1,0:T(8,128)(2,1)S(1)}, u32[]{:S(2)}, u32[]{:S(2)}) collective-permute-start(bf16[4,2,64,768]{3,2,1,0:T(8,128)(2,1)S(1)} %get-tuple-element.24), channel_id=1, source_target_pairs={{0,1},{1,0},{2,3},{3,2},{4,5},{5,4},{6,7},{7,6},{8,9},{9,8},{10,11... | collective-permute-start | bytes 2359304 | tf_op jit(solution)/shard_map/ppermute | solution.py:428
  18.4 13.8 %collective-permute-start.1 = (bf16[2,2,64,768]{3,2,1,0:T(8,128)(2,1)S(1)}, bf16[2,2,64,768]{3,2,1,0:T(8,128)(2,1)S(1)}, u32[]{:S(2)}, u32[]{:S(2)}) collective-permute-start(bf16[2,2,64,768]{3,2,1,0:T(8,128)(2,1)S(1)} %get-tuple-element.25), channel_id=1, source_target_pairs={{0,2},{1,3},{2,0},{3,1},{4,6},{5,7},{6,4},{7,5},{8,10},{9,11},{10,... | collective-permute-start | bytes 1179656 | tf_op jit(solution)/shard_map/ppermute | solution.py:428
  22.4 5.8 %collective-permute-start.6 = (bf16[256,384]{1,0:T(8,128)(2,1)S(1)}, bf16[256,384]{1,0:T(8,128)(2,1)S(1)}, u32[]{:S(2)}, u32[]{:S(2)}) collective-permute-start(bf16[256,384]{1,0:T(8,128)(2,1)S(1)} %pad_maximum_fusion.rest_0_), channel_id=1, source_target_pairs={{0,8},{1,9},{2,10},{3,11},{4,12},{5,13},{6,14},{7,15},{8,16},{9,17... | collective-permute-start | bytes 589832 | tf_op jit(solution)/shard_map/ppermute | solution.py:428
  23.7 9.7 %collective-permute-start.7 = (bf16[256,384]{1,0:T(8,128)(2,1)S(1)}, bf16[256,384]{1,0:T(8,128)(2,1)S(1)}, u32[]{:S(2)}, u32[]{:S(2)}) collective-permute-start(bf16[256,384]{1,0:T(8,128)(2,1)S(1)} %pad_maximum_fusion.rest_0_), channel_id=1, source_target_pairs={{0,16},{1,17},{2,18},{3,19},{4,20},{5,21},{6,22},{7,23},{8,24},{9,... | collective-permute-start | bytes 589832 | tf_op jit(solution)/shard_map/ppermute | solution.py:428
  26.1 10.1 %collective-permute-start.8 = (bf16[256,384]{1,0:T(8,128)(2,1)S(1)}, bf16[256,384]{1,0:T(8,128)(2,1)S(1)}, u32[]{:S(2)}, u32[]{:S(2)}) collective-permute-start(bf16[256,384]{1,0:T(8,128)(2,1)S(1)} %pad_maximum_fusion.rest_0_), channel_id=1, source_target_pairs={{0,24},{1,25},{2,26},{3,27},{4,28},{5,29},{6,30},{7,31},{8,0},{9,1... | collective-permute-start | bytes 589832 | tf_op jit(solution)/shard_map/ppermute | solution.py:428
  28.2 8.0 %collective-permute-start.9 = (bf16[256,384]{1,0:T(8,128)(2,1)S(1)}, bf16[256,384]{1,0:T(8,128)(2,1)S(1)}, u32[]{:S(2)}, u32[]{:S(2)}) collective-permute-start(bf16[256,384]{1,0:T(8,128)(2,1)S(1)} %pad_maximum_fusion.rest_0_), channel_id=1, source_target_pairs={{0,1},{1,0},{2,3},{3,2},{4,5},{5,4},{6,7},{7,6},{8,9},{9,8},{10,11... | collective-permute-start | bytes 589832 | tf_op jit(solution)/shard_map/ppermute | solution.py:428
  32.2 31.4 %collective-permute-start.2 = (bf16[2,2,64,768]{3,2,1,0:T(8,128)(2,1)S(1)}, bf16[2,2,64,768]{3,2,1,0:T(8,128)(2,1)S(1)}, u32[]{:S(2)}, u32[]{:S(2)}) collective-permute-start(bf16[2,2,64,768]{3,2,1,0:T(8,128)(2,1)S(1)} %collective-permute-done.1.rest_1_), channel_id=1, source_target_pairs={{0,1},{1,0},{2,3},{3,2},{4,5},{5,4},{6,7},{7,6},{8,9},{9,8},{10,11... | collective-permute-start | bytes 1179656 | tf_op jit(solution)/shard_map/ppermute | solution.py:428
  33.4 22.0 %collective-permute-start.10 = (bf16[256,384]{1,0:T(8,128)(2,1)S(1)}, bf16[256,384]{1,0:T(8,128)(2,1)S(1)}, u32[]{:S(2)}, u32[]{:S(2)}) collective-permute-start(bf16[256,384]{1,0:T(8,128)(2,1)S(1)} %collective-permute-done.6.rest_1_), channel_id=1, source_target_pairs={{0,1},{1,0},{2,3},{3,2},{4,5},{5,4},{6,7},{7,6},{8,9},{9,8},{10,11... | collective-permute-start | bytes 589832 | tf_op jit(solution)/shard_map/ppermute | solution.py:428
  36.2 19.2 %collective-permute-start.11 = (bf16[256,384]{1,0:T(8,128)(2,1)S(1)}, bf16[256,384]{1,0:T(8,128)(2,1)S(1)}, u32[]{:S(2)}, u32[]{:S(2)}) collective-permute-start(bf16[256,384]{1,0:T(8,128)(2,1)S(1)} %collective-permute-done.7.rest_2_), channel_id=1, source_target_pairs={{0,1},{1,0},{2,3},{3,2},{4,5},{5,4},{6,7},{7,6},{8,9},{9,8},{10,11... | collective-permute-start | bytes 589832 | tf_op jit(solution)/shard_map/ppermute | solution.py:428
  36.2 19.2 %collective-permute-start.12 = (bf16[256,384]{1,0:T(8,128)(2,1)S(1)}, bf16[256,384]{1,0:T(8,128)(2,1)S(1)}, u32[]{:S(2)}, u32[]{:S(2)}) collective-permute-start(bf16[256,384]{1,0:T(8,128)(2,1)S(1)} %collective-permute-done.8.rest_3_), channel_id=1, source_target_pairs={{0,1},{1,0},{2,3},{3,2},{4,5},{5,4},{6,7},{7,6},{8,9},{9,8},{10,11... | collective-permute-start | bytes 589832 | tf_op jit(solution)/shard_map/ppermute | solution.py:428
  61.8 22.2 %collective-permute-start.13 = (f32[64,384]{1,0:T(8,128)S(1)}, f32[64,384]{1,0:T(8,128)S(1)}, u32[]{:S(2)}, u32[]{:S(2)}) collective-permute-start(f32[64,384]{1,0:T(8,128)S(1)} %get-tuple-element.34), channel_id=1, source_target_pairs={{0,6},{1,7},{2,0},{3,1},{4,2},{5,3},{6,4},{7,5},{8,14},{9,15},{10,... | collective-permute-start | bytes 294920 | tf_op jit(solution)/shard_map/ppermute | solution.py:428
  62.6 21.4 %collective-permute-start.14 = (f32[64,384]{1,0:T(8,128)S(1)}, f32[64,384]{1,0:T(8,128)S(1)}, u32[]{:S(2)}, u32[]{:S(2)}) collective-permute-start(f32[64,384]{1,0:T(8,128)S(1)} %get-tuple-element.35), channel_id=1, source_target_pairs={{0,4},{1,5},{2,6},{3,7},{4,0},{5,1},{6,2},{7,3},{8,12},{9,13},{10,... | collective-permute-start | bytes 294920 | tf_op jit(solution)/shard_map/ppermute | solution.py:428
  62.9 21.1 %collective-permute-start.15 = (f32[64,384]{1,0:T(8,128)S(1)}, f32[64,384]{1,0:T(8,128)S(1)}, u32[]{:S(2)}, u32[]{:S(2)}) collective-permute-start(f32[64,384]{1,0:T(8,128)S(1)} %get-tuple-element.36), channel_id=1, source_target_pairs={{0,2},{1,3},{2,4},{3,5},{4,6},{5,7},{6,0},{7,1},{8,10},{9,11},{10,... | collective-permute-start | bytes 294920 | tf_op jit(solution)/shard_map/ppermute | solution.py:428
where the time goes:
time: 86.7 us; the launch traced here: 86.5 us
  Pallas kernels  54.4 us (63%)
  starting transfers between devices  22.7 us (26%)
  local copies, waits for them, and re-layouts  4.27 us (5%)
  waiting for transfers between devices  4.21 us (5%)
    ppermute x16, starting transfers between devices, move(): return lax.ppermute(block, 'seq', route)  22.7 us
    pallas_call x1, Pallas kernels, local_far(): pl.pallas_call(functools.partial(local_kernel, 'CD'), grid=(PAIRS,), in_s...  20.5 us
    pallas_call x1, Pallas kernels, local_near(): pl.pallas_call(functools.partial(local_kernel, 'AB'), grid=(PAIRS,), in_s...  18.6 us
    pallas_call x1, Pallas kernels, split(): pl.pallas_call(split_kernel, grid=(PAIRS,), in_specs=[smem(), rows, rows,...  6.52 us
    pallas_call x1, Pallas kernels, slide_wide(): pl.pallas_call(far_kernel, in_specs=[smem()] + [vmem()] * 12, out_specs=[...  6.41 us
    unnamed x10, local copies, waits for them, and re-layouts  4.23 us
    ppermute x16, waiting for transfers between devices, move(): return lax.ppermute(block, 'seq', route)  4.21 us
    pallas_call x1, Pallas kernels, merge(): pl.pallas_call(merge_kernel, in_specs=[smem()] + [vmem()] * 7, out_specs=...  2.45 us
  transfers between devices with their start and end apart: 16, of which 4 were waited for; matrix products, arithmetic and copies ran while one was open for 0% of the time, Pallas kernels for 53%

commit v1 on v0

--- a/solution.py
+++ b/solution.py
@@ -132,7 +132,24 @@
     return total, peak
 
 
-def local_kernel(classes, meta, ints, floats, q_ref, k_ref, v_ref, *rest):
+def local_kernel(classes, first, many, meta, ints, floats, *refs):
+    def body(step, carry):
+        lanes = pl.ds(pl.multiple_of((first + step) * 128, 128), 128)
+        here = pl.ds(pl.multiple_of(step * 128, 128), 128)
+        views = [ref.at[:, :, lanes] for ref in refs[:3]]
+        if classes == "CD":
+            views += [ref.at[:, :, :, lanes] for ref in refs[3:6]]
+            views += [ref.at[:, :, here] for ref in refs[6:8]]
+            views += [ref.at[:, here] for ref in refs[8:10]]
+        else:
+            views += [refs[3].at[:, :, here]]
+        local_pair(classes, first + step, meta, ints, floats, *views)
+        return carry
+
+    lax.fori_loop(0, many, body, 0)
+
+
+def local_pair(classes, pair, meta, ints, floats, q_ref, k_ref, v_ref, *rest):
     far = classes == "CD"
     if far:
         sel, near, cross, before, out, o0, lse0 = rest
@@ -142,8 +159,10 @@
     bound = meta[0]
     device = meta[1]
     low = lane_low(256)
+    low_all = lane_low(256 if far else 768)
+    high_all = jnp.logical_not(low_all)
     for parity in range(2):
-        head = 2 * pl.program_id(0) + parity
+        head = 2 * pair + parity
         mine = low if parity == 0 else jnp.logical_not(low)
 
         def gathered(ref, order, half):
@@ -176,45 +195,92 @@
             )
             lane = lax.broadcasted_iota(jnp.int32, (1, 256), 1)
             next_device = jnp.where(lane < 128, device ^ 2, device ^ 3)
+        groups = [(name, 0) for name in classes] + [(name, 1) for name in classes[::-1]]
+        tiles = []
         for half in range(2):
-            own = half * 512
-            away = 512 - own
-            for name in classes:
-                order = CLASS_U[name]
-                query = gathered(q_ref, order, half)
-                count = query.shape[0]
-                query = jnp.where(mine[:count], query, jnp.zeros_like(query)) * 0.125
-                query = query.astype(BF)
-                keys = [odd_k[half], even_k[half]]
-                values = [odd_v[half], even_v[half]]
-                cap = "ABCD".index(name)
-                biases = [bias(0, 2, device, own, 0), bias(1, 2, device, own, cap)]
-                if cap >= 1:
-                    keys.append(even_k[1 - half])
-                    values.append(even_v[1 - half])
-                    biases.append(bias(1, 2, device, away, (0, 0, 4, 5)[cap]))
-                if cap >= 2:
-                    keys.append(pair_k)
-                    values.append(pair_v)
-                    biases.append(bias(3, 4, device ^ 1, 0, (0, 0, 0, 6)[cap]))
-                if cap >= 3:
-                    keys.append(next_k)
-                    values.append(next_v)
-                    biases.append(bias(5, 4, next_device, 0, 0))
-                total, peak = softmax_parts(query, keys, values, biases)
-                sums = pltpu.roll(total, 64, 1)
-                result = total / sums
-                rounded = result.astype(BF)
-                for at, u in enumerate(order):
-                    spot = ((u + head) & 15, slice(half * HALF, (half + 1) * HALF), slice(None))
-                    out[spot] = jnp.where(
-                        mine[:HALF], rounded[at * HALF : (at + 1) * HALF, :], out[spot]
+            tiles.append((odd_k[half], odd_v[half], lambda cap, side, half=half: side == half))
+            tiles.append(
+                (even_k[half], even_v[half], lambda cap, side, half=half: side == half or cap >= 1)
+            )
+        if far:
+            tiles.append((pair_k, pair_v, lambda cap, side: True))
+            tiles.append((next_k, next_v, lambda cap, side: cap >= 3))
+
+        def tile_bias(tile, cap, side):
+            if tile >= 4:
+                if tile == 5:
+                    return bias(5, 4, next_device, 0, 0)
+                return bias(3, 4, device ^ 1, 0, (0, 0, 0, 6)[cap])
+            offset = tile // 2 * 512
+            if tile % 2 == 0:
+                return bias(0, 2, device, offset, 0)
+            row = cap if tile // 2 == side else (0, 0, 4, 5)[cap]
+            return bias(1, 2, device, offset, row)
+
+        pieces, starts, count = [], [], 0
+        for name, side in groups:
+            pieces.append(gathered(q_ref, CLASS_U[name], side))
+            starts.append(count)
+            count += pieces[-1].shape[0]
+        starts.append(count)
+        query = jnp.concatenate(pieces, axis=0)
+        query = (jnp.where(low_all if parity == 0 else high_all, query, jnp.zeros_like(query)) * 0.125).astype(BF)
+        caps = [("ABCD".index(name), side) for name, side in groups]
+        scores, spans = [], []
+        for key, value, member in tiles:
+            inside = [at for at, (cap, side) in enumerate(caps) if member(cap, side)]
+            first, last = inside[0], inside[-1] + 1
+            spans.append((first, last))
+            scores.append(
+                lax.dot_general(
+                    query[starts[first] : starts[last]],
+                    key,
+                    (((1,), (1,)), ((), ())),
+                    preferred_element_type=F32,
+                )
+            )
+        weights = [[] for _ in tiles]
+        peaks = []
+        for at, (cap, side) in enumerate(caps):
+            held = []
+            for tile, (first, last) in enumerate(spans):
+                if first <= at < last:
+                    base = starts[first]
+                    held.append(
+                        (
+                            tile,
+                            scores[tile][starts[at] - base : starts[at + 1] - base]
+                            + tile_bias(tile, cap, side),
+                        )
                     )
-                if name == "D":
-                    rows = slice(half * HALF, (half + 1) * HALF)
-                    log_total = peak[HALF:] + jnp.log(sums[HALF:])
-                    o0[rows, :] = jnp.where(mine[:HALF], result[HALF:], o0[rows, :])
-                    lse0[rows, :] = jnp.where(mine[:HALF], log_total, lse0[rows, :])
+            peak = functools.reduce(jnp.maximum, [score for _, score in held])
+            peak = jnp.max(peak, axis=1, keepdims=True)
+            peaks.append(peak)
+            for tile, score in held:
+                weights[tile].append(jnp.exp(score - peak).astype(BF))
+        totals = [None] * len(caps)
+        for tile, (first, last) in enumerate(spans):
+            part = jnp.dot(
+                jnp.concatenate(weights[tile], axis=0), tiles[tile][1], preferred_element_type=F32
+            )
+            for at in range(first, last):
+                rows = part[starts[at] - starts[first] : starts[at + 1] - starts[first]]
+                totals[at] = rows if totals[at] is None else totals[at] + rows
+        for at, (name, half) in enumerate(groups):
+            total, peak = totals[at], peaks[at]
+            sums = pltpu.roll(total, 64, 1)
+            result = total / sums
+            rounded = result.astype(BF)
+            for row, u in enumerate(CLASS_U[name]):
+                spot = ((u + head) & 15, slice(half * HALF, (half + 1) * HALF), slice(None))
+                out[spot] = jnp.where(
+                    mine[:HALF], rounded[row * HALF : (row + 1) * HALF, :], out[spot]
+                )
+            if name == "D":
+                rows = slice(half * HALF, (half + 1) * HALF)
+                log_total = peak[HALF:] + jnp.log(sums[HALF:])
+                o0[rows, :] = jnp.where(mine[:HALF], result[HALF:], o0[rows, :])
+                lse0[rows, :] = jnp.where(mine[:HALF], log_total, lse0[rows, :])
 
 
 def far_kernel(meta, a0, a1, a2, a3, *rest):
@@ -268,7 +334,9 @@
         out[:, 256:384] = jnp.where(low, first[1], second[1])
 
 
-def merge_kernel(meta, mixed, o0, lse0, r0, r1, r2, r3, out, stage, grid_rows):
+def merge_kernel(meta, *refs):
+    mixed, o0, lse0 = refs[0:2], refs[2:4], refs[4:6]
+    r0, r1, r2, r3, out, stage, grid_rows = refs[6:]
     bound = meta[0]
     device = meta[1]
     zpos = device // 2 % NZ
@@ -277,6 +345,7 @@
     low = lane_low(GROUPS)
     for pair in range(PAIRS):
         lanes = slice(pair * 128, pair * 128 + 128)
+        piece, inner = pair // 3, slice(pair % 3 * 128, pair % 3 * 128 + 128)
         if pair in PAIR_OF:
             slot = (PAIR_OF.index(pair) - zpos) & 3
             away, away_lse = stage[slot, :, 0:128], stage[slot, :, 256:384]
@@ -286,14 +355,14 @@
             right = stage[(first + 1 - zpos) & 3, :, 128:256]
             away = jnp.where(low, pltpu.roll(left, 64, 1), right)
             away_lse = jnp.where(low, left, pltpu.roll(right, 64, 1))
-        here, here_lse = o0[:, lanes], lse0[:, lanes]
+        here, here_lse = o0[piece][:, inner], lse0[piece][:, inner]
         top = jnp.maximum(here_lse, away_lse)
         weight = jnp.exp(here_lse - top)
         away_weight = jnp.exp(away_lse - top)
         blended = (here * weight + away * away_weight) / (weight + away_weight)
         blended = blended.astype(BF)
         for res in range(RES):
-            rows = mixed[res, :, lanes]
+            rows = mixed[piece][res, :, inner]
             if res == 2 * pair:
                 rows = jnp.where(low, blended, rows)
             if res == 2 * pair + 1:
@@ -358,34 +427,34 @@
     )(meta, q, k, v)
 
 
-def local_near(meta, ints, floats, q, k, v):
+def local_near(first, many, meta, ints, floats, q, k, v):
     return pl.pallas_call(
-        functools.partial(local_kernel, "AB"),
-        grid=(PAIRS,),
-        in_specs=[smem(), whole((8, 256)), whole((8, 256))] + [by_residue()] * 3,
-        out_specs=by_residue(),
-        out_shape=shape((RES, GROUPS, WIDTH)),
+        functools.partial(local_kernel, "AB", first, many),
+        in_specs=[smem()] + [vmem()] * 5,
+        out_specs=vmem(),
+        out_shape=shape((RES, GROUPS, many * 128)),
         compiler_params=params(40),
-        cost_estimate=pl.CostEstimate(flops=3000000000, bytes_accessed=6000000, transcendentals=6000000),
+        cost_estimate=pl.CostEstimate(
+            flops=many * 500000000, bytes_accessed=1000000, transcendentals=many * 900000
+        ),
         name="near_queries",
     )(meta, ints, floats, q, k, v)
 
 
-def local_far(meta, ints, floats, q, k, v, sel, near, cross, before):
+def local_far(first, many, meta, ints, floats, q, k, v, sel, near, cross, before):
     return pl.pallas_call(
-        functools.partial(local_kernel, "CD"),
-        grid=(PAIRS,),
-        in_specs=[smem(), whole((8, 256)), whole((8, 256))]
-        + [by_residue()] * 3
-        + [by_part(4), by_part(2), by_part(2), by_residue()],
-        out_specs=[by_residue(), flat(None), flat(None)],
+        functools.partial(local_kernel, "CD", first, many),
+        in_specs=[smem()] + [vmem()] * 9,
+        out_specs=[vmem()] * 3,
         out_shape=[
-            shape((RES, GROUPS, WIDTH)),
-            shape((GROUPS, WIDTH), F32),
-            shape((GROUPS, WIDTH), F32),
+            shape((RES, GROUPS, many * 128)),
+            shape((GROUPS, many * 128), F32),
+            shape((GROUPS, many * 128), F32),
         ],
         compiler_params=params(40),
-        cost_estimate=pl.CostEstimate(flops=2000000000, bytes_accessed=9000000, transcendentals=4000000),
+        cost_estimate=pl.CostEstimate(
+            flops=many * 400000000, bytes_accessed=1000000, transcendentals=many * 600000
+        ),
         name="wide_queries",
     )(meta, ints, floats, q, k, v, sel, near, cross, before)
 
@@ -405,7 +474,7 @@
 def merge(meta, mixed, o0, lse0, back):
     return pl.pallas_call(
         merge_kernel,
-        in_specs=[smem()] + [vmem()] * 7,
+        in_specs=[smem()] + [vmem()] * 10,
         out_specs=vmem(),
         out_shape=shape((ROWS, WIDTH)),
         scratch_shapes=[
@@ -414,7 +483,7 @@
         ],
         compiler_params=params(40),
         name="merge_rows",
-    )(meta, mixed, o0, lse0, *back)
+    )(meta, *mixed, *o0, *lse0, *back)
 
 
 def at(x, z, c):
@@ -452,14 +521,25 @@
     slabs = [z0] + [move(slab, along_z(step)) for step, slab in ((1, z1), (2, z2), (3, z3))]
     near = move(sel8, next_chip)
     pair = move(sel, other_core)
-    mixed = local_near(meta, ints, floats, qt, kt, vt)
+    local = (ints, floats, qt, kt, vt)
+    mixed = [local_near(0, 3, meta, *local)]
+    slabs, mixed[0] = lax.optimization_barrier((slabs, mixed[0]))
     own = jnp.concatenate([slab[:, 256:640] for slab in slabs], axis=0)
-    blocks = [own] + [move(own, along_x(step)) for step in (1, 2, 3)]
+    own, later = lax.optimization_barrier((own, meta))
+    moved = [move(own, along_x(step)) for step in (1, 2, 3)]
     cross = move(near, other_core)
+    mixed.append(local_near(3, 3, later, *local))
+    moved, mixed[1] = lax.optimization_barrier((moved, mixed[1]))
+    blocks = [own] + moved
     blocks += [move(block, other_core) for block in blocks]
-    mixed, o0, lse0 = local_far(meta, ints, floats, qt, kt, vt, pair, near, cross, mixed)
+    moved, last = lax.optimization_barrier((moved, meta))
+    wide = [local_far(0, 3, last, *local, pair, near, cross, mixed[0])]
+    blocks, wide[0] = lax.optimization_barrier((blocks, wide[0]))
     back = slide_wide(meta, [slab[:, 0:256] for slab in slabs], blocks)
+    back, last = lax.optimization_barrier((back, meta))
     back = [back[0]] + [move(back[step], along_z(-step)) for step in (1, 2, 3)]
+    wide.append(local_far(3, 3, last, *local, pair, near, cross, mixed[1]))
+    mixed, o0, lse0 = zip(*wide)
     return merge(meta, mixed, o0, lse0, back)
 
 

time: 86.7 us -> 71 us (0.82)
  Pallas kernels: 54.4 us -> 36.7 us
  waiting for transfers between devices: 4.21 us -> 6.11 us
    pallas_call x3 -> x5, Pallas kernels: 41.5 us -> 23.8 us  [the longest x2 11.8 us: local_near(): pl.pallas_call(functools.partial(local_kernel, 'AB', first, many), in_spe...]
    ppermute x16, waiting for transfers between devices: 4.21 us -> 6.11 us  [move(): return lax.ppermute(block, 'seq', route)]
  transfers between devices with their start and end apart: 16 -> 16, of which waited for: 4 -> 4; matrix products, arithmetic and copies ran while one was open for 0% -> 0% of each run, Pallas kernels for 53% -> 30%
where the time goes in v1:
time: 71 us; the launch traced here: 70.8 us
  Pallas kernels  36.7 us (52%)
  starting transfers between devices  22.7 us (32%)
  waiting for transfers between devices  6.11 us (9%)
  local copies, waits for them, and re-layouts  4.27 us (6%)
  between operations  0.85 us (1%)
    ppermute x16, starting transfers between devices, move(): return lax.ppermute(block, 'seq', route)  22.7 us
    pallas_call x2, Pallas kernels, local_near(): pl.pallas_call(functools.partial(local_kernel, 'AB', first, many), in_spe...  11.8 us
    pallas_call x2, Pallas kernels, local_far(): pl.pallas_call(functools.partial(local_kernel, 'CD', first, many), in_spe...  9.52 us
    pallas_call x1, Pallas kernels, split(): pl.pallas_call(split_kernel, grid=(PAIRS,), in_specs=[smem(), rows, rows,...  6.52 us
    pallas_call x1, Pallas kernels, slide_wide(): pl.pallas_call(far_kernel, in_specs=[smem()] + [vmem()] * 12, out_specs=[...  6.42 us
    ppermute x16, waiting for transfers between devices, move(): return lax.ppermute(block, 'seq', route)  6.11 us
    unnamed x10, local copies, waits for them, and re-layouts  4.23 us
    pallas_call x1, Pallas kernels, merge(): pl.pallas_call(merge_kernel, in_specs=[smem()] + [vmem()] * 10, out_specs...  2.47 us
  transfers between devices with their start and end apart: 16, of which 4 were waited for; matrix products, arithmetic and copies ran while one was open for 0% of the time, Pallas kernels for 30%

profile of v1, /device:TPU:1, one launch (start us, length us, event | category | flops | bytes accessed | tf_op | source)
XLA Modules:
  0.0 70.8 jit_solution(14665421681516750754)
XLA Ops:
  0.7 0.1 pad_add_fusion.meta
  0.7 1.4 %copy-done = bf16[1024,768]{1,0:T(8,128)(2,1)S(1)} copy-done((bf16[1024,768]{1,0:T(8,128)(2,1)S(1)}, bf16[1024,768]{1,0:T(8,128)(2,1)}, u32[]{:S(2)}) %copy-start) | copy-done | bytes 1572888
  2.1 1.4 %copy-done.1 = bf16[1024,768]{1,0:T(8,128)(2,1)S(1)} copy-done((bf16[1024,768]{1,0:T(8,128)(2,1)S(1)}, bf16[1024,768]{1,0:T(8,128)(2,1)}, u32[]{:S(2)}) %copy-start.1) | copy-done | bytes 1572888
  3.5 1.4 %copy-done.2 = bf16[1024,768]{1,0:T(8,128)(2,1)S(1)} copy-done((bf16[1024,768]{1,0:T(8,128)(2,1)S(1)}, bf16[1024,768]{1,0:T(8,128)(2,1)}, u32[]{:S(2)}) %copy-start.2) | copy-done | bytes 1572888
  5.0 6.5 %split_rows.1 = (bf16[16,64,768]{2,1,0:T(8,128)(2,1)S(1)}, bf16[16,64,768]{2,1,0:T(8,128)(2,1)S(1)}, bf16[16,64,768]{2,1,0:T(8,128)(2,1)S(1)}, bf16[4,2,64,768]{...) custom-call(s32[2]{0:T(128)S(1)} %pad_add_fusion.meta, ...), custom_call_target="tpu_custom_call" | custom-call | tf_op jit(solution)/shard_map/split_rows/pallas_call | solution.py:416
  11.5 2.5 %collective-permute-start.11 = (bf16[2,2,64,768]{3,2,1,0:T(8,128)(2,1)S(1)}, bf16[2,2,64,768]{3,2,1,0:T(8,128)(2,1)S(1)}, u32[]{:S(2)}, u32[]{:S(2)}) collective-permute-start(bf16[2,2,64,768]{3,2,1,0:T(8,128)(2,1)S(1)} %get-tuple-element.70), channel_id=1, source_target_pairs={{0,2},{1,3},{2,0},{3,1},{4,6},{5,7},{6,4},{7,5},{8,10},{9,11},{10,... | collective-permute-start | bytes 1179656 | tf_op jit(solution)/shard_map/ppermute | solution.py:497
  14.0 1.0 %collective-permute-start.10 = (bf16[4,2,64,768]{3,2,1,0:T(8,128)(2,1)S(1)}, bf16[4,2,64,768]{3,2,1,0:T(8,128)(2,1)S(1)}, u32[]{:S(2)}, u32[]{:S(2)}) collective-permute-start(bf16[4,2,64,768]{3,2,1,0:T(8,128)(2,1)S(1)} %get-tuple-element.69), channel_id=1, source_target_pairs={{0,1},{1,0},{2,3},{3,2},{4,5},{5,4},{6,7},{7,6},{8,9},{9,8},{10,11... | collective-permute-start | bytes 2359304 | tf_op jit(solution)/shard_map/ppermute | solution.py:497
  15.0 0.0 collective-permute-start
  15.0 3.4 %collective-permute-start.1 = (bf16[64,640]{1,0:T(8,128)(2,1)S(1)}, bf16[64,640]{1,0:T(8,128)(2,1)S(1)}, u32[]{:S(2)}, u32[]{:S(2)}) collective-permute-start(bf16[64,640]{1,0:T(8,128)(2,1)S(1)} %get-tuple-element.54), channel_id=1, source_target_pairs={{0,4},{1,5},{2,6},{3,7},{4,0},{5,1},{6,2},{7,3},{8,12},{9,13},{10,... | collective-permute-start | bytes 245768 | tf_op jit(solution)/shard_map/ppermute | solution.py:497
  18.4 1.9 %collective-permute-start.2 = (bf16[64,640]{1,0:T(8,128)(2,1)S(1)}, bf16[64,640]{1,0:T(8,128)(2,1)S(1)}, u32[]{:S(2)}, u32[]{:S(2)}) collective-permute-start(bf16[64,640]{1,0:T(8,128)(2,1)S(1)} %get-tuple-element.55), channel_id=1, source_target_pairs={{0,6},{1,7},{2,0},{3,1},{4,2},{5,3},{6,4},{7,5},{8,14},{9,15},{10,... | collective-permute-start | bytes 245768 | tf_op jit(solution)/shard_map/ppermute | solution.py:497
  20.4 2.5 %collective-permute-done.11.refs_4_ = bf16[2,2,64,768]{3,2,1,0:T(8,128)(2,1)S(1)} collective-permute-done((bf16[2,2,64,768]{3,2,1,0:T(8,128)(2,1)S(1)}, bf16[2,2,64,768]{3,2,1,0:T(8,128)(2,1)S(1)}, u32[]{:S(2)}, u32[]{:S(2)}) %collective-permute-start.11) | collective-permute-done | bytes 393248 | tf_op jit(solution)/shard_map/ppermute | solution.py:497
  22.9 2.1 %collective-permute-start.12 = (bf16[2,2,64,768]{3,2,1,0:T(8,128)(2,1)S(1)}, bf16[2,2,64,768]{3,2,1,0:T(8,128)(2,1)S(1)}, u32[]{:S(2)}, u32[]{:S(2)}) collective-permute-start(bf16[2,2,64,768]{3,2,1,0:T(8,128)(2,1)S(1)} %collective-permute-done.11.refs_4_), channel_id=1, source_target_pairs={{0,1},{1,0},{2,3},{3,2},{4,5},{5,4},{6,7},{7,6},{8,9},{9,8},{10,11... | collective-permute-start | bytes 1179656 | tf_op jit(solution)/shard_map/ppermute | solution.py:497
  25.0 5.9 %near_queries.2.refs_6_ = bf16[16,64,384]{2,1,0:T(8,128)(2,1)S(1)} custom-call(s32[2]{0:T(128)S(1)} %pad_add_fusion.meta, s32[8,256]{1,0:T(8,128)S(1)} %copy-done.3, f32[8,256]{1,0:T(8,128)S(1)} %copy-done.4, bf16[16,64,768]{2,1,0:T(8,128)(2,1)S(1)} %get-tuple-element.56.refs_0_, bf16[16,64,768]{2,1,0:T(8,128)(2,1)S(1)} %get-tuple-element.57.refs_1_, ...), custom_call_target="tpu_custom_call" | custom-call | flops 1500000000 | bytes 1000000 | tf_op jit(solution)/shard_map/near_queries/pallas_call | solution.py:431
  30.9 0.0 collective-permute-done
  30.9 0.0 collective-permute-done.1
  31.0 1.4 %collective-permute-start.3 = (bf16[256,384]{1,0:T(8,128)(2,1)S(1)}, bf16[256,384]{1,0:T(8,128)(2,1)S(1)}, u32[]{:S(2)}, u32[]{:S(2)}) collective-permute-start(bf16[256,384]{1,0:T(8,128)(2,1)S(1)} %pad_maximum_fusion.rest_0_), channel_id=1, source_target_pairs={{0,8},{1,9},{2,10},{3,11},{4,12},{5,13},{6,14},{7,15},{8,16},{9,17... | collective-permute-start | bytes 589832 | tf_op jit(solution)/shard_map/ppermute | solution.py:497
  32.3 2.4 %collective-permute-start.4 = (bf16[256,384]{1,0:T(8,128)(2,1)S(1)}, bf16[256,384]{1,0:T(8,128)(2,1)S(1)}, u32[]{:S(2)}, u32[]{:S(2)}) collective-permute-start(bf16[256,384]{1,0:T(8,128)(2,1)S(1)} %pad_maximum_fusion.rest_0_), channel_id=1, source_target_pairs={{0,16},{1,17},{2,18},{3,19},{4,20},{5,21},{6,22},{7,23},{8,24},{9,... | collective-permute-start | bytes 589832 | tf_op jit(solution)/shard_map/ppermute | solution.py:497
  34.8 1.2 %collective-permute-start.5 = (bf16[256,384]{1,0:T(8,128)(2,1)S(1)}, bf16[256,384]{1,0:T(8,128)(2,1)S(1)}, u32[]{:S(2)}, u32[]{:S(2)}) collective-permute-start(bf16[256,384]{1,0:T(8,128)(2,1)S(1)} %pad_maximum_fusion.rest_0_), channel_id=1, source_target_pairs={{0,24},{1,25},{2,26},{3,27},{4,28},{5,29},{6,30},{7,31},{8,0},{9,1... | collective-permute-start | bytes 589832 | tf_op jit(solution)/shard_map/ppermute | solution.py:497
  36.0 5.9 %near_queries.3.refs_6_ = bf16[16,64,384]{2,1,0:T(8,128)(2,1)S(1)} custom-call(s32[2]{0:T(128)S(1)} %pad_add_fusion.meta, s32[8,256]{1,0:T(8,128)S(1)} %copy-done.3, f32[8,256]{1,0:T(8,128)S(1)} %copy-done.4, bf16[16,64,768]{2,1,0:T(8,128)(2,1)S(1)} %get-tuple-element.56.refs_0_, bf16[16,64,768]{2,1,0:T(8,128)(2,1)S(1)} %get-tuple-element.57.refs_1_, ...), custom_call_target="tpu_custom_call" | custom-call | flops 1500000000 | bytes 1000000 | tf_op jit(solution)/shard_map/near_queries/pallas_call | solution.py:431
  41.9 0.9 %collective-permute-start.6 = (bf16[256,384]{1,0:T(8,128)(2,1)S(1)}, bf16[256,384]{1,0:T(8,128)(2,1)S(1)}, u32[]{:S(2)}, u32[]{:S(2)}) collective-permute-start(bf16[256,384]{1,0:T(8,128)(2,1)S(1)} %pad_maximum_fusion.rest_0_), channel_id=1, source_target_pairs={{0,1},{1,0},{2,3},{3,2},{4,5},{5,4},{6,7},{7,6},{8,9},{9,8},{10,11... | collective-permute-start | bytes 589832 | tf_op jit(solution)/shard_map/ppermute | solution.py:497
  42.8 1.3 %collective-permute-done.4.rest_2_ = bf16[256,384]{1,0:T(8,128)(2,1)S(1)} collective-permute-done((bf16[256,384]{1,0:T(8,128)(2,1)S(1)}, bf16[256,384]{1,0:T(8,128)(2,1)S(1)}, u32[]{:S(2)}, u32[]{:S(2)}) %collective-permute-start.4) | collective-permute-done | bytes 196640 | tf_op jit(solution)/shard_map/ppermute | solution.py:497
  44.1 0.8 %collective-permute-start.7 = (bf16[256,384]{1,0:T(8,128)(2,1)S(1)}, bf16[256,384]{1,0:T(8,128)(2,1)S(1)}, u32[]{:S(2)}, u32[]{:S(2)}) collective-permute-start(bf16[256,384]{1,0:T(8,128)(2,1)S(1)} %collective-permute-done.3.rest_1_), channel_id=1, source_target_pairs={{0,1},{1,0},{2,3},{3,2},{4,5},{5,4},{6,7},{7,6},{8,9},{9,8},{10,11... | collective-permute-start | bytes 589832 | tf_op jit(solution)/shard_map/ppermute | solution.py:497
  44.9 0.0 collective-permute-start.8
  44.9 0.5 collective-permute-start.9
  45.4 4.8 %wide_queries.2 = (bf16[16,64,384]{2,1,0:T(8,128)(2,1)S(1)}, f32[64,384]{1,0:T(8,128)S(1)}, f32[64,384]{1,0:T(8,128)S(1)}) custom-call(s32[2]{0:T(128)S(1)} %pad_add_fusion.meta, s32[8,256]{1,0:T(8,128)S(1)} %copy-done.3, f32[8,256]{1,0:T(8,128)S(1)} %copy-done.4, bf16[16,64,768]{2,1,0:T(8,128)(2,1)S(1)} %get-tuple-element.56.refs_0_, ...), custom_call_target="tpu_custom_call" | custom-call | flops 1200000000 | bytes 1000000 | tf_op jit(solution)/shard_map/wide_queries/pallas_call | solution.py:445
  50.2 6.4 %slide_queries.1 = (f32[64,384]{1,0:T(8,128)S(1)}, f32[64,384]{1,0:T(8,128)S(1)}, f32[64,384]{1,0:T(8,128)S(1)}, f32[64,384]{1,0:T(8,128)S(1)}) custom-call(s32[2]{0:T(128)S(1)} %pad_add_fusion.meta, bf16[64,256]{1,0:T(8,128)(2,1)S(1)} %slice.28.a0, bf16[64,256]{1,0:T(8,128)(2,1)S(1)} %slice.29.a1, bf16[64,256]{1,0:T(8,128)(2,1)S(1)} %slice.30.a2, ...), custom_call_target="tpu_custom_call" | custom-call | flops 800000000 | bytes 2000000 | tf_op jit(solution)/shard_map/slide_queries/pallas_call | solution.py:463
  56.7 3.8 %collective-permute-start.13 = (f32[64,384]{1,0:T(8,128)S(1)}, f32[64,384]{1,0:T(8,128)S(1)}, u32[]{:S(2)}, u32[]{:S(2)}) collective-permute-start(f32[64,384]{1,0:T(8,128)S(1)} %get-tuple-element.96), channel_id=1, source_target_pairs={{0,6},{1,7},{2,0},{3,1},{4,2},{5,3},{6,4},{7,5},{8,14},{9,15},{10,... | collective-permute-start | bytes 294920 | tf_op jit(solution)/shard_map/ppermute | solution.py:497
  60.5 0.7 collective-permute-start.15
  61.2 4.7 %wide_queries.3 = (bf16[16,64,384]{2,1,0:T(8,128)(2,1)S(1)}, f32[64,384]{1,0:T(8,128)S(1)}, f32[64,384]{1,0:T(8,128)S(1)}) custom-call(s32[2]{0:T(128)S(1)} %pad_add_fusion.meta, s32[8,256]{1,0:T(8,128)S(1)} %copy-done.3, f32[8,256]{1,0:T(8,128)S(1)} %copy-done.4, bf16[16,64,768]{2,1,0:T(8,128)(2,1)S(1)} %get-tuple-element.56.refs_0_, ...), custom_call_target="tpu_custom_call" | custom-call | flops 1200000000 | bytes 1000000 | tf_op jit(solution)/shard_map/wide_queries/pallas_call | solution.py:445
  66.0 0.2 collective-permute-done.14.refs_8_
  66.2 2.1 %collective-permute-done.15.refs_9_ = f32[64,384]{1,0:T(8,128)S(1)} collective-permute-done((f32[64,384]{1,0:T(8,128)S(1)}, f32[64,384]{1,0:T(8,128)S(1)}, u32[]{:S(2)}, u32[]{:S(2)}) %collective-permute-start.15) | collective-permute-done | bytes 98336 | tf_op jit(solution)/shard_map/ppermute | solution.py:497
  68.3 2.5 %merge_rows.1 = bf16[1024,768]{1,0:T(8,128)(2,1)} custom-call(s32[2]{0:T(128)S(1)} %pad_add_fusion.meta, bf16[16,64,384]{2,1,0:T(8,128)(2,1)S(1)} %get-tuple-element.75.refs_0_, bf16[16,64,384]{2,1,0:T(8,128)(2,1)S(1)} %get-tuple-element.90.refs_1_, f32[64,384]{1,0:T(8,128)S(1)} %get-tuple-element.91.refs_2_, f32[64,384]{1,0:T(8,128)S(1)} %get-tuple-element.92.refs_3_, ...), custom_call_target="tpu_custom_call" | custom-call | tf_op jit(solution)/shard_map/merge_rows/pallas_call | solution.py:475
  (27 shorter events, 0.1 us)
Async XLA Ops:
  0.7 1.4 %copy-start = (bf16[1024,768]{1,0:T(8,128)(2,1)S(1)}, bf16[1024,768]{1,0:T(8,128)(2,1)}, u32[]{:S(2)}) copy-start(bf16[1024,768]{1,0:T(8,128)(2,1)} %q_ref.1) | copy-start | bytes 4718596
  2.1 1.4 %copy-start.1 = (bf16[1024,768]{1,0:T(8,128)(2,1)S(1)}, bf16[1024,768]{1,0:T(8,128)(2,1)}, u32[]{:S(2)}) copy-start(bf16[1024,768]{1,0:T(8,128)(2,1)} %k_ref.1) | copy-start | bytes 4718596
  3.5 1.4 %copy-start.2 = (bf16[1024,768]{1,0:T(8,128)(2,1)S(1)}, bf16[1024,768]{1,0:T(8,128)(2,1)}, u32[]{:S(2)}) copy-start(bf16[1024,768]{1,0:T(8,128)(2,1)} %v_ref.1) | copy-start | bytes 4718596
  5.0 20.0 %copy-start.3 = (s32[8,256]{1,0:T(8,128)S(1)}, s32[8,256]{1,0:T(8,128)}, u32[]{:S(2)}) copy-start(s32[8,256]{1,0:T(8,128)} %constant.8.clone.ints) | copy-start | bytes 24580
  5.0 20.0 %copy-start.4 = (f32[8,256]{1,0:T(8,128)S(1)}, f32[8,256]{1,0:T(8,128)}, u32[]{:S(2)}) copy-start(f32[8,256]{1,0:T(8,128)} %constant.9.clone.floats) | copy-start | bytes 24580
  11.5 11.4 %collective-permute-start.11 = (bf16[2,2,64,768]{3,2,1,0:T(8,128)(2,1)S(1)}, bf16[2,2,64,768]{3,2,1,0:T(8,128)(2,1)S(1)}, u32[]{:S(2)}, u32[]{:S(2)}) collective-permute-start(bf16[2,2,64,768]{3,2,1,0:T(8,128)(2,1)S(1)} %get-tuple-element.70), channel_id=1, source_target_pairs={{0,2},{1,3},{2,0},{3,1},{4,6},{5,7},{6,4},{7,5},{8,10},{9,11},{10,... | collective-permute-start | bytes 1179656 | tf_op jit(solution)/shard_map/ppermute | solution.py:497
  14.0 31.4 %collective-permute-start.10 = (bf16[4,2,64,768]{3,2,1,0:T(8,128)(2,1)S(1)}, bf16[4,2,64,768]{3,2,1,0:T(8,128)(2,1)S(1)}, u32[]{:S(2)}, u32[]{:S(2)}) collective-permute-start(bf16[4,2,64,768]{3,2,1,0:T(8,128)(2,1)S(1)} %get-tuple-element.69), channel_id=1, source_target_pairs={{0,1},{1,0},{2,3},{3,2},{4,5},{5,4},{6,7},{7,6},{8,9},{9,8},{10,11... | collective-permute-start | bytes 2359304 | tf_op jit(solution)/shard_map/ppermute | solution.py:497
  15.0 15.9 %collective-permute-start = (bf16[64,640]{1,0:T(8,128)(2,1)S(1)}, bf16[64,640]{1,0:T(8,128)(2,1)S(1)}, u32[]{:S(2)}, u32[]{:S(2)}) collective-permute-start(bf16[64,640]{1,0:T(8,128)(2,1)S(1)} %get-tuple-element.53), channel_id=1, source_target_pairs={{0,2},{1,3},{2,4},{3,5},{4,6},{5,7},{6,0},{7,1},{8,10},{9,11},{10,... | collective-permute-start | bytes 245768 | tf_op jit(solution)/shard_map/ppermute | solution.py:497
  15.0 15.9 %collective-permute-start.1 = (bf16[64,640]{1,0:T(8,128)(2,1)S(1)}, bf16[64,640]{1,0:T(8,128)(2,1)S(1)}, u32[]{:S(2)}, u32[]{:S(2)}) collective-permute-start(bf16[64,640]{1,0:T(8,128)(2,1)S(1)} %get-tuple-element.54), channel_id=1, source_target_pairs={{0,4},{1,5},{2,6},{3,7},{4,0},{5,1},{6,2},{7,3},{8,12},{9,13},{10,... | collective-permute-start | bytes 245768 | tf_op jit(solution)/shard_map/ppermute | solution.py:497
  18.4 12.5 %collective-permute-start.2 = (bf16[64,640]{1,0:T(8,128)(2,1)S(1)}, bf16[64,640]{1,0:T(8,128)(2,1)S(1)}, u32[]{:S(2)}, u32[]{:S(2)}) collective-permute-start(bf16[64,640]{1,0:T(8,128)(2,1)S(1)} %get-tuple-element.55), channel_id=1, source_target_pairs={{0,6},{1,7},{2,0},{3,1},{4,2},{5,3},{6,4},{7,5},{8,14},{9,15},{10,... | collective-permute-start | bytes 245768 | tf_op jit(solution)/shard_map/ppermute | solution.py:497
  22.9 22.0 %collective-permute-start.12 = (bf16[2,2,64,768]{3,2,1,0:T(8,128)(2,1)S(1)}, bf16[2,2,64,768]{3,2,1,0:T(8,128)(2,1)S(1)}, u32[]{:S(2)}, u32[]{:S(2)}) collective-permute-start(bf16[2,2,64,768]{3,2,1,0:T(8,128)(2,1)S(1)} %collective-permute-done.11.refs_4_), channel_id=1, source_target_pairs={{0,1},{1,0},{2,3},{3,2},{4,5},{5,4},{6,7},{7,6},{8,9},{9,8},{10,11... | collective-permute-start | bytes 1179656 | tf_op jit(solution)/shard_map/ppermute | solution.py:497
  31.0 10.9 %collective-permute-start.3 = (bf16[256,384]{1,0:T(8,128)(2,1)S(1)}, bf16[256,384]{1,0:T(8,128)(2,1)S(1)}, u32[]{:S(2)}, u32[]{:S(2)}) collective-permute-start(bf16[256,384]{1,0:T(8,128)(2,1)S(1)} %pad_maximum_fusion.rest_0_), channel_id=1, source_target_pairs={{0,8},{1,9},{2,10},{3,11},{4,12},{5,13},{6,14},{7,15},{8,16},{9,17... | collective-permute-start | bytes 589832 | tf_op jit(solution)/shard_map/ppermute | solution.py:497
  32.3 11.7 %collective-permute-start.4 = (bf16[256,384]{1,0:T(8,128)(2,1)S(1)}, bf16[256,384]{1,0:T(8,128)(2,1)S(1)}, u32[]{:S(2)}, u32[]{:S(2)}) collective-permute-start(bf16[256,384]{1,0:T(8,128)(2,1)S(1)} %pad_maximum_fusion.rest_0_), channel_id=1, source_target_pairs={{0,16},{1,17},{2,18},{3,19},{4,20},{5,21},{6,22},{7,23},{8,24},{9,... | collective-permute-start | bytes 589832 | tf_op jit(solution)/shard_map/ppermute | solution.py:497
  34.8 9.3 %collective-permute-start.5 = (bf16[256,384]{1,0:T(8,128)(2,1)S(1)}, bf16[256,384]{1,0:T(8,128)(2,1)S(1)}, u32[]{:S(2)}, u32[]{:S(2)}) collective-permute-start(bf16[256,384]{1,0:T(8,128)(2,1)S(1)} %pad_maximum_fusion.rest_0_), channel_id=1, source_target_pairs={{0,24},{1,25},{2,26},{3,27},{4,28},{5,29},{6,30},{7,31},{8,0},{9,1... | collective-permute-start | bytes 589832 | tf_op jit(solution)/shard_map/ppermute | solution.py:497
  41.9 8.3 %collective-permute-start.6 = (bf16[256,384]{1,0:T(8,128)(2,1)S(1)}, bf16[256,384]{1,0:T(8,128)(2,1)S(1)}, u32[]{:S(2)}, u32[]{:S(2)}) collective-permute-start(bf16[256,384]{1,0:T(8,128)(2,1)S(1)} %pad_maximum_fusion.rest_0_), channel_id=1, source_target_pairs={{0,1},{1,0},{2,3},{3,2},{4,5},{5,4},{6,7},{7,6},{8,9},{9,8},{10,11... | collective-permute-start | bytes 589832 | tf_op jit(solution)/shard_map/ppermute | solution.py:497
  44.1 6.1 %collective-permute-start.7 = (bf16[256,384]{1,0:T(8,128)(2,1)S(1)}, bf16[256,384]{1,0:T(8,128)(2,1)S(1)}, u32[]{:S(2)}, u32[]{:S(2)}) collective-permute-start(bf16[256,384]{1,0:T(8,128)(2,1)S(1)} %collective-permute-done.3.rest_1_), channel_id=1, source_target_pairs={{0,1},{1,0},{2,3},{3,2},{4,5},{5,4},{6,7},{7,6},{8,9},{9,8},{10,11... | collective-permute-start | bytes 589832 | tf_op jit(solution)/shard_map/ppermute | solution.py:497
  44.9 5.4 %collective-permute-start.8 = (bf16[256,384]{1,0:T(8,128)(2,1)S(1)}, bf16[256,384]{1,0:T(8,128)(2,1)S(1)}, u32[]{:S(2)}, u32[]{:S(2)}) collective-permute-start(bf16[256,384]{1,0:T(8,128)(2,1)S(1)} %collective-permute-done.4.rest_2_), channel_id=1, source_target_pairs={{0,1},{1,0},{2,3},{3,2},{4,5},{5,4},{6,7},{7,6},{8,9},{9,8},{10,11... | collective-permute-start | bytes 589832 | tf_op jit(solution)/shard_map/ppermute | solution.py:497
  44.9 5.4 %collective-permute-start.9 = (bf16[256,384]{1,0:T(8,128)(2,1)S(1)}, bf16[256,384]{1,0:T(8,128)(2,1)S(1)}, u32[]{:S(2)}, u32[]{:S(2)}) collective-permute-start(bf16[256,384]{1,0:T(8,128)(2,1)S(1)} %collective-permute-done.5.rest_3_), channel_id=1, source_target_pairs={{0,1},{1,0},{2,3},{3,2},{4,5},{5,4},{6,7},{7,6},{8,9},{9,8},{10,11... | collective-permute-start | bytes 589832 | tf_op jit(solution)/shard_map/ppermute | solution.py:497
  56.7 9.3 %collective-permute-start.13 = (f32[64,384]{1,0:T(8,128)S(1)}, f32[64,384]{1,0:T(8,128)S(1)}, u32[]{:S(2)}, u32[]{:S(2)}) collective-permute-start(f32[64,384]{1,0:T(8,128)S(1)} %get-tuple-element.96), channel_id=1, source_target_pairs={{0,6},{1,7},{2,0},{3,1},{4,2},{5,3},{6,4},{7,5},{8,14},{9,15},{10,... | collective-permute-start | bytes 294920 | tf_op jit(solution)/shard_map/ppermute | solution.py:497
  60.5 5.6 %collective-permute-start.14 = (f32[64,384]{1,0:T(8,128)S(1)}, f32[64,384]{1,0:T(8,128)S(1)}, u32[]{:S(2)}, u32[]{:S(2)}) collective-permute-start(f32[64,384]{1,0:T(8,128)S(1)} %get-tuple-element.97), channel_id=1, source_target_pairs={{0,4},{1,5},{2,6},{3,7},{4,0},{5,1},{6,2},{7,3},{8,12},{9,13},{10,... | collective-permute-start | bytes 294920 | tf_op jit(solution)/shard_map/ppermute | solution.py:497
  60.5 7.8 %collective-permute-start.15 = (f32[64,384]{1,0:T(8,128)S(1)}, f32[64,384]{1,0:T(8,128)S(1)}, u32[]{:S(2)}, u32[]{:S(2)}) collective-permute-start(f32[64,384]{1,0:T(8,128)S(1)} %get-tuple-element.98), channel_id=1, source_target_pairs={{0,2},{1,3},{2,4},{3,5},{4,6},{5,7},{6,0},{7,1},{8,10},{9,11},{10,... | collective-permute-start | bytes 294920 | tf_op jit(solution)/shard_map/ppermute | solution.py:497

commit v2 on v1

--- a/solution.py
+++ b/solution.py
@@ -28,6 +28,8 @@
 CLASS_U = {"A": ODD, "B": [2, 6, 10, 14], "C": [4, 12], "D": [8, 0]}
 PAIR_OF = [0, 2, 3, 5]
 LONE_OF = [2, 3, 8, 9]
+NEAR_PARTS = [(0, 2), (2, 3), (5, 1)]
+WIDE_PARTS = [(0, 3), (3, 3)]
 
 
 def level(u):
@@ -65,56 +67,58 @@
     return lax.broadcasted_iota(jnp.int32, (rows, 128), 1) < 64
 
 
-def split_kernel(meta, q_ref, k_ref, v_ref, qt, kt, vt, sel, sel8, z0, z1, z2, z3, stage):
-    step = pl.program_id(0)
+def reorder(source, target):
+    swap = swap_matrix()
+    for block in range(4):
+        moved = jnp.dot(
+            swap, source[block * 256 : (block + 1) * 256, :], preferred_element_type=F32
+        ).astype(BF)
+        for res in range(RES):
+            target[res, block * 16 : (block + 1) * 16, :] = moved[res * 16 : (res + 1) * 16, :]
+
+
+def split_kernel(meta, q_in, kt, vt, qt, sel, sel8, z0, z1, z2, z3, stage):
+    reorder(q_in, qt)
     zpos = meta[1] // 2 % NZ
-    swap = swap_matrix()
-    for source, target in ((q_ref, qt), (k_ref, kt), (v_ref, vt)):
-        for block in range(4):
-            moved = jnp.dot(
-                swap, source[block * 256 : (block + 1) * 256, :], preferred_element_type=F32
-            ).astype(BF)
-            for res in range(RES):
-                target[res, block * 16 : (block + 1) * 16, :] = moved[res * 16 : (res + 1) * 16, :]
     low = lane_low(GROUPS)
 
-    def picked(ref, u):
-        return jnp.where(low, ref[(u + 2 * step) & 15], ref[(u + 2 * step + 1) & 15])
-
-    for at, u in enumerate(SHARED):
-        for kv, ref in enumerate((kt, vt)):
-            rows = picked(ref, u)
-            sel[at, kv] = rows
-            if at < 2:
-                sel8[at, kv] = rows
-    q0, k0, v0 = picked(qt, 0), sel[0, 0], sel[0, 1]
-    zero = jnp.zeros_like(q0)
-
-    for group in range(NZ):
-        slot = (group - zpos) & 3
-
-        @pl.when(step == PAIR_OF[group])
-        def _():
-            stage[slot, :, 0:128] = q0
-            stage[slot, :, 256:384] = k0
-            stage[slot, :, 384:512] = v0
-
-        @pl.when(step == LONE_OF[group] // 2)
-        def _():
-            def other(rows):
-                return pltpu.roll(rows.astype(F32), 64, 1).astype(BF)
-
-            if LONE_OF[group] % 2 == 0:
-                lone_q, lone_k, lone_v = q0, k0, other(v0)
-            else:
-                lone_q, lone_k, lone_v = other(q0), other(k0), v0
-            stage[slot, :, 128:256] = jnp.where(low, lone_q, zero)
-            stage[slot, :, 512:640] = jnp.where(low, lone_k, lone_v)
-
-    @pl.when(step == PAIRS - 1)
-    def _():
-        for slot, out in enumerate((z0, z1, z2, z3)):
-            out[...] = stage[slot]
+    def other(rows):
+        return pltpu.roll(rows.astype(F32), 64, 1).astype(BF)
+
+    for pair in range(PAIRS):
+        lanes = slice(pair * 128, pair * 128 + 128)
+
+        def picked(ref, u):
+            return jnp.where(
+                low, ref[(u + 2 * pair) % RES, :, lanes], ref[(u + 2 * pair + 1) % RES, :, lanes]
+            )
+
+        for at, u in enumerate(SHARED):
+            for kv, ref in enumerate((kt, vt)):
+                rows = picked(ref, u)
+                sel[at, kv, :, lanes] = rows
+                if at < 2:
+                    sel8[at, kv, :, lanes] = rows
+                if at == 0 and kv == 0:
+                    k0 = rows
+                if at == 0 and kv == 1:
+                    v0 = rows
+        q0 = picked(qt, 0)
+        for group in range(NZ):
+            slot = (group - zpos) & 3
+            if pair == PAIR_OF[group]:
+                stage[slot, :, 0:128] = q0
+                stage[slot, :, 256:384] = k0
+                stage[slot, :, 384:512] = v0
+            if pair == LONE_OF[group] // 2:
+                if LONE_OF[group] % 2 == 0:
+                    lone_q, lone_k, lone_v = q0, k0, other(v0)
+                else:
+                    lone_q, lone_k, lone_v = other(q0), other(k0), v0
+                stage[slot, :, 128:256] = jnp.where(low, lone_q, jnp.zeros_like(lone_q))
+                stage[slot, :, 512:640] = jnp.where(low, lone_k, lone_v)
+    for slot, out in enumerate((z0, z1, z2, z3)):
+        out[...] = stage[slot]
 
 
 def softmax_parts(query, keys, values, biases):
@@ -139,8 +143,8 @@
         views = [ref.at[:, :, lanes] for ref in refs[:3]]
         if classes == "CD":
             views += [ref.at[:, :, :, lanes] for ref in refs[3:6]]
-            views += [ref.at[:, :, here] for ref in refs[6:8]]
-            views += [ref.at[:, here] for ref in refs[8:10]]
+            views += [refs[6].at[:, :, here]]
+            views += [ref.at[:, here] for ref in refs[7:9]]
         else:
             views += [refs[3].at[:, :, here]]
         local_pair(classes, first + step, meta, ints, floats, *views)
@@ -152,8 +156,7 @@
 def local_pair(classes, pair, meta, ints, floats, q_ref, k_ref, v_ref, *rest):
     far = classes == "CD"
     if far:
-        sel, near, cross, before, out, o0, lse0 = rest
-        out[...] = before[...]
+        sel, near, cross, out, o0, lse0 = rest
     else:
         (out,) = rest
     bound = meta[0]
@@ -315,28 +318,37 @@
                 keys.append(block[:, 256:384])
                 value = block[:, 256:384]
             values.append(jnp.where(mine, value, jnp.ones_like(value)))
-        parts = []
-        for source in (a0, a1, a2, a3):
-            if which < 2:
-                query = jnp.where(mine[:64], source[:, 0:128], jnp.zeros((64, 128), BF))
-            else:
-                query = source[:, 128:256]
-            query = (query * 0.125).astype(BF)
-            total, peak = softmax_parts(query, keys, values, biases)
-            sums = pltpu.roll(total, 64, 1)
-            parts.append((total / sums, peak + jnp.log(sums), peak + jnp.log(total)))
+        lanes = slice(0, 128) if which < 2 else slice(128, 256)
+        query = jnp.concatenate([source[:, lanes] for source in (a0, a1, a2, a3)], axis=0)
+        if which < 2:
+            query = jnp.where(mine, query, jnp.zeros_like(query))
+        query = (query * 0.125).astype(BF)
+        total, peak = softmax_parts(query, keys, values, biases)
+        sums = pltpu.roll(total, 64, 1)
+        parts = (total / sums, peak + jnp.log(sums), peak + jnp.log(total))
         results.append(parts)
     low = low256[:64]
     for at, out in enumerate(outs):
-        first, second, third = (results[which][at] for which in range(3))
+        first, second, third = (
+            [part[at * 64 : (at + 1) * 64] for part in results[which]] for which in range(3)
+        )
         out[:, 0:128] = jnp.where(low, first[0], second[0])
         out[:, 128:256] = jnp.where(low, third[2], third[0])
         out[:, 256:384] = jnp.where(low, first[1], second[1])
 
 
+def part_of(parts, pair):
+    for at, (first, many) in enumerate(parts):
+        if first <= pair < first + many:
+            return at, slice((pair - first) * 128, (pair - first) * 128 + 128)
+
+
 def merge_kernel(meta, *refs):
-    mixed, o0, lse0 = refs[0:2], refs[2:4], refs[4:6]
-    r0, r1, r2, r3, out, stage, grid_rows = refs[6:]
+    count = len(NEAR_PARTS)
+    close, refs = refs[:count], refs[count:]
+    count = len(WIDE_PARTS)
+    wide, o0, lse0 = refs[:count], refs[count : 2 * count], refs[2 * count : 3 * count]
+    r0, r1, r2, r3, out, stage, grid_rows = refs[3 * count :]
     bound = meta[0]
     device = meta[1]
     zpos = device // 2 % NZ
@@ -345,7 +357,8 @@
     low = lane_low(GROUPS)
     for pair in range(PAIRS):
         lanes = slice(pair * 128, pair * 128 + 128)
-        piece, inner = pair // 3, slice(pair % 3 * 128, pair % 3 * 128 + 128)
+        close_part, close_lanes = part_of(NEAR_PARTS, pair)
+        piece, inner = part_of(WIDE_PARTS, pair)
         if pair in PAIR_OF:
             slot = (PAIR_OF.index(pair) - zpos) & 3
             away, away_lse = stage[slot, :, 0:128], stage[slot, :, 256:384]
@@ -362,11 +375,16 @@
         blended = (here * weight + away * away_weight) / (weight + away_weight)
         blended = blended.astype(BF)
         for res in range(RES):
-            rows = mixed[piece][res, :, inner]
-            if res == 2 * pair:
-                rows = jnp.where(low, blended, rows)
-            if res == 2 * pair + 1:
-                rows = jnp.where(low, rows, blended)
+            sides = []
+            for head in (2 * pair, 2 * pair + 1):
+                rank = level((res - head) % RES)
+                if rank == 4:
+                    sides.append(blended)
+                elif rank >= 2:
+                    sides.append(wide[piece][res, :, inner])
+                else:
+                    sides.append(close[close_part][res, :, close_lanes])
+            rows = jnp.where(low, *sides)
             for block in range(4):
                 grid_rows[block, res * 16 : (res + 1) * 16, lanes] = rows[
                     block * 16 : (block + 1) * 16, :
@@ -411,20 +429,34 @@
     return pl.BlockSpec((GROUPS, 128), lambda i: (0, i))
 
 
+def reordered(rows):
+    return pl.pallas_call(
+        reorder,
+        in_specs=[vmem()],
+        out_specs=vmem(),
+        out_shape=shape((RES, GROUPS, WIDTH)),
+        compiler_params=params(20),
+        name="residue_order",
+    )(rows)
+
+
 def split(meta, q, k, v):
-    rows = pl.BlockSpec((ROWS, 128), lambda i: (0, i))
-    return pl.pallas_call(
+    kt, vt = reordered(k), reordered(v)
+    qt, *rest = pl.pallas_call(
         split_kernel,
-        grid=(PAIRS,),
-        in_specs=[smem(), rows, rows, rows],
-        out_specs=[by_residue()] * 3 + [by_part(4), by_part(2)] + [whole((GROUPS, 640))] * 4,
-        out_shape=[shape((RES, GROUPS, WIDTH))] * 3
-        + [shape((4, 2, GROUPS, WIDTH)), shape((2, 2, GROUPS, WIDTH))]
+        in_specs=[smem()] + [vmem()] * 3,
+        out_specs=[vmem()] * 7,
+        out_shape=[
+            shape((RES, GROUPS, WIDTH)),
+            shape((4, 2, GROUPS, WIDTH)),
+            shape((2, 2, GROUPS, WIDTH)),
+        ]
         + [shape((GROUPS, 640))] * 4,
         scratch_shapes=[pltpu.VMEM((4, GROUPS, 640), BF)],
-        compiler_params=params(40),
+        compiler_params=params(20),
         name="split_rows",
-    )(meta, q, k, v)
+    )(meta, q, kt, vt)
+    return qt, kt, vt, *rest
 
 
 def local_near(first, many, meta, ints, floats, q, k, v):
@@ -441,10 +473,10 @@
     )(meta, ints, floats, q, k, v)
 
 
-def local_far(first, many, meta, ints, floats, q, k, v, sel, near, cross, before):
+def local_far(first, many, meta, ints, floats, q, k, v, sel, near, cross):
     return pl.pallas_call(
         functools.partial(local_kernel, "CD", first, many),
-        in_specs=[smem()] + [vmem()] * 9,
+        in_specs=[smem()] + [vmem()] * 8,
         out_specs=[vmem()] * 3,
         out_shape=[
             shape((RES, GROUPS, many * 128)),
@@ -456,7 +488,7 @@
             flops=many * 400000000, bytes_accessed=1000000, transcendentals=many * 600000
         ),
         name="wide_queries",
-    )(meta, ints, floats, q, k, v, sel, near, cross, before)
+    )(meta, ints, floats, q, k, v, sel, near, cross)
 
 
 def slide_wide(meta, queries, blocks):
@@ -471,10 +503,10 @@
     )(meta, *queries, *blocks)
 
 
-def merge(meta, mixed, o0, lse0, back):
+def merge(meta, close, wide, back):
     return pl.pallas_call(
         merge_kernel,
-        in_specs=[smem()] + [vmem()] * 10,
+        in_specs=[smem()] + [vmem()] * (len(NEAR_PARTS) + 3 * len(WIDE_PARTS) + 4),
         out_specs=vmem(),
         out_shape=shape((ROWS, WIDTH)),
         scratch_shapes=[
@@ -483,7 +515,7 @@
         ],
         compiler_params=params(40),
         name="merge_rows",
-    )(meta, *mixed, *o0, *lse0, *back)
+    )(meta, *close, *[part for parts in zip(*wide) for part in parts], *back)
 
 
 def at(x, z, c):
@@ -518,29 +550,31 @@
     meta = jnp.stack([slide_length[0], device])
     ints, floats = (jnp.asarray(table) for table in tables())
     qt, kt, vt, sel, sel8, z0, z1, z2, z3 = split(meta, query_tiles, key_tiles, value_tiles)
+    local = (ints, floats, qt, kt, vt)
     slabs = [z0] + [move(slab, along_z(step)) for step, slab in ((1, z1), (2, z2), (3, z3))]
+    close = [local_near(*NEAR_PARTS[0], meta, *local)]
+    slabs, close[0], sel, sel8, later = lax.optimization_barrier(
+        (slabs, close[0], sel, sel8, meta)
+    )
+    own = jnp.concatenate([slab[:, 256:640] for slab in slabs], axis=0)
+    own, later = lax.optimization_barrier((own, later))
+    moved = [move(own, along_x(step)) for step in (1, 2, 3)]
     near = move(sel8, next_chip)
     pair = move(sel, other_core)
-    local = (ints, floats, qt, kt, vt)
-    mixed = [local_near(0, 3, meta, *local)]
-    slabs, mixed[0] = lax.optimization_barrier((slabs, mixed[0]))
-    own = jnp.concatenate([slab[:, 256:640] for slab in slabs], axis=0)
-    own, later = lax.optimization_barrier((own, meta))
-    moved = [move(own, along_x(step)) for step in (1, 2, 3)]
+    close.append(local_near(*NEAR_PARTS[1], later, *local))
+    near, close[1], last = lax.optimization_barrier((near, close[1], later))
     cross = move(near, other_core)
-    mixed.append(local_near(3, 3, later, *local))
-    moved, mixed[1] = lax.optimization_barrier((moved, mixed[1]))
+    close.append(local_near(*NEAR_PARTS[2], last, *local))
+    moved, close[2], last = lax.optimization_barrier((moved, close[2], last))
     blocks = [own] + moved
     blocks += [move(block, other_core) for block in blocks]
-    moved, last = lax.optimization_barrier((moved, meta))
-    wide = [local_far(0, 3, last, *local, pair, near, cross, mixed[0])]
+    wide = [local_far(*WIDE_PARTS[0], last, *local, pair, near, cross)]
     blocks, wide[0] = lax.optimization_barrier((blocks, wide[0]))
     back = slide_wide(meta, [slab[:, 0:256] for slab in slabs], blocks)
-    back, last = lax.optimization_barrier((back, meta))
+    back, last = lax.optimization_barrier((back, last))
     back = [back[0]] + [move(back[step], along_z(-step)) for step in (1, 2, 3)]
-    wide.append(local_far(3, 3, last, *local, pair, near, cross, mixed[1]))
-    mixed, o0, lse0 = zip(*wide)
-    return merge(meta, mixed, o0, lse0, back)
+    wide.append(local_far(*WIDE_PARTS[1], last, *local, pair, near, cross))
+    return merge(meta, close, wide, back)
 
 
 def solution(mesh):

time: 71 us -> 64.3 us (0.906)
  Pallas kernels: 36.7 us -> 30.1 us
  waiting for transfers between devices: 6.11 us -> 10.3 us
  starting transfers between devices: 22.7 us -> 19.7 us
  local copies, waits for them, and re-layouts: 4.27 us -> 3.02 us
    ppermute x16, waiting for transfers between devices: 6.11 us -> 10.3 us  [move(): return lax.ppermute(block, 'seq', route)]
    pallas_call x2 -> x4, Pallas kernels: 8.99 us -> 5.16 us  [the longest x1 2.58 us: merge(): pl.pallas_call(merge_kernel, in_specs=[smem()] + [vmem()] * (len(NEAR_PAR...]
    ppermute x16, starting transfers between devices: 22.7 us -> 19.7 us  [move(): return lax.ppermute(block, 'seq', route)]
    pallas_call x1, Pallas kernels: 6.42 us -> 3.41 us  [slide_wide(): pl.pallas_call(far_kernel, in_specs=[smem()] + [vmem()] * 12, out_specs=[...]
    unnamed x10, local copies, waits for them, and re-layouts: 4.23 us -> 2.98 us
    pallas_call x2 -> x3, Pallas kernels: 11.8 us -> 12.3 us  [local_near(): pl.pallas_call(functools.partial(local_kernel, 'AB', first, many), in_spe...]
  transfers between devices with their start and end apart: 16 -> 16, of which waited for: 4 -> 4; matrix products, arithmetic and copies ran while one was open for 0% -> 0% of each run, Pallas kernels for 30% -> 34%
where the time goes in v2:
time: 64.3 us; the launch traced here: 64.1 us
  Pallas kernels  30.1 us (47%)
  starting transfers between devices  19.7 us (31%)
  waiting for transfers between devices  10.3 us (16%)
  local copies, waits for them, and re-layouts  3.02 us (5%)
  between operations  0.86 us (1%)
    ppermute x16, starting transfers between devices, move(): return lax.ppermute(block, 'seq', route)  19.7 us
    pallas_call x3, Pallas kernels, local_near(): pl.pallas_call(functools.partial(local_kernel, 'AB', first, many), in_spe...  12.3 us
    ppermute x16, waiting for transfers between devices, move(): return lax.ppermute(block, 'seq', route)  10.3 us
    pallas_call x2, Pallas kernels, local_far(): pl.pallas_call(functools.partial(local_kernel, 'CD', first, many), in_spe...  9.24 us
    pallas_call x1, Pallas kernels, slide_wide(): pl.pallas_call(far_kernel, in_specs=[smem()] + [vmem()] * 12, out_specs=[...  3.41 us
    unnamed x10, local copies, waits for them, and re-layouts  2.98 us
    pallas_call x1, Pallas kernels, merge(): pl.pallas_call(merge_kernel, in_specs=[smem()] + [vmem()] * (len(NEAR_PAR...  2.58 us
    pallas_call x1, Pallas kernels, split(): pl.pallas_call(split_kernel, in_specs=[smem()] + [vmem()] * 3, out_specs=...  1.43 us
  transfers between devices with their start and end apart: 16, of which 4 were waited for; matrix products, arithmetic and copies ran while one was open for 0% of the time, Pallas kernels for 34%

profile of v2, /device:TPU:1, one launch (start us, length us, event | category | flops | bytes accessed | tf_op | source)
XLA Modules:
  0.0 64.1 jit_solution(6764187739351080217)
XLA Ops:
  0.7 1.4 %copy-done.1 = bf16[1024,768]{1,0:T(8,128)(2,1)S(1)} copy-done((bf16[1024,768]{1,0:T(8,128)(2,1)S(1)}, bf16[1024,768]{1,0:T(8,128)(2,1)}, u32[]{:S(2)}) %copy-start.1) | copy-done | bytes 1572888
  2.1 0.6 residue_order.2.kt.refs_1_
  2.6 0.8 %copy-done.2 = bf16[1024,768]{1,0:T(8,128)(2,1)S(1)} copy-done((bf16[1024,768]{1,0:T(8,128)(2,1)S(1)}, bf16[1024,768]{1,0:T(8,128)(2,1)}, u32[]{:S(2)}) %copy-start.2) | copy-done | bytes 1572888
  3.5 0.6 residue_order.3.vt.refs_2_
  4.1 0.1 pad_add_fusion.meta
  4.1 0.7 %copy-done = bf16[1024,768]{1,0:T(8,128)(2,1)S(1)} copy-done((bf16[1024,768]{1,0:T(8,128)(2,1)S(1)}, bf16[1024,768]{1,0:T(8,128)(2,1)}, u32[]{:S(2)}) %copy-start) | copy-done | bytes 1572888
  4.9 1.4 %split_rows.1 = (bf16[16,64,768]{2,1,0:T(8,128)(2,1)S(1)}, bf16[4,2,64,768]{3,2,1,0:T(8,128)(2,1)S(1)}, bf16[2,2,64,768]{3,2,1,0:T(8,128)(2,1)S(1)}, bf16[64,640...) custom-call(s32[2]{0:T(128)S(1)} %pad_add_fusion.meta, ...), custom_call_target="tpu_custom_call" | custom-call | tf_op jit(solution)/shard_map/split_rows/pallas_call | solution.py:445
  6.3 2.5 %collective-permute-start = (bf16[64,640]{1,0:T(8,128)(2,1)S(1)}, bf16[64,640]{1,0:T(8,128)(2,1)S(1)}, u32[]{:S(2)}, u32[]{:S(2)}) collective-permute-start(bf16[64,640]{1,0:T(8,128)(2,1)S(1)} %get-tuple-element.57), channel_id=1, source_target_pairs={{0,2},{1,3},{2,4},{3,5},{4,6},{5,7},{6,0},{7,1},{8,10},{9,11},{10,... | collective-permute-start | bytes 245768 | tf_op jit(solution)/shard_map/ppermute | solution.py:529
  8.8 3.3 %collective-permute-start.1 = (bf16[64,640]{1,0:T(8,128)(2,1)S(1)}, bf16[64,640]{1,0:T(8,128)(2,1)S(1)}, u32[]{:S(2)}, u32[]{:S(2)}) collective-permute-start(bf16[64,640]{1,0:T(8,128)(2,1)S(1)} %get-tuple-element.58), channel_id=1, source_target_pairs={{0,4},{1,5},{2,6},{3,7},{4,0},{5,1},{6,2},{7,3},{8,12},{9,13},{10,... | collective-permute-start | bytes 245768 | tf_op jit(solution)/shard_map/ppermute | solution.py:529
  12.1 0.7 %collective-permute-start.2 = (bf16[64,640]{1,0:T(8,128)(2,1)S(1)}, bf16[64,640]{1,0:T(8,128)(2,1)S(1)}, u32[]{:S(2)}, u32[]{:S(2)}) collective-permute-start(bf16[64,640]{1,0:T(8,128)(2,1)S(1)} %get-tuple-element.59), channel_id=1, source_target_pairs={{0,6},{1,7},{2,0},{3,1},{4,2},{5,3},{6,4},{7,5},{8,14},{9,15},{10,... | collective-permute-start | bytes 245768 | tf_op jit(solution)/shard_map/ppermute | solution.py:529
  12.9 4.1 %near_queries.3.refs_0_ = bf16[16,64,256]{2,1,0:T(8,128)(2,1)S(1)} custom-call(s32[2]{0:T(128)S(1)} %pad_add_fusion.meta, s32[8,256]{1,0:T(8,128)S(1)} %copy-done.4, f32[8,256]{1,0:T(8,128)S(1)} %copy-done.3, bf16[16,64,768]{2,1,0:T(8,128)(2,1)S(1)} %get-tuple-element.60.refs_0_, bf16[16,64,768]{2,1,0:T(8,128)(2,1)S(1)} %residue_order.2.kt.refs_1_, ...), custom_call_target="tpu_custom_call" | custom-call | flops 1000000000 | bytes 1000000 | tf_op jit(solution)/shard_map/near_queries/pallas_call | solution.py:463
  17.0 0.8 %collective-permute-start.3 = (bf16[2,2,64,768]{3,2,1,0:T(8,128)(2,1)S(1)}, bf16[2,2,64,768]{3,2,1,0:T(8,128)(2,1)S(1)}, u32[]{:S(2)}, u32[]{:S(2)}) collective-permute-start(bf16[2,2,64,768]{3,2,1,0:T(8,128)(2,1)S(1)} %get-tuple-element.64), channel_id=1, source_target_pairs={{0,2},{1,3},{2,0},{3,1},{4,6},{5,7},{6,4},{7,5},{8,10},{9,11},{10,... | collective-permute-start | bytes 1179656 | tf_op jit(solution)/shard_map/ppermute | solution.py:529
  17.8 1.8 %collective-permute-start.11 = (bf16[4,2,64,768]{3,2,1,0:T(8,128)(2,1)S(1)}, bf16[4,2,64,768]{3,2,1,0:T(8,128)(2,1)S(1)}, u32[]{:S(2)}, u32[]{:S(2)}) collective-permute-start(bf16[4,2,64,768]{3,2,1,0:T(8,128)(2,1)S(1)} %get-tuple-element.79), channel_id=1, source_target_pairs={{0,1},{1,0},{2,3},{3,2},{4,5},{5,4},{6,7},{7,6},{8,9},{9,8},{10,11... | collective-permute-start | bytes 2359304 | tf_op jit(solution)/shard_map/ppermute | solution.py:529
  19.7 5.9 %near_queries.4.refs_1_ = bf16[16,64,384]{2,1,0:T(8,128)(2,1)S(1)} custom-call(s32[2]{0:T(128)S(1)} %pad_add_fusion.meta, s32[8,256]{1,0:T(8,128)S(1)} %copy-done.4, f32[8,256]{1,0:T(8,128)S(1)} %copy-done.3, bf16[16,64,768]{2,1,0:T(8,128)(2,1)S(1)} %get-tuple-element.60.refs_0_, bf16[16,64,768]{2,1,0:T(8,128)(2,1)S(1)} %residue_order.2.kt.refs_1_, ...), custom_call_target="tpu_custom_call" | custom-call | flops 1500000000 | bytes 1000000 | tf_op jit(solution)/shard_map/near_queries/pallas_call | solution.py:463
  25.6 0.6 collective-permute-done.3.refs_4_
  26.2 2.4 %collective-permute-start.12 = (bf16[2,2,64,768]{3,2,1,0:T(8,128)(2,1)S(1)}, bf16[2,2,64,768]{3,2,1,0:T(8,128)(2,1)S(1)}, u32[]{:S(2)}, u32[]{:S(2)}) collective-permute-start(bf16[2,2,64,768]{3,2,1,0:T(8,128)(2,1)S(1)} %collective-permute-done.3.refs_4_), channel_id=1, source_target_pairs={{0,1},{1,0},{2,3},{3,2},{4,5},{5,4},{6,7},{7,6},{8,9},{9,8},{10,11... | collective-permute-start | bytes 1179656 | tf_op jit(solution)/shard_map/ppermute | solution.py:529
  28.6 2.5 %collective-permute-start.6 = (bf16[256,384]{1,0:T(8,128)(2,1)S(1)}, bf16[256,384]{1,0:T(8,128)(2,1)S(1)}, u32[]{:S(2)}, u32[]{:S(2)}) collective-permute-start(bf16[256,384]{1,0:T(8,128)(2,1)S(1)} %pad_maximum_fusion.rest_0_), channel_id=1, source_target_pairs={{0,24},{1,25},{2,26},{3,27},{4,28},{5,29},{6,30},{7,31},{8,0},{9,1... | collective-permute-start | bytes 589832 | tf_op jit(solution)/shard_map/ppermute | solution.py:529
  31.1 0.5 collective-permute-start.5
  31.6 0.6 collective-permute-start.4
  32.2 2.3 %near_queries.5.refs_2_ = bf16[16,64,128]{2,1,0:T(8,128)(2,1)S(1)} custom-call(s32[2]{0:T(128)S(1)} %pad_add_fusion.meta, s32[8,256]{1,0:T(8,128)S(1)} %copy-done.4, f32[8,256]{1,0:T(8,128)S(1)} %copy-done.3, bf16[16,64,768]{2,1,0:T(8,128)(2,1)S(1)} %get-tuple-element.60.refs_0_, bf16[16,64,768]{2,1,0:T(8,128)(2,1)S(1)} %residue_order.2.kt.refs_1_, ...), custom_call_target="tpu_custom_call" | custom-call | flops 500000000 | bytes 1000000 | tf_op jit(solution)/shard_map/near_queries/pallas_call | solution.py:463
  34.5 5.0 %collective-permute-done.6.rest_3_ = bf16[256,384]{1,0:T(8,128)(2,1)S(1)} collective-permute-done((bf16[256,384]{1,0:T(8,128)(2,1)S(1)}, bf16[256,384]{1,0:T(8,128)(2,1)S(1)}, u32[]{:S(2)}, u32[]{:S(2)}) %collective-permute-start.6) | collective-permute-done | bytes 196640 | tf_op jit(solution)/shard_map/ppermute | solution.py:529
  39.5 1.0 %collective-permute-start.7 = (bf16[256,384]{1,0:T(8,128)(2,1)S(1)}, bf16[256,384]{1,0:T(8,128)(2,1)S(1)}, u32[]{:S(2)}, u32[]{:S(2)}) collective-permute-start(bf16[256,384]{1,0:T(8,128)(2,1)S(1)} %pad_maximum_fusion.rest_0_), channel_id=1, source_target_pairs={{0,1},{1,0},{2,3},{3,2},{4,5},{5,4},{6,7},{7,6},{8,9},{9,8},{10,11... | collective-permute-start | bytes 589832 | tf_op jit(solution)/shard_map/ppermute | solution.py:529
  40.5 3.2 %collective-permute-done.4.rest_1_ = bf16[256,384]{1,0:T(8,128)(2,1)S(1)} collective-permute-done((bf16[256,384]{1,0:T(8,128)(2,1)S(1)}, bf16[256,384]{1,0:T(8,128)(2,1)S(1)}, u32[]{:S(2)}, u32[]{:S(2)}) %collective-permute-start.4) | collective-permute-done | bytes 196640 | tf_op jit(solution)/shard_map/ppermute | solution.py:529
  43.6 0.5 collective-permute-start.8
  44.2 0.5 collective-permute-start.10
  44.7 4.6 %wide_queries.2 = (bf16[16,64,384]{2,1,0:T(8,128)(2,1)S(1)}, f32[64,384]{1,0:T(8,128)S(1)}, f32[64,384]{1,0:T(8,128)S(1)}) custom-call(s32[2]{0:T(128)S(1)} %pad_add_fusion.meta, s32[8,256]{1,0:T(8,128)S(1)} %copy-done.4, f32[8,256]{1,0:T(8,128)S(1)} %copy-done.3, bf16[16,64,768]{2,1,0:T(8,128)(2,1)S(1)} %get-tuple-element.60.refs_0_, ...), custom_call_target="tpu_custom_call" | custom-call | flops 1200000000 | bytes 1000000 | tf_op jit(solution)/shard_map/wide_queries/pallas_call | solution.py:477
  49.4 3.4 %slide_queries.1 = (f32[64,384]{1,0:T(8,128)S(1)}, f32[64,384]{1,0:T(8,128)S(1)}, f32[64,384]{1,0:T(8,128)S(1)}, f32[64,384]{1,0:T(8,128)S(1)}) custom-call(s32[2]{0:T(128)S(1)} %pad_add_fusion.meta, bf16[64,256]{1,0:T(8,128)(2,1)S(1)} %slice.28.a0, bf16[64,256]{1,0:T(8,128)(2,1)S(1)} %slice.29.a1, bf16[64,256]{1,0:T(8,128)(2,1)S(1)} %slice.30.a2, ...), custom_call_target="tpu_custom_call" | custom-call | flops 800000000 | bytes 2000000 | tf_op jit(solution)/shard_map/slide_queries/pallas_call | solution.py:495
  52.8 0.8 %collective-permute-start.13 = (f32[64,384]{1,0:T(8,128)S(1)}, f32[64,384]{1,0:T(8,128)S(1)}, u32[]{:S(2)}, u32[]{:S(2)}) collective-permute-start(f32[64,384]{1,0:T(8,128)S(1)} %get-tuple-element.104), channel_id=1, source_target_pairs={{0,6},{1,7},{2,0},{3,1},{4,2},{5,3},{6,4},{7,5},{8,14},{9,15},{10,... | collective-permute-start | bytes 294920 | tf_op jit(solution)/shard_map/ppermute | solution.py:529
  53.6 1.7 %collective-permute-start.14 = (f32[64,384]{1,0:T(8,128)S(1)}, f32[64,384]{1,0:T(8,128)S(1)}, u32[]{:S(2)}, u32[]{:S(2)}) collective-permute-start(f32[64,384]{1,0:T(8,128)S(1)} %get-tuple-element.105), channel_id=1, source_target_pairs={{0,4},{1,5},{2,6},{3,7},{4,0},{5,1},{6,2},{7,3},{8,12},{9,13},{10,... | collective-permute-start | bytes 294920 | tf_op jit(solution)/shard_map/ppermute | solution.py:529
  55.4 4.6 %wide_queries.3 = (bf16[16,64,384]{2,1,0:T(8,128)(2,1)S(1)}, f32[64,384]{1,0:T(8,128)S(1)}, f32[64,384]{1,0:T(8,128)S(1)}) custom-call(s32[2]{0:T(128)S(1)} %pad_add_fusion.meta, s32[8,256]{1,0:T(8,128)S(1)} %copy-done.4, f32[8,256]{1,0:T(8,128)S(1)} %copy-done.3, bf16[16,64,768]{2,1,0:T(8,128)(2,1)S(1)} %get-tuple-element.60.refs_0_, ...), custom_call_target="tpu_custom_call" | custom-call | flops 1200000000 | bytes 1000000 | tf_op jit(solution)/shard_map/wide_queries/pallas_call | solution.py:477
  60.0 1.5 %collective-permute-done.15.refs_12_ = f32[64,384]{1,0:T(8,128)S(1)} collective-permute-done((f32[64,384]{1,0:T(8,128)S(1)}, f32[64,384]{1,0:T(8,128)S(1)}, u32[]{:S(2)}, u32[]{:S(2)}) %collective-permute-start.15) | collective-permute-done | bytes 98336 | tf_op jit(solution)/shard_map/ppermute | solution.py:529
  61.5 2.6 %merge_rows.1 = bf16[1024,768]{1,0:T(8,128)(2,1)} custom-call(s32[2]{0:T(128)S(1)} %pad_add_fusion.meta, bf16[16,64,256]{2,1,0:T(8,128)(2,1)S(1)} %near_queries.3.refs_0_, bf16[16,64,384]{2,1,0:T(8,128)(2,1)S(1)} %near_queries.4.refs_1_, bf16[16,64,128]{2,1,0:T(8,128)(2,1)S(1)} %near_queries.5.refs_2_, bf16[16,64,384]{2,1,0:T(8,128)(2,1)S(1)} %get-tuple-element.84.refs_3_, ...), custom_call_target="tpu_custom_call" | custom-call | tf_op jit(solution)/shard_map/merge_rows/pallas_call | solution.py:507
  (30 shorter events, 0.1 us)
Async XLA Ops:
  0.7 1.4 %copy-start.1 = (bf16[1024,768]{1,0:T(8,128)(2,1)S(1)}, bf16[1024,768]{1,0:T(8,128)(2,1)}, u32[]{:S(2)}) copy-start(bf16[1024,768]{1,0:T(8,128)(2,1)} %source.2) | copy-start | bytes 4718596
  2.1 1.4 %copy-start.2 = (bf16[1024,768]{1,0:T(8,128)(2,1)S(1)}, bf16[1024,768]{1,0:T(8,128)(2,1)}, u32[]{:S(2)}) copy-start(bf16[1024,768]{1,0:T(8,128)(2,1)} %source.3) | copy-start | bytes 4718596
  3.5 1.4 %copy-start = (bf16[1024,768]{1,0:T(8,128)(2,1)S(1)}, bf16[1024,768]{1,0:T(8,128)(2,1)}, u32[]{:S(2)}) copy-start(bf16[1024,768]{1,0:T(8,128)(2,1)} %q_in.1) | copy-start | bytes 4718596
  4.9 8.0 %copy-start.3 = (f32[8,256]{1,0:T(8,128)S(1)}, f32[8,256]{1,0:T(8,128)}, u32[]{:S(2)}) copy-start(f32[8,256]{1,0:T(8,128)} %constant.9.clone.floats) | copy-start | bytes 24580
  4.9 8.0 %copy-start.4 = (s32[8,256]{1,0:T(8,128)S(1)}, s32[8,256]{1,0:T(8,128)}, u32[]{:S(2)}) copy-start(s32[8,256]{1,0:T(8,128)} %constant.8.clone.ints) | copy-start | bytes 24580
  6.3 10.7 %collective-permute-start = (bf16[64,640]{1,0:T(8,128)(2,1)S(1)}, bf16[64,640]{1,0:T(8,128)(2,1)S(1)}, u32[]{:S(2)}, u32[]{:S(2)}) collective-permute-start(bf16[64,640]{1,0:T(8,128)(2,1)S(1)} %get-tuple-element.57), channel_id=1, source_target_pairs={{0,2},{1,3},{2,4},{3,5},{4,6},{5,7},{6,0},{7,1},{8,10},{9,11},{10,... | collective-permute-start | bytes 245768 | tf_op jit(solution)/shard_map/ppermute | solution.py:529
  8.8 8.2 %collective-permute-start.1 = (bf16[64,640]{1,0:T(8,128)(2,1)S(1)}, bf16[64,640]{1,0:T(8,128)(2,1)S(1)}, u32[]{:S(2)}, u32[]{:S(2)}) collective-permute-start(bf16[64,640]{1,0:T(8,128)(2,1)S(1)} %get-tuple-element.58), channel_id=1, source_target_pairs={{0,4},{1,5},{2,6},{3,7},{4,0},{5,1},{6,2},{7,3},{8,12},{9,13},{10,... | collective-permute-start | bytes 245768 | tf_op jit(solution)/shard_map/ppermute | solution.py:529
  12.1 4.9 %collective-permute-start.2 = (bf16[64,640]{1,0:T(8,128)(2,1)S(1)}, bf16[64,640]{1,0:T(8,128)(2,1)S(1)}, u32[]{:S(2)}, u32[]{:S(2)}) collective-permute-start(bf16[64,640]{1,0:T(8,128)(2,1)S(1)} %get-tuple-element.59), channel_id=1, source_target_pairs={{0,6},{1,7},{2,0},{3,1},{4,2},{5,3},{6,4},{7,5},{8,14},{9,15},{10,... | collective-permute-start | bytes 245768 | tf_op jit(solution)/shard_map/ppermute | solution.py:529
  17.0 9.2 %collective-permute-start.3 = (bf16[2,2,64,768]{3,2,1,0:T(8,128)(2,1)S(1)}, bf16[2,2,64,768]{3,2,1,0:T(8,128)(2,1)S(1)}, u32[]{:S(2)}, u32[]{:S(2)}) collective-permute-start(bf16[2,2,64,768]{3,2,1,0:T(8,128)(2,1)S(1)} %get-tuple-element.64), channel_id=1, source_target_pairs={{0,2},{1,3},{2,0},{3,1},{4,6},{5,7},{6,4},{7,5},{8,10},{9,11},{10,... | collective-permute-start | bytes 1179656 | tf_op jit(solution)/shard_map/ppermute | solution.py:529
  17.8 26.9 %collective-permute-start.11 = (bf16[4,2,64,768]{3,2,1,0:T(8,128)(2,1)S(1)}, bf16[4,2,64,768]{3,2,1,0:T(8,128)(2,1)S(1)}, u32[]{:S(2)}, u32[]{:S(2)}) collective-permute-start(bf16[4,2,64,768]{3,2,1,0:T(8,128)(2,1)S(1)} %get-tuple-element.79), channel_id=1, source_target_pairs={{0,1},{1,0},{2,3},{3,2},{4,5},{5,4},{6,7},{7,6},{8,9},{9,8},{10,11... | collective-permute-start | bytes 2359304 | tf_op jit(solution)/shard_map/ppermute | solution.py:529
  26.2 18.0 %collective-permute-start.12 = (bf16[2,2,64,768]{3,2,1,0:T(8,128)(2,1)S(1)}, bf16[2,2,64,768]{3,2,1,0:T(8,128)(2,1)S(1)}, u32[]{:S(2)}, u32[]{:S(2)}) collective-permute-start(bf16[2,2,64,768]{3,2,1,0:T(8,128)(2,1)S(1)} %collective-permute-done.3.refs_4_), channel_id=1, source_target_pairs={{0,1},{1,0},{2,3},{3,2},{4,5},{5,4},{6,7},{7,6},{8,9},{9,8},{10,11... | collective-permute-start | bytes 1179656 | tf_op jit(solution)/shard_map/ppermute | solution.py:529
  28.6 10.9 %collective-permute-start.6 = (bf16[256,384]{1,0:T(8,128)(2,1)S(1)}, bf16[256,384]{1,0:T(8,128)(2,1)S(1)}, u32[]{:S(2)}, u32[]{:S(2)}) collective-permute-start(bf16[256,384]{1,0:T(8,128)(2,1)S(1)} %pad_maximum_fusion.rest_0_), channel_id=1, source_target_pairs={{0,24},{1,25},{2,26},{3,27},{4,28},{5,29},{6,30},{7,31},{8,0},{9,1... | collective-permute-start | bytes 589832 | tf_op jit(solution)/shard_map/ppermute | solution.py:529
  31.1 9.4 %collective-permute-start.5 = (bf16[256,384]{1,0:T(8,128)(2,1)S(1)}, bf16[256,384]{1,0:T(8,128)(2,1)S(1)}, u32[]{:S(2)}, u32[]{:S(2)}) collective-permute-start(bf16[256,384]{1,0:T(8,128)(2,1)S(1)} %pad_maximum_fusion.rest_0_), channel_id=1, source_target_pairs={{0,16},{1,17},{2,18},{3,19},{4,20},{5,21},{6,22},{7,23},{8,24},{9,... | collective-permute-start | bytes 589832 | tf_op jit(solution)/shard_map/ppermute | solution.py:529
  31.6 12.0 %collective-permute-start.4 = (bf16[256,384]{1,0:T(8,128)(2,1)S(1)}, bf16[256,384]{1,0:T(8,128)(2,1)S(1)}, u32[]{:S(2)}, u32[]{:S(2)}) collective-permute-start(bf16[256,384]{1,0:T(8,128)(2,1)S(1)} %pad_maximum_fusion.rest_0_), channel_id=1, source_target_pairs={{0,8},{1,9},{2,10},{3,11},{4,12},{5,13},{6,14},{7,15},{8,16},{9,17... | collective-permute-start | bytes 589832 | tf_op jit(solution)/shard_map/ppermute | solution.py:529
  39.5 9.8 %collective-permute-start.7 = (bf16[256,384]{1,0:T(8,128)(2,1)S(1)}, bf16[256,384]{1,0:T(8,128)(2,1)S(1)}, u32[]{:S(2)}, u32[]{:S(2)}) collective-permute-start(bf16[256,384]{1,0:T(8,128)(2,1)S(1)} %pad_maximum_fusion.rest_0_), channel_id=1, source_target_pairs={{0,1},{1,0},{2,3},{3,2},{4,5},{5,4},{6,7},{7,6},{8,9},{9,8},{10,11... | collective-permute-start | bytes 589832 | tf_op jit(solution)/shard_map/ppermute | solution.py:529
  43.6 5.7 %collective-permute-start.8 = (bf16[256,384]{1,0:T(8,128)(2,1)S(1)}, bf16[256,384]{1,0:T(8,128)(2,1)S(1)}, u32[]{:S(2)}, u32[]{:S(2)}) collective-permute-start(bf16[256,384]{1,0:T(8,128)(2,1)S(1)} %collective-permute-done.4.rest_1_), channel_id=1, source_target_pairs={{0,1},{1,0},{2,3},{3,2},{4,5},{5,4},{6,7},{7,6},{8,9},{9,8},{10,11... | collective-permute-start | bytes 589832 | tf_op jit(solution)/shard_map/ppermute | solution.py:529
  44.1 5.2 %collective-permute-start.9 = (bf16[256,384]{1,0:T(8,128)(2,1)S(1)}, bf16[256,384]{1,0:T(8,128)(2,1)S(1)}, u32[]{:S(2)}, u32[]{:S(2)}) collective-permute-start(bf16[256,384]{1,0:T(8,128)(2,1)S(1)} %collective-permute-done.5.rest_2_), channel_id=1, source_target_pairs={{0,1},{1,0},{2,3},{3,2},{4,5},{5,4},{6,7},{7,6},{8,9},{9,8},{10,11... | collective-permute-start | bytes 589832 | tf_op jit(solution)/shard_map/ppermute | solution.py:529
  44.2 5.2 %collective-permute-start.10 = (bf16[256,384]{1,0:T(8,128)(2,1)S(1)}, bf16[256,384]{1,0:T(8,128)(2,1)S(1)}, u32[]{:S(2)}, u32[]{:S(2)}) collective-permute-start(bf16[256,384]{1,0:T(8,128)(2,1)S(1)} %collective-permute-done.6.rest_3_), channel_id=1, source_target_pairs={{0,1},{1,0},{2,3},{3,2},{4,5},{5,4},{6,7},{7,6},{8,9},{9,8},{10,11... | collective-permute-start | bytes 589832 | tf_op jit(solution)/shard_map/ppermute | solution.py:529
  52.8 7.2 %collective-permute-start.13 = (f32[64,384]{1,0:T(8,128)S(1)}, f32[64,384]{1,0:T(8,128)S(1)}, u32[]{:S(2)}, u32[]{:S(2)}) collective-permute-start(f32[64,384]{1,0:T(8,128)S(1)} %get-tuple-element.104), channel_id=1, source_target_pairs={{0,6},{1,7},{2,0},{3,1},{4,2},{5,3},{6,4},{7,5},{8,14},{9,15},{10,... | collective-permute-start | bytes 294920 | tf_op jit(solution)/shard_map/ppermute | solution.py:529
  53.6 6.4 %collective-permute-start.14 = (f32[64,384]{1,0:T(8,128)S(1)}, f32[64,384]{1,0:T(8,128)S(1)}, u32[]{:S(2)}, u32[]{:S(2)}) collective-permute-start(f32[64,384]{1,0:T(8,128)S(1)} %get-tuple-element.105), channel_id=1, source_target_pairs={{0,4},{1,5},{2,6},{3,7},{4,0},{5,1},{6,2},{7,3},{8,12},{9,13},{10,... | collective-permute-start | bytes 294920 | tf_op jit(solution)/shard_map/ppermute | solution.py:529
  55.4 6.2 %collective-permute-start.15 = (f32[64,384]{1,0:T(8,128)S(1)}, f32[64,384]{1,0:T(8,128)S(1)}, u32[]{:S(2)}, u32[]{:S(2)}) collective-permute-start(f32[64,384]{1,0:T(8,128)S(1)} %get-tuple-element.106), channel_id=1, source_target_pairs={{0,2},{1,3},{2,4},{3,5},{4,6},{5,7},{6,0},{7,1},{8,10},{9,11},{10,... | collective-permute-start | bytes 294920 | tf_op jit(solution)/shard_map/ppermute | solution.py:529

commit v3 on v2

--- a/solution.py
+++ b/solution.py
@@ -28,8 +28,7 @@
 CLASS_U = {"A": ODD, "B": [2, 6, 10, 14], "C": [4, 12], "D": [8, 0]}
 PAIR_OF = [0, 2, 3, 5]
 LONE_OF = [2, 3, 8, 9]
-NEAR_PARTS = [(0, 2), (2, 3), (5, 1)]
-WIDE_PARTS = [(0, 3), (3, 3)]
+NEAR_PARTS = [(0, 1), (1, 4), (5, 1)]
 
 
 def level(u):
@@ -140,29 +139,29 @@
     def body(step, carry):
         lanes = pl.ds(pl.multiple_of((first + step) * 128, 128), 128)
         here = pl.ds(pl.multiple_of(step * 128, 128), 128)
-        views = [ref.at[:, :, lanes] for ref in refs[:3]]
-        if classes == "CD":
-            views += [ref.at[:, :, :, lanes] for ref in refs[3:6]]
+        views = [ref.at[:, :, lanes] for ref in refs[:3]] + [refs[3].at[:, :, :, lanes]]
+        if classes == "D":
+            views += [ref.at[:, :, :, lanes] for ref in refs[4:6]]
             views += [refs[6].at[:, :, here]]
             views += [ref.at[:, here] for ref in refs[7:9]]
         else:
-            views += [refs[3].at[:, :, here]]
+            views += [refs[4].at[:, :, here]]
         local_pair(classes, first + step, meta, ints, floats, *views)
         return carry
 
     lax.fori_loop(0, many, body, 0)
 
 
-def local_pair(classes, pair, meta, ints, floats, q_ref, k_ref, v_ref, *rest):
-    far = classes == "CD"
+def local_pair(classes, pair, meta, ints, floats, q_ref, k_ref, v_ref, sel, *rest):
+    far = classes == "D"
     if far:
-        sel, near, cross, out, o0, lse0 = rest
+        near, cross, out, o0, lse0 = rest
     else:
         (out,) = rest
     bound = meta[0]
     device = meta[1]
     low = lane_low(256)
-    low_all = lane_low(256 if far else 768)
+    low_all = lane_low(128 if far else 896)
     high_all = jnp.logical_not(low_all)
     for parity in range(2):
         head = 2 * pair + parity
@@ -189,9 +188,9 @@
         even_k = [gathered(k_ref, EVEN, half) for half in range(2)]
         odd_v = [widened(gathered(v_ref, ODD, half)) for half in range(2)]
         even_v = [widened(gathered(v_ref, EVEN, half)) for half in range(2)]
+        pair_k = sel[:, 0].reshape(256, 128)
+        pair_v = widened(sel[:, 1].reshape(256, 128))
         if far:
-            pair_k = sel[:, 0].reshape(256, 128)
-            pair_v = widened(sel[:, 1].reshape(256, 128))
             next_k = jnp.concatenate([near[0, 0], near[1, 0], cross[0, 0], cross[1, 0]], axis=0)
             next_v = widened(
                 jnp.concatenate([near[0, 1], near[1, 1], cross[0, 1], cross[1, 1]], axis=0)
@@ -205,8 +204,8 @@
             tiles.append(
                 (even_k[half], even_v[half], lambda cap, side, half=half: side == half or cap >= 1)
             )
+        tiles.append((pair_k, pair_v, lambda cap, side: cap >= 2))
         if far:
-            tiles.append((pair_k, pair_v, lambda cap, side: True))
             tiles.append((next_k, next_v, lambda cap, side: cap >= 3))
 
         def tile_bias(tile, cap, side):
@@ -325,16 +324,21 @@
         query = (query * 0.125).astype(BF)
         total, peak = softmax_parts(query, keys, values, biases)
         sums = pltpu.roll(total, 64, 1)
-        parts = (total / sums, peak + jnp.log(sums), peak + jnp.log(total))
-        results.append(parts)
+        logs = peak + jnp.log(sums if which < 2 else total)
+        results.append((total / sums, logs))
     low = low256[:64]
+    lane = lax.broadcasted_iota(jnp.int32, (64, 128), 1)
     for at, out in enumerate(outs):
-        first, second, third = (
-            [part[at * 64 : (at + 1) * 64] for part in results[which]] for which in range(3)
-        )
-        out[:, 0:128] = jnp.where(low, first[0], second[0])
-        out[:, 128:256] = jnp.where(low, third[2], third[0])
-        out[:, 256:384] = jnp.where(low, first[1], second[1])
+        rows = slice(at * 64, (at + 1) * 64)
+        out[:, 0:128] = jnp.where(low, results[0][0][rows], results[1][0][rows]).astype(BF)
+        mixed = results[2][0][rows].astype(BF)
+        for which, place in ((0, 0), (1, 64), (2, 0)):
+            rest = results[which][1][rows, place : place + 1]
+            for term in range(3):
+                kept = rest.astype(BF)
+                rest = rest - kept.astype(F32)
+                mixed = jnp.where(lane == which * 3 + term, kept, mixed)
+        out[:, 128:256] = mixed
 
 
 def part_of(parts, pair):
@@ -346,29 +350,31 @@
 def merge_kernel(meta, *refs):
     count = len(NEAR_PARTS)
     close, refs = refs[:count], refs[count:]
-    count = len(WIDE_PARTS)
-    wide, o0, lse0 = refs[:count], refs[count : 2 * count], refs[2 * count : 3 * count]
-    r0, r1, r2, r3, out, stage, grid_rows = refs[3 * count :]
+    wide, o0, lse0, r0, r1, r2, r3, out, stage, grid_rows = refs
     bound = meta[0]
     device = meta[1]
     zpos = device // 2 % NZ
     for slot, ref in enumerate((r0, r1, r2, r3)):
-        stage[slot] = ref[...]
+        stage[slot] = ref[...].astype(F32)
     low = lane_low(GROUPS)
+
+    def log_of(slot, which):
+        terms = [stage[slot, :, 128 + which * 3 + term : 129 + which * 3 + term] for term in range(3)]
+        return terms[0] + terms[1] + terms[2]
+
     for pair in range(PAIRS):
         lanes = slice(pair * 128, pair * 128 + 128)
         close_part, close_lanes = part_of(NEAR_PARTS, pair)
-        piece, inner = part_of(WIDE_PARTS, pair)
         if pair in PAIR_OF:
             slot = (PAIR_OF.index(pair) - zpos) & 3
-            away, away_lse = stage[slot, :, 0:128], stage[slot, :, 256:384]
+            away = stage[slot, :, 0:128]
+            away_lse = jnp.where(low, log_of(slot, 0), log_of(slot, 1))
         else:
-            first = LONE_OF.index(2 * pair)
-            left = stage[(first - zpos) & 3, :, 128:256]
-            right = stage[(first + 1 - zpos) & 3, :, 128:256]
-            away = jnp.where(low, pltpu.roll(left, 64, 1), right)
-            away_lse = jnp.where(low, left, pltpu.roll(right, 64, 1))
-        here, here_lse = o0[piece][:, inner], lse0[piece][:, inner]
+            left = (LONE_OF.index(2 * pair) - zpos) & 3
+            right = (left + 1) & 3
+            away = jnp.where(low, pltpu.roll(stage[left, :, 128:256], 64, 1), stage[right, :, 128:256])
+            away_lse = jnp.where(low, log_of(left, 2), log_of(right, 2))
+        here, here_lse = o0[:, lanes], lse0[:, lanes]
         top = jnp.maximum(here_lse, away_lse)
         weight = jnp.exp(here_lse - top)
         away_weight = jnp.exp(away_lse - top)
@@ -380,8 +386,8 @@
                 rank = level((res - head) % RES)
                 if rank == 4:
                     sides.append(blended)
-                elif rank >= 2:
-                    sides.append(wide[piece][res, :, inner])
+                elif rank == 3:
+                    sides.append(wide[res, :, lanes])
                 else:
                     sides.append(close[close_part][res, :, close_lanes])
             rows = jnp.where(low, *sides)
@@ -459,33 +465,33 @@
     return qt, kt, vt, *rest
 
 
-def local_near(first, many, meta, ints, floats, q, k, v):
+def local_near(first, many, meta, ints, floats, q, k, v, sel):
     return pl.pallas_call(
-        functools.partial(local_kernel, "AB", first, many),
-        in_specs=[smem()] + [vmem()] * 5,
+        functools.partial(local_kernel, "ABC", first, many),
+        in_specs=[smem()] + [vmem()] * 6,
         out_specs=vmem(),
         out_shape=shape((RES, GROUPS, many * 128)),
         compiler_params=params(40),
         cost_estimate=pl.CostEstimate(
-            flops=many * 500000000, bytes_accessed=1000000, transcendentals=many * 900000
+            flops=many * 600000000, bytes_accessed=1000000, transcendentals=many * 1200000
         ),
         name="near_queries",
-    )(meta, ints, floats, q, k, v)
-
-
-def local_far(first, many, meta, ints, floats, q, k, v, sel, near, cross):
+    )(meta, ints, floats, q, k, v, sel)
+
+
+def local_far(meta, ints, floats, q, k, v, sel, near, cross):
     return pl.pallas_call(
-        functools.partial(local_kernel, "CD", first, many),
+        functools.partial(local_kernel, "D", 0, PAIRS),
         in_specs=[smem()] + [vmem()] * 8,
         out_specs=[vmem()] * 3,
         out_shape=[
-            shape((RES, GROUPS, many * 128)),
-            shape((GROUPS, many * 128), F32),
-            shape((GROUPS, many * 128), F32),
+            shape((RES, GROUPS, WIDTH)),
+            shape((GROUPS, WIDTH), F32),
+            shape((GROUPS, WIDTH), F32),
         ],
         compiler_params=params(40),
         cost_estimate=pl.CostEstimate(
-            flops=many * 400000000, bytes_accessed=1000000, transcendentals=many * 600000
+            flops=1000000000, bytes_accessed=1000000, transcendentals=2000000
         ),
         name="wide_queries",
     )(meta, ints, floats, q, k, v, sel, near, cross)
@@ -496,7 +502,7 @@
         far_kernel,
         in_specs=[smem()] + [vmem()] * 12,
         out_specs=[vmem()] * 4,
-        out_shape=[shape((GROUPS, 384), F32)] * 4,
+        out_shape=[shape((GROUPS, 256))] * 4,
         compiler_params=params(40),
         cost_estimate=pl.CostEstimate(flops=800000000, bytes_accessed=2000000, transcendentals=1600000),
         name="slide_queries",
@@ -506,16 +512,16 @@
 def merge(meta, close, wide, back):
     return pl.pallas_call(
         merge_kernel,
-        in_specs=[smem()] + [vmem()] * (len(NEAR_PARTS) + 3 * len(WIDE_PARTS) + 4),
+        in_specs=[smem()] + [vmem()] * (len(NEAR_PARTS) + 7),
         out_specs=vmem(),
         out_shape=shape((ROWS, WIDTH)),
         scratch_shapes=[
-            pltpu.VMEM((4, GROUPS, 384), F32),
+            pltpu.VMEM((4, GROUPS, 256), F32),
             pltpu.VMEM((4, 256, WIDTH), BF),
         ],
         compiler_params=params(40),
         name="merge_rows",
-    )(meta, *close, *[part for parts in zip(*wide) for part in parts], *back)
+    )(meta, *close, *wide, *back)
 
 
 def at(x, z, c):
@@ -550,30 +556,26 @@
     meta = jnp.stack([slide_length[0], device])
     ints, floats = (jnp.asarray(table) for table in tables())
     qt, kt, vt, sel, sel8, z0, z1, z2, z3 = split(meta, query_tiles, key_tiles, value_tiles)
-    local = (ints, floats, qt, kt, vt)
     slabs = [z0] + [move(slab, along_z(step)) for step, slab in ((1, z1), (2, z2), (3, z3))]
+    pair = move(sel, other_core)
+    local = (ints, floats, qt, kt, vt, pair)
     close = [local_near(*NEAR_PARTS[0], meta, *local)]
-    slabs, close[0], sel, sel8, later = lax.optimization_barrier(
-        (slabs, close[0], sel, sel8, meta)
-    )
+    slabs, close[0], sel8, later = lax.optimization_barrier((slabs, close[0], sel8, meta))
     own = jnp.concatenate([slab[:, 256:640] for slab in slabs], axis=0)
     own, later = lax.optimization_barrier((own, later))
     moved = [move(own, along_x(step)) for step in (1, 2, 3)]
     near = move(sel8, next_chip)
-    pair = move(sel, other_core)
     close.append(local_near(*NEAR_PARTS[1], later, *local))
-    near, close[1], last = lax.optimization_barrier((near, close[1], later))
+    moved, near, close[1], later = lax.optimization_barrier((moved, near, close[1], later))
     cross = move(near, other_core)
-    close.append(local_near(*NEAR_PARTS[2], last, *local))
-    moved, close[2], last = lax.optimization_barrier((moved, close[2], last))
     blocks = [own] + moved
     blocks += [move(block, other_core) for block in blocks]
-    wide = [local_far(*WIDE_PARTS[0], last, *local, pair, near, cross)]
-    blocks, wide[0] = lax.optimization_barrier((blocks, wide[0]))
+    close.append(local_near(*NEAR_PARTS[2], later, *local))
+    blocks, close[2], later = lax.optimization_barrier((blocks, close[2], later))
     back = slide_wide(meta, [slab[:, 0:256] for slab in slabs], blocks)
-    back, last = lax.optimization_barrier((back, last))
+    back, later = lax.optimization_barrier((back, later))
     back = [back[0]] + [move(back[step], along_z(-step)) for step in (1, 2, 3)]
-    wide.append(local_far(*WIDE_PARTS[1], last, *local, pair, near, cross))
+    wide = local_far(later, *local, near, cross)
     return merge(meta, close, wide, back)
 
 

time: 64.3 us -> 53.4 us (0.83)
  waiting for transfers between devices: 10.3 us -> 2.95 us
  starting transfers between devices: 19.7 us -> 15.9 us
    ppermute x16, waiting for transfers between devices: 10.3 us -> 2.95 us  [move(): return lax.ppermute(block, 'seq', route)]
    ppermute x16, starting transfers between devices: 19.7 us -> 15.9 us  [move(): return lax.ppermute(block, 'seq', route)]
    pallas_call x5 -> x4, Pallas kernels: 21.5 us -> 21.4 us  [the longest x3 14.6 us: local_near(): pl.pallas_call(functools.partial(local_kernel, 'ABC', first, many), in_sp...]
  transfers between devices with their start and end apart: 16 -> 16, of which waited for: 4 -> 2; matrix products, arithmetic and copies ran while one was open for 0% -> 0% of each run, Pallas kernels for 34% -> 47%
where the time goes in v3:
time: 53.4 us; the launch traced here: 53.2 us
  Pallas kernels  30.3 us (57%)
  starting transfers between devices  15.9 us (30%)
  local copies, waits for them, and re-layouts  3.02 us (6%)
  waiting for transfers between devices  2.95 us (6%)
  between operations  0.85 us (2%)
    ppermute x16, starting transfers between devices, move(): return lax.ppermute(block, 'seq', route)  15.9 us
    pallas_call x3, Pallas kernels, local_near(): pl.pallas_call(functools.partial(local_kernel, 'ABC', first, many), in_sp...  14.6 us
    pallas_call x1, Pallas kernels, local_far(): pl.pallas_call(functools.partial(local_kernel, 'D', 0, PAIRS), in_specs=[...  6.81 us
    pallas_call x1, Pallas kernels, slide_wide(): pl.pallas_call(far_kernel, in_specs=[smem()] + [vmem()] * 12, out_specs=[...  3.49 us
    unnamed x10, local copies, waits for them, and re-layouts  2.98 us
    ppermute x16, waiting for transfers between devices, move(): return lax.ppermute(block, 'seq', route)  2.95 us
    pallas_call x1, Pallas kernels, merge(): pl.pallas_call(merge_kernel, in_specs=[smem()] + [vmem()] * (len(NEAR_PAR...  2.86 us
    pallas_call x1, Pallas kernels, split(): pl.pallas_call(split_kernel, in_specs=[smem()] + [vmem()] * 3, out_specs=...  1.43 us
  transfers between devices with their start and end apart: 16, of which 2 were waited for; matrix products, arithmetic and copies ran while one was open for 0% of the time, Pallas kernels for 47%

profile of v3, /device:TPU:1, one launch (start us, length us, event | category | flops | bytes accessed | tf_op | source)
XLA Modules:
  0.0 53.2 jit_solution(1622309620413994391)
XLA Ops:
  0.7 1.4 %copy-done.1 = bf16[1024,768]{1,0:T(8,128)(2,1)S(1)} copy-done((bf16[1024,768]{1,0:T(8,128)(2,1)S(1)}, bf16[1024,768]{1,0:T(8,128)(2,1)}, u32[]{:S(2)}) %copy-start.1) | copy-done | bytes 1572888
  2.1 0.6 %residue_order.2.kt.refs_1_ = bf16[16,64,768]{2,1,0:T(8,128)(2,1)S(1)} custom-call(bf16[1024,768]{1,0:T(8,128)(2,1)S(1)} %copy-done.1), custom_call_target="tpu_custom_call" | custom-call | tf_op jit(solution)/shard_map/residue_order/pallas_call | solution.py:439
  2.6 0.8 %copy-done.2 = bf16[1024,768]{1,0:T(8,128)(2,1)S(1)} copy-done((bf16[1024,768]{1,0:T(8,128)(2,1)S(1)}, bf16[1024,768]{1,0:T(8,128)(2,1)}, u32[]{:S(2)}) %copy-start.2) | copy-done | bytes 1572888
  3.5 0.6 %residue_order.3.vt.refs_2_ = bf16[16,64,768]{2,1,0:T(8,128)(2,1)S(1)} custom-call(bf16[1024,768]{1,0:T(8,128)(2,1)S(1)} %copy-done.2), custom_call_target="tpu_custom_call" | custom-call | tf_op jit(solution)/shard_map/residue_order/pallas_call | solution.py:439
  4.1 0.1 pad_add_fusion.meta
  4.1 0.7 %copy-done = bf16[1024,768]{1,0:T(8,128)(2,1)S(1)} copy-done((bf16[1024,768]{1,0:T(8,128)(2,1)S(1)}, bf16[1024,768]{1,0:T(8,128)(2,1)}, u32[]{:S(2)}) %copy-start) | copy-done | bytes 1572888
  4.9 1.4 %split_rows.1 = (bf16[16,64,768]{2,1,0:T(8,128)(2,1)S(1)}, bf16[4,2,64,768]{3,2,1,0:T(8,128)(2,1)S(1)}, bf16[2,2,64,768]{3,2,1,0:T(8,128)(2,1)S(1)}, bf16[64,640...) custom-call(s32[2]{0:T(128)S(1)} %pad_add_fusion.meta, ...), custom_call_target="tpu_custom_call" | custom-call | tf_op jit(solution)/shard_map/split_rows/pallas_call | solution.py:451
  6.3 1.5 %collective-permute-start.3 = (bf16[4,2,64,768]{3,2,1,0:T(8,128)(2,1)S(1)}, bf16[4,2,64,768]{3,2,1,0:T(8,128)(2,1)S(1)}, u32[]{:S(2)}, u32[]{:S(2)}) collective-permute-start(bf16[4,2,64,768]{3,2,1,0:T(8,128)(2,1)S(1)} %get-tuple-element.54), channel_id=1, source_target_pairs={{0,1},{1,0},{2,3},{3,2},{4,5},{5,4},{6,7},{7,6},{8,9},{9,8},{10,11... | collective-permute-start | bytes 2359304 | tf_op jit(solution)/shard_map/ppermute | solution.py:535
  7.8 1.7 %collective-permute-start = (bf16[64,640]{1,0:T(8,128)(2,1)S(1)}, bf16[64,640]{1,0:T(8,128)(2,1)S(1)}, u32[]{:S(2)}, u32[]{:S(2)}) collective-permute-start(bf16[64,640]{1,0:T(8,128)(2,1)S(1)} %get-tuple-element.50), channel_id=1, source_target_pairs={{0,2},{1,3},{2,4},{3,5},{4,6},{5,7},{6,0},{7,1},{8,10},{9,11},{10,... | collective-permute-start | bytes 245768 | tf_op jit(solution)/shard_map/ppermute | solution.py:535
  9.6 3.3 %collective-permute-start.1 = (bf16[64,640]{1,0:T(8,128)(2,1)S(1)}, bf16[64,640]{1,0:T(8,128)(2,1)S(1)}, u32[]{:S(2)}, u32[]{:S(2)}) collective-permute-start(bf16[64,640]{1,0:T(8,128)(2,1)S(1)} %get-tuple-element.51), channel_id=1, source_target_pairs={{0,4},{1,5},{2,6},{3,7},{4,0},{5,1},{6,2},{7,3},{8,12},{9,13},{10,... | collective-permute-start | bytes 245768 | tf_op jit(solution)/shard_map/ppermute | solution.py:535
  12.8 0.7 %collective-permute-start.2 = (bf16[64,640]{1,0:T(8,128)(2,1)S(1)}, bf16[64,640]{1,0:T(8,128)(2,1)S(1)}, u32[]{:S(2)}, u32[]{:S(2)}) collective-permute-start(bf16[64,640]{1,0:T(8,128)(2,1)S(1)} %get-tuple-element.52), channel_id=1, source_target_pairs={{0,6},{1,7},{2,0},{3,1},{4,2},{5,3},{6,4},{7,5},{8,14},{9,15},{10,... | collective-permute-start | bytes 245768 | tf_op jit(solution)/shard_map/ppermute | solution.py:535
  13.6 2.7 %near_queries.3.refs_0_ = bf16[16,64,128]{2,1,0:T(8,128)(2,1)S(1)} custom-call(s32[2]{0:T(128)S(1)} %pad_add_fusion.meta, s32[8,256]{1,0:T(8,128)S(1)} %copy-done.4, f32[8,256]{1,0:T(8,128)S(1)} %copy-done.3, bf16[16,64,768]{2,1,0:T(8,128)(2,1)S(1)} %get-tuple-element.53.refs_0_, bf16[16,64,768]{2,1,0:T(8,128)(2,1)S(1)} %residue_order.2.kt.refs_1_, ...), custom_call_target="tpu_custom_call" | custom-call | flops 600000000 | bytes 1000000 | tf_op jit(solution)/shard_map/near_queries/pallas_call | solution.py:469
  16.3 0.0 collective-permute-done
  16.3 0.8 %collective-permute-done.1 = bf16[64,640]{1,0:T(8,128)(2,1)S(1)} collective-permute-done((bf16[64,640]{1,0:T(8,128)(2,1)S(1)}, bf16[64,640]{1,0:T(8,128)(2,1)S(1)}, u32[]{:S(2)}, u32[]{:S(2)}) %collective-permute-start.1) | collective-permute-done | bytes 81952 | tf_op jit(solution)/shard_map/ppermute | solution.py:535
  17.1 0.7 %collective-permute-start.7 = (bf16[2,2,64,768]{3,2,1,0:T(8,128)(2,1)S(1)}, bf16[2,2,64,768]{3,2,1,0:T(8,128)(2,1)S(1)}, u32[]{:S(2)}, u32[]{:S(2)}) collective-permute-start(bf16[2,2,64,768]{3,2,1,0:T(8,128)(2,1)S(1)} %get-tuple-element.63), channel_id=1, source_target_pairs={{0,2},{1,3},{2,0},{3,1},{4,6},{5,7},{6,4},{7,5},{8,10},{9,11},{10,... | collective-permute-start | bytes 1179656 | tf_op jit(solution)/shard_map/ppermute | solution.py:535
  17.9 2.5 %collective-permute-start.6 = (bf16[256,384]{1,0:T(8,128)(2,1)S(1)}, bf16[256,384]{1,0:T(8,128)(2,1)S(1)}, u32[]{:S(2)}, u32[]{:S(2)}) collective-permute-start(bf16[256,384]{1,0:T(8,128)(2,1)S(1)} %pad_maximum_fusion.rest_0_), channel_id=1, source_target_pairs={{0,24},{1,25},{2,26},{3,27},{4,28},{5,29},{6,30},{7,31},{8,0},{9,1... | collective-permute-start | bytes 589832 | tf_op jit(solution)/shard_map/ppermute | solution.py:535
  20.4 0.6 %collective-permute-start.5 = (bf16[256,384]{1,0:T(8,128)(2,1)S(1)}, bf16[256,384]{1,0:T(8,128)(2,1)S(1)}, u32[]{:S(2)}, u32[]{:S(2)}) collective-permute-start(bf16[256,384]{1,0:T(8,128)(2,1)S(1)} %pad_maximum_fusion.rest_0_), channel_id=1, source_target_pairs={{0,16},{1,17},{2,18},{3,19},{4,20},{5,21},{6,22},{7,23},{8,24},{9,... | collective-permute-start | bytes 589832 | tf_op jit(solution)/shard_map/ppermute | solution.py:535
  21.0 0.6 %collective-permute-start.4 = (bf16[256,384]{1,0:T(8,128)(2,1)S(1)}, bf16[256,384]{1,0:T(8,128)(2,1)S(1)}, u32[]{:S(2)}, u32[]{:S(2)}) collective-permute-start(bf16[256,384]{1,0:T(8,128)(2,1)S(1)} %pad_maximum_fusion.rest_0_), channel_id=1, source_target_pairs={{0,8},{1,9},{2,10},{3,11},{4,12},{5,13},{6,14},{7,15},{8,16},{9,17... | collective-permute-start | bytes 589832 | tf_op jit(solution)/shard_map/ppermute | solution.py:535
  21.5 9.2 %near_queries.4.refs_1_ = bf16[16,64,512]{2,1,0:T(8,128)(2,1)S(1)} custom-call(s32[2]{0:T(128)S(1)} %pad_add_fusion.meta, s32[8,256]{1,0:T(8,128)S(1)} %copy-done.4, f32[8,256]{1,0:T(8,128)S(1)} %copy-done.3, bf16[16,64,768]{2,1,0:T(8,128)(2,1)S(1)} %get-tuple-element.53.refs_0_, bf16[16,64,768]{2,1,0:T(8,128)(2,1)S(1)} %residue_order.2.kt.refs_1_, ...), custom_call_target="tpu_custom_call" | custom-call | flops 2400000000 | bytes 1000000 | tf_op jit(solution)/shard_map/near_queries/pallas_call | solution.py:469
  30.8 2.1 %collective-permute-done.4.rest_1_ = bf16[256,384]{1,0:T(8,128)(2,1)S(1)} collective-permute-done((bf16[256,384]{1,0:T(8,128)(2,1)S(1)}, bf16[256,384]{1,0:T(8,128)(2,1)S(1)}, u32[]{:S(2)}, u32[]{:S(2)}) %collective-permute-start.4) | collective-permute-done | bytes 196640 | tf_op jit(solution)/shard_map/ppermute | solution.py:535
  32.8 0.6 %collective-permute-start.12 = (bf16[2,2,64,768]{3,2,1,0:T(8,128)(2,1)S(1)}, bf16[2,2,64,768]{3,2,1,0:T(8,128)(2,1)S(1)}, u32[]{:S(2)}, u32[]{:S(2)}) collective-permute-start(bf16[2,2,64,768]{3,2,1,0:T(8,128)(2,1)S(1)} %collective-permute-done.7.refs_4_), channel_id=1, source_target_pairs={{0,1},{1,0},{2,3},{3,2},{4,5},{5,4},{6,7},{7,6},{8,9},{9,8},{10,11... | collective-permute-start | bytes 1179656 | tf_op jit(solution)/shard_map/ppermute | solution.py:535
  33.5 0.0 collective-permute-start.8
  33.5 0.5 collective-permute-start.9
  34.0 0.0 collective-permute-start.10
  34.0 0.5 collective-permute-start.11
  34.5 2.7 %near_queries.5.refs_2_ = bf16[16,64,128]{2,1,0:T(8,128)(2,1)S(1)} custom-call(s32[2]{0:T(128)S(1)} %pad_add_fusion.meta, s32[8,256]{1,0:T(8,128)S(1)} %copy-done.4, f32[8,256]{1,0:T(8,128)S(1)} %copy-done.3, bf16[16,64,768]{2,1,0:T(8,128)(2,1)S(1)} %get-tuple-element.53.refs_0_, bf16[16,64,768]{2,1,0:T(8,128)(2,1)S(1)} %residue_order.2.kt.refs_1_, ...), custom_call_target="tpu_custom_call" | custom-call | flops 600000000 | bytes 1000000 | tf_op jit(solution)/shard_map/near_queries/pallas_call | solution.py:469
  37.3 3.5 %slide_queries.1 = (bf16[64,256]{1,0:T(8,128)(2,1)S(1)}, bf16[64,256]{1,0:T(8,128)(2,1)S(1)}, bf16[64,256]{1,0:T(8,128)(2,1)S(1)}, bf16[64,256]{1,0:T(8,128)(2,1)S(1)}) custom-call(s32[2]{0:T(128)S(1)} %pad_add_fusion.meta, bf16[64,256]{1,0:T(8,128)(2,1)S(1)} %slice.28.a0, bf16[64,256]{1,0:T(8,128)(2,1)S(1)} %slice.29.a1, bf16[64,256]{1,0:T(8,128)(2,1)S(1)} %slice.30.a2, ...), custom_call_target="tpu_custom_call" | custom-call | flops 800000000 | bytes 2000000 | tf_op jit(solution)/shard_map/slide_queries/pallas_call | solution.py:501
  40.8 1.3 %collective-permute-start.13 = (bf16[64,256]{1,0:T(8,128)(2,1)S(1)}, bf16[64,256]{1,0:T(8,128)(2,1)S(1)}, u32[]{:S(2)}, u32[]{:S(2)}) collective-permute-start(bf16[64,256]{1,0:T(8,128)(2,1)S(1)} %get-tuple-element.90), channel_id=1, source_target_pairs={{0,6},{1,7},{2,0},{3,1},{4,2},{5,3},{6,4},{7,5},{8,14},{9,15},{10,... | collective-permute-start | bytes 98312 | tf_op jit(solution)/shard_map/ppermute | solution.py:535
  42.1 1.3 %collective-permute-start.14 = (bf16[64,256]{1,0:T(8,128)(2,1)S(1)}, bf16[64,256]{1,0:T(8,128)(2,1)S(1)}, u32[]{:S(2)}, u32[]{:S(2)}) collective-permute-start(bf16[64,256]{1,0:T(8,128)(2,1)S(1)} %get-tuple-element.91), channel_id=1, source_target_pairs={{0,4},{1,5},{2,6},{3,7},{4,0},{5,1},{6,2},{7,3},{8,12},{9,13},{10,... | collective-permute-start | bytes 98312 | tf_op jit(solution)/shard_map/ppermute | solution.py:535
  43.4 0.1 collective-permute-start.15
  43.5 6.8 %wide_queries.1 = (bf16[16,64,768]{2,1,0:T(8,128)(2,1)S(1)}, f32[64,768]{1,0:T(8,128)S(1)}, f32[64,768]{1,0:T(8,128)S(1)}) custom-call(s32[2]{0:T(128)S(1)} %pad_add_fusion.meta, s32[8,256]{1,0:T(8,128)S(1)} %copy-done.4, f32[8,256]{1,0:T(8,128)S(1)} %copy-done.3, bf16[16,64,768]{2,1,0:T(8,128)(2,1)S(1)} %get-tuple-element.53.refs_0_, ...), custom_call_target="tpu_custom_call" | custom-call | flops 1000000000 | bytes 1000000 | tf_op jit(solution)/shard_map/wide_queries/pallas_call | solution.py:483
  50.3 2.9 %merge_rows.1 = bf16[1024,768]{1,0:T(8,128)(2,1)} custom-call(s32[2]{0:T(128)S(1)} %pad_add_fusion.meta, bf16[16,64,128]{2,1,0:T(8,128)(2,1)S(1)} %near_queries.3.refs_0_, bf16[16,64,512]{2,1,0:T(8,128)(2,1)S(1)} %near_queries.4.refs_1_, bf16[16,64,128]{2,1,0:T(8,128)(2,1)S(1)} %near_queries.5.refs_2_, bf16[16,64,768]{2,1,0:T(8,128)(2,1)S(1)} %get-tuple-element.86.refs_3_, ...), custom_call_target="tpu_custom_call" | custom-call | tf_op jit(solution)/shard_map/merge_rows/pallas_call | solution.py:513
  (29 shorter events, 0.1 us)
Async XLA Ops:
  0.7 1.4 %copy-start.1 = (bf16[1024,768]{1,0:T(8,128)(2,1)S(1)}, bf16[1024,768]{1,0:T(8,128)(2,1)}, u32[]{:S(2)}) copy-start(bf16[1024,768]{1,0:T(8,128)(2,1)} %source.2) | copy-start | bytes 4718596
  2.1 1.4 %copy-start.2 = (bf16[1024,768]{1,0:T(8,128)(2,1)S(1)}, bf16[1024,768]{1,0:T(8,128)(2,1)}, u32[]{:S(2)}) copy-start(bf16[1024,768]{1,0:T(8,128)(2,1)} %source.3) | copy-start | bytes 4718596
  3.5 1.4 %copy-start = (bf16[1024,768]{1,0:T(8,128)(2,1)S(1)}, bf16[1024,768]{1,0:T(8,128)(2,1)}, u32[]{:S(2)}) copy-start(bf16[1024,768]{1,0:T(8,128)(2,1)} %q_in.1) | copy-start | bytes 4718596
  4.9 8.7 %copy-start.3 = (f32[8,256]{1,0:T(8,128)S(1)}, f32[8,256]{1,0:T(8,128)}, u32[]{:S(2)}) copy-start(f32[8,256]{1,0:T(8,128)} %constant.9.clone.floats) | copy-start | bytes 24580
  4.9 8.7 %copy-start.4 = (s32[8,256]{1,0:T(8,128)S(1)}, s32[8,256]{1,0:T(8,128)}, u32[]{:S(2)}) copy-start(s32[8,256]{1,0:T(8,128)} %constant.8.clone.ints) | copy-start | bytes 24580
  6.3 7.3 %collective-permute-start.3 = (bf16[4,2,64,768]{3,2,1,0:T(8,128)(2,1)S(1)}, bf16[4,2,64,768]{3,2,1,0:T(8,128)(2,1)S(1)}, u32[]{:S(2)}, u32[]{:S(2)}) collective-permute-start(bf16[4,2,64,768]{3,2,1,0:T(8,128)(2,1)S(1)} %get-tuple-element.54), channel_id=1, source_target_pairs={{0,1},{1,0},{2,3},{3,2},{4,5},{5,4},{6,7},{7,6},{8,9},{9,8},{10,11... | collective-permute-start | bytes 2359304 | tf_op jit(solution)/shard_map/ppermute | solution.py:535
  7.8 8.5 %collective-permute-start = (bf16[64,640]{1,0:T(8,128)(2,1)S(1)}, bf16[64,640]{1,0:T(8,128)(2,1)S(1)}, u32[]{:S(2)}, u32[]{:S(2)}) collective-permute-start(bf16[64,640]{1,0:T(8,128)(2,1)S(1)} %get-tuple-element.50), channel_id=1, source_target_pairs={{0,2},{1,3},{2,4},{3,5},{4,6},{5,7},{6,0},{7,1},{8,10},{9,11},{10,... | collective-permute-start | bytes 245768 | tf_op jit(solution)/shard_map/ppermute | solution.py:535
  9.6 7.6 %collective-permute-start.1 = (bf16[64,640]{1,0:T(8,128)(2,1)S(1)}, bf16[64,640]{1,0:T(8,128)(2,1)S(1)}, u32[]{:S(2)}, u32[]{:S(2)}) collective-permute-start(bf16[64,640]{1,0:T(8,128)(2,1)S(1)} %get-tuple-element.51), channel_id=1, source_target_pairs={{0,4},{1,5},{2,6},{3,7},{4,0},{5,1},{6,2},{7,3},{8,12},{9,13},{10,... | collective-permute-start | bytes 245768 | tf_op jit(solution)/shard_map/ppermute | solution.py:535
  12.8 4.3 %collective-permute-start.2 = (bf16[64,640]{1,0:T(8,128)(2,1)S(1)}, bf16[64,640]{1,0:T(8,128)(2,1)S(1)}, u32[]{:S(2)}, u32[]{:S(2)}) collective-permute-start(bf16[64,640]{1,0:T(8,128)(2,1)S(1)} %get-tuple-element.52), channel_id=1, source_target_pairs={{0,6},{1,7},{2,0},{3,1},{4,2},{5,3},{6,4},{7,5},{8,14},{9,15},{10,... | collective-permute-start | bytes 245768 | tf_op jit(solution)/shard_map/ppermute | solution.py:535
  17.1 15.7 %collective-permute-start.7 = (bf16[2,2,64,768]{3,2,1,0:T(8,128)(2,1)S(1)}, bf16[2,2,64,768]{3,2,1,0:T(8,128)(2,1)S(1)}, u32[]{:S(2)}, u32[]{:S(2)}) collective-permute-start(bf16[2,2,64,768]{3,2,1,0:T(8,128)(2,1)S(1)} %get-tuple-element.63), channel_id=1, source_target_pairs={{0,2},{1,3},{2,0},{3,1},{4,6},{5,7},{6,4},{7,5},{8,10},{9,11},{10,... | collective-permute-start | bytes 1179656 | tf_op jit(solution)/shard_map/ppermute | solution.py:535
  17.9 12.8 %collective-permute-start.6 = (bf16[256,384]{1,0:T(8,128)(2,1)S(1)}, bf16[256,384]{1,0:T(8,128)(2,1)S(1)}, u32[]{:S(2)}, u32[]{:S(2)}) collective-permute-start(bf16[256,384]{1,0:T(8,128)(2,1)S(1)} %pad_maximum_fusion.rest_0_), channel_id=1, source_target_pairs={{0,24},{1,25},{2,26},{3,27},{4,28},{5,29},{6,30},{7,31},{8,0},{9,1... | collective-permute-start | bytes 589832 | tf_op jit(solution)/shard_map/ppermute | solution.py:535
  20.4 10.3 %collective-permute-start.5 = (bf16[256,384]{1,0:T(8,128)(2,1)S(1)}, bf16[256,384]{1,0:T(8,128)(2,1)S(1)}, u32[]{:S(2)}, u32[]{:S(2)}) collective-permute-start(bf16[256,384]{1,0:T(8,128)(2,1)S(1)} %pad_maximum_fusion.rest_0_), channel_id=1, source_target_pairs={{0,16},{1,17},{2,18},{3,19},{4,20},{5,21},{6,22},{7,23},{8,24},{9,... | collective-permute-start | bytes 589832 | tf_op jit(solution)/shard_map/ppermute | solution.py:535
  21.0 11.8 %collective-permute-start.4 = (bf16[256,384]{1,0:T(8,128)(2,1)S(1)}, bf16[256,384]{1,0:T(8,128)(2,1)S(1)}, u32[]{:S(2)}, u32[]{:S(2)}) collective-permute-start(bf16[256,384]{1,0:T(8,128)(2,1)S(1)} %pad_maximum_fusion.rest_0_), channel_id=1, source_target_pairs={{0,8},{1,9},{2,10},{3,11},{4,12},{5,13},{6,14},{7,15},{8,16},{9,17... | collective-permute-start | bytes 589832 | tf_op jit(solution)/shard_map/ppermute | solution.py:535
  32.8 10.6 %collective-permute-start.12 = (bf16[2,2,64,768]{3,2,1,0:T(8,128)(2,1)S(1)}, bf16[2,2,64,768]{3,2,1,0:T(8,128)(2,1)S(1)}, u32[]{:S(2)}, u32[]{:S(2)}) collective-permute-start(bf16[2,2,64,768]{3,2,1,0:T(8,128)(2,1)S(1)} %collective-permute-done.7.refs_4_), channel_id=1, source_target_pairs={{0,1},{1,0},{2,3},{3,2},{4,5},{5,4},{6,7},{7,6},{8,9},{9,8},{10,11... | collective-permute-start | bytes 1179656 | tf_op jit(solution)/shard_map/ppermute | solution.py:535
  33.5 3.7 %collective-permute-start.8 = (bf16[256,384]{1,0:T(8,128)(2,1)S(1)}, bf16[256,384]{1,0:T(8,128)(2,1)S(1)}, u32[]{:S(2)}, u32[]{:S(2)}) collective-permute-start(bf16[256,384]{1,0:T(8,128)(2,1)S(1)} %pad_maximum_fusion.rest_0_), channel_id=1, source_target_pairs={{0,1},{1,0},{2,3},{3,2},{4,5},{5,4},{6,7},{7,6},{8,9},{9,8},{10,11... | collective-permute-start | bytes 589832 | tf_op jit(solution)/shard_map/ppermute | solution.py:535
  33.5 3.8 %collective-permute-start.9 = (bf16[256,384]{1,0:T(8,128)(2,1)S(1)}, bf16[256,384]{1,0:T(8,128)(2,1)S(1)}, u32[]{:S(2)}, u32[]{:S(2)}) collective-permute-start(bf16[256,384]{1,0:T(8,128)(2,1)S(1)} %collective-permute-done.4.rest_1_), channel_id=1, source_target_pairs={{0,1},{1,0},{2,3},{3,2},{4,5},{5,4},{6,7},{7,6},{8,9},{9,8},{10,11... | collective-permute-start | bytes 589832 | tf_op jit(solution)/shard_map/ppermute | solution.py:535
  34.0 3.3 %collective-permute-start.10 = (bf16[256,384]{1,0:T(8,128)(2,1)S(1)}, bf16[256,384]{1,0:T(8,128)(2,1)S(1)}, u32[]{:S(2)}, u32[]{:S(2)}) collective-permute-start(bf16[256,384]{1,0:T(8,128)(2,1)S(1)} %collective-permute-done.5.rest_2_), channel_id=1, source_target_pairs={{0,1},{1,0},{2,3},{3,2},{4,5},{5,4},{6,7},{7,6},{8,9},{9,8},{10,11... | collective-permute-start | bytes 589832 | tf_op jit(solution)/shard_map/ppermute | solution.py:535
  34.0 3.3 %collective-permute-start.11 = (bf16[256,384]{1,0:T(8,128)(2,1)S(1)}, bf16[256,384]{1,0:T(8,128)(2,1)S(1)}, u32[]{:S(2)}, u32[]{:S(2)}) collective-permute-start(bf16[256,384]{1,0:T(8,128)(2,1)S(1)} %collective-permute-done.6.rest_3_), channel_id=1, source_target_pairs={{0,1},{1,0},{2,3},{3,2},{4,5},{5,4},{6,7},{7,6},{8,9},{9,8},{10,11... | collective-permute-start | bytes 589832 | tf_op jit(solution)/shard_map/ppermute | solution.py:535
  40.8 9.5 %collective-permute-start.13 = (bf16[64,256]{1,0:T(8,128)(2,1)S(1)}, bf16[64,256]{1,0:T(8,128)(2,1)S(1)}, u32[]{:S(2)}, u32[]{:S(2)}) collective-permute-start(bf16[64,256]{1,0:T(8,128)(2,1)S(1)} %get-tuple-element.90), channel_id=1, source_target_pairs={{0,6},{1,7},{2,0},{3,1},{4,2},{5,3},{6,4},{7,5},{8,14},{9,15},{10,... | collective-permute-start | bytes 98312 | tf_op jit(solution)/shard_map/ppermute | solution.py:535
  42.1 8.2 %collective-permute-start.14 = (bf16[64,256]{1,0:T(8,128)(2,1)S(1)}, bf16[64,256]{1,0:T(8,128)(2,1)S(1)}, u32[]{:S(2)}, u32[]{:S(2)}) collective-permute-start(bf16[64,256]{1,0:T(8,128)(2,1)S(1)} %get-tuple-element.91), channel_id=1, source_target_pairs={{0,4},{1,5},{2,6},{3,7},{4,0},{5,1},{6,2},{7,3},{8,12},{9,13},{10,... | collective-permute-start | bytes 98312 | tf_op jit(solution)/shard_map/ppermute | solution.py:535
  43.4 6.9 %collective-permute-start.15 = (bf16[64,256]{1,0:T(8,128)(2,1)S(1)}, bf16[64,256]{1,0:T(8,128)(2,1)S(1)}, u32[]{:S(2)}, u32[]{:S(2)}) collective-permute-start(bf16[64,256]{1,0:T(8,128)(2,1)S(1)} %get-tuple-element.92), channel_id=1, source_target_pairs={{0,2},{1,3},{2,4},{3,5},{4,6},{5,7},{6,0},{7,1},{8,10},{9,11},{10,... | collective-permute-start | bytes 98312 | tf_op jit(solution)/shard_map/ppermute | solution.py:535

commit v4 on v3

--- a/solution.py
+++ b/solution.py
@@ -23,7 +23,6 @@
 F32 = jnp.float32
 
 ODD = [1, 3, 5, 7, 9, 11, 13, 15]
-EVEN = [2, 6, 10, 14, 4, 12, 8, 0]
 SHARED = [0, 8, 4, 12]
 CLASS_U = {"A": ODD, "B": [2, 6, 10, 14], "C": [4, 12], "D": [8, 0]}
 PAIR_OF = [0, 2, 3, 5]
@@ -33,27 +32,6 @@
 
 def level(u):
     return 4 if u == 0 else min((u & -u).bit_length() - 1, 4)
-
-
-def tables():
-    lane = np.arange(256)
-    ints = np.zeros((8, 256), np.int32)
-    ints[0] = np.array(ODD)[lane // 32]
-    ints[1] = np.array(EVEN)[lane // 32]
-    ints[2] = lane % 32 * 16
-    ints[3] = np.array(SHARED)[lane // 64]
-    ints[4] = lane % 64 * 16
-    ints[5] = np.array([0, 8, 0, 8])[lane // 64]
-    even = np.array([level(u) for u in EVEN])[lane // 32]
-    shared = np.array([level(u) for u in SHARED])[lane // 64]
-    floats = np.zeros((8, 256), np.float32)
-    floats[1] = np.log(1.0 + np.minimum(even, 1))
-    floats[2] = np.log(1.0 + np.minimum(even, 2))
-    floats[3] = np.log(1.0 + np.minimum(even, 3))
-    floats[4] = np.log(1.0 * np.minimum(even, 2))
-    floats[5] = np.log(1.0 * np.minimum(even, 3))
-    floats[6] = np.log(np.minimum(shared, 3) - 1.0)
-    return ints, floats
 
 
 def swap_matrix():
@@ -135,7 +113,7 @@
     return total, peak
 
 
-def local_kernel(classes, first, many, meta, ints, floats, *refs):
+def local_kernel(classes, first, many, meta, *refs):
     def body(step, carry):
         lanes = pl.ds(pl.multiple_of((first + step) * 128, 128), 128)
         here = pl.ds(pl.multiple_of(step * 128, 128), 128)
@@ -146,13 +124,13 @@
             views += [ref.at[:, here] for ref in refs[7:9]]
         else:
             views += [refs[4].at[:, :, here]]
-        local_pair(classes, first + step, meta, ints, floats, *views)
+        local_pair(classes, first + step, meta, *views)
         return carry
 
-    lax.fori_loop(0, many, body, 0)
-
-
-def local_pair(classes, pair, meta, ints, floats, q_ref, k_ref, v_ref, sel, *rest):
+    lax.fori_loop(0, many, body, 0, unroll=True)
+
+
+def local_pair(classes, pair, meta, q_ref, k_ref, v_ref, sel, *rest):
     far = classes == "D"
     if far:
         near, cross, out, o0, lse0 = rest
@@ -160,129 +138,138 @@
         (out,) = rest
     bound = meta[0]
     device = meta[1]
-    low = lane_low(256)
-    low_all = lane_low(128 if far else 896)
-    high_all = jnp.logical_not(low_all)
+    lane = lax.broadcasted_iota(jnp.int32, (1, 256), 1)
+    groups = [(name, 0) for name in classes] + [(name, 1) for name in classes[::-1]]
+    caps = [("ABCD".index(name), side) for name, side in groups]
+    starts = [0]
+    for name, _ in groups:
+        starts.append(starts[-1] + len(CLASS_U[name]) * HALF)
+    low = lane_low(starts[-1])
+
+    def rows_of(ref, tile):
+        half, odd = tile // 2, tile % 2
+        rows = slice(half * HALF, (half + 1) * HALF)
+        return jnp.concatenate([ref[2 * at + odd, rows, :] for at in range(8)], axis=0)
+
+    keys = [rows_of(k_ref, tile) for tile in range(4)] + [sel[:, 0].reshape(256, 128)]
+    values = [rows_of(v_ref, tile) for tile in range(4)] + [sel[:, 1].reshape(256, 128)]
+    if far:
+        for kv, rows in enumerate((keys, values)):
+            rows.append(
+                jnp.concatenate([near[0, kv], near[1, kv], cross[0, kv], cross[1, kv]], axis=0)
+            )
+
+    def inside(tile, parity, cap, side):
+        if tile >= 4:
+            return cap >= tile - 2
+        return side == tile // 2 or (tile % 2 == parity and cap >= 1)
+
+    def bias(tile, parity, cap, side):
+        head = 2 * pair + parity
+        logs = jnp.zeros((1, 256), F32)
+        if tile < 4:
+            half, odd = tile // 2, tile % 2
+            res = 2 * (lane >> 5) + odd
+            position = device * ROWS + half * 512 + (lane & 31) * 16 + res
+            if odd == parity and cap >= 1:
+                u = (res - head) & 15
+                extra = 1.0 if side == half else 0.0
+                one, two, three = (float(np.log(extra + min(cap, rank))) for rank in (1, 2, 3))
+                logs = jnp.where(
+                    (u & 2) != 0, one, jnp.where((u & 4) != 0, two, three)
+                ) + jnp.zeros((1, 256), F32)
+        elif tile == 4:
+            u = ((lane >> 6) & 1) * 8 + (lane >> 7) * 4
+            position = (device ^ 1) * ROWS + (lane & 63) * 16 + ((u + head) & 15)
+            if cap == 3:
+                logs = jnp.where(lane < 128, float(np.log(2.0)), 0.0)
+        else:
+            u = ((lane >> 6) & 1) * 8
+            source = jnp.where(lane < 128, device ^ 2, device ^ 3)
+            position = source * ROWS + (lane & 63) * 16 + ((u + head) & 15)
+        return jnp.where(position < bound, logs, MASKED)
+
+    queries = []
     for parity in range(2):
         head = 2 * pair + parity
+        query = jnp.concatenate(
+            [
+                q_ref[(u + head) & 15, side * HALF : (side + 1) * HALF, :]
+                for name, side in groups
+                for u in CLASS_U[name]
+            ],
+            axis=0,
+        )
         mine = low if parity == 0 else jnp.logical_not(low)
-
-        def gathered(ref, order, half):
-            return jnp.concatenate(
-                [ref[(u + head) & 15, half * HALF : (half + 1) * HALF, :] for u in order], axis=0
-            )
-
-        def widened(value):
-            return jnp.where(mine, value, jnp.ones_like(value))
-
-        def bias(kind, place, device_of, offset, row):
-            position = (
-                device_of * ROWS
-                + offset
-                + ints[place : place + 1, :]
-                + ((ints[kind : kind + 1, :] + head) & 15)
-            )
-            return jnp.where(position < bound, floats[row : row + 1, :], MASKED)
-
-        odd_k = [gathered(k_ref, ODD, half) for half in range(2)]
-        even_k = [gathered(k_ref, EVEN, half) for half in range(2)]
-        odd_v = [widened(gathered(v_ref, ODD, half)) for half in range(2)]
-        even_v = [widened(gathered(v_ref, EVEN, half)) for half in range(2)]
-        pair_k = sel[:, 0].reshape(256, 128)
-        pair_v = widened(sel[:, 1].reshape(256, 128))
-        if far:
-            next_k = jnp.concatenate([near[0, 0], near[1, 0], cross[0, 0], cross[1, 0]], axis=0)
-            next_v = widened(
-                jnp.concatenate([near[0, 1], near[1, 1], cross[0, 1], cross[1, 1]], axis=0)
-            )
-            lane = lax.broadcasted_iota(jnp.int32, (1, 256), 1)
-            next_device = jnp.where(lane < 128, device ^ 2, device ^ 3)
-        groups = [(name, 0) for name in classes] + [(name, 1) for name in classes[::-1]]
-        tiles = []
-        for half in range(2):
-            tiles.append((odd_k[half], odd_v[half], lambda cap, side, half=half: side == half))
-            tiles.append(
-                (even_k[half], even_v[half], lambda cap, side, half=half: side == half or cap >= 1)
-            )
-        tiles.append((pair_k, pair_v, lambda cap, side: cap >= 2))
-        if far:
-            tiles.append((next_k, next_v, lambda cap, side: cap >= 3))
-
-        def tile_bias(tile, cap, side):
-            if tile >= 4:
-                if tile == 5:
-                    return bias(5, 4, next_device, 0, 0)
-                return bias(3, 4, device ^ 1, 0, (0, 0, 0, 6)[cap])
-            offset = tile // 2 * 512
-            if tile % 2 == 0:
-                return bias(0, 2, device, offset, 0)
-            row = cap if tile // 2 == side else (0, 0, 4, 5)[cap]
-            return bias(1, 2, device, offset, row)
-
-        pieces, starts, count = [], [], 0
-        for name, side in groups:
-            pieces.append(gathered(q_ref, CLASS_U[name], side))
-            starts.append(count)
-            count += pieces[-1].shape[0]
-        starts.append(count)
-        query = jnp.concatenate(pieces, axis=0)
-        query = (jnp.where(low_all if parity == 0 else high_all, query, jnp.zeros_like(query)) * 0.125).astype(BF)
-        caps = [("ABCD".index(name), side) for name, side in groups]
-        scores, spans = [], []
-        for key, value, member in tiles:
-            inside = [at for at, (cap, side) in enumerate(caps) if member(cap, side)]
-            first, last = inside[0], inside[-1] + 1
-            spans.append((first, last))
-            scores.append(
-                lax.dot_general(
-                    query[starts[first] : starts[last]],
-                    key,
-                    (((1,), (1,)), ((), ())),
-                    preferred_element_type=F32,
-                )
-            )
-        weights = [[] for _ in tiles]
-        peaks = []
+        queries.append((jnp.where(mine, query, jnp.zeros_like(query)) * 0.125).astype(BF))
+    scores, spans = {}, {}
+    for tile, key in enumerate(keys):
+        parts = []
+        for parity in range(2):
+            held = [at for at, (cap, side) in enumerate(caps) if inside(tile, parity, cap, side)]
+            spans[tile, parity] = (held[0], held[-1] + 1)
+            parts.append(queries[parity][starts[held[0]] : starts[held[-1] + 1]])
+        both = lax.dot_general(
+            jnp.concatenate(parts, axis=0),
+            key,
+            (((1,), (1,)), ((), ())),
+            preferred_element_type=F32,
+        )
+        cut = parts[0].shape[0]
+        scores[tile, 0], scores[tile, 1] = both[:cut], both[cut:]
+    weights = {spot: [] for spot in spans}
+    peaks = {}
+    for parity in range(2):
         for at, (cap, side) in enumerate(caps):
             held = []
-            for tile, (first, last) in enumerate(spans):
+            for tile in range(len(keys)):
+                first, last = spans[tile, parity]
                 if first <= at < last:
                     base = starts[first]
                     held.append(
                         (
                             tile,
-                            scores[tile][starts[at] - base : starts[at + 1] - base]
-                            + tile_bias(tile, cap, side),
+                            scores[tile, parity][starts[at] - base : starts[at + 1] - base]
+                            + bias(tile, parity, cap, side),
                         )
                     )
             peak = functools.reduce(jnp.maximum, [score for _, score in held])
             peak = jnp.max(peak, axis=1, keepdims=True)
-            peaks.append(peak)
+            peaks[parity, at] = peak
             for tile, score in held:
-                weights[tile].append(jnp.exp(score - peak).astype(BF))
-        totals = [None] * len(caps)
-        for tile, (first, last) in enumerate(spans):
+                weights[tile, parity].append(jnp.exp(score - peak).astype(BF))
+    totals = {}
+    for tile, value in enumerate(values):
+        for parity in range(2):
+            side = lane_low(256) if parity == 0 else jnp.logical_not(lane_low(256))
             part = jnp.dot(
-                jnp.concatenate(weights[tile], axis=0), tiles[tile][1], preferred_element_type=F32
+                jnp.concatenate(weights[tile, parity], axis=0),
+                jnp.where(side, value, jnp.ones_like(value)),
+                preferred_element_type=F32,
             )
-            for at in range(first, last):
-                rows = part[starts[at] - starts[first] : starts[at + 1] - starts[first]]
-                totals[at] = rows if totals[at] is None else totals[at] + rows
+            base = 0
+            for at in range(*spans[tile, parity]):
+                count = starts[at + 1] - starts[at]
+                rows = part[base : base + count]
+                base += count
+                spot = (parity, at)
+                totals[spot] = totals[spot] + rows if spot in totals else rows
+    for parity in range(2):
+        head = 2 * pair + parity
+        mine = low[:HALF] if parity == 0 else jnp.logical_not(low[:HALF])
         for at, (name, half) in enumerate(groups):
-            total, peak = totals[at], peaks[at]
+            total = totals[parity, at]
             sums = pltpu.roll(total, 64, 1)
             result = total / sums
             rounded = result.astype(BF)
+            rows = slice(half * HALF, (half + 1) * HALF)
             for row, u in enumerate(CLASS_U[name]):
-                spot = ((u + head) & 15, slice(half * HALF, (half + 1) * HALF), slice(None))
-                out[spot] = jnp.where(
-                    mine[:HALF], rounded[row * HALF : (row + 1) * HALF, :], out[spot]
-                )
+                spot = ((u + head) & 15, rows, slice(None))
+                out[spot] = jnp.where(mine, rounded[row * HALF : (row + 1) * HALF, :], out[spot])
             if name == "D":
-                rows = slice(half * HALF, (half + 1) * HALF)
-                log_total = peak[HALF:] + jnp.log(sums[HALF:])
-                o0[rows, :] = jnp.where(mine[:HALF], result[HALF:], o0[rows, :])
-                lse0[rows, :] = jnp.where(mine[:HALF], log_total, lse0[rows, :])
+                log_total = peaks[parity, at][HALF:] + jnp.log(sums[HALF:])
+                o0[rows, :] = jnp.where(mine, result[HALF:], o0[rows, :])
+                lse0[rows, :] = jnp.where(mine, log_total, lse0[rows, :])
 
 
 def far_kernel(meta, a0, a1, a2, a3, *rest):
@@ -350,7 +337,7 @@
 def merge_kernel(meta, *refs):
     count = len(NEAR_PARTS)
     close, refs = refs[:count], refs[count:]
-    wide, o0, lse0, r0, r1, r2, r3, out, stage, grid_rows = refs
+    wide, o0, lse0, r0, r1, r2, r3, out, stage, grid_rows, ready, sent = refs
     bound = meta[0]
     device = meta[1]
     zpos = device // 2 % NZ
@@ -397,10 +384,17 @@
                 ]
     swap = swap_matrix()
     index = lax.broadcasted_iota(jnp.int32, (256, WIDTH), 0)
+    copies = []
     for block in range(4):
         rows = jnp.dot(swap, grid_rows[block], preferred_element_type=F32)
         position = device * ROWS + block * 256 + index
-        out[block * 256 : (block + 1) * 256, :] = jnp.where(position < bound, rows, 0.0).astype(BF)
+        ready[block] = jnp.where(position < bound, rows, 0.0).astype(BF)
+        copies.append(
+            pltpu.make_async_copy(ready.at[block], out.at[pl.ds(block * 256, 256)], sent.at[block])
+        )
+        copies[-1].start()
+    for copy in copies:
+        copy.wait()
 
 
 def smem():
@@ -465,10 +459,10 @@
     return qt, kt, vt, *rest
 
 
-def local_near(first, many, meta, ints, floats, q, k, v, sel):
+def local_near(first, many, meta, q, k, v, sel):
     return pl.pallas_call(
         functools.partial(local_kernel, "ABC", first, many),
-        in_specs=[smem()] + [vmem()] * 6,
+        in_specs=[smem()] + [vmem()] * 4,
         out_specs=vmem(),
         out_shape=shape((RES, GROUPS, many * 128)),
         compiler_params=params(40),
@@ -476,13 +470,13 @@
             flops=many * 600000000, bytes_accessed=1000000, transcendentals=many * 1200000
         ),
         name="near_queries",
-    )(meta, ints, floats, q, k, v, sel)
-
-
-def local_far(meta, ints, floats, q, k, v, sel, near, cross):
+    )(meta, q, k, v, sel)
+
+
+def local_far(meta, q, k, v, sel, near, cross):
     return pl.pallas_call(
         functools.partial(local_kernel, "D", 0, PAIRS),
-        in_specs=[smem()] + [vmem()] * 8,
+        in_specs=[smem()] + [vmem()] * 6,
         out_specs=[vmem()] * 3,
         out_shape=[
             shape((RES, GROUPS, WIDTH)),
@@ -494,7 +488,7 @@
             flops=1000000000, bytes_accessed=1000000, transcendentals=2000000
         ),
         name="wide_queries",
-    )(meta, ints, floats, q, k, v, sel, near, cross)
+    )(meta, q, k, v, sel, near, cross)
 
 
 def slide_wide(meta, queries, blocks):
@@ -513,11 +507,13 @@
     return pl.pallas_call(
         merge_kernel,
         in_specs=[smem()] + [vmem()] * (len(NEAR_PARTS) + 7),
-        out_specs=vmem(),
+        out_specs=pl.BlockSpec(memory_space=pltpu.HBM),
         out_shape=shape((ROWS, WIDTH)),
         scratch_shapes=[
             pltpu.VMEM((4, GROUPS, 256), F32),
             pltpu.VMEM((4, 256, WIDTH), BF),
+            pltpu.VMEM((4, 256, WIDTH), BF),
+            pltpu.SemaphoreType.DMA((4,)),
         ],
         compiler_params=params(40),
         name="merge_rows",
@@ -554,11 +550,10 @@
 def per_device(query_tiles, key_tiles, value_tiles, slide_length):
     device = lax.axis_index("seq").astype(jnp.int32)
     meta = jnp.stack([slide_length[0], device])
-    ints, floats = (jnp.asarray(table) for table in tables())
     qt, kt, vt, sel, sel8, z0, z1, z2, z3 = split(meta, query_tiles, key_tiles, value_tiles)
     slabs = [z0] + [move(slab, along_z(step)) for step, slab in ((1, z1), (2, z2), (3, z3))]
     pair = move(sel, other_core)
-    local = (ints, floats, qt, kt, vt, pair)
+    local = (qt, kt, vt, pair)
     close = [local_near(*NEAR_PARTS[0], meta, *local)]
     slabs, close[0], sel8, later = lax.optimization_barrier((slabs, close[0], sel8, meta))
     own = jnp.concatenate([slab[:, 256:640] for slab in slabs], axis=0)

time: 53.4 us -> 50.6 us (0.948)
  Pallas kernels: 30.3 us -> 26 us
  waiting for transfers between devices: 2.95 us -> 4.39 us
    pallas_call x1, Pallas kernels: 6.81 us -> 4.37 us  [local_far(): pl.pallas_call(functools.partial(local_kernel, 'D', 0, PAIRS), in_specs=[...]
    pallas_call x3, Pallas kernels: 14.6 us -> 13 us  [local_near(): pl.pallas_call(functools.partial(local_kernel, 'ABC', first, many), in_sp...]
    ppermute x16, waiting for transfers between devices: 2.95 us -> 4.39 us  [move(): return lax.ppermute(block, 'seq', route)]
    unnamed x10 -> x6, local copies, waits for them, and re-layouts: 2.98 us -> 2.98 us
  transfers between devices with their start and end apart: 16 -> 16, of which waited for: 2 -> 2; matrix products, arithmetic and copies ran while one was open for 0% -> 0% of each run, Pallas kernels for 47% -> 41%
where the time goes in v4:
time: 50.6 us; the launch traced here: 50.4 us
  Pallas kernels  26 us (51%)
  starting transfers between devices  15.9 us (31%)
  waiting for transfers between devices  4.39 us (9%)
  local copies, waits for them, and re-layouts  3.02 us (6%)
  between operations  1.03 us (2%)
    ppermute x16, starting transfers between devices, move(): return lax.ppermute(block, 'seq', route)  15.9 us
    pallas_call x3, Pallas kernels, local_near(): pl.pallas_call(functools.partial(local_kernel, 'ABC', first, many), in_sp...  13 us
    ppermute x16, waiting for transfers between devices, move(): return lax.ppermute(block, 'seq', route)  4.39 us
    pallas_call x1, Pallas kernels, local_far(): pl.pallas_call(functools.partial(local_kernel, 'D', 0, PAIRS), in_specs=[...  4.37 us
    pallas_call x1, Pallas kernels, slide_wide(): pl.pallas_call(far_kernel, in_specs=[smem()] + [vmem()] * 12, out_specs=[...  3.49 us
    unnamed x6, local copies, waits for them, and re-layouts  2.98 us
    pallas_call x1, Pallas kernels, merge(): pl.pallas_call(merge_kernel, in_specs=[smem()] + [vmem()] * (len(NEAR_PAR...  2.51 us
    pallas_call x1, Pallas kernels, split(): pl.pallas_call(split_kernel, in_specs=[smem()] + [vmem()] * 3, out_specs=...  1.42 us
  transfers between devices with their start and end apart: 16, of which 2 were waited for; matrix products, arithmetic and copies ran while one was open for 0% of the time, Pallas kernels for 41%

profile of v4, /device:TPU:1, one launch (start us, length us, event | category | flops | bytes accessed | tf_op | source)
XLA Modules:
  0.0 50.4 jit_solution(17599229169501046323)
XLA Ops:
  0.7 1.4 %copy-done.1 = bf16[1024,768]{1,0:T(8,128)(2,1)S(1)} copy-done((bf16[1024,768]{1,0:T(8,128)(2,1)S(1)}, bf16[1024,768]{1,0:T(8,128)(2,1)}, u32[]{:S(2)}) %copy-start.1) | copy-done | bytes 1572888
  2.1 0.6 %residue_order.2.kt.refs_1_ = bf16[16,64,768]{2,1,0:T(8,128)(2,1)S(1)} custom-call(bf16[1024,768]{1,0:T(8,128)(2,1)S(1)} %copy-done.1), custom_call_target="tpu_custom_call" | custom-call | tf_op jit(solution)/shard_map/residue_order/pallas_call | solution.py:433
  2.6 0.8 %copy-done.2 = bf16[1024,768]{1,0:T(8,128)(2,1)S(1)} copy-done((bf16[1024,768]{1,0:T(8,128)(2,1)S(1)}, bf16[1024,768]{1,0:T(8,128)(2,1)}, u32[]{:S(2)}) %copy-start.2) | copy-done | bytes 1572888
  3.5 0.6 %residue_order.3.vt.refs_2_ = bf16[16,64,768]{2,1,0:T(8,128)(2,1)S(1)} custom-call(bf16[1024,768]{1,0:T(8,128)(2,1)S(1)} %copy-done.2), custom_call_target="tpu_custom_call" | custom-call | tf_op jit(solution)/shard_map/residue_order/pallas_call | solution.py:433
  4.1 0.1 pad_add_fusion.meta
  4.1 0.7 %copy-done = bf16[1024,768]{1,0:T(8,128)(2,1)S(1)} copy-done((bf16[1024,768]{1,0:T(8,128)(2,1)S(1)}, bf16[1024,768]{1,0:T(8,128)(2,1)}, u32[]{:S(2)}) %copy-start) | copy-done | bytes 1572888
  4.9 1.4 %split_rows.1 = (bf16[16,64,768]{2,1,0:T(8,128)(2,1)S(1)}, bf16[4,2,64,768]{3,2,1,0:T(8,128)(2,1)S(1)}, bf16[2,2,64,768]{3,2,1,0:T(8,128)(2,1)S(1)}, bf16[64,640...) custom-call(s32[2]{0:T(128)S(1)} %pad_add_fusion.meta, ...), custom_call_target="tpu_custom_call" | custom-call | tf_op jit(solution)/shard_map/split_rows/pallas_call | solution.py:445
  6.3 1.5 %collective-permute-start.3 = (bf16[4,2,64,768]{3,2,1,0:T(8,128)(2,1)S(1)}, bf16[4,2,64,768]{3,2,1,0:T(8,128)(2,1)S(1)}, u32[]{:S(2)}, u32[]{:S(2)}) collective-permute-start(bf16[4,2,64,768]{3,2,1,0:T(8,128)(2,1)S(1)} %get-tuple-element.54), channel_id=1, source_target_pairs={{0,1},{1,0},{2,3},{3,2},{4,5},{5,4},{6,7},{7,6},{8,9},{9,8},{10,11... | collective-permute-start | bytes 2359304 | tf_op jit(solution)/shard_map/ppermute | solution.py:531
  7.8 1.7 %collective-permute-start = (bf16[64,640]{1,0:T(8,128)(2,1)S(1)}, bf16[64,640]{1,0:T(8,128)(2,1)S(1)}, u32[]{:S(2)}, u32[]{:S(2)}) collective-permute-start(bf16[64,640]{1,0:T(8,128)(2,1)S(1)} %get-tuple-element.50), channel_id=1, source_target_pairs={{0,2},{1,3},{2,4},{3,5},{4,6},{5,7},{6,0},{7,1},{8,10},{9,11},{10,... | collective-permute-start | bytes 245768 | tf_op jit(solution)/shard_map/ppermute | solution.py:531
  9.5 3.3 %collective-permute-start.1 = (bf16[64,640]{1,0:T(8,128)(2,1)S(1)}, bf16[64,640]{1,0:T(8,128)(2,1)S(1)}, u32[]{:S(2)}, u32[]{:S(2)}) collective-permute-start(bf16[64,640]{1,0:T(8,128)(2,1)S(1)} %get-tuple-element.51), channel_id=1, source_target_pairs={{0,4},{1,5},{2,6},{3,7},{4,0},{5,1},{6,2},{7,3},{8,12},{9,13},{10,... | collective-permute-start | bytes 245768 | tf_op jit(solution)/shard_map/ppermute | solution.py:531
  12.8 0.7 %collective-permute-start.2 = (bf16[64,640]{1,0:T(8,128)(2,1)S(1)}, bf16[64,640]{1,0:T(8,128)(2,1)S(1)}, u32[]{:S(2)}, u32[]{:S(2)}) collective-permute-start(bf16[64,640]{1,0:T(8,128)(2,1)S(1)} %get-tuple-element.52), channel_id=1, source_target_pairs={{0,6},{1,7},{2,0},{3,1},{4,2},{5,3},{6,4},{7,5},{8,14},{9,15},{10,... | collective-permute-start | bytes 245768 | tf_op jit(solution)/shard_map/ppermute | solution.py:531
  13.6 0.0 collective-permute-done.3.refs_3_
  13.6 2.6 %near_queries.3.refs_0_ = bf16[16,64,128]{2,1,0:T(8,128)(2,1)S(1)} custom-call(s32[2]{0:T(128)S(1)} %pad_add_fusion.meta, bf16[16,64,768]{2,1,0:T(8,128)(2,1)S(1)} %get-tuple-element.53.refs_0_, bf16[16,64,768]{2,1,0:T(8,128)(2,1)S(1)} %residue_order.2.kt.refs_1_, bf16[16,64,768]{2,1,0:T(8,128)(2,1)S(1)} %residue_order.3.vt.refs_2_, ...), custom_call_target="tpu_custom_call" | custom-call | flops 600000000 | bytes 1000000 | tf_op jit(solution)/shard_map/near_queries/pallas_call | solution.py:463
  16.2 1.0 %collective-permute-done.1 = bf16[64,640]{1,0:T(8,128)(2,1)S(1)} collective-permute-done((bf16[64,640]{1,0:T(8,128)(2,1)S(1)}, bf16[64,640]{1,0:T(8,128)(2,1)S(1)}, u32[]{:S(2)}, u32[]{:S(2)}) %collective-permute-start.1) | collective-permute-done | bytes 81952 | tf_op jit(solution)/shard_map/ppermute | solution.py:531
  17.1 0.0 collective-permute-done.2
  17.1 0.7 %collective-permute-start.7 = (bf16[2,2,64,768]{3,2,1,0:T(8,128)(2,1)S(1)}, bf16[2,2,64,768]{3,2,1,0:T(8,128)(2,1)S(1)}, u32[]{:S(2)}, u32[]{:S(2)}) collective-permute-start(bf16[2,2,64,768]{3,2,1,0:T(8,128)(2,1)S(1)} %get-tuple-element.63), channel_id=1, source_target_pairs={{0,2},{1,3},{2,0},{3,1},{4,6},{5,7},{6,4},{7,5},{8,10},{9,11},{10,... | collective-permute-start | bytes 1179656 | tf_op jit(solution)/shard_map/ppermute | solution.py:531
  17.9 2.5 %collective-permute-start.6 = (bf16[256,384]{1,0:T(8,128)(2,1)S(1)}, bf16[256,384]{1,0:T(8,128)(2,1)S(1)}, u32[]{:S(2)}, u32[]{:S(2)}) collective-permute-start(bf16[256,384]{1,0:T(8,128)(2,1)S(1)} %pad_maximum_fusion.rest_0_), channel_id=1, source_target_pairs={{0,24},{1,25},{2,26},{3,27},{4,28},{5,29},{6,30},{7,31},{8,0},{9,1... | collective-permute-start | bytes 589832 | tf_op jit(solution)/shard_map/ppermute | solution.py:531
  20.5 0.5 collective-permute-start.5
  20.9 0.7 %collective-permute-start.4 = (bf16[256,384]{1,0:T(8,128)(2,1)S(1)}, bf16[256,384]{1,0:T(8,128)(2,1)S(1)}, u32[]{:S(2)}, u32[]{:S(2)}) collective-permute-start(bf16[256,384]{1,0:T(8,128)(2,1)S(1)} %pad_maximum_fusion.rest_0_), channel_id=1, source_target_pairs={{0,8},{1,9},{2,10},{3,11},{4,12},{5,13},{6,14},{7,15},{8,16},{9,17... | collective-permute-start | bytes 589832 | tf_op jit(solution)/shard_map/ppermute | solution.py:531
  21.6 7.9 %near_queries.4.refs_1_ = bf16[16,64,512]{2,1,0:T(8,128)(2,1)S(1)} custom-call(s32[2]{0:T(128)S(1)} %pad_add_fusion.meta, bf16[16,64,768]{2,1,0:T(8,128)(2,1)S(1)} %get-tuple-element.53.refs_0_, bf16[16,64,768]{2,1,0:T(8,128)(2,1)S(1)} %residue_order.2.kt.refs_1_, bf16[16,64,768]{2,1,0:T(8,128)(2,1)S(1)} %residue_order.3.vt.refs_2_, ...), custom_call_target="tpu_custom_call" | custom-call | flops 2400000000 | bytes 1000000 | tf_op jit(solution)/shard_map/near_queries/pallas_call | solution.py:463
  29.5 3.4 %collective-permute-done.4.rest_1_ = bf16[256,384]{1,0:T(8,128)(2,1)S(1)} collective-permute-done((bf16[256,384]{1,0:T(8,128)(2,1)S(1)}, bf16[256,384]{1,0:T(8,128)(2,1)S(1)}, u32[]{:S(2)}, u32[]{:S(2)}) %collective-permute-start.4) | collective-permute-done | bytes 196640 | tf_op jit(solution)/shard_map/ppermute | solution.py:531
  32.9 0.6 %collective-permute-start.12 = (bf16[2,2,64,768]{3,2,1,0:T(8,128)(2,1)S(1)}, bf16[2,2,64,768]{3,2,1,0:T(8,128)(2,1)S(1)}, u32[]{:S(2)}, u32[]{:S(2)}) collective-permute-start(bf16[2,2,64,768]{3,2,1,0:T(8,128)(2,1)S(1)} %collective-permute-done.7.refs_4_), channel_id=1, source_target_pairs={{0,1},{1,0},{2,3},{3,2},{4,5},{5,4},{6,7},{7,6},{8,9},{9,8},{10,11... | collective-permute-start | bytes 1179656 | tf_op jit(solution)/shard_map/ppermute | solution.py:531
  33.5 0.0 collective-permute-start.8
  33.5 0.5 %collective-permute-start.9 = (bf16[256,384]{1,0:T(8,128)(2,1)S(1)}, bf16[256,384]{1,0:T(8,128)(2,1)S(1)}, u32[]{:S(2)}, u32[]{:S(2)}) collective-permute-start(bf16[256,384]{1,0:T(8,128)(2,1)S(1)} %collective-permute-done.4.rest_1_), channel_id=1, source_target_pairs={{0,1},{1,0},{2,3},{3,2},{4,5},{5,4},{6,7},{7,6},{8,9},{9,8},{10,11... | collective-permute-start | bytes 589832 | tf_op jit(solution)/shard_map/ppermute | solution.py:531
  34.0 0.0 collective-permute-start.10
  34.0 0.5 %collective-permute-start.11 = (bf16[256,384]{1,0:T(8,128)(2,1)S(1)}, bf16[256,384]{1,0:T(8,128)(2,1)S(1)}, u32[]{:S(2)}, u32[]{:S(2)}) collective-permute-start(bf16[256,384]{1,0:T(8,128)(2,1)S(1)} %collective-permute-done.6.rest_3_), channel_id=1, source_target_pairs={{0,1},{1,0},{2,3},{3,2},{4,5},{5,4},{6,7},{7,6},{8,9},{9,8},{10,11... | collective-permute-start | bytes 589832 | tf_op jit(solution)/shard_map/ppermute | solution.py:531
  34.5 2.6 %near_queries.5.refs_2_ = bf16[16,64,128]{2,1,0:T(8,128)(2,1)S(1)} custom-call(s32[2]{0:T(128)S(1)} %pad_add_fusion.meta, bf16[16,64,768]{2,1,0:T(8,128)(2,1)S(1)} %get-tuple-element.53.refs_0_, bf16[16,64,768]{2,1,0:T(8,128)(2,1)S(1)} %residue_order.2.kt.refs_1_, bf16[16,64,768]{2,1,0:T(8,128)(2,1)S(1)} %residue_order.3.vt.refs_2_, ...), custom_call_target="tpu_custom_call" | custom-call | flops 600000000 | bytes 1000000 | tf_op jit(solution)/shard_map/near_queries/pallas_call | solution.py:463
  37.2 3.5 %slide_queries.1 = (bf16[64,256]{1,0:T(8,128)(2,1)S(1)}, bf16[64,256]{1,0:T(8,128)(2,1)S(1)}, bf16[64,256]{1,0:T(8,128)(2,1)S(1)}, bf16[64,256]{1,0:T(8,128)(2,1)S(1)}) custom-call(s32[2]{0:T(128)S(1)} %pad_add_fusion.meta, bf16[64,256]{1,0:T(8,128)(2,1)S(1)} %slice.28.a0, bf16[64,256]{1,0:T(8,128)(2,1)S(1)} %slice.29.a1, bf16[64,256]{1,0:T(8,128)(2,1)S(1)} %slice.30.a2, ...), custom_call_target="tpu_custom_call" | custom-call | flops 800000000 | bytes 2000000 | tf_op jit(solution)/shard_map/slide_queries/pallas_call | solution.py:495
  40.7 1.3 %collective-permute-start.13 = (bf16[64,256]{1,0:T(8,128)(2,1)S(1)}, bf16[64,256]{1,0:T(8,128)(2,1)S(1)}, u32[]{:S(2)}, u32[]{:S(2)}) collective-permute-start(bf16[64,256]{1,0:T(8,128)(2,1)S(1)} %get-tuple-element.90), channel_id=1, source_target_pairs={{0,6},{1,7},{2,0},{3,1},{4,2},{5,3},{6,4},{7,5},{8,14},{9,15},{10,... | collective-permute-start | bytes 98312 | tf_op jit(solution)/shard_map/ppermute | solution.py:531
  41.9 1.3 %collective-permute-start.14 = (bf16[64,256]{1,0:T(8,128)(2,1)S(1)}, bf16[64,256]{1,0:T(8,128)(2,1)S(1)}, u32[]{:S(2)}, u32[]{:S(2)}) collective-permute-start(bf16[64,256]{1,0:T(8,128)(2,1)S(1)} %get-tuple-element.91), channel_id=1, source_target_pairs={{0,4},{1,5},{2,6},{3,7},{4,0},{5,1},{6,2},{7,3},{8,12},{9,13},{10,... | collective-permute-start | bytes 98312 | tf_op jit(solution)/shard_map/ppermute | solution.py:531
  43.3 4.4 %wide_queries.1 = (bf16[16,64,768]{2,1,0:T(8,128)(2,1)S(1)}, f32[64,768]{1,0:T(8,128)S(1)}, f32[64,768]{1,0:T(8,128)S(1)}) custom-call(s32[2]{0:T(128)S(1)} %pad_add_fusion.meta, bf16[16,64,768]{2,1,0:T(8,128)(2,1)S(1)} %get-tuple-element.53.refs_0_, bf16[16,64,768]{2,1,0:T(8,128)(2,1)S(1)} %residue_order.2.kt.refs_1_, ...), custom_call_target="tpu_custom_call" | custom-call | flops 1000000000 | bytes 1000000 | tf_op jit(solution)/shard_map/wide_queries/pallas_call | solution.py:477
  47.7 2.5 %merge_rows.1 = bf16[1024,768]{1,0:T(8,128)(2,1)} custom-call(s32[2]{0:T(128)S(1)} %pad_add_fusion.meta, bf16[16,64,128]{2,1,0:T(8,128)(2,1)S(1)} %near_queries.3.refs_0_, bf16[16,64,512]{2,1,0:T(8,128)(2,1)S(1)} %near_queries.4.refs_1_, bf16[16,64,128]{2,1,0:T(8,128)(2,1)S(1)} %near_queries.5.refs_2_, bf16[16,64,768]{2,1,0:T(8,128)(2,1)S(1)} %get-tuple-element.86.refs_3_, ...), custom_call_target="tpu_custom_call" | custom-call | tf_op jit(solution)/shard_map/merge_rows/pallas_call | solution.py:507
  (25 shorter events, 0.1 us)
Async XLA Ops:
  0.7 1.4 %copy-start.1 = (bf16[1024,768]{1,0:T(8,128)(2,1)S(1)}, bf16[1024,768]{1,0:T(8,128)(2,1)}, u32[]{:S(2)}) copy-start(bf16[1024,768]{1,0:T(8,128)(2,1)} %source.2) | copy-start | bytes 4718596
  2.1 1.4 %copy-start.2 = (bf16[1024,768]{1,0:T(8,128)(2,1)S(1)}, bf16[1024,768]{1,0:T(8,128)(2,1)}, u32[]{:S(2)}) copy-start(bf16[1024,768]{1,0:T(8,128)(2,1)} %source.3) | copy-start | bytes 4718596
  3.5 1.4 %copy-start = (bf16[1024,768]{1,0:T(8,128)(2,1)S(1)}, bf16[1024,768]{1,0:T(8,128)(2,1)}, u32[]{:S(2)}) copy-start(bf16[1024,768]{1,0:T(8,128)(2,1)} %q_in.1) | copy-start | bytes 4718596
  6.3 7.3 %collective-permute-start.3 = (bf16[4,2,64,768]{3,2,1,0:T(8,128)(2,1)S(1)}, bf16[4,2,64,768]{3,2,1,0:T(8,128)(2,1)S(1)}, u32[]{:S(2)}, u32[]{:S(2)}) collective-permute-start(bf16[4,2,64,768]{3,2,1,0:T(8,128)(2,1)S(1)} %get-tuple-element.54), channel_id=1, source_target_pairs={{0,1},{1,0},{2,3},{3,2},{4,5},{5,4},{6,7},{7,6},{8,9},{9,8},{10,11... | collective-permute-start | bytes 2359304 | tf_op jit(solution)/shard_map/ppermute | solution.py:531
  7.8 8.3 %collective-permute-start = (bf16[64,640]{1,0:T(8,128)(2,1)S(1)}, bf16[64,640]{1,0:T(8,128)(2,1)S(1)}, u32[]{:S(2)}, u32[]{:S(2)}) collective-permute-start(bf16[64,640]{1,0:T(8,128)(2,1)S(1)} %get-tuple-element.50), channel_id=1, source_target_pairs={{0,2},{1,3},{2,4},{3,5},{4,6},{5,7},{6,0},{7,1},{8,10},{9,11},{10,... | collective-permute-start | bytes 245768 | tf_op jit(solution)/shard_map/ppermute | solution.py:531
  9.5 7.6 %collective-permute-start.1 = (bf16[64,640]{1,0:T(8,128)(2,1)S(1)}, bf16[64,640]{1,0:T(8,128)(2,1)S(1)}, u32[]{:S(2)}, u32[]{:S(2)}) collective-permute-start(bf16[64,640]{1,0:T(8,128)(2,1)S(1)} %get-tuple-element.51), channel_id=1, source_target_pairs={{0,4},{1,5},{2,6},{3,7},{4,0},{5,1},{6,2},{7,3},{8,12},{9,13},{10,... | collective-permute-start | bytes 245768 | tf_op jit(solution)/shard_map/ppermute | solution.py:531
  12.8 4.3 %collective-permute-start.2 = (bf16[64,640]{1,0:T(8,128)(2,1)S(1)}, bf16[64,640]{1,0:T(8,128)(2,1)S(1)}, u32[]{:S(2)}, u32[]{:S(2)}) collective-permute-start(bf16[64,640]{1,0:T(8,128)(2,1)S(1)} %get-tuple-element.52), channel_id=1, source_target_pairs={{0,6},{1,7},{2,0},{3,1},{4,2},{5,3},{6,4},{7,5},{8,14},{9,15},{10,... | collective-permute-start | bytes 245768 | tf_op jit(solution)/shard_map/ppermute | solution.py:531
  17.1 15.8 %collective-permute-start.7 = (bf16[2,2,64,768]{3,2,1,0:T(8,128)(2,1)S(1)}, bf16[2,2,64,768]{3,2,1,0:T(8,128)(2,1)S(1)}, u32[]{:S(2)}, u32[]{:S(2)}) collective-permute-start(bf16[2,2,64,768]{3,2,1,0:T(8,128)(2,1)S(1)} %get-tuple-element.63), channel_id=1, source_target_pairs={{0,2},{1,3},{2,0},{3,1},{4,6},{5,7},{6,4},{7,5},{8,10},{9,11},{10,... | collective-permute-start | bytes 1179656 | tf_op jit(solution)/shard_map/ppermute | solution.py:531
  17.9 11.6 %collective-permute-start.6 = (bf16[256,384]{1,0:T(8,128)(2,1)S(1)}, bf16[256,384]{1,0:T(8,128)(2,1)S(1)}, u32[]{:S(2)}, u32[]{:S(2)}) collective-permute-start(bf16[256,384]{1,0:T(8,128)(2,1)S(1)} %pad_maximum_fusion.rest_0_), channel_id=1, source_target_pairs={{0,24},{1,25},{2,26},{3,27},{4,28},{5,29},{6,30},{7,31},{8,0},{9,1... | collective-permute-start | bytes 589832 | tf_op jit(solution)/shard_map/ppermute | solution.py:531
  20.5 9.0 %collective-permute-start.5 = (bf16[256,384]{1,0:T(8,128)(2,1)S(1)}, bf16[256,384]{1,0:T(8,128)(2,1)S(1)}, u32[]{:S(2)}, u32[]{:S(2)}) collective-permute-start(bf16[256,384]{1,0:T(8,128)(2,1)S(1)} %pad_maximum_fusion.rest_0_), channel_id=1, source_target_pairs={{0,16},{1,17},{2,18},{3,19},{4,20},{5,21},{6,22},{7,23},{8,24},{9,... | collective-permute-start | bytes 589832 | tf_op jit(solution)/shard_map/ppermute | solution.py:531
  20.9 12.0 %collective-permute-start.4 = (bf16[256,384]{1,0:T(8,128)(2,1)S(1)}, bf16[256,384]{1,0:T(8,128)(2,1)S(1)}, u32[]{:S(2)}, u32[]{:S(2)}) collective-permute-start(bf16[256,384]{1,0:T(8,128)(2,1)S(1)} %pad_maximum_fusion.rest_0_), channel_id=1, source_target_pairs={{0,8},{1,9},{2,10},{3,11},{4,12},{5,13},{6,14},{7,15},{8,16},{9,17... | collective-permute-start | bytes 589832 | tf_op jit(solution)/shard_map/ppermute | solution.py:531
  32.9 10.4 %collective-permute-start.12 = (bf16[2,2,64,768]{3,2,1,0:T(8,128)(2,1)S(1)}, bf16[2,2,64,768]{3,2,1,0:T(8,128)(2,1)S(1)}, u32[]{:S(2)}, u32[]{:S(2)}) collective-permute-start(bf16[2,2,64,768]{3,2,1,0:T(8,128)(2,1)S(1)} %collective-permute-done.7.refs_4_), channel_id=1, source_target_pairs={{0,1},{1,0},{2,3},{3,2},{4,5},{5,4},{6,7},{7,6},{8,9},{9,8},{10,11... | collective-permute-start | bytes 1179656 | tf_op jit(solution)/shard_map/ppermute | solution.py:531
  33.5 3.6 %collective-permute-start.8 = (bf16[256,384]{1,0:T(8,128)(2,1)S(1)}, bf16[256,384]{1,0:T(8,128)(2,1)S(1)}, u32[]{:S(2)}, u32[]{:S(2)}) collective-permute-start(bf16[256,384]{1,0:T(8,128)(2,1)S(1)} %pad_maximum_fusion.rest_0_), channel_id=1, source_target_pairs={{0,1},{1,0},{2,3},{3,2},{4,5},{5,4},{6,7},{7,6},{8,9},{9,8},{10,11... | collective-permute-start | bytes 589832 | tf_op jit(solution)/shard_map/ppermute | solution.py:531
  33.5 3.6 %collective-permute-start.9 = (bf16[256,384]{1,0:T(8,128)(2,1)S(1)}, bf16[256,384]{1,0:T(8,128)(2,1)S(1)}, u32[]{:S(2)}, u32[]{:S(2)}) collective-permute-start(bf16[256,384]{1,0:T(8,128)(2,1)S(1)} %collective-permute-done.4.rest_1_), channel_id=1, source_target_pairs={{0,1},{1,0},{2,3},{3,2},{4,5},{5,4},{6,7},{7,6},{8,9},{9,8},{10,11... | collective-permute-start | bytes 589832 | tf_op jit(solution)/shard_map/ppermute | solution.py:531
  34.0 3.1 %collective-permute-start.10 = (bf16[256,384]{1,0:T(8,128)(2,1)S(1)}, bf16[256,384]{1,0:T(8,128)(2,1)S(1)}, u32[]{:S(2)}, u32[]{:S(2)}) collective-permute-start(bf16[256,384]{1,0:T(8,128)(2,1)S(1)} %collective-permute-done.5.rest_2_), channel_id=1, source_target_pairs={{0,1},{1,0},{2,3},{3,2},{4,5},{5,4},{6,7},{7,6},{8,9},{9,8},{10,11... | collective-permute-start | bytes 589832 | tf_op jit(solution)/shard_map/ppermute | solution.py:531
  34.0 3.1 %collective-permute-start.11 = (bf16[256,384]{1,0:T(8,128)(2,1)S(1)}, bf16[256,384]{1,0:T(8,128)(2,1)S(1)}, u32[]{:S(2)}, u32[]{:S(2)}) collective-permute-start(bf16[256,384]{1,0:T(8,128)(2,1)S(1)} %collective-permute-done.6.rest_3_), channel_id=1, source_target_pairs={{0,1},{1,0},{2,3},{3,2},{4,5},{5,4},{6,7},{7,6},{8,9},{9,8},{10,11... | collective-permute-start | bytes 589832 | tf_op jit(solution)/shard_map/ppermute | solution.py:531
  40.7 7.0 %collective-permute-start.13 = (bf16[64,256]{1,0:T(8,128)(2,1)S(1)}, bf16[64,256]{1,0:T(8,128)(2,1)S(1)}, u32[]{:S(2)}, u32[]{:S(2)}) collective-permute-start(bf16[64,256]{1,0:T(8,128)(2,1)S(1)} %get-tuple-element.90), channel_id=1, source_target_pairs={{0,6},{1,7},{2,0},{3,1},{4,2},{5,3},{6,4},{7,5},{8,14},{9,15},{10,... | collective-permute-start | bytes 98312 | tf_op jit(solution)/shard_map/ppermute | solution.py:531
  41.9 5.7 %collective-permute-start.14 = (bf16[64,256]{1,0:T(8,128)(2,1)S(1)}, bf16[64,256]{1,0:T(8,128)(2,1)S(1)}, u32[]{:S(2)}, u32[]{:S(2)}) collective-permute-start(bf16[64,256]{1,0:T(8,128)(2,1)S(1)} %get-tuple-element.91), channel_id=1, source_target_pairs={{0,4},{1,5},{2,6},{3,7},{4,0},{5,1},{6,2},{7,3},{8,12},{9,13},{10,... | collective-permute-start | bytes 98312 | tf_op jit(solution)/shard_map/ppermute | solution.py:531
  43.3 4.4 %collective-permute-start.15 = (bf16[64,256]{1,0:T(8,128)(2,1)S(1)}, bf16[64,256]{1,0:T(8,128)(2,1)S(1)}, u32[]{:S(2)}, u32[]{:S(2)}) collective-permute-start(bf16[64,256]{1,0:T(8,128)(2,1)S(1)} %get-tuple-element.92), channel_id=1, source_target_pairs={{0,2},{1,3},{2,4},{3,5},{4,6},{5,7},{6,0},{7,1},{8,10},{9,11},{10,... | collective-permute-start | bytes 98312 | tf_op jit(solution)/shard_map/ppermute | solution.py:531

commit v5 on v4

--- a/solution.py
+++ b/solution.py
@@ -27,7 +27,8 @@
 CLASS_U = {"A": ODD, "B": [2, 6, 10, 14], "C": [4, 12], "D": [8, 0]}
 PAIR_OF = [0, 2, 3, 5]
 LONE_OF = [2, 3, 8, 9]
-NEAR_PARTS = [(0, 1), (1, 4), (5, 1)]
+NEAR_PARTS = [(0, 1), (1, 5)]
+WIDE_PARTS = [(0, 3), (3, 3)]
 
 
 def level(u):
@@ -44,18 +45,31 @@
     return lax.broadcasted_iota(jnp.int32, (rows, 128), 1) < 64
 
 
-def reorder(source, target):
+def split_kernel(
+    meta, q_in, k_in, v_in, qt, kt, vt, sel, sel8, z0, z1, z2, z3, held, stage, arrived
+):
+    copies = []
+    for at, source in enumerate((k_in, v_in, q_in)):
+        copies.append(
+            [
+                pltpu.make_async_copy(
+                    source.at[pl.ds(block * 256, 256)], held.at[at, block], arrived.at[at, block]
+                )
+                for block in range(4)
+            ]
+        )
+    for copy in copies[0] + copies[1]:
+        copy.start()
     swap = swap_matrix()
-    for block in range(4):
-        moved = jnp.dot(
-            swap, source[block * 256 : (block + 1) * 256, :], preferred_element_type=F32
-        ).astype(BF)
-        for res in range(RES):
-            target[res, block * 16 : (block + 1) * 16, :] = moved[res * 16 : (res + 1) * 16, :]
-
-
-def split_kernel(meta, q_in, kt, vt, qt, sel, sel8, z0, z1, z2, z3, stage):
-    reorder(q_in, qt)
+    for at, target in enumerate((kt, vt, qt)):
+        for block in range(4):
+            copies[at][block].wait()
+            if at == 0:
+                copies[2][block].start()
+        for block in range(4):
+            moved = jnp.dot(swap, held[at, block], preferred_element_type=F32).astype(BF)
+            for res in range(RES):
+                target[res, block * 16 : (block + 1) * 16, :] = moved[res * 16 : (res + 1) * 16, :]
     zpos = meta[1] // 2 % NZ
     low = lane_low(GROUPS)
 
@@ -96,21 +110,6 @@
                 stage[slot, :, 512:640] = jnp.where(low, lone_k, lone_v)
     for slot, out in enumerate((z0, z1, z2, z3)):
         out[...] = stage[slot]
-
-
-def softmax_parts(query, keys, values, biases):
-    scores = [
-        lax.dot_general(query, key, (((1,), (1,)), ((), ())), preferred_element_type=F32) + bias
-        for key, bias in zip(keys, biases)
-    ]
-    peak = functools.reduce(jnp.maximum, scores)
-    peak = jnp.max(peak, axis=1, keepdims=True)
-    total = None
-    for score, value in zip(scores, values):
-        weight = jnp.exp(score - peak).astype(BF)
-        part = jnp.dot(weight, value, preferred_element_type=F32)
-        total = part if total is None else total + part
-    return total, peak
 
 
 def local_kernel(classes, first, many, meta, *refs):
@@ -283,36 +282,49 @@
     part = lane >> 6
     pair = jnp.where(group == 0, 0, jnp.where(group == 1, 4, jnp.where(group == 2, 6, 10)))
     lone = jnp.where(group == 0, 2, jnp.where(group == 1, 3, jnp.where(group == 2, 8, 9)))
+    def positions(at, head):
+        from_x = (xpos - at % 4) & 3
+        from_c = core if at < 4 else 1 - core
+        from_z = (zpos - part) & 3
+        return ((from_x * NZ + from_z) * NC + from_c) * ROWS + (lane & 63) * 16 + head
+
     results = []
-    for which in range(3):
-        head = (pair, pair + 1, lone)[which]
-        if which < 2:
-            mine = low256 if which == 0 else jnp.logical_not(low256)
-        else:
-            mine = jnp.logical_not(low256)
-        keys, values, biases = [], [], []
-        for at, block in enumerate(blocks):
-            from_x = (xpos - at % 4) & 3
-            from_c = core if at < 4 else 1 - core
-            from_z = (zpos - part) & 3
-            position = ((from_x * NZ + from_z) * NC + from_c) * ROWS + (lane & 63) * 16 + head
-            biases.append(jnp.where(position < bound, 0.0, MASKED))
-            if which < 2:
-                keys.append(block[:, 0:128])
-                value = block[:, 128:256]
-            else:
-                keys.append(block[:, 256:384])
-                value = block[:, 256:384]
-            values.append(jnp.where(mine, value, jnp.ones_like(value)))
-        lanes = slice(0, 128) if which < 2 else slice(128, 256)
+    for heads in ((0, 1), (2,)):
+        lanes = slice(0, 128) if heads[0] == 0 else slice(128, 256)
         query = jnp.concatenate([source[:, lanes] for source in (a0, a1, a2, a3)], axis=0)
-        if which < 2:
-            query = jnp.where(mine, query, jnp.zeros_like(query))
         query = (query * 0.125).astype(BF)
-        total, peak = softmax_parts(query, keys, values, biases)
-        sums = pltpu.roll(total, 64, 1)
-        logs = peak + jnp.log(sums if which < 2 else total)
-        results.append((total / sums, logs))
+        sides = [jnp.logical_not(low256) if head else low256 for head in heads]
+        queries = [jnp.where(side, query, jnp.zeros_like(query)) for side in sides]
+        if heads[0] == 2:
+            queries = [query]
+        both = jnp.concatenate(queries, axis=0)
+        key_lanes = slice(0, 128) if heads[0] == 0 else slice(256, 384)
+        value_lanes = slice(128, 256) if heads[0] == 0 else slice(256, 384)
+        scores = [
+            lax.dot_general(
+                both, block[:, key_lanes], (((1,), (1,)), ((), ())), preferred_element_type=F32
+            )
+            for block in blocks
+        ]
+        for at, head in enumerate(heads):
+            mine = sides[at]
+            held = [
+                score[at * 256 : (at + 1) * 256]
+                + jnp.where(positions(spot, (pair, pair + 1, lone)[head]) < bound, 0.0, MASKED)
+                for spot, score in enumerate(scores)
+            ]
+            peak = jnp.max(functools.reduce(jnp.maximum, held), axis=1, keepdims=True)
+            total = None
+            for score, block in zip(held, blocks):
+                value = block[:, value_lanes]
+                weighed = jnp.dot(
+                    jnp.exp(score - peak).astype(BF),
+                    jnp.where(mine, value, jnp.ones_like(value)),
+                    preferred_element_type=F32,
+                )
+                total = weighed if total is None else total + weighed
+            sums = pltpu.roll(total, 64, 1)
+            results.append((total / sums, peak + jnp.log(sums if head < 2 else total)))
     low = low256[:64]
     lane = lax.broadcasted_iota(jnp.int32, (64, 128), 1)
     for at, out in enumerate(outs):
@@ -337,7 +349,9 @@
 def merge_kernel(meta, *refs):
     count = len(NEAR_PARTS)
     close, refs = refs[:count], refs[count:]
-    wide, o0, lse0, r0, r1, r2, r3, out, stage, grid_rows, ready, sent = refs
+    count = len(WIDE_PARTS)
+    wide, o0, lse0 = refs[:count], refs[count : 2 * count], refs[2 * count : 3 * count]
+    r0, r1, r2, r3, out, stage, grid_rows, ready, sent = refs[3 * count :]
     bound = meta[0]
     device = meta[1]
     zpos = device // 2 % NZ
@@ -352,6 +366,7 @@
     for pair in range(PAIRS):
         lanes = slice(pair * 128, pair * 128 + 128)
         close_part, close_lanes = part_of(NEAR_PARTS, pair)
+        wide_part, wide_lanes = part_of(WIDE_PARTS, pair)
         if pair in PAIR_OF:
             slot = (PAIR_OF.index(pair) - zpos) & 3
             away = stage[slot, :, 0:128]
@@ -361,7 +376,7 @@
             right = (left + 1) & 3
             away = jnp.where(low, pltpu.roll(stage[left, :, 128:256], 64, 1), stage[right, :, 128:256])
             away_lse = jnp.where(low, log_of(left, 2), log_of(right, 2))
-        here, here_lse = o0[:, lanes], lse0[:, lanes]
+        here, here_lse = o0[wide_part][:, wide_lanes], lse0[wide_part][:, wide_lanes]
         top = jnp.maximum(here_lse, away_lse)
         weight = jnp.exp(here_lse - top)
         away_weight = jnp.exp(away_lse - top)
@@ -374,7 +389,7 @@
                 if rank == 4:
                     sides.append(blended)
                 elif rank == 3:
-                    sides.append(wide[res, :, lanes])
+                    sides.append(wide[wide_part][res, :, wide_lanes])
                 else:
                     sides.append(close[close_part][res, :, close_lanes])
             rows = jnp.where(low, *sides)
@@ -429,34 +444,23 @@
     return pl.BlockSpec((GROUPS, 128), lambda i: (0, i))
 
 
-def reordered(rows):
+def split(meta, q, k, v):
+    rows = [pltpu.with_memory_space_constraint(array, pltpu.HBM) for array in (q, k, v)]
     return pl.pallas_call(
-        reorder,
-        in_specs=[vmem()],
-        out_specs=vmem(),
-        out_shape=shape((RES, GROUPS, WIDTH)),
-        compiler_params=params(20),
-        name="residue_order",
-    )(rows)
-
-
-def split(meta, q, k, v):
-    kt, vt = reordered(k), reordered(v)
-    qt, *rest = pl.pallas_call(
         split_kernel,
-        in_specs=[smem()] + [vmem()] * 3,
-        out_specs=[vmem()] * 7,
-        out_shape=[
-            shape((RES, GROUPS, WIDTH)),
-            shape((4, 2, GROUPS, WIDTH)),
-            shape((2, 2, GROUPS, WIDTH)),
-        ]
+        in_specs=[smem()] + [pl.BlockSpec(memory_space=pltpu.HBM)] * 3,
+        out_specs=[vmem()] * 9,
+        out_shape=[shape((RES, GROUPS, WIDTH))] * 3
+        + [shape((4, 2, GROUPS, WIDTH)), shape((2, 2, GROUPS, WIDTH))]
         + [shape((GROUPS, 640))] * 4,
-        scratch_shapes=[pltpu.VMEM((4, GROUPS, 640), BF)],
-        compiler_params=params(20),
+        scratch_shapes=[
+            pltpu.VMEM((3, 4, 256, WIDTH), BF),
+            pltpu.VMEM((4, GROUPS, 640), BF),
+            pltpu.SemaphoreType.DMA((3, 4)),
+        ],
+        compiler_params=params(40),
         name="split_rows",
-    )(meta, q, kt, vt)
-    return qt, kt, vt, *rest
+    )(meta, *rows)
 
 
 def local_near(first, many, meta, q, k, v, sel):
@@ -473,19 +477,19 @@
     )(meta, q, k, v, sel)
 
 
-def local_far(meta, q, k, v, sel, near, cross):
+def local_far(first, many, meta, q, k, v, sel, near, cross):
     return pl.pallas_call(
-        functools.partial(local_kernel, "D", 0, PAIRS),
+        functools.partial(local_kernel, "D", first, many),
         in_specs=[smem()] + [vmem()] * 6,
         out_specs=[vmem()] * 3,
         out_shape=[
-            shape((RES, GROUPS, WIDTH)),
-            shape((GROUPS, WIDTH), F32),
-            shape((GROUPS, WIDTH), F32),
+            shape((RES, GROUPS, many * 128)),
+            shape((GROUPS, many * 128), F32),
+            shape((GROUPS, many * 128), F32),
         ],
         compiler_params=params(40),
         cost_estimate=pl.CostEstimate(
-            flops=1000000000, bytes_accessed=1000000, transcendentals=2000000
+            flops=many * 200000000, bytes_accessed=1000000, transcendentals=many * 400000
         ),
         name="wide_queries",
     )(meta, q, k, v, sel, near, cross)
@@ -506,7 +510,7 @@
 def merge(meta, close, wide, back):
     return pl.pallas_call(
         merge_kernel,
-        in_specs=[smem()] + [vmem()] * (len(NEAR_PARTS) + 7),
+        in_specs=[smem()] + [vmem()] * (len(NEAR_PARTS) + 3 * len(WIDE_PARTS) + 4),
         out_specs=pl.BlockSpec(memory_space=pltpu.HBM),
         out_shape=shape((ROWS, WIDTH)),
         scratch_shapes=[
@@ -517,7 +521,7 @@
         ],
         compiler_params=params(40),
         name="merge_rows",
-    )(meta, *close, *wide, *back)
+    )(meta, *close, *[part for parts in zip(*wide) for part in parts], *back)
 
 
 def at(x, z, c):
@@ -565,12 +569,12 @@
     cross = move(near, other_core)
     blocks = [own] + moved
     blocks += [move(block, other_core) for block in blocks]
-    close.append(local_near(*NEAR_PARTS[2], later, *local))
-    blocks, close[2], later = lax.optimization_barrier((blocks, close[2], later))
+    wide = [local_far(*WIDE_PARTS[0], later, *local, near, cross)]
+    blocks, wide[0], later = lax.optimization_barrier((blocks, wide[0], later))
     back = slide_wide(meta, [slab[:, 0:256] for slab in slabs], blocks)
     back, later = lax.optimization_barrier((back, later))
     back = [back[0]] + [move(back[step], along_z(-step)) for step in (1, 2, 3)]
-    wide = local_far(later, *local, near, cross)
+    wide.append(local_far(*WIDE_PARTS[1], later, *local, near, cross))
     return merge(meta, close, wide, back)
 
 

time: 50.6 us -> 49.6 us (0.980)
  local copies, waits for them, and re-layouts: 3.02 us -> 0.04 us
  Pallas kernels: 26 us -> 27.3 us
  starting transfers between devices: 15.9 us -> 16.5 us
    unnamed x6 -> x0, local copies, waits for them, and re-layouts: 2.98 us -> none
    pallas_call x4 -> x3, Pallas kernels: 6.93 us -> 9.25 us  [the longest x2 5.13 us: local_far(): pl.pallas_call(functools.partial(local_kernel, 'D', first, many), in_spec...]
    pallas_call x3 -> x2, Pallas kernels: 13 us -> 12.2 us  [local_near(): pl.pallas_call(functools.partial(local_kernel, 'ABC', first, many), in_sp...]
    ppermute x16, starting transfers between devices: 15.9 us -> 16.5 us  [move(): return lax.ppermute(block, 'seq', route)]
  transfers between devices with their start and end apart: 16 -> 16, of which waited for: 2 -> 4; matrix products, arithmetic and copies ran while one was open for 0% -> 0% of each run, Pallas kernels for 41% -> 35%
where the time goes in v5:
time: 49.6 us; the launch traced here: 49.3 us
  Pallas kernels  27.3 us (55%)
  starting transfers between devices  16.5 us (33%)
  waiting for transfers between devices  4.33 us (9%)
  between operations  1 us (2%)
    ppermute x16, starting transfers between devices, move(): return lax.ppermute(block, 'seq', route)  16.5 us
    pallas_call x2, Pallas kernels, local_near(): pl.pallas_call(functools.partial(local_kernel, 'ABC', first, many), in_sp...  12.2 us
    pallas_call x2, Pallas kernels, local_far(): pl.pallas_call(functools.partial(local_kernel, 'D', first, many), in_spec...  5.13 us
    ppermute x16, waiting for transfers between devices, move(): return lax.ppermute(block, 'seq', route)  4.33 us
    pallas_call x1, Pallas kernels, split(): pl.pallas_call(split_kernel, in_specs=[smem()] + [pl.BlockSpec(memory_spa...  4.11 us
    pallas_call x1, Pallas kernels, slide_wide(): pl.pallas_call(far_kernel, in_specs=[smem()] + [vmem()] * 12, out_specs=[...  3.34 us
    pallas_call x1, Pallas kernels, merge(): pl.pallas_call(merge_kernel, in_specs=[smem()] + [vmem()] * (len(NEAR_PAR...  2.5 us
  transfers between devices with their start and end apart: 16, of which 4 were waited for; matrix products, arithmetic and copies ran while one was open for 0% of the time, Pallas kernels for 35%

profile of v5, /device:TPU:1, one launch (start us, length us, event | category | flops | bytes accessed | tf_op | source)
XLA Modules:
  0.0 49.3 jit_solution(6667975321353225031)
XLA Ops:
  0.7 0.1 pad_add_fusion.meta
  0.7 4.1 %split_rows.1 = (bf16[16,64,768]{2,1,0:T(8,128)(2,1)S(1)}, bf16[16,64,768]{2,1,0:T(8,128)(2,1)S(1)}, bf16[16,64,768]{2,1,0:T(8,128)(2,1)S(1)}, bf16[4,2,64,768]{...) custom-call(s32[2]{0:T(128)S(1)} %pad_add_fusion.meta, ...), custom_call_target="tpu_custom_call" | custom-call | tf_op jit(solution)/shard_map/split_rows/pallas_call | solution.py:449
  4.8 1.5 %collective-permute-start.3 = (bf16[4,2,64,768]{3,2,1,0:T(8,128)(2,1)S(1)}, bf16[4,2,64,768]{3,2,1,0:T(8,128)(2,1)S(1)}, u32[]{:S(2)}, u32[]{:S(2)}) collective-permute-start(bf16[4,2,64,768]{3,2,1,0:T(8,128)(2,1)S(1)} %get-tuple-element.63), channel_id=1, source_target_pairs={{0,1},{1,0},{2,3},{3,2},{4,5},{5,4},{6,7},{7,6},{8,9},{9,8},{10,11... | collective-permute-start | bytes 2359304 | tf_op jit(solution)/shard_map/ppermute | solution.py:535
  6.4 1.7 %collective-permute-start = (bf16[64,640]{1,0:T(8,128)(2,1)S(1)}, bf16[64,640]{1,0:T(8,128)(2,1)S(1)}, u32[]{:S(2)}, u32[]{:S(2)}) collective-permute-start(bf16[64,640]{1,0:T(8,128)(2,1)S(1)} %get-tuple-element.57), channel_id=1, source_target_pairs={{0,2},{1,3},{2,4},{3,5},{4,6},{5,7},{6,0},{7,1},{8,10},{9,11},{10,... | collective-permute-start | bytes 245768 | tf_op jit(solution)/shard_map/ppermute | solution.py:535
  8.1 3.3 %collective-permute-start.1 = (bf16[64,640]{1,0:T(8,128)(2,1)S(1)}, bf16[64,640]{1,0:T(8,128)(2,1)S(1)}, u32[]{:S(2)}, u32[]{:S(2)}) collective-permute-start(bf16[64,640]{1,0:T(8,128)(2,1)S(1)} %get-tuple-element.58), channel_id=1, source_target_pairs={{0,4},{1,5},{2,6},{3,7},{4,0},{5,1},{6,2},{7,3},{8,12},{9,13},{10,... | collective-permute-start | bytes 245768 | tf_op jit(solution)/shard_map/ppermute | solution.py:535
  11.4 0.7 %collective-permute-start.2 = (bf16[64,640]{1,0:T(8,128)(2,1)S(1)}, bf16[64,640]{1,0:T(8,128)(2,1)S(1)}, u32[]{:S(2)}, u32[]{:S(2)}) collective-permute-start(bf16[64,640]{1,0:T(8,128)(2,1)S(1)} %get-tuple-element.59), channel_id=1, source_target_pairs={{0,6},{1,7},{2,0},{3,1},{4,2},{5,3},{6,4},{7,5},{8,14},{9,15},{10,... | collective-permute-start | bytes 245768 | tf_op jit(solution)/shard_map/ppermute | solution.py:535
  12.1 0.0 collective-permute-done.3.refs_3_
  12.1 2.6 %near_queries.2.refs_0_ = bf16[16,64,128]{2,1,0:T(8,128)(2,1)S(1)} custom-call(s32[2]{0:T(128)S(1)} %pad_add_fusion.meta, bf16[16,64,768]{2,1,0:T(8,128)(2,1)S(1)} %get-tuple-element.60.refs_0_, bf16[16,64,768]{2,1,0:T(8,128)(2,1)S(1)} %get-tuple-element.61.refs_1_, bf16[16,64,768]{2,1,0:T(8,128)(2,1)S(1)} %get-tuple-element.62.refs_2_, ...), custom_call_target="tpu_custom_call" | custom-call | flops 600000000 | bytes 1000000 | tf_op jit(solution)/shard_map/near_queries/pallas_call | solution.py:467
  14.7 1.0 %collective-permute-done.1 = bf16[64,640]{1,0:T(8,128)(2,1)S(1)} collective-permute-done((bf16[64,640]{1,0:T(8,128)(2,1)S(1)}, bf16[64,640]{1,0:T(8,128)(2,1)S(1)}, u32[]{:S(2)}, u32[]{:S(2)}) %collective-permute-start.1) | collective-permute-done | bytes 81952 | tf_op jit(solution)/shard_map/ppermute | solution.py:535
  15.7 0.0 collective-permute-done.2
  15.7 0.8 %collective-permute-start.7 = (bf16[2,2,64,768]{3,2,1,0:T(8,128)(2,1)S(1)}, bf16[2,2,64,768]{3,2,1,0:T(8,128)(2,1)S(1)}, u32[]{:S(2)}, u32[]{:S(2)}) collective-permute-start(bf16[2,2,64,768]{3,2,1,0:T(8,128)(2,1)S(1)} %get-tuple-element.72), channel_id=1, source_target_pairs={{0,2},{1,3},{2,0},{3,1},{4,6},{5,7},{6,4},{7,5},{8,10},{9,11},{10,... | collective-permute-start | bytes 1179656 | tf_op jit(solution)/shard_map/ppermute | solution.py:535
  16.5 2.6 %collective-permute-start.6 = (bf16[256,384]{1,0:T(8,128)(2,1)S(1)}, bf16[256,384]{1,0:T(8,128)(2,1)S(1)}, u32[]{:S(2)}, u32[]{:S(2)}) collective-permute-start(bf16[256,384]{1,0:T(8,128)(2,1)S(1)} %pad_maximum_fusion.rest_0_), channel_id=1, source_target_pairs={{0,24},{1,25},{2,26},{3,27},{4,28},{5,29},{6,30},{7,31},{8,0},{9,1... | collective-permute-start | bytes 589832 | tf_op jit(solution)/shard_map/ppermute | solution.py:535
  19.1 0.5 %collective-permute-start.5 = (bf16[256,384]{1,0:T(8,128)(2,1)S(1)}, bf16[256,384]{1,0:T(8,128)(2,1)S(1)}, u32[]{:S(2)}, u32[]{:S(2)}) collective-permute-start(bf16[256,384]{1,0:T(8,128)(2,1)S(1)} %pad_maximum_fusion.rest_0_), channel_id=1, source_target_pairs={{0,16},{1,17},{2,18},{3,19},{4,20},{5,21},{6,22},{7,23},{8,24},{9,... | collective-permute-start | bytes 589832 | tf_op jit(solution)/shard_map/ppermute | solution.py:535
  19.6 0.6 %collective-permute-start.4 = (bf16[256,384]{1,0:T(8,128)(2,1)S(1)}, bf16[256,384]{1,0:T(8,128)(2,1)S(1)}, u32[]{:S(2)}, u32[]{:S(2)}) collective-permute-start(bf16[256,384]{1,0:T(8,128)(2,1)S(1)} %pad_maximum_fusion.rest_0_), channel_id=1, source_target_pairs={{0,8},{1,9},{2,10},{3,11},{4,12},{5,13},{6,14},{7,15},{8,16},{9,17... | collective-permute-start | bytes 589832 | tf_op jit(solution)/shard_map/ppermute | solution.py:535
  20.2 9.7 %near_queries.3.refs_1_ = bf16[16,64,640]{2,1,0:T(8,128)(2,1)S(1)} custom-call(s32[2]{0:T(128)S(1)} %pad_add_fusion.meta, bf16[16,64,768]{2,1,0:T(8,128)(2,1)S(1)} %get-tuple-element.60.refs_0_, bf16[16,64,768]{2,1,0:T(8,128)(2,1)S(1)} %get-tuple-element.61.refs_1_, bf16[16,64,768]{2,1,0:T(8,128)(2,1)S(1)} %get-tuple-element.62.refs_2_, ...), custom_call_target="tpu_custom_call" | custom-call | flops 3000000000 | bytes 1000000 | tf_op jit(solution)/shard_map/near_queries/pallas_call | solution.py:467
  29.9 1.6 %collective-permute-done.4.rest_1_ = bf16[256,384]{1,0:T(8,128)(2,1)S(1)} collective-permute-done((bf16[256,384]{1,0:T(8,128)(2,1)S(1)}, bf16[256,384]{1,0:T(8,128)(2,1)S(1)}, u32[]{:S(2)}, u32[]{:S(2)}) %collective-permute-start.4) | collective-permute-done | bytes 196640 | tf_op jit(solution)/shard_map/ppermute | solution.py:535
  31.5 0.6 %collective-permute-start.12 = (bf16[2,2,64,768]{3,2,1,0:T(8,128)(2,1)S(1)}, bf16[2,2,64,768]{3,2,1,0:T(8,128)(2,1)S(1)}, u32[]{:S(2)}, u32[]{:S(2)}) collective-permute-start(bf16[2,2,64,768]{3,2,1,0:T(8,128)(2,1)S(1)} %collective-permute-done.7.refs_4_), channel_id=1, source_target_pairs={{0,1},{1,0},{2,3},{3,2},{4,5},{5,4},{6,7},{7,6},{8,9},{9,8},{10,11... | collective-permute-start | bytes 1179656 | tf_op jit(solution)/shard_map/ppermute | solution.py:535
  32.1 0.1 collective-permute-start.8
  32.2 0.4 collective-permute-start.9
  32.7 0.1 collective-permute-start.10
  32.7 0.4 collective-permute-start.11
  33.2 0.3 collective-permute-done.12.refs_5_
  33.5 2.6 %wide_queries.2 = (bf16[16,64,384]{2,1,0:T(8,128)(2,1)S(1)}, f32[64,384]{1,0:T(8,128)S(1)}, f32[64,384]{1,0:T(8,128)S(1)}) custom-call(s32[2]{0:T(128)S(1)} %pad_add_fusion.meta, bf16[16,64,768]{2,1,0:T(8,128)(2,1)S(1)} %get-tuple-element.60.refs_0_, bf16[16,64,768]{2,1,0:T(8,128)(2,1)S(1)} %get-tuple-element.61.refs_1_, ...), custom_call_target="tpu_custom_call" | custom-call | flops 600000000 | bytes 1000000 | tf_op jit(solution)/shard_map/wide_queries/pallas_call | solution.py:481
  36.1 0.0 collective-permute-done.10.rest_6_
  36.1 3.3 %slide_queries.1 = (bf16[64,256]{1,0:T(8,128)(2,1)S(1)}, bf16[64,256]{1,0:T(8,128)(2,1)S(1)}, bf16[64,256]{1,0:T(8,128)(2,1)S(1)}, bf16[64,256]{1,0:T(8,128)(2,1)S(1)}) custom-call(s32[2]{0:T(128)S(1)} %pad_add_fusion.meta, bf16[64,256]{1,0:T(8,128)(2,1)S(1)} %slice.28.a0, bf16[64,256]{1,0:T(8,128)(2,1)S(1)} %slice.29.a1, bf16[64,256]{1,0:T(8,128)(2,1)S(1)} %slice.30.a2, ...), custom_call_target="tpu_custom_call" | custom-call | flops 800000000 | bytes 2000000 | tf_op jit(solution)/shard_map/slide_queries/pallas_call | solution.py:499
  39.5 1.4 %collective-permute-start.13 = (bf16[64,256]{1,0:T(8,128)(2,1)S(1)}, bf16[64,256]{1,0:T(8,128)(2,1)S(1)}, u32[]{:S(2)}, u32[]{:S(2)}) collective-permute-start(bf16[64,256]{1,0:T(8,128)(2,1)S(1)} %get-tuple-element.104), channel_id=1, source_target_pairs={{0,6},{1,7},{2,0},{3,1},{4,2},{5,3},{6,4},{7,5},{8,14},{9,15},{10,... | collective-permute-start | bytes 98312 | tf_op jit(solution)/shard_map/ppermute | solution.py:535
  40.9 1.2 %collective-permute-start.14 = (bf16[64,256]{1,0:T(8,128)(2,1)S(1)}, bf16[64,256]{1,0:T(8,128)(2,1)S(1)}, u32[]{:S(2)}, u32[]{:S(2)}) collective-permute-start(bf16[64,256]{1,0:T(8,128)(2,1)S(1)} %get-tuple-element.105), channel_id=1, source_target_pairs={{0,4},{1,5},{2,6},{3,7},{4,0},{5,1},{6,2},{7,3},{8,12},{9,13},{10,... | collective-permute-start | bytes 98312 | tf_op jit(solution)/shard_map/ppermute | solution.py:535
  42.1 0.5 %collective-permute-start.15 = (bf16[64,256]{1,0:T(8,128)(2,1)S(1)}, bf16[64,256]{1,0:T(8,128)(2,1)S(1)}, u32[]{:S(2)}, u32[]{:S(2)}) collective-permute-start(bf16[64,256]{1,0:T(8,128)(2,1)S(1)} %get-tuple-element.106), channel_id=1, source_target_pairs={{0,2},{1,3},{2,4},{3,5},{4,6},{5,7},{6,0},{7,1},{8,10},{9,11},{10,... | collective-permute-start | bytes 98312 | tf_op jit(solution)/shard_map/ppermute | solution.py:535
  42.6 2.6 %wide_queries.3 = (bf16[16,64,384]{2,1,0:T(8,128)(2,1)S(1)}, f32[64,384]{1,0:T(8,128)S(1)}, f32[64,384]{1,0:T(8,128)S(1)}) custom-call(s32[2]{0:T(128)S(1)} %pad_add_fusion.meta, bf16[16,64,768]{2,1,0:T(8,128)(2,1)S(1)} %get-tuple-element.60.refs_0_, bf16[16,64,768]{2,1,0:T(8,128)(2,1)S(1)} %get-tuple-element.61.refs_1_, ...), custom_call_target="tpu_custom_call" | custom-call | flops 600000000 | bytes 1000000 | tf_op jit(solution)/shard_map/wide_queries/pallas_call | solution.py:481
  45.2 0.0 collective-permute-done.14.refs_10_
  45.2 1.4 %collective-permute-done.15.refs_11_ = bf16[64,256]{1,0:T(8,128)(2,1)S(1)} collective-permute-done((bf16[64,256]{1,0:T(8,128)(2,1)S(1)}, bf16[64,256]{1,0:T(8,128)(2,1)S(1)}, u32[]{:S(2)}, u32[]{:S(2)}) %collective-permute-start.15) | collective-permute-done | bytes 32800 | tf_op jit(solution)/shard_map/ppermute | solution.py:535
  46.6 2.5 %merge_rows.1 = bf16[1024,768]{1,0:T(8,128)(2,1)} custom-call(s32[2]{0:T(128)S(1)} %pad_add_fusion.meta, bf16[16,64,128]{2,1,0:T(8,128)(2,1)S(1)} %near_queries.2.refs_0_, bf16[16,64,640]{2,1,0:T(8,128)(2,1)S(1)} %near_queries.3.refs_1_, bf16[16,64,384]{2,1,0:T(8,128)(2,1)S(1)} %get-tuple-element.83.refs_2_, ...), custom_call_target="tpu_custom_call" | custom-call | tf_op jit(solution)/shard_map/merge_rows/pallas_call | solution.py:511
  (17 shorter events, 0.1 us)
Async XLA Ops:
  4.8 7.3 %collective-permute-start.3 = (bf16[4,2,64,768]{3,2,1,0:T(8,128)(2,1)S(1)}, bf16[4,2,64,768]{3,2,1,0:T(8,128)(2,1)S(1)}, u32[]{:S(2)}, u32[]{:S(2)}) collective-permute-start(bf16[4,2,64,768]{3,2,1,0:T(8,128)(2,1)S(1)} %get-tuple-element.63), channel_id=1, source_target_pairs={{0,1},{1,0},{2,3},{3,2},{4,5},{5,4},{6,7},{7,6},{8,9},{9,8},{10,11... | collective-permute-start | bytes 2359304 | tf_op jit(solution)/shard_map/ppermute | solution.py:535
  6.4 8.4 %collective-permute-start = (bf16[64,640]{1,0:T(8,128)(2,1)S(1)}, bf16[64,640]{1,0:T(8,128)(2,1)S(1)}, u32[]{:S(2)}, u32[]{:S(2)}) collective-permute-start(bf16[64,640]{1,0:T(8,128)(2,1)S(1)} %get-tuple-element.57), channel_id=1, source_target_pairs={{0,2},{1,3},{2,4},{3,5},{4,6},{5,7},{6,0},{7,1},{8,10},{9,11},{10,... | collective-permute-start | bytes 245768 | tf_op jit(solution)/shard_map/ppermute | solution.py:535
  8.1 7.6 %collective-permute-start.1 = (bf16[64,640]{1,0:T(8,128)(2,1)S(1)}, bf16[64,640]{1,0:T(8,128)(2,1)S(1)}, u32[]{:S(2)}, u32[]{:S(2)}) collective-permute-start(bf16[64,640]{1,0:T(8,128)(2,1)S(1)} %get-tuple-element.58), channel_id=1, source_target_pairs={{0,4},{1,5},{2,6},{3,7},{4,0},{5,1},{6,2},{7,3},{8,12},{9,13},{10,... | collective-permute-start | bytes 245768 | tf_op jit(solution)/shard_map/ppermute | solution.py:535
  11.4 4.3 %collective-permute-start.2 = (bf16[64,640]{1,0:T(8,128)(2,1)S(1)}, bf16[64,640]{1,0:T(8,128)(2,1)S(1)}, u32[]{:S(2)}, u32[]{:S(2)}) collective-permute-start(bf16[64,640]{1,0:T(8,128)(2,1)S(1)} %get-tuple-element.59), channel_id=1, source_target_pairs={{0,6},{1,7},{2,0},{3,1},{4,2},{5,3},{6,4},{7,5},{8,14},{9,15},{10,... | collective-permute-start | bytes 245768 | tf_op jit(solution)/shard_map/ppermute | solution.py:535
  15.7 15.8 %collective-permute-start.7 = (bf16[2,2,64,768]{3,2,1,0:T(8,128)(2,1)S(1)}, bf16[2,2,64,768]{3,2,1,0:T(8,128)(2,1)S(1)}, u32[]{:S(2)}, u32[]{:S(2)}) collective-permute-start(bf16[2,2,64,768]{3,2,1,0:T(8,128)(2,1)S(1)} %get-tuple-element.72), channel_id=1, source_target_pairs={{0,2},{1,3},{2,0},{3,1},{4,6},{5,7},{6,4},{7,5},{8,10},{9,11},{10,... | collective-permute-start | bytes 1179656 | tf_op jit(solution)/shard_map/ppermute | solution.py:535
  16.5 13.4 %collective-permute-start.6 = (bf16[256,384]{1,0:T(8,128)(2,1)S(1)}, bf16[256,384]{1,0:T(8,128)(2,1)S(1)}, u32[]{:S(2)}, u32[]{:S(2)}) collective-permute-start(bf16[256,384]{1,0:T(8,128)(2,1)S(1)} %pad_maximum_fusion.rest_0_), channel_id=1, source_target_pairs={{0,24},{1,25},{2,26},{3,27},{4,28},{5,29},{6,30},{7,31},{8,0},{9,1... | collective-permute-start | bytes 589832 | tf_op jit(solution)/shard_map/ppermute | solution.py:535
  19.1 10.8 %collective-permute-start.5 = (bf16[256,384]{1,0:T(8,128)(2,1)S(1)}, bf16[256,384]{1,0:T(8,128)(2,1)S(1)}, u32[]{:S(2)}, u32[]{:S(2)}) collective-permute-start(bf16[256,384]{1,0:T(8,128)(2,1)S(1)} %pad_maximum_fusion.rest_0_), channel_id=1, source_target_pairs={{0,16},{1,17},{2,18},{3,19},{4,20},{5,21},{6,22},{7,23},{8,24},{9,... | collective-permute-start | bytes 589832 | tf_op jit(solution)/shard_map/ppermute | solution.py:535
  19.6 11.9 %collective-permute-start.4 = (bf16[256,384]{1,0:T(8,128)(2,1)S(1)}, bf16[256,384]{1,0:T(8,128)(2,1)S(1)}, u32[]{:S(2)}, u32[]{:S(2)}) collective-permute-start(bf16[256,384]{1,0:T(8,128)(2,1)S(1)} %pad_maximum_fusion.rest_0_), channel_id=1, source_target_pairs={{0,8},{1,9},{2,10},{3,11},{4,12},{5,13},{6,14},{7,15},{8,16},{9,17... | collective-permute-start | bytes 589832 | tf_op jit(solution)/shard_map/ppermute | solution.py:535
  31.5 2.0 %collective-permute-start.12 = (bf16[2,2,64,768]{3,2,1,0:T(8,128)(2,1)S(1)}, bf16[2,2,64,768]{3,2,1,0:T(8,128)(2,1)S(1)}, u32[]{:S(2)}, u32[]{:S(2)}) collective-permute-start(bf16[2,2,64,768]{3,2,1,0:T(8,128)(2,1)S(1)} %collective-permute-done.7.refs_4_), channel_id=1, source_target_pairs={{0,1},{1,0},{2,3},{3,2},{4,5},{5,4},{6,7},{7,6},{8,9},{9,8},{10,11... | collective-permute-start | bytes 1179656 | tf_op jit(solution)/shard_map/ppermute | solution.py:535
  32.1 3.9 %collective-permute-start.8 = (bf16[256,384]{1,0:T(8,128)(2,1)S(1)}, bf16[256,384]{1,0:T(8,128)(2,1)S(1)}, u32[]{:S(2)}, u32[]{:S(2)}) collective-permute-start(bf16[256,384]{1,0:T(8,128)(2,1)S(1)} %pad_maximum_fusion.rest_0_), channel_id=1, source_target_pairs={{0,1},{1,0},{2,3},{3,2},{4,5},{5,4},{6,7},{7,6},{8,9},{9,8},{10,11... | collective-permute-start | bytes 589832 | tf_op jit(solution)/shard_map/ppermute | solution.py:535
  32.2 3.9 %collective-permute-start.9 = (bf16[256,384]{1,0:T(8,128)(2,1)S(1)}, bf16[256,384]{1,0:T(8,128)(2,1)S(1)}, u32[]{:S(2)}, u32[]{:S(2)}) collective-permute-start(bf16[256,384]{1,0:T(8,128)(2,1)S(1)} %collective-permute-done.4.rest_1_), channel_id=1, source_target_pairs={{0,1},{1,0},{2,3},{3,2},{4,5},{5,4},{6,7},{7,6},{8,9},{9,8},{10,11... | collective-permute-start | bytes 589832 | tf_op jit(solution)/shard_map/ppermute | solution.py:535
  32.7 3.4 %collective-permute-start.10 = (bf16[256,384]{1,0:T(8,128)(2,1)S(1)}, bf16[256,384]{1,0:T(8,128)(2,1)S(1)}, u32[]{:S(2)}, u32[]{:S(2)}) collective-permute-start(bf16[256,384]{1,0:T(8,128)(2,1)S(1)} %collective-permute-done.5.rest_2_), channel_id=1, source_target_pairs={{0,1},{1,0},{2,3},{3,2},{4,5},{5,4},{6,7},{7,6},{8,9},{9,8},{10,11... | collective-permute-start | bytes 589832 | tf_op jit(solution)/shard_map/ppermute | solution.py:535
  32.7 3.4 %collective-permute-start.11 = (bf16[256,384]{1,0:T(8,128)(2,1)S(1)}, bf16[256,384]{1,0:T(8,128)(2,1)S(1)}, u32[]{:S(2)}, u32[]{:S(2)}) collective-permute-start(bf16[256,384]{1,0:T(8,128)(2,1)S(1)} %collective-permute-done.6.rest_3_), channel_id=1, source_target_pairs={{0,1},{1,0},{2,3},{3,2},{4,5},{5,4},{6,7},{7,6},{8,9},{9,8},{10,11... | collective-permute-start | bytes 589832 | tf_op jit(solution)/shard_map/ppermute | solution.py:535
  39.5 5.7 %collective-permute-start.13 = (bf16[64,256]{1,0:T(8,128)(2,1)S(1)}, bf16[64,256]{1,0:T(8,128)(2,1)S(1)}, u32[]{:S(2)}, u32[]{:S(2)}) collective-permute-start(bf16[64,256]{1,0:T(8,128)(2,1)S(1)} %get-tuple-element.104), channel_id=1, source_target_pairs={{0,6},{1,7},{2,0},{3,1},{4,2},{5,3},{6,4},{7,5},{8,14},{9,15},{10,... | collective-permute-start | bytes 98312 | tf_op jit(solution)/shard_map/ppermute | solution.py:535
  40.9 4.3 %collective-permute-start.14 = (bf16[64,256]{1,0:T(8,128)(2,1)S(1)}, bf16[64,256]{1,0:T(8,128)(2,1)S(1)}, u32[]{:S(2)}, u32[]{:S(2)}) collective-permute-start(bf16[64,256]{1,0:T(8,128)(2,1)S(1)} %get-tuple-element.105), channel_id=1, source_target_pairs={{0,4},{1,5},{2,6},{3,7},{4,0},{5,1},{6,2},{7,3},{8,12},{9,13},{10,... | collective-permute-start | bytes 98312 | tf_op jit(solution)/shard_map/ppermute | solution.py:535
  42.1 4.5 %collective-permute-start.15 = (bf16[64,256]{1,0:T(8,128)(2,1)S(1)}, bf16[64,256]{1,0:T(8,128)(2,1)S(1)}, u32[]{:S(2)}, u32[]{:S(2)}) collective-permute-start(bf16[64,256]{1,0:T(8,128)(2,1)S(1)} %get-tuple-element.106), channel_id=1, source_target_pairs={{0,2},{1,3},{2,4},{3,5},{4,6},{5,7},{6,0},{7,1},{8,10},{9,11},{10,... | collective-permute-start | bytes 98312 | tf_op jit(solution)/shard_map/ppermute | solution.py:535

commit v6 on v5

--- a/solution.py
+++ b/solution.py
@@ -28,7 +28,7 @@
 PAIR_OF = [0, 2, 3, 5]
 LONE_OF = [2, 3, 8, 9]
 NEAR_PARTS = [(0, 1), (1, 5)]
-WIDE_PARTS = [(0, 3), (3, 3)]
+WIDE_PARTS = [(0, 2), (2, 4)]
 
 
 def level(u):
@@ -96,7 +96,7 @@
                     v0 = rows
         q0 = picked(qt, 0)
         for group in range(NZ):
-            slot = (group - zpos) & 3
+            slot = group ^ zpos
             if pair == PAIR_OF[group]:
                 stage[slot, :, 0:128] = q0
                 stage[slot, :, 256:384] = k0
@@ -283,9 +283,9 @@
     pair = jnp.where(group == 0, 0, jnp.where(group == 1, 4, jnp.where(group == 2, 6, 10)))
     lone = jnp.where(group == 0, 2, jnp.where(group == 1, 3, jnp.where(group == 2, 8, 9)))
     def positions(at, head):
-        from_x = (xpos - at % 4) & 3
+        from_x = xpos ^ (at % 4)
         from_c = core if at < 4 else 1 - core
-        from_z = (zpos - part) & 3
+        from_z = zpos ^ part
         return ((from_x * NZ + from_z) * NC + from_c) * ROWS + (lane & 63) * 16 + head
 
     results = []
@@ -368,12 +368,12 @@
         close_part, close_lanes = part_of(NEAR_PARTS, pair)
         wide_part, wide_lanes = part_of(WIDE_PARTS, pair)
         if pair in PAIR_OF:
-            slot = (PAIR_OF.index(pair) - zpos) & 3
+            slot = PAIR_OF.index(pair) ^ zpos
             away = stage[slot, :, 0:128]
             away_lse = jnp.where(low, log_of(slot, 0), log_of(slot, 1))
         else:
-            left = (LONE_OF.index(2 * pair) - zpos) & 3
-            right = (left + 1) & 3
+            left = LONE_OF.index(2 * pair) ^ zpos
+            right = (LONE_OF.index(2 * pair) + 1) ^ zpos
             away = jnp.where(low, pltpu.roll(stage[left, :, 128:256], 64, 1), stage[right, :, 128:256])
             away_lse = jnp.where(low, log_of(left, 2), log_of(right, 2))
         here, here_lse = o0[wide_part][:, wide_lanes], lse0[wide_part][:, wide_lanes]
@@ -525,7 +525,7 @@
 
 
 def at(x, z, c):
-    return (x % NX * NZ + z % NZ) * NC + c
+    return (x * NZ + z) * NC + c
 
 
 def move(block, to):
@@ -536,11 +536,11 @@
 
 
 def along_x(steps):
-    return lambda x, z, c: (x + steps, z, c)
+    return lambda x, z, c: (x ^ steps, z, c)
 
 
 def along_z(steps):
-    return lambda x, z, c: (x, z + steps, c)
+    return lambda x, z, c: (x, z ^ steps, c)
 
 
 def other_core(x, z, c):
@@ -573,7 +573,7 @@
     blocks, wide[0], later = lax.optimization_barrier((blocks, wide[0], later))
     back = slide_wide(meta, [slab[:, 0:256] for slab in slabs], blocks)
     back, later = lax.optimization_barrier((back, later))
-    back = [back[0]] + [move(back[step], along_z(-step)) for step in (1, 2, 3)]
+    back = [back[0]] + [move(back[step], along_z(step)) for step in (1, 2, 3)]
     wide.append(local_far(*WIDE_PARTS[1], later, *local, near, cross))
     return merge(meta, close, wide, back)
 

time: 49.6 us -> 49.5 us (level)
  transfers between devices with their start and end apart: 16 -> 16, of which waited for: 4 -> 3; matrix products, arithmetic and copies ran while one was open for 0% -> 0% of each run, Pallas kernels for 35% -> 35%
where the time goes in v6:
time: 49.5 us; the launch traced here: 49.3 us
  Pallas kernels  27.3 us (55%)
  starting transfers between devices  16.9 us (34%)
  waiting for transfers between devices  3.98 us (8%)
  between operations  1.03 us (2%)
    ppermute x16, starting transfers between devices, move(): return lax.ppermute(block, 'seq', route)  16.9 us
    pallas_call x2, Pallas kernels, local_near(): pl.pallas_call(functools.partial(local_kernel, 'ABC', first, many), in_sp...  12.2 us
    pallas_call x2, Pallas kernels, local_far(): pl.pallas_call(functools.partial(local_kernel, 'D', first, many), in_spec...  5.17 us
    pallas_call x1, Pallas kernels, split(): pl.pallas_call(split_kernel, in_specs=[smem()] + [pl.BlockSpec(memory_spa...  4.07 us
    ppermute x16, waiting for transfers between devices, move(): return lax.ppermute(block, 'seq', route)  3.98 us
    pallas_call x1, Pallas kernels, slide_wide(): pl.pallas_call(far_kernel, in_specs=[smem()] + [vmem()] * 12, out_specs=[...  3.35 us
    pallas_call x1, Pallas kernels, merge(): pl.pallas_call(merge_kernel, in_specs=[smem()] + [vmem()] * (len(NEAR_PAR...  2.49 us
  transfers between devices with their start and end apart: 16, of which 3 were waited for; matrix products, arithmetic and copies ran while one was open for 0% of the time, Pallas kernels for 35%

profile of v6, /device:TPU:1, one launch (start us, length us, event | category | flops | bytes accessed | tf_op | source)
XLA Modules:
  0.0 49.3 jit_solution(10987989026869399709)
XLA Ops:
  0.7 0.1 pad_add_fusion.meta
  0.7 4.1 %split_rows.1 = (bf16[16,64,768]{2,1,0:T(8,128)(2,1)S(1)}, bf16[16,64,768]{2,1,0:T(8,128)(2,1)S(1)}, bf16[16,64,768]{2,1,0:T(8,128)(2,1)S(1)}, bf16[4,2,64,768]{...) custom-call(s32[2]{0:T(128)S(1)} %pad_add_fusion.meta, ...), custom_call_target="tpu_custom_call" | custom-call | tf_op jit(solution)/shard_map/split_rows/pallas_call | solution.py:449
  4.8 1.5 %collective-permute-start.3 = (bf16[4,2,64,768]{3,2,1,0:T(8,128)(2,1)S(1)}, bf16[4,2,64,768]{3,2,1,0:T(8,128)(2,1)S(1)}, u32[]{:S(2)}, u32[]{:S(2)}) collective-permute-start(bf16[4,2,64,768]{3,2,1,0:T(8,128)(2,1)S(1)} %get-tuple-element.63), channel_id=1, source_target_pairs={{0,1},{1,0},{2,3},{3,2},{4,5},{5,4},{6,7},{7,6},{8,9},{9,8},{10,11... | collective-permute-start | bytes 2359304 | tf_op jit(solution)/shard_map/ppermute | solution.py:535
  6.3 1.7 %collective-permute-start = (bf16[64,640]{1,0:T(8,128)(2,1)S(1)}, bf16[64,640]{1,0:T(8,128)(2,1)S(1)}, u32[]{:S(2)}, u32[]{:S(2)}) collective-permute-start(bf16[64,640]{1,0:T(8,128)(2,1)S(1)} %get-tuple-element.57), channel_id=1, source_target_pairs={{0,2},{1,3},{2,0},{3,1},{4,6},{5,7},{6,4},{7,5},{8,10},{9,11},{10,... | collective-permute-start | bytes 245768 | tf_op jit(solution)/shard_map/ppermute | solution.py:535
  8.0 3.3 %collective-permute-start.1 = (bf16[64,640]{1,0:T(8,128)(2,1)S(1)}, bf16[64,640]{1,0:T(8,128)(2,1)S(1)}, u32[]{:S(2)}, u32[]{:S(2)}) collective-permute-start(bf16[64,640]{1,0:T(8,128)(2,1)S(1)} %get-tuple-element.58), channel_id=1, source_target_pairs={{0,4},{1,5},{2,6},{3,7},{4,0},{5,1},{6,2},{7,3},{8,12},{9,13},{10,... | collective-permute-start | bytes 245768 | tf_op jit(solution)/shard_map/ppermute | solution.py:535
  11.4 0.0 collective-permute-start.2
  11.4 0.0 collective-permute-done.3.refs_3_
  11.4 2.6 %near_queries.2.refs_0_ = bf16[16,64,128]{2,1,0:T(8,128)(2,1)S(1)} custom-call(s32[2]{0:T(128)S(1)} %pad_add_fusion.meta, bf16[16,64,768]{2,1,0:T(8,128)(2,1)S(1)} %get-tuple-element.60.refs_0_, bf16[16,64,768]{2,1,0:T(8,128)(2,1)S(1)} %get-tuple-element.61.refs_1_, bf16[16,64,768]{2,1,0:T(8,128)(2,1)S(1)} %get-tuple-element.62.refs_2_, ...), custom_call_target="tpu_custom_call" | custom-call | flops 600000000 | bytes 1000000 | tf_op jit(solution)/shard_map/near_queries/pallas_call | solution.py:467
  13.9 0.0 collective-permute-done
  13.9 1.7 %collective-permute-done.1 = bf16[64,640]{1,0:T(8,128)(2,1)S(1)} collective-permute-done((bf16[64,640]{1,0:T(8,128)(2,1)S(1)}, bf16[64,640]{1,0:T(8,128)(2,1)S(1)}, u32[]{:S(2)}, u32[]{:S(2)}) %collective-permute-start.1) | collective-permute-done | bytes 81952 | tf_op jit(solution)/shard_map/ppermute | solution.py:535
  15.6 2.0 %collective-permute-done.2 = bf16[64,640]{1,0:T(8,128)(2,1)S(1)} collective-permute-done((bf16[64,640]{1,0:T(8,128)(2,1)S(1)}, bf16[64,640]{1,0:T(8,128)(2,1)S(1)}, u32[]{:S(2)}, u32[]{:S(2)}) %collective-permute-start.2) | collective-permute-done | bytes 81952 | tf_op jit(solution)/shard_map/ppermute | solution.py:535
  17.6 0.1 collective-permute-start.7
  17.8 2.6 %collective-permute-start.6 = (bf16[256,384]{1,0:T(8,128)(2,1)S(1)}, bf16[256,384]{1,0:T(8,128)(2,1)S(1)}, u32[]{:S(2)}, u32[]{:S(2)}) collective-permute-start(bf16[256,384]{1,0:T(8,128)(2,1)S(1)} %pad_maximum_fusion.rest_0_), channel_id=1, source_target_pairs={{0,24},{1,25},{2,26},{3,27},{4,28},{5,29},{6,30},{7,31},{8,16},{9,... | collective-permute-start | bytes 589832 | tf_op jit(solution)/shard_map/ppermute | solution.py:535
  20.3 0.5 %collective-permute-start.5 = (bf16[256,384]{1,0:T(8,128)(2,1)S(1)}, bf16[256,384]{1,0:T(8,128)(2,1)S(1)}, u32[]{:S(2)}, u32[]{:S(2)}) collective-permute-start(bf16[256,384]{1,0:T(8,128)(2,1)S(1)} %pad_maximum_fusion.rest_0_), channel_id=1, source_target_pairs={{0,16},{1,17},{2,18},{3,19},{4,20},{5,21},{6,22},{7,23},{8,24},{9,... | collective-permute-start | bytes 589832 | tf_op jit(solution)/shard_map/ppermute | solution.py:535
  20.8 0.3 collective-permute-start.4
  21.1 9.7 %near_queries.3.refs_1_ = bf16[16,64,640]{2,1,0:T(8,128)(2,1)S(1)} custom-call(s32[2]{0:T(128)S(1)} %pad_add_fusion.meta, bf16[16,64,768]{2,1,0:T(8,128)(2,1)S(1)} %get-tuple-element.60.refs_0_, bf16[16,64,768]{2,1,0:T(8,128)(2,1)S(1)} %get-tuple-element.61.refs_1_, bf16[16,64,768]{2,1,0:T(8,128)(2,1)S(1)} %get-tuple-element.62.refs_2_, ...), custom_call_target="tpu_custom_call" | custom-call | flops 3000000000 | bytes 1000000 | tf_op jit(solution)/shard_map/near_queries/pallas_call | solution.py:467
  30.8 0.0 collective-permute-done.6.rest_3_
  30.8 0.0 collective-permute-done.7.refs_4_
  30.8 1.6 %collective-permute-start.12 = (bf16[2,2,64,768]{3,2,1,0:T(8,128)(2,1)S(1)}, bf16[2,2,64,768]{3,2,1,0:T(8,128)(2,1)S(1)}, u32[]{:S(2)}, u32[]{:S(2)}) collective-permute-start(bf16[2,2,64,768]{3,2,1,0:T(8,128)(2,1)S(1)} %collective-permute-done.7.refs_4_), channel_id=1, source_target_pairs={{0,1},{1,0},{2,3},{3,2},{4,5},{5,4},{6,7},{7,6},{8,9},{9,8},{10,11... | collective-permute-start | bytes 1179656 | tf_op jit(solution)/shard_map/ppermute | solution.py:535
  32.4 0.1 collective-permute-start.8
  32.5 0.4 collective-permute-start.9
  32.9 0.1 collective-permute-start.10
  33.0 0.4 collective-permute-start.11
  33.4 0.3 collective-permute-done.12.refs_5_
  33.8 2.0 %wide_queries.2 = (bf16[16,64,256]{2,1,0:T(8,128)(2,1)S(1)}, f32[64,256]{1,0:T(8,128)S(1)}, f32[64,256]{1,0:T(8,128)S(1)}) custom-call(s32[2]{0:T(128)S(1)} %pad_add_fusion.meta, bf16[16,64,768]{2,1,0:T(8,128)(2,1)S(1)} %get-tuple-element.60.refs_0_, bf16[16,64,768]{2,1,0:T(8,128)(2,1)S(1)} %get-tuple-element.61.refs_1_, ...), custom_call_target="tpu_custom_call" | custom-call | flops 400000000 | bytes 1000000 | tf_op jit(solution)/shard_map/wide_queries/pallas_call | solution.py:481
  35.7 0.0 collective-permute-done.9.rest_5_
  35.8 3.4 %slide_queries.1 = (bf16[64,256]{1,0:T(8,128)(2,1)S(1)}, bf16[64,256]{1,0:T(8,128)(2,1)S(1)}, bf16[64,256]{1,0:T(8,128)(2,1)S(1)}, bf16[64,256]{1,0:T(8,128)(2,1)S(1)}) custom-call(s32[2]{0:T(128)S(1)} %pad_add_fusion.meta, bf16[64,256]{1,0:T(8,128)(2,1)S(1)} %slice.28.a0, bf16[64,256]{1,0:T(8,128)(2,1)S(1)} %slice.29.a1, bf16[64,256]{1,0:T(8,128)(2,1)S(1)} %slice.30.a2, ...), custom_call_target="tpu_custom_call" | custom-call | flops 800000000 | bytes 2000000 | tf_op jit(solution)/shard_map/slide_queries/pallas_call | solution.py:499
  39.1 1.8 %collective-permute-start.13 = (bf16[64,256]{1,0:T(8,128)(2,1)S(1)}, bf16[64,256]{1,0:T(8,128)(2,1)S(1)}, u32[]{:S(2)}, u32[]{:S(2)}) collective-permute-start(bf16[64,256]{1,0:T(8,128)(2,1)S(1)} %get-tuple-element.104), channel_id=1, source_target_pairs={{0,2},{1,3},{2,0},{3,1},{4,6},{5,7},{6,4},{7,5},{8,10},{9,11},{10,... | collective-permute-start | bytes 98312 | tf_op jit(solution)/shard_map/ppermute | solution.py:535
  40.9 2.5 %collective-permute-start.15 = (bf16[64,256]{1,0:T(8,128)(2,1)S(1)}, bf16[64,256]{1,0:T(8,128)(2,1)S(1)}, u32[]{:S(2)}, u32[]{:S(2)}) collective-permute-start(bf16[64,256]{1,0:T(8,128)(2,1)S(1)} %get-tuple-element.106), channel_id=1, source_target_pairs={{0,6},{1,7},{2,4},{3,5},{4,2},{5,3},{6,0},{7,1},{8,14},{9,15},{10,... | collective-permute-start | bytes 98312 | tf_op jit(solution)/shard_map/ppermute | solution.py:535
  43.4 3.2 %wide_queries.3 = (bf16[16,64,512]{2,1,0:T(8,128)(2,1)S(1)}, f32[64,512]{1,0:T(8,128)S(1)}, f32[64,512]{1,0:T(8,128)S(1)}) custom-call(s32[2]{0:T(128)S(1)} %pad_add_fusion.meta, bf16[16,64,768]{2,1,0:T(8,128)(2,1)S(1)} %get-tuple-element.60.refs_0_, bf16[16,64,768]{2,1,0:T(8,128)(2,1)S(1)} %get-tuple-element.61.refs_1_, ...), custom_call_target="tpu_custom_call" | custom-call | flops 800000000 | bytes 1000000 | tf_op jit(solution)/shard_map/wide_queries/pallas_call | solution.py:481
  46.6 0.0 collective-permute-done.13.refs_9_
  46.7 2.5 %merge_rows.1 = bf16[1024,768]{1,0:T(8,128)(2,1)} custom-call(s32[2]{0:T(128)S(1)} %pad_add_fusion.meta, bf16[16,64,128]{2,1,0:T(8,128)(2,1)S(1)} %near_queries.2.refs_0_, bf16[16,64,640]{2,1,0:T(8,128)(2,1)S(1)} %near_queries.3.refs_1_, bf16[16,64,256]{2,1,0:T(8,128)(2,1)S(1)} %get-tuple-element.83.refs_2_, ...), custom_call_target="tpu_custom_call" | custom-call | tf_op jit(solution)/shard_map/merge_rows/pallas_call | solution.py:511
  (17 shorter events, 0.1 us)
Async XLA Ops:
  4.8 6.5 %collective-permute-start.3 = (bf16[4,2,64,768]{3,2,1,0:T(8,128)(2,1)S(1)}, bf16[4,2,64,768]{3,2,1,0:T(8,128)(2,1)S(1)}, u32[]{:S(2)}, u32[]{:S(2)}) collective-permute-start(bf16[4,2,64,768]{3,2,1,0:T(8,128)(2,1)S(1)} %get-tuple-element.63), channel_id=1, source_target_pairs={{0,1},{1,0},{2,3},{3,2},{4,5},{5,4},{6,7},{7,6},{8,9},{9,8},{10,11... | collective-permute-start | bytes 2359304 | tf_op jit(solution)/shard_map/ppermute | solution.py:535
  6.3 7.6 %collective-permute-start = (bf16[64,640]{1,0:T(8,128)(2,1)S(1)}, bf16[64,640]{1,0:T(8,128)(2,1)S(1)}, u32[]{:S(2)}, u32[]{:S(2)}) collective-permute-start(bf16[64,640]{1,0:T(8,128)(2,1)S(1)} %get-tuple-element.57), channel_id=1, source_target_pairs={{0,2},{1,3},{2,0},{3,1},{4,6},{5,7},{6,4},{7,5},{8,10},{9,11},{10,... | collective-permute-start | bytes 245768 | tf_op jit(solution)/shard_map/ppermute | solution.py:535
  8.0 7.6 %collective-permute-start.1 = (bf16[64,640]{1,0:T(8,128)(2,1)S(1)}, bf16[64,640]{1,0:T(8,128)(2,1)S(1)}, u32[]{:S(2)}, u32[]{:S(2)}) collective-permute-start(bf16[64,640]{1,0:T(8,128)(2,1)S(1)} %get-tuple-element.58), channel_id=1, source_target_pairs={{0,4},{1,5},{2,6},{3,7},{4,0},{5,1},{6,2},{7,3},{8,12},{9,13},{10,... | collective-permute-start | bytes 245768 | tf_op jit(solution)/shard_map/ppermute | solution.py:535
  11.4 6.2 %collective-permute-start.2 = (bf16[64,640]{1,0:T(8,128)(2,1)S(1)}, bf16[64,640]{1,0:T(8,128)(2,1)S(1)}, u32[]{:S(2)}, u32[]{:S(2)}) collective-permute-start(bf16[64,640]{1,0:T(8,128)(2,1)S(1)} %get-tuple-element.59), channel_id=1, source_target_pairs={{0,6},{1,7},{2,4},{3,5},{4,2},{5,3},{6,0},{7,1},{8,14},{9,15},{10,... | collective-permute-start | bytes 245768 | tf_op jit(solution)/shard_map/ppermute | solution.py:535
  17.6 13.2 %collective-permute-start.7 = (bf16[2,2,64,768]{3,2,1,0:T(8,128)(2,1)S(1)}, bf16[2,2,64,768]{3,2,1,0:T(8,128)(2,1)S(1)}, u32[]{:S(2)}, u32[]{:S(2)}) collective-permute-start(bf16[2,2,64,768]{3,2,1,0:T(8,128)(2,1)S(1)} %get-tuple-element.72), channel_id=1, source_target_pairs={{0,2},{1,3},{2,0},{3,1},{4,6},{5,7},{6,4},{7,5},{8,10},{9,11},{10,... | collective-permute-start | bytes 1179656 | tf_op jit(solution)/shard_map/ppermute | solution.py:535
  17.8 13.0 %collective-permute-start.6 = (bf16[256,384]{1,0:T(8,128)(2,1)S(1)}, bf16[256,384]{1,0:T(8,128)(2,1)S(1)}, u32[]{:S(2)}, u32[]{:S(2)}) collective-permute-start(bf16[256,384]{1,0:T(8,128)(2,1)S(1)} %pad_maximum_fusion.rest_0_), channel_id=1, source_target_pairs={{0,24},{1,25},{2,26},{3,27},{4,28},{5,29},{6,30},{7,31},{8,16},{9,... | collective-permute-start | bytes 589832 | tf_op jit(solution)/shard_map/ppermute | solution.py:535
  20.3 10.5 %collective-permute-start.5 = (bf16[256,384]{1,0:T(8,128)(2,1)S(1)}, bf16[256,384]{1,0:T(8,128)(2,1)S(1)}, u32[]{:S(2)}, u32[]{:S(2)}) collective-permute-start(bf16[256,384]{1,0:T(8,128)(2,1)S(1)} %pad_maximum_fusion.rest_0_), channel_id=1, source_target_pairs={{0,16},{1,17},{2,18},{3,19},{4,20},{5,21},{6,22},{7,23},{8,24},{9,... | collective-permute-start | bytes 589832 | tf_op jit(solution)/shard_map/ppermute | solution.py:535
  20.8 10.0 %collective-permute-start.4 = (bf16[256,384]{1,0:T(8,128)(2,1)S(1)}, bf16[256,384]{1,0:T(8,128)(2,1)S(1)}, u32[]{:S(2)}, u32[]{:S(2)}) collective-permute-start(bf16[256,384]{1,0:T(8,128)(2,1)S(1)} %pad_maximum_fusion.rest_0_), channel_id=1, source_target_pairs={{0,8},{1,9},{2,10},{3,11},{4,12},{5,13},{6,14},{7,15},{8,0},{9,1},... | collective-permute-start | bytes 589832 | tf_op jit(solution)/shard_map/ppermute | solution.py:535
  30.8 2.9 %collective-permute-start.12 = (bf16[2,2,64,768]{3,2,1,0:T(8,128)(2,1)S(1)}, bf16[2,2,64,768]{3,2,1,0:T(8,128)(2,1)S(1)}, u32[]{:S(2)}, u32[]{:S(2)}) collective-permute-start(bf16[2,2,64,768]{3,2,1,0:T(8,128)(2,1)S(1)} %collective-permute-done.7.refs_4_), channel_id=1, source_target_pairs={{0,1},{1,0},{2,3},{3,2},{4,5},{5,4},{6,7},{7,6},{8,9},{9,8},{10,11... | collective-permute-start | bytes 1179656 | tf_op jit(solution)/shard_map/ppermute | solution.py:535
  32.4 3.3 %collective-permute-start.8 = (bf16[256,384]{1,0:T(8,128)(2,1)S(1)}, bf16[256,384]{1,0:T(8,128)(2,1)S(1)}, u32[]{:S(2)}, u32[]{:S(2)}) collective-permute-start(bf16[256,384]{1,0:T(8,128)(2,1)S(1)} %pad_maximum_fusion.rest_0_), channel_id=1, source_target_pairs={{0,1},{1,0},{2,3},{3,2},{4,5},{5,4},{6,7},{7,6},{8,9},{9,8},{10,11... | collective-permute-start | bytes 589832 | tf_op jit(solution)/shard_map/ppermute | solution.py:535
  32.5 3.2 %collective-permute-start.9 = (bf16[256,384]{1,0:T(8,128)(2,1)S(1)}, bf16[256,384]{1,0:T(8,128)(2,1)S(1)}, u32[]{:S(2)}, u32[]{:S(2)}) collective-permute-start(bf16[256,384]{1,0:T(8,128)(2,1)S(1)} %collective-permute-done.4.rest_1_), channel_id=1, source_target_pairs={{0,1},{1,0},{2,3},{3,2},{4,5},{5,4},{6,7},{7,6},{8,9},{9,8},{10,11... | collective-permute-start | bytes 589832 | tf_op jit(solution)/shard_map/ppermute | solution.py:535
  32.9 2.8 %collective-permute-start.10 = (bf16[256,384]{1,0:T(8,128)(2,1)S(1)}, bf16[256,384]{1,0:T(8,128)(2,1)S(1)}, u32[]{:S(2)}, u32[]{:S(2)}) collective-permute-start(bf16[256,384]{1,0:T(8,128)(2,1)S(1)} %collective-permute-done.5.rest_2_), channel_id=1, source_target_pairs={{0,1},{1,0},{2,3},{3,2},{4,5},{5,4},{6,7},{7,6},{8,9},{9,8},{10,11... | collective-permute-start | bytes 589832 | tf_op jit(solution)/shard_map/ppermute | solution.py:535
  33.0 2.8 %collective-permute-start.11 = (bf16[256,384]{1,0:T(8,128)(2,1)S(1)}, bf16[256,384]{1,0:T(8,128)(2,1)S(1)}, u32[]{:S(2)}, u32[]{:S(2)}) collective-permute-start(bf16[256,384]{1,0:T(8,128)(2,1)S(1)} %collective-permute-done.6.rest_3_), channel_id=1, source_target_pairs={{0,1},{1,0},{2,3},{3,2},{4,5},{5,4},{6,7},{7,6},{8,9},{9,8},{10,11... | collective-permute-start | bytes 589832 | tf_op jit(solution)/shard_map/ppermute | solution.py:535
  39.1 7.5 %collective-permute-start.13 = (bf16[64,256]{1,0:T(8,128)(2,1)S(1)}, bf16[64,256]{1,0:T(8,128)(2,1)S(1)}, u32[]{:S(2)}, u32[]{:S(2)}) collective-permute-start(bf16[64,256]{1,0:T(8,128)(2,1)S(1)} %get-tuple-element.104), channel_id=1, source_target_pairs={{0,2},{1,3},{2,0},{3,1},{4,6},{5,7},{6,4},{7,5},{8,10},{9,11},{10,... | collective-permute-start | bytes 98312 | tf_op jit(solution)/shard_map/ppermute | solution.py:535
  40.9 5.7 %collective-permute-start.14 = (bf16[64,256]{1,0:T(8,128)(2,1)S(1)}, bf16[64,256]{1,0:T(8,128)(2,1)S(1)}, u32[]{:S(2)}, u32[]{:S(2)}) collective-permute-start(bf16[64,256]{1,0:T(8,128)(2,1)S(1)} %get-tuple-element.105), channel_id=1, source_target_pairs={{0,4},{1,5},{2,6},{3,7},{4,0},{5,1},{6,2},{7,3},{8,12},{9,13},{10,... | collective-permute-start | bytes 98312 | tf_op jit(solution)/shard_map/ppermute | solution.py:535
  40.9 5.7 %collective-permute-start.15 = (bf16[64,256]{1,0:T(8,128)(2,1)S(1)}, bf16[64,256]{1,0:T(8,128)(2,1)S(1)}, u32[]{:S(2)}, u32[]{:S(2)}) collective-permute-start(bf16[64,256]{1,0:T(8,128)(2,1)S(1)} %get-tuple-element.106), channel_id=1, source_target_pairs={{0,6},{1,7},{2,4},{3,5},{4,2},{5,3},{6,0},{7,1},{8,14},{9,15},{10,... | collective-permute-start | bytes 98312 | tf_op jit(solution)/shard_map/ppermute | solution.py:535

commit v7 on v6

--- a/solution.py
+++ b/solution.py
@@ -27,7 +27,7 @@
 CLASS_U = {"A": ODD, "B": [2, 6, 10, 14], "C": [4, 12], "D": [8, 0]}
 PAIR_OF = [0, 2, 3, 5]
 LONE_OF = [2, 3, 8, 9]
-NEAR_PARTS = [(0, 1), (1, 5)]
+NEAR_PARTS = [(0, 3), (3, 2), (5, 1)]
 WIDE_PARTS = [(0, 2), (2, 4)]
 
 
@@ -543,6 +543,10 @@
     return lambda x, z, c: (x, z ^ steps, c)
 
 
+def relay(x, z, c):
+    return (x ^ (3 if c else 1), z, c)
+
+
 def other_core(x, z, c):
     return (x, z, 1 - c)
 
@@ -562,13 +566,19 @@
     slabs, close[0], sel8, later = lax.optimization_barrier((slabs, close[0], sel8, meta))
     own = jnp.concatenate([slab[:, 256:640] for slab in slabs], axis=0)
     own, later = lax.optimization_barrier((own, later))
-    moved = [move(own, along_x(step)) for step in (1, 2, 3)]
+    first, third = move(own, along_x(1)), move(own, along_x(3))
     near = move(sel8, next_chip)
     close.append(local_near(*NEAR_PARTS[1], later, *local))
-    moved, near, close[1], later = lax.optimization_barrier((moved, near, close[1], later))
+    first, third, near, close[1], later = lax.optimization_barrier(
+        (first, third, near, close[1], later)
+    )
+    relayed = move(jnp.where(device % 2 == 0, third, first), relay)
+    others = [move(block, other_core) for block in (own, first, third)]
     cross = move(near, other_core)
-    blocks = [own] + moved
-    blocks += [move(block, other_core) for block in blocks]
+    close.append(local_near(*NEAR_PARTS[2], later, *local))
+    relayed, close[2], later = lax.optimization_barrier((relayed, close[2], later))
+    others.insert(2, move(relayed, other_core))
+    blocks = [own, first, relayed, third] + others
     wide = [local_far(*WIDE_PARTS[0], later, *local, near, cross)]
     blocks, wide[0], later = lax.optimization_barrier((blocks, wide[0], later))
     back = slide_wide(meta, [slab[:, 0:256] for slab in slabs], blocks)

time: 49.5 us -> 58.6 us (1.18); the launches traced: 49.3 us -> 57.8 us
  local copies, waits for them, and re-layouts: 0.04 us -> 6.54 us
  waiting for transfers between devices: 3.98 us -> 1.19 us
  Pallas kernels: 27.3 us -> 29.2 us
  other arithmetic: 0.1 us -> 1.72 us
  starting transfers between devices: 16.9 us -> 18 us
    unnamed x0 -> x24, local copies, waits for them, and re-layouts: none -> 3.47 us
    slice x4, local copies, waits for them, and re-layouts: 0.01 us -> 3.04 us  [per_device(): back = slide_wide(meta, [slab[:, 0:256] for slab in slabs], blocks)]
    ppermute x16, waiting for transfers between devices: 3.98 us -> 1.19 us  [move(): return lax.ppermute(block, 'seq', route)]
    ppermute x16, starting transfers between devices: 16.9 us -> 18 us  [move(): return lax.ppermute(block, 'seq', route)]
    select_n x0 -> x1, other arithmetic: none -> 0.95 us  [per_device(): relayed = move(jnp.where(device % 2 == 0, third, first), relay)]
    pallas_call x1, Pallas kernels: 3.35 us -> 4.05 us  [slide_wide(): pl.pallas_call(far_kernel, in_specs=[smem()] + [vmem()] * 12, out_specs=[...]
    concatenate x1, other arithmetic: 0.02 us -> 0.69 us  [per_device(): own = jnp.concatenate([slab[:, 256:640] for slab in slabs], axis=0)]
    pallas_call x1, Pallas kernels: 4.07 us -> 4.7 us  [split(): pl.pallas_call(split_kernel, in_specs=[smem()] + [pl.BlockSpec(memory_spa...]
  transfers between devices with their start and end apart: 16 -> 16, of which waited for: 3 -> 3; matrix products, arithmetic and copies ran while one was open for 0% -> 8% of each run, Pallas kernels for 35% -> 31%
where the time goes in v7:
time: 58.6 us; the launch traced here: 57.8 us
  Pallas kernels  29.2 us (50%)
  starting transfers between devices  18 us (31%)
  local copies, waits for them, and re-layouts  6.54 us (11%)
  other arithmetic  1.72 us (3%)
  waiting for transfers between devices  1.19 us (2%)
  between operations  1.14 us (2%)
    ppermute x16, starting transfers between devices, move(): return lax.ppermute(block, 'seq', route)  18 us
    pallas_call x3, Pallas kernels, local_near(): pl.pallas_call(functools.partial(local_kernel, 'ABC', first, many), in_sp...  12.8 us
    pallas_call x2, Pallas kernels, local_far(): pl.pallas_call(functools.partial(local_kernel, 'D', first, many), in_spec...  5.15 us
    pallas_call x1, Pallas kernels, split(): pl.pallas_call(split_kernel, in_specs=[smem()] + [pl.BlockSpec(memory_spa...  4.7 us
    pallas_call x1, Pallas kernels, slide_wide(): pl.pallas_call(far_kernel, in_specs=[smem()] + [vmem()] * 12, out_specs=[...  4.05 us
    unnamed x24, local copies, waits for them, and re-layouts  3.47 us
    slice x4, local copies, waits for them, and re-layouts, per_device(): back = slide_wide(meta, [slab[:, 0:256] for slab in slabs], blocks)  3.04 us
    pallas_call x1, Pallas kernels, merge(): pl.pallas_call(merge_kernel, in_specs=[smem()] + [vmem()] * (len(NEAR_PAR...  2.5 us
  transfers between devices with their start and end apart: 16, of which 3 were waited for; matrix products, arithmetic and copies ran while one was open for 8% of the time, Pallas kernels for 31%

profile of v7, /device:TPU:1, one launch (start us, length us, event | category | flops | bytes accessed | tf_op | source)
XLA Modules:
  0.0 57.8 jit_solution(16700300303900306368)
XLA Ops:
  0.7 0.1 pad_add_fusion.meta
  0.7 4.7 %split_rows.1 = (bf16[16,64,768]{2,1,0:T(8,128)(2,1)S(1)}, bf16[16,64,768]{2,1,0:T(8,128)(2,1)S(1)}, bf16[16,64,768]{2,1,0:T(8,128)(2,1)S(1)}, bf16[4,2,64,768]{...) custom-call(s32[2]{0:T(128)S(1)} %pad_add_fusion.meta, ...), custom_call_target="tpu_custom_call" | custom-call | tf_op jit(solution)/shard_map/split_rows/pallas_call | solution.py:449
  5.5 1.5 %collective-permute-start.3 = (bf16[4,2,64,768]{3,2,1,0:T(8,128)(2,1)S(1)}, bf16[4,2,64,768]{3,2,1,0:T(8,128)(2,1)S(1)}, u32[]{:S(2)}, u32[]{:S(2)}) collective-permute-start(bf16[4,2,64,768]{3,2,1,0:T(8,128)(2,1)S(1)} %get-tuple-element.65), channel_id=1, source_target_pairs={{0,1},{1,0},{2,3},{3,2},{4,5},{5,4},{6,7},{7,6},{8,9},{9,8},{10,11... | collective-permute-start | bytes 2359304 | tf_op jit(solution)/shard_map/ppermute | solution.py:535
  7.0 1.7 %collective-permute-start = (bf16[64,640]{1,0:T(8,128)(2,1)S(1)}, bf16[64,640]{1,0:T(8,128)(2,1)S(1)}, u32[]{:S(2)}, u32[]{:S(2)}) collective-permute-start(bf16[64,640]{1,0:T(8,128)(2,1)S(1)} %get-tuple-element.59), channel_id=1, source_target_pairs={{0,2},{1,3},{2,0},{3,1},{4,6},{5,7},{6,4},{7,5},{8,10},{9,11},{10,... | collective-permute-start | bytes 245768 | tf_op jit(solution)/shard_map/ppermute | solution.py:535
  8.7 3.3 %collective-permute-start.1 = (bf16[64,640]{1,0:T(8,128)(2,1)S(1)}, bf16[64,640]{1,0:T(8,128)(2,1)S(1)}, u32[]{:S(2)}, u32[]{:S(2)}) collective-permute-start(bf16[64,640]{1,0:T(8,128)(2,1)S(1)} %get-tuple-element.60), channel_id=1, source_target_pairs={{0,4},{1,5},{2,6},{3,7},{4,0},{5,1},{6,2},{7,3},{8,12},{9,13},{10,... | collective-permute-start | bytes 245768 | tf_op jit(solution)/shard_map/ppermute | solution.py:535
  12.0 6.0 %near_queries.3.refs_0_ = bf16[16,64,384]{2,1,0:T(8,128)(2,1)S(1)} custom-call(s32[2]{0:T(128)S(1)} %pad_add_fusion.meta, bf16[16,64,768]{2,1,0:T(8,128)(2,1)S(1)} %get-tuple-element.62.refs_0_, bf16[16,64,768]{2,1,0:T(8,128)(2,1)S(1)} %get-tuple-element.63.refs_1_, bf16[16,64,768]{2,1,0:T(8,128)(2,1)S(1)} %get-tuple-element.64.refs_2_, ...), custom_call_target="tpu_custom_call" | custom-call | flops 1800000000 | bytes 1000000 | tf_op jit(solution)/shard_map/near_queries/pallas_call | solution.py:467
  18.1 0.9 %copy-done.6 = bf16[16,64,384]{2,1,0:T(8,128)(2,1)} copy-done((bf16[16,64,384]{2,1,0:T(8,128)(2,1)}, bf16[16,64,384]{2,1,0:T(8,128)(2,1)S(1)}, u32[]{:S(2)}) %copy-start.6) | copy-done | bytes 786456
  19.0 0.1 collective-permute-start.6
  19.2 0.7 %pad_maximum_fusion.rest_0_ = bf16[256,384]{1,0:T(8,128)(2,1)} fusion(bf16[64,384]{1,0:T(8,128)(2,1)S(1)} %slice.27, bf16[64,384]{1,0:T(8,128)(2,1)S(1)} %slice.26, bf16[64,384]{1,0:T(8,128)(2,1)S(1)} %slice.25, bf16[64,384]{1,0:T(8,128)(2,1)S(1)} %slice.24), kind=kLoop, calls=%fused_computation | loop fusion | flops 786432 | bytes 393216 | tf_op jit(solution)/shard_map/concatenate | solution.py:567
  19.9 2.5 %collective-permute-start.5 = (bf16[256,384]{1,0:T(8,128)(2,1)}, bf16[256,384]{1,0:T(8,128)(2,1)}, u32[]{:S(2)}, u32[]{:S(2)}) collective-permute-start(bf16[256,384]{1,0:T(8,128)(2,1)} %pad_maximum_fusion.rest_0_), channel_id=1, source_target_pairs={{0,24},{1,25},{2,26},{3,27},{4,28},{5,29},{6,30},{7,31},{8,16},{9,... | collective-permute-start | bytes 589832 | tf_op jit(solution)/shard_map/ppermute | solution.py:535
  22.4 1.4 %copy-done.1 = bf16[16,64,768]{2,1,0:T(8,128)(2,1)S(1)} copy-done((bf16[16,64,768]{2,1,0:T(8,128)(2,1)S(1)}, bf16[16,64,768]{2,1,0:T(8,128)(2,1)}, u32[]{:S(2)}) %copy-start.1) | copy-done | bytes 1572888
  23.8 1.1 %copy-done.4 = bf16[4,2,64,768]{3,2,1,0:T(8,128)(2,1)S(1)} copy-done((bf16[4,2,64,768]{3,2,1,0:T(8,128)(2,1)S(1)}, bf16[4,2,64,768]{3,2,1,0:T(8,128)(2,1)}, u32[]{:S(2)}) %copy-start.4) | copy-done | bytes 786456
  24.9 4.2 %near_queries.4.refs_1_ = bf16[16,64,256]{2,1,0:T(8,128)(2,1)S(1)} custom-call(s32[2]{0:T(128)S(1)} %pad_add_fusion.meta, bf16[16,64,768]{2,1,0:T(8,128)(2,1)S(1)} %get-tuple-element.62.refs_0_, bf16[16,64,768]{2,1,0:T(8,128)(2,1)S(1)} %get-tuple-element.63.refs_1_, bf16[16,64,768]{2,1,0:T(8,128)(2,1)S(1)} %copy-done.1, bf16[4,2,64,768]{3,2,1,0:T(8,128)(2,1)S(1)} %copy-done.4), custom_call_target="tpu_custom_call" | custom-call | flops 1200000000 | bytes 1000000 | tf_op jit(solution)/shard_map/near_queries/pallas_call | solution.py:467
  29.2 0.2 collective-permute-done.6.refs_4_
  29.4 1.4 %collective-permute-start.12 = (bf16[2,2,64,768]{3,2,1,0:T(8,128)(2,1)S(1)}, bf16[2,2,64,768]{3,2,1,0:T(8,128)(2,1)S(1)}, u32[]{:S(2)}, u32[]{:S(2)}) collective-permute-start(bf16[2,2,64,768]{3,2,1,0:T(8,128)(2,1)S(1)} %collective-permute-done.6.refs_4_), channel_id=1, source_target_pairs={{0,1},{1,0},{2,3},{3,2},{4,5},{5,4},{6,7},{7,6},{8,9},{9,8},{10,11... | collective-permute-start | bytes 1179656 | tf_op jit(solution)/shard_map/ppermute | solution.py:535
  30.8 1.0 %broadcast_select_fusion = bf16[256,384]{1,0:T(8,128)(2,1)S(1)} fusion(bf16[256,384]{1,0:T(8,128)(2,1)} %collective-permute-done.5.rest_3_, bf16[256,384]{1,0:T(8,128)(2,1)} %collective-permute-done.4.rest_1_, pred[]{:T(512)S(6)} %eq.5), kind=kLoop, calls=%fused_computation.1 | loop fusion | flops 98304 | bytes 589825 | tf_op jit(solution)/shard_map/jit(_where)/select_n | solution.py:575
  31.8 2.6 %collective-permute-start.7 = (bf16[256,384]{1,0:T(8,128)(2,1)S(1)}, bf16[256,384]{1,0:T(8,128)(2,1)S(1)}, u32[]{:S(2)}, u32[]{:S(2)}) collective-permute-start(bf16[256,384]{1,0:T(8,128)(2,1)S(1)} %broadcast_select_fusion), channel_id=1, source_target_pairs={{0,8},{1,25},{2,10},{3,27},{4,12},{5,29},{6,14},{7,31},{8,0},{9,17... | collective-permute-start | bytes 589832 | tf_op jit(solution)/shard_map/ppermute | solution.py:535
  34.3 0.5 collective-permute-start.11
  34.8 2.6 %near_queries.5.refs_2_ = bf16[16,64,128]{2,1,0:T(8,128)(2,1)S(1)} custom-call(s32[2]{0:T(128)S(1)} %pad_add_fusion.meta, bf16[16,64,768]{2,1,0:T(8,128)(2,1)S(1)} %get-tuple-element.62.refs_0_, bf16[16,64,768]{2,1,0:T(8,128)(2,1)S(1)} %get-tuple-element.63.refs_1_, bf16[16,64,768]{2,1,0:T(8,128)(2,1)S(1)} %copy-done.1, bf16[4,2,64,768]{3,2,1,0:T(8,128)(2,1)S(1)} %copy-done.4), custom_call_target="tpu_custom_call" | custom-call | flops 600000000 | bytes 1000000 | tf_op jit(solution)/shard_map/near_queries/pallas_call | solution.py:467
  37.4 0.2 collective-permute-done.7.rest_2_
  37.6 0.4 collective-permute-start.10
  38.0 0.8 %slice.28.a0 = bf16[64,256]{1,0:T(8,128)(2,1)S(1)} slice(bf16[64,640]{1,0:T(8,128)(2,1)} %copy-done.8), slice={[0:64], [0:256]} | slice | bytes 65536 | tf_op jit(solution)/shard_map/slice | solution.py:584
  38.8 0.8 %slice.29.a1 = bf16[64,256]{1,0:T(8,128)(2,1)S(1)} slice(bf16[64,640]{1,0:T(8,128)(2,1)} %copy-done.9), slice={[0:64], [0:256]} | slice | bytes 65536 | tf_op jit(solution)/shard_map/slice | solution.py:584
  39.5 0.8 %slice.30.a2 = bf16[64,256]{1,0:T(8,128)(2,1)S(1)} slice(bf16[64,640]{1,0:T(8,128)(2,1)} %copy-done.10), slice={[0:64], [0:256]} | slice | bytes 65536 | tf_op jit(solution)/shard_map/slice | solution.py:584
  40.3 0.8 %slice.31.a3 = bf16[64,256]{1,0:T(8,128)(2,1)S(1)} slice(bf16[64,640]{1,0:T(8,128)(2,1)} %copy-done.11), slice={[0:64], [0:256]} | slice | bytes 65536 | tf_op jit(solution)/shard_map/slice | solution.py:584
  41.1 2.0 %wide_queries.2 = (bf16[16,64,256]{2,1,0:T(8,128)(2,1)S(1)}, f32[64,256]{1,0:T(8,128)S(1)}, f32[64,256]{1,0:T(8,128)S(1)}) custom-call(s32[2]{0:T(128)S(1)} %pad_add_fusion.meta, bf16[16,64,768]{2,1,0:T(8,128)(2,1)S(1)} %get-tuple-element.62.refs_0_, bf16[16,64,768]{2,1,0:T(8,128)(2,1)S(1)} %get-tuple-element.63.refs_1_, bf16[16,64,768]{2,1,0:T(8,128)(2,1)S(1)} %copy-done.1, ...), custom_call_target="tpu_custom_call" | custom-call | flops 400000000 | bytes 1000000 | tf_op jit(solution)/shard_map/wide_queries/pallas_call | solution.py:481
  43.1 4.0 %slide_queries.1 = (bf16[64,256]{1,0:T(8,128)(2,1)S(1)}, bf16[64,256]{1,0:T(8,128)(2,1)S(1)}, bf16[64,256]{1,0:T(8,128)(2,1)S(1)}, bf16[64,256]{1,0:T(8,128)(2,1)S(1)}) custom-call(s32[2]{0:T(128)S(1)} %pad_add_fusion.meta, bf16[64,256]{1,0:T(8,128)(2,1)S(1)} %slice.28.a0, bf16[64,256]{1,0:T(8,128)(2,1)S(1)} %slice.29.a1, bf16[64,256]{1,0:T(8,128)(2,1)S(1)} %slice.30.a2, ...), custom_call_target="tpu_custom_call" | custom-call | flops 800000000 | bytes 2000000 | tf_op jit(solution)/shard_map/slide_queries/pallas_call | solution.py:499
  47.2 0.9 %collective-permute-start.13 = (bf16[64,256]{1,0:T(8,128)(2,1)S(1)}, bf16[64,256]{1,0:T(8,128)(2,1)S(1)}, u32[]{:S(2)}, u32[]{:S(2)}) collective-permute-start(bf16[64,256]{1,0:T(8,128)(2,1)S(1)} %get-tuple-element.108), channel_id=1, source_target_pairs={{0,2},{1,3},{2,0},{3,1},{4,6},{5,7},{6,4},{7,5},{8,10},{9,11},{10,... | collective-permute-start | bytes 98312 | tf_op jit(solution)/shard_map/ppermute | solution.py:535
  48.1 3.0 %collective-permute-start.14 = (bf16[64,256]{1,0:T(8,128)(2,1)S(1)}, bf16[64,256]{1,0:T(8,128)(2,1)S(1)}, u32[]{:S(2)}, u32[]{:S(2)}) collective-permute-start(bf16[64,256]{1,0:T(8,128)(2,1)S(1)} %get-tuple-element.109), channel_id=1, source_target_pairs={{0,4},{1,5},{2,6},{3,7},{4,0},{5,1},{6,2},{7,3},{8,12},{9,13},{10,... | collective-permute-start | bytes 98312 | tf_op jit(solution)/shard_map/ppermute | solution.py:535
  51.1 3.2 %wide_queries.3 = (bf16[16,64,512]{2,1,0:T(8,128)(2,1)S(1)}, f32[64,512]{1,0:T(8,128)S(1)}, f32[64,512]{1,0:T(8,128)S(1)}) custom-call(s32[2]{0:T(128)S(1)} %pad_add_fusion.meta, bf16[16,64,768]{2,1,0:T(8,128)(2,1)S(1)} %get-tuple-element.62.refs_0_, bf16[16,64,768]{2,1,0:T(8,128)(2,1)S(1)} %get-tuple-element.63.refs_1_, bf16[16,64,768]{2,1,0:T(8,128)(2,1)S(1)} %copy-done.2, ...), custom_call_target="tpu_custom_call" | custom-call | flops 800000000 | bytes 1000000 | tf_op jit(solution)/shard_map/wide_queries/pallas_call | solution.py:481
  54.3 0.7 %collective-permute-done.15.refs_12_ = bf16[64,256]{1,0:T(8,128)(2,1)S(1)} collective-permute-done((bf16[64,256]{1,0:T(8,128)(2,1)S(1)}, bf16[64,256]{1,0:T(8,128)(2,1)S(1)}, u32[]{:S(2)}, u32[]{:S(2)}) %collective-permute-start.15) | collective-permute-done | bytes 32800 | tf_op jit(solution)/shard_map/ppermute | solution.py:535
  55.1 2.5 %merge_rows.1 = bf16[1024,768]{1,0:T(8,128)(2,1)} custom-call(s32[2]{0:T(128)S(1)} %pad_add_fusion.meta, bf16[16,64,384]{2,1,0:T(8,128)(2,1)S(1)} %copy-done.7, bf16[16,64,256]{2,1,0:T(8,128)(2,1)S(1)} %near_queries.4.refs_1_, bf16[16,64,128]{2,1,0:T(8,128)(2,1)S(1)} %near_queries.5.refs_2_, bf16[16,64,256]{2,1,0:T(8,128)(2,1)S(1)} %get-tuple-element.87.refs_3_, ...), custom_call_target="tpu_custom_call" | custom-call | tf_op jit(solution)/shard_map/merge_rows/pallas_call | solution.py:511
  (43 shorter events, 0.1 us)
Async XLA Ops:
  5.4 12.6 %copy-start = (bf16[16,64,768]{2,1,0:T(8,128)(2,1)}, bf16[16,64,768]{2,1,0:T(8,128)(2,1)S(1)}, u32[]{:S(2)}) copy-start(bf16[16,64,768]{2,1,0:T(8,128)(2,1)S(1)} %get-tuple-element.64.refs_2_) | copy-start | bytes 4718596
  5.4 13.6 %copy-start.8 = (bf16[64,640]{1,0:T(8,128)(2,1)}, bf16[64,640]{1,0:T(8,128)(2,1)S(1)}, u32[]{:S(2)}) copy-start(bf16[64,640]{1,0:T(8,128)(2,1)S(1)} %get-tuple-element.68) | copy-start | bytes 245764
  5.5 6.5 %collective-permute-start.3 = (bf16[4,2,64,768]{3,2,1,0:T(8,128)(2,1)S(1)}, bf16[4,2,64,768]{3,2,1,0:T(8,128)(2,1)S(1)}, u32[]{:S(2)}, u32[]{:S(2)}) collective-permute-start(bf16[4,2,64,768]{3,2,1,0:T(8,128)(2,1)S(1)} %get-tuple-element.65), channel_id=1, source_target_pairs={{0,1},{1,0},{2,3},{3,2},{4,5},{5,4},{6,7},{7,6},{8,9},{9,8},{10,11... | collective-permute-start | bytes 2359304 | tf_op jit(solution)/shard_map/ppermute | solution.py:535
  7.0 12.0 %collective-permute-start = (bf16[64,640]{1,0:T(8,128)(2,1)S(1)}, bf16[64,640]{1,0:T(8,128)(2,1)S(1)}, u32[]{:S(2)}, u32[]{:S(2)}) collective-permute-start(bf16[64,640]{1,0:T(8,128)(2,1)S(1)} %get-tuple-element.59), channel_id=1, source_target_pairs={{0,2},{1,3},{2,0},{3,1},{4,6},{5,7},{6,4},{7,5},{8,10},{9,11},{10,... | collective-permute-start | bytes 245768 | tf_op jit(solution)/shard_map/ppermute | solution.py:535
  8.7 10.3 %collective-permute-start.1 = (bf16[64,640]{1,0:T(8,128)(2,1)S(1)}, bf16[64,640]{1,0:T(8,128)(2,1)S(1)}, u32[]{:S(2)}, u32[]{:S(2)}) collective-permute-start(bf16[64,640]{1,0:T(8,128)(2,1)S(1)} %get-tuple-element.60), channel_id=1, source_target_pairs={{0,4},{1,5},{2,6},{3,7},{4,0},{5,1},{6,2},{7,3},{8,12},{9,13},{10,... | collective-permute-start | bytes 245768 | tf_op jit(solution)/shard_map/ppermute | solution.py:535
  12.0 7.0 %collective-permute-start.2 = (bf16[64,640]{1,0:T(8,128)(2,1)S(1)}, bf16[64,640]{1,0:T(8,128)(2,1)S(1)}, u32[]{:S(2)}, u32[]{:S(2)}) collective-permute-start(bf16[64,640]{1,0:T(8,128)(2,1)S(1)} %get-tuple-element.61), channel_id=1, source_target_pairs={{0,6},{1,7},{2,4},{3,5},{4,2},{5,3},{6,0},{7,1},{8,14},{9,15},{10,... | collective-permute-start | bytes 245768 | tf_op jit(solution)/shard_map/ppermute | solution.py:535
  12.0 6.0 %copy-start.3 = (bf16[4,2,64,768]{3,2,1,0:T(8,128)(2,1)}, bf16[4,2,64,768]{3,2,1,0:T(8,128)(2,1)S(1)}, u32[]{:S(2)}) copy-start(bf16[4,2,64,768]{3,2,1,0:T(8,128)(2,1)S(1)} %collective-permute-done.3.refs_3_) | copy-start | bytes 2359300
  18.1 0.9 %copy-start.6 = (bf16[16,64,384]{2,1,0:T(8,128)(2,1)}, bf16[16,64,384]{2,1,0:T(8,128)(2,1)S(1)}, u32[]{:S(2)}) copy-start(bf16[16,64,384]{2,1,0:T(8,128)(2,1)S(1)} %near_queries.3.refs_0_) | copy-start | bytes 2359300
  19.0 0.9 %copy-start.9 = (bf16[64,640]{1,0:T(8,128)(2,1)}, bf16[64,640]{1,0:T(8,128)(2,1)S(1)}, u32[]{:S(2)}) copy-start(bf16[64,640]{1,0:T(8,128)(2,1)S(1)} %collective-permute-done) | copy-start | bytes 245764
  19.0 3.4 %copy-start.10 = (bf16[64,640]{1,0:T(8,128)(2,1)}, bf16[64,640]{1,0:T(8,128)(2,1)S(1)}, u32[]{:S(2)}) copy-start(bf16[64,640]{1,0:T(8,128)(2,1)S(1)} %collective-permute-done.1) | copy-start | bytes 245764
  19.0 3.4 %copy-start.11 = (bf16[64,640]{1,0:T(8,128)(2,1)}, bf16[64,640]{1,0:T(8,128)(2,1)S(1)}, u32[]{:S(2)}) copy-start(bf16[64,640]{1,0:T(8,128)(2,1)S(1)} %collective-permute-done.2) | copy-start | bytes 245764
  19.0 10.4 %collective-permute-start.6 = (bf16[2,2,64,768]{3,2,1,0:T(8,128)(2,1)}, bf16[2,2,64,768]{3,2,1,0:T(8,128)(2,1)S(1)}, u32[]{:S(2)}, u32[]{:S(2)}) collective-permute-start(bf16[2,2,64,768]{3,2,1,0:T(8,128)(2,1)} %get-tuple-element.74), channel_id=1, source_target_pairs={{0,2},{1,3},{2,0},{3,1},{4,6},{5,7},{6,4},{7,5},{8,10},{9,11},{10,... | collective-permute-start | bytes 1179656 | tf_op jit(solution)/shard_map/ppermute | solution.py:535
  19.9 9.3 %collective-permute-start.5 = (bf16[256,384]{1,0:T(8,128)(2,1)}, bf16[256,384]{1,0:T(8,128)(2,1)}, u32[]{:S(2)}, u32[]{:S(2)}) collective-permute-start(bf16[256,384]{1,0:T(8,128)(2,1)} %pad_maximum_fusion.rest_0_), channel_id=1, source_target_pairs={{0,24},{1,25},{2,26},{3,27},{4,28},{5,29},{6,30},{7,31},{8,16},{9,... | collective-permute-start | bytes 589832 | tf_op jit(solution)/shard_map/ppermute | solution.py:535
  22.3 6.8 %collective-permute-start.4 = (bf16[256,384]{1,0:T(8,128)(2,1)}, bf16[256,384]{1,0:T(8,128)(2,1)}, u32[]{:S(2)}, u32[]{:S(2)}) collective-permute-start(bf16[256,384]{1,0:T(8,128)(2,1)} %pad_maximum_fusion.rest_0_), channel_id=1, source_target_pairs={{0,8},{1,9},{2,10},{3,11},{4,12},{5,13},{6,14},{7,15},{8,0},{9,1},... | collective-permute-start | bytes 589832 | tf_op jit(solution)/shard_map/ppermute | solution.py:535
  22.4 1.4 %copy-start.1 = (bf16[16,64,768]{2,1,0:T(8,128)(2,1)S(1)}, bf16[16,64,768]{2,1,0:T(8,128)(2,1)}, u32[]{:S(2)}) copy-start(bf16[16,64,768]{2,1,0:T(8,128)(2,1)} %copy-done) | copy-start | bytes 4718596
  23.8 1.1 %copy-start.4 = (bf16[4,2,64,768]{3,2,1,0:T(8,128)(2,1)S(1)}, bf16[4,2,64,768]{3,2,1,0:T(8,128)(2,1)}, u32[]{:S(2)}) copy-start(bf16[4,2,64,768]{3,2,1,0:T(8,128)(2,1)} %copy-done.3) | copy-start | bytes 2359300
  29.4 11.7 %collective-permute-start.12 = (bf16[2,2,64,768]{3,2,1,0:T(8,128)(2,1)S(1)}, bf16[2,2,64,768]{3,2,1,0:T(8,128)(2,1)S(1)}, u32[]{:S(2)}, u32[]{:S(2)}) collective-permute-start(bf16[2,2,64,768]{3,2,1,0:T(8,128)(2,1)S(1)} %collective-permute-done.6.refs_4_), channel_id=1, source_target_pairs={{0,1},{1,0},{2,3},{3,2},{4,5},{5,4},{6,7},{7,6},{8,9},{9,8},{10,11... | collective-permute-start | bytes 1179656 | tf_op jit(solution)/shard_map/ppermute | solution.py:535
  31.8 5.8 %collective-permute-start.7 = (bf16[256,384]{1,0:T(8,128)(2,1)S(1)}, bf16[256,384]{1,0:T(8,128)(2,1)S(1)}, u32[]{:S(2)}, u32[]{:S(2)}) collective-permute-start(bf16[256,384]{1,0:T(8,128)(2,1)S(1)} %broadcast_select_fusion), channel_id=1, source_target_pairs={{0,8},{1,25},{2,10},{3,27},{4,12},{5,29},{6,14},{7,31},{8,0},{9,17... | collective-permute-start | bytes 589832 | tf_op jit(solution)/shard_map/ppermute | solution.py:535
  34.3 8.7 %collective-permute-start.8 = (bf16[256,384]{1,0:T(8,128)(2,1)}, bf16[256,384]{1,0:T(8,128)(2,1)S(1)}, u32[]{:S(2)}, u32[]{:S(2)}) collective-permute-start(bf16[256,384]{1,0:T(8,128)(2,1)} %pad_maximum_fusion.rest_0_), channel_id=1, source_target_pairs={{0,1},{1,0},{2,3},{3,2},{4,5},{5,4},{6,7},{7,6},{8,9},{9,8},{10,11... | collective-permute-start | bytes 589832 | tf_op jit(solution)/shard_map/ppermute | solution.py:535
  34.3 8.7 %collective-permute-start.11 = (bf16[256,384]{1,0:T(8,128)(2,1)}, bf16[256,384]{1,0:T(8,128)(2,1)S(1)}, u32[]{:S(2)}, u32[]{:S(2)}) collective-permute-start(bf16[256,384]{1,0:T(8,128)(2,1)} %collective-permute-done.5.rest_3_), channel_id=1, source_target_pairs={{0,1},{1,0},{2,3},{3,2},{4,5},{5,4},{6,7},{7,6},{8,9},{9,8},{10,11... | collective-permute-start | bytes 589832 | tf_op jit(solution)/shard_map/ppermute | solution.py:535
  34.8 8.2 %collective-permute-start.9 = (bf16[256,384]{1,0:T(8,128)(2,1)}, bf16[256,384]{1,0:T(8,128)(2,1)S(1)}, u32[]{:S(2)}, u32[]{:S(2)}) collective-permute-start(bf16[256,384]{1,0:T(8,128)(2,1)} %collective-permute-done.4.rest_1_), channel_id=1, source_target_pairs={{0,1},{1,0},{2,3},{3,2},{4,5},{5,4},{6,7},{7,6},{8,9},{9,8},{10,11... | collective-permute-start | bytes 589832 | tf_op jit(solution)/shard_map/ppermute | solution.py:535
  37.6 5.5 %collective-permute-start.10 = (bf16[256,384]{1,0:T(8,128)(2,1)S(1)}, bf16[256,384]{1,0:T(8,128)(2,1)S(1)}, u32[]{:S(2)}, u32[]{:S(2)}) collective-permute-start(bf16[256,384]{1,0:T(8,128)(2,1)S(1)} %collective-permute-done.7.rest_2_), channel_id=1, source_target_pairs={{0,1},{1,0},{2,3},{3,2},{4,5},{5,4},{6,7},{7,6},{8,9},{9,8},{10,11... | collective-permute-start | bytes 589832 | tf_op jit(solution)/shard_map/ppermute | solution.py:535
  43.0 8.1 %copy-start.2 = (bf16[16,64,768]{2,1,0:T(8,128)(2,1)S(1)}, bf16[16,64,768]{2,1,0:T(8,128)(2,1)}, u32[]{:S(2)}) copy-start(bf16[16,64,768]{2,1,0:T(8,128)(2,1)} %copy-done) | copy-start | bytes 4718596
  43.1 8.1 %copy-start.5 = (bf16[4,2,64,768]{3,2,1,0:T(8,128)(2,1)S(1)}, bf16[4,2,64,768]{3,2,1,0:T(8,128)(2,1)}, u32[]{:S(2)}) copy-start(bf16[4,2,64,768]{3,2,1,0:T(8,128)(2,1)} %copy-done.3) | copy-start | bytes 2359300
  47.2 7.9 %copy-start.7 = (bf16[16,64,384]{2,1,0:T(8,128)(2,1)S(1)}, bf16[16,64,384]{2,1,0:T(8,128)(2,1)}, u32[]{:S(2)}) copy-start(bf16[16,64,384]{2,1,0:T(8,128)(2,1)} %copy-done.6) | copy-start | bytes 2359300
  47.2 7.1 %collective-permute-start.13 = (bf16[64,256]{1,0:T(8,128)(2,1)S(1)}, bf16[64,256]{1,0:T(8,128)(2,1)S(1)}, u32[]{:S(2)}, u32[]{:S(2)}) collective-permute-start(bf16[64,256]{1,0:T(8,128)(2,1)S(1)} %get-tuple-element.108), channel_id=1, source_target_pairs={{0,2},{1,3},{2,0},{3,1},{4,6},{5,7},{6,4},{7,5},{8,10},{9,11},{10,... | collective-permute-start | bytes 98312 | tf_op jit(solution)/shard_map/ppermute | solution.py:535
  48.1 6.2 %collective-permute-start.14 = (bf16[64,256]{1,0:T(8,128)(2,1)S(1)}, bf16[64,256]{1,0:T(8,128)(2,1)S(1)}, u32[]{:S(2)}, u32[]{:S(2)}) collective-permute-start(bf16[64,256]{1,0:T(8,128)(2,1)S(1)} %get-tuple-element.109), channel_id=1, source_target_pairs={{0,4},{1,5},{2,6},{3,7},{4,0},{5,1},{6,2},{7,3},{8,12},{9,13},{10,... | collective-permute-start | bytes 98312 | tf_op jit(solution)/shard_map/ppermute | solution.py:535
  51.1 4.0 %collective-permute-start.15 = (bf16[64,256]{1,0:T(8,128)(2,1)S(1)}, bf16[64,256]{1,0:T(8,128)(2,1)S(1)}, u32[]{:S(2)}, u32[]{:S(2)}) collective-permute-start(bf16[64,256]{1,0:T(8,128)(2,1)S(1)} %get-tuple-element.110), channel_id=1, source_target_pairs={{0,6},{1,7},{2,4},{3,5},{4,2},{5,3},{6,0},{7,1},{8,14},{9,15},{10,... | collective-permute-start | bytes 98312 | tf_op jit(solution)/shard_map/ppermute | solution.py:535

commit v8 on v7

--- a/solution.py
+++ b/solution.py
@@ -458,7 +458,7 @@
             pltpu.VMEM((4, GROUPS, 640), BF),
             pltpu.SemaphoreType.DMA((3, 4)),
         ],
-        compiler_params=params(40),
+        compiler_params=params(28),
         name="split_rows",
     )(meta, *rows)
 
@@ -469,7 +469,7 @@
         in_specs=[smem()] + [vmem()] * 4,
         out_specs=vmem(),
         out_shape=shape((RES, GROUPS, many * 128)),
-        compiler_params=params(40),
+        compiler_params=params(28),
         cost_estimate=pl.CostEstimate(
             flops=many * 600000000, bytes_accessed=1000000, transcendentals=many * 1200000
         ),
@@ -487,7 +487,7 @@
             shape((GROUPS, many * 128), F32),
             shape((GROUPS, many * 128), F32),
         ],
-        compiler_params=params(40),
+        compiler_params=params(28),
         cost_estimate=pl.CostEstimate(
             flops=many * 200000000, bytes_accessed=1000000, transcendentals=many * 400000
         ),
@@ -501,7 +501,7 @@
         in_specs=[smem()] + [vmem()] * 12,
         out_specs=[vmem()] * 4,
         out_shape=[shape((GROUPS, 256))] * 4,
-        compiler_params=params(40),
+        compiler_params=params(28),
         cost_estimate=pl.CostEstimate(flops=800000000, bytes_accessed=2000000, transcendentals=1600000),
         name="slide_queries",
     )(meta, *queries, *blocks)
@@ -519,7 +519,7 @@
             pltpu.VMEM((4, 256, WIDTH), BF),
             pltpu.SemaphoreType.DMA((4,)),
         ],
-        compiler_params=params(40),
+        compiler_params=params(28),
         name="merge_rows",
     )(meta, *close, *[part for parts in zip(*wide) for part in parts], *back)
 
@@ -569,19 +569,17 @@
     first, third = move(own, along_x(1)), move(own, along_x(3))
     near = move(sel8, next_chip)
     close.append(local_near(*NEAR_PARTS[1], later, *local))
-    first, third, near, close[1], later = lax.optimization_barrier(
-        (first, third, near, close[1], later)
-    )
+    first, third, close[1], later = lax.optimization_barrier((first, third, close[1], later))
     relayed = move(jnp.where(device % 2 == 0, third, first), relay)
     others = [move(block, other_core) for block in (own, first, third)]
+    close.append(local_near(*NEAR_PARTS[2], later, *local))
+    relayed, near, close[2], later = lax.optimization_barrier((relayed, near, close[2], later))
     cross = move(near, other_core)
-    close.append(local_near(*NEAR_PARTS[2], later, *local))
-    relayed, close[2], later = lax.optimization_barrier((relayed, close[2], later))
     others.insert(2, move(relayed, other_core))
     blocks = [own, first, relayed, third] + others
     wide = [local_far(*WIDE_PARTS[0], later, *local, near, cross)]
     blocks, wide[0], later = lax.optimization_barrier((blocks, wide[0], later))
-    back = slide_wide(meta, [slab[:, 0:256] for slab in slabs], blocks)
+    back = slide_wide(meta, slabs, blocks)
     back, later = lax.optimization_barrier((back, later))
     back = [back[0]] + [move(back[step], along_z(step)) for step in (1, 2, 3)]
     wide.append(local_far(*WIDE_PARTS[1], later, *local, near, cross))

time: 58.6 us -> 55.2 us (0.942)
  starting transfers between devices: 18 us -> 15 us
  waiting for transfers between devices: 1.19 us -> 3.9 us
  local copies, waits for them, and re-layouts: 6.54 us -> 4.71 us
  Pallas kernels: 29.2 us -> 28.5 us
  other arithmetic: 1.72 us -> 1.07 us
    slice x4 -> x0, local copies, waits for them, and re-layouts: 3.04 us -> none  [per_device(): back = slide_wide(meta, [slab[:, 0:256] for slab in slabs], blocks)]
    ppermute x16, starting transfers between devices: 18 us -> 15 us  [move(): return lax.ppermute(block, 'seq', route)]
    ppermute x16, waiting for transfers between devices: 1.19 us -> 3.9 us  [move(): return lax.ppermute(block, 'seq', route)]
    unnamed x24 -> x34, local copies, waits for them, and re-layouts: 3.47 us -> 4.68 us
    concatenate x1, other arithmetic: 0.69 us -> 0.02 us  [per_device(): own = jnp.concatenate([slab[:, 256:640] for slab in slabs], axis=0)]
    pallas_call x1, Pallas kernels: 4.7 us -> 4.08 us  [split(): pl.pallas_call(split_kernel, in_specs=[smem()] + [pl.BlockSpec(memory_spa...]
  transfers between devices with their start and end apart: 16 -> 16, of which waited for: 3 -> 3; matrix products, arithmetic and copies ran while one was open for 8% -> 2% of each run, Pallas kernels for 31% -> 33%
where the time goes in v8:
time: 55.2 us; the launch traced here: 54.4 us
  Pallas kernels  28.5 us (52%)
  starting transfers between devices  15 us (27%)
  local copies, waits for them, and re-layouts  4.71 us (9%)
  waiting for transfers between devices  3.9 us (7%)
  between operations  1.2 us (2%)
  other arithmetic  1.07 us (2%)
    ppermute x16, starting transfers between devices, move(): return lax.ppermute(block, 'seq', route)  15 us
    pallas_call x3, Pallas kernels, local_near(): pl.pallas_call(functools.partial(local_kernel, 'ABC', first, many), in_sp...  12.9 us
    pallas_call x2, Pallas kernels, local_far(): pl.pallas_call(functools.partial(local_kernel, 'D', first, many), in_spec...  5.14 us
    unnamed x34, local copies, waits for them, and re-layouts  4.68 us
    pallas_call x1, Pallas kernels, split(): pl.pallas_call(split_kernel, in_specs=[smem()] + [pl.BlockSpec(memory_spa...  4.08 us
    ppermute x16, waiting for transfers between devices, move(): return lax.ppermute(block, 'seq', route)  3.9 us
    pallas_call x1, Pallas kernels, slide_wide(): pl.pallas_call(far_kernel, in_specs=[smem()] + [vmem()] * 12, out_specs=[...  3.88 us
    pallas_call x1, Pallas kernels, merge(): pl.pallas_call(merge_kernel, in_specs=[smem()] + [vmem()] * (len(NEAR_PAR...  2.5 us
  transfers between devices with their start and end apart: 16, of which 3 were waited for; matrix products, arithmetic and copies ran while one was open for 2% of the time, Pallas kernels for 33%

profile of v8, /device:TPU:1, one launch (start us, length us, event | category | flops | bytes accessed | tf_op | source)
XLA Modules:
  0.0 54.4 jit_solution(1035198207601887562)
XLA Ops:
  0.7 0.1 pad_add_fusion.meta
  0.7 4.1 %split_rows.1 = (bf16[16,64,768]{2,1,0:T(8,128)(2,1)S(1)}, bf16[16,64,768]{2,1,0:T(8,128)(2,1)S(1)}, bf16[16,64,768]{2,1,0:T(8,128)(2,1)S(1)}, bf16[4,2,64,768]{...) custom-call(s32[2]{0:T(128)S(1)} %pad_add_fusion.meta, ...), custom_call_target="tpu_custom_call" | custom-call | tf_op jit(solution)/shard_map/split_rows/pallas_call | solution.py:449
  4.8 0.7 %copy-done.16 = bf16[2,2,64,768]{3,2,1,0:T(8,128)(2,1)} copy-done((bf16[2,2,64,768]{3,2,1,0:T(8,128)(2,1)}, bf16[2,2,64,768]{3,2,1,0:T(8,128)(2,1)S(1)}, u32[]{:S(2)}) %copy-start.16) | copy-done | bytes 393240
  5.6 1.4 %collective-permute-start.3 = (bf16[4,2,64,768]{3,2,1,0:T(8,128)(2,1)S(1)}, bf16[4,2,64,768]{3,2,1,0:T(8,128)(2,1)S(1)}, u32[]{:S(2)}, u32[]{:S(2)}) collective-permute-start(bf16[4,2,64,768]{3,2,1,0:T(8,128)(2,1)S(1)} %get-tuple-element.65), channel_id=1, source_target_pairs={{0,1},{1,0},{2,3},{3,2},{4,5},{5,4},{6,7},{7,6},{8,9},{9,8},{10,11... | collective-permute-start | bytes 2359304 | tf_op jit(solution)/shard_map/ppermute | solution.py:535
  7.0 1.7 %collective-permute-start = (bf16[64,640]{1,0:T(8,128)(2,1)S(1)}, bf16[64,640]{1,0:T(8,128)(2,1)S(1)}, u32[]{:S(2)}, u32[]{:S(2)}) collective-permute-start(bf16[64,640]{1,0:T(8,128)(2,1)S(1)} %get-tuple-element.59), channel_id=1, source_target_pairs={{0,2},{1,3},{2,0},{3,1},{4,6},{5,7},{6,4},{7,5},{8,10},{9,11},{10,... | collective-permute-start | bytes 245768 | tf_op jit(solution)/shard_map/ppermute | solution.py:535
  8.7 3.3 %collective-permute-start.1 = (bf16[64,640]{1,0:T(8,128)(2,1)S(1)}, bf16[64,640]{1,0:T(8,128)(2,1)S(1)}, u32[]{:S(2)}, u32[]{:S(2)}) collective-permute-start(bf16[64,640]{1,0:T(8,128)(2,1)S(1)} %get-tuple-element.60), channel_id=1, source_target_pairs={{0,4},{1,5},{2,6},{3,7},{4,0},{5,1},{6,2},{7,3},{8,12},{9,13},{10,... | collective-permute-start | bytes 245768 | tf_op jit(solution)/shard_map/ppermute | solution.py:535
  12.0 6.0 %near_queries.3.refs_0_ = bf16[16,64,384]{2,1,0:T(8,128)(2,1)S(1)} custom-call(s32[2]{0:T(128)S(1)} %pad_add_fusion.meta, bf16[16,64,768]{2,1,0:T(8,128)(2,1)S(1)} %get-tuple-element.62.refs_0_, bf16[16,64,768]{2,1,0:T(8,128)(2,1)S(1)} %get-tuple-element.63.refs_1_, bf16[16,64,768]{2,1,0:T(8,128)(2,1)S(1)} %get-tuple-element.64.refs_2_, ...), custom_call_target="tpu_custom_call" | custom-call | flops 1800000000 | bytes 1000000 | tf_op jit(solution)/shard_map/near_queries/pallas_call | solution.py:467
  18.1 0.9 %copy-done.6 = bf16[16,64,384]{2,1,0:T(8,128)(2,1)} copy-done((bf16[16,64,384]{2,1,0:T(8,128)(2,1)}, bf16[16,64,384]{2,1,0:T(8,128)(2,1)S(1)}, u32[]{:S(2)}) %copy-start.6) | copy-done | bytes 786456
  19.1 0.5 copy-done.10
  19.6 2.5 %collective-permute-start.5 = (bf16[256,384]{1,0:T(8,128)(2,1)S(1)}, bf16[256,384]{1,0:T(8,128)(2,1)S(1)}, u32[]{:S(2)}, u32[]{:S(2)}) collective-permute-start(bf16[256,384]{1,0:T(8,128)(2,1)S(1)} %pad_maximum_fusion.rest_0_), channel_id=1, source_target_pairs={{0,24},{1,25},{2,26},{3,27},{4,28},{5,29},{6,30},{7,31},{8,16},{9,... | collective-permute-start | bytes 589832 | tf_op jit(solution)/shard_map/ppermute | solution.py:535
  22.1 0.3 collective-permute-start.7
  22.4 0.0 copy-start.1
  22.4 1.4 %copy-done.1 = bf16[16,64,768]{2,1,0:T(8,128)(2,1)S(1)} copy-done((bf16[16,64,768]{2,1,0:T(8,128)(2,1)S(1)}, bf16[16,64,768]{2,1,0:T(8,128)(2,1)}, u32[]{:S(2)}) %copy-start.1) | copy-done | bytes 1572888
  23.8 1.1 %copy-done.4 = bf16[4,2,64,768]{3,2,1,0:T(8,128)(2,1)S(1)} copy-done((bf16[4,2,64,768]{3,2,1,0:T(8,128)(2,1)S(1)}, bf16[4,2,64,768]{3,2,1,0:T(8,128)(2,1)}, u32[]{:S(2)}) %copy-start.4) | copy-done | bytes 786456
  24.9 4.3 %near_queries.4.refs_1_ = bf16[16,64,256]{2,1,0:T(8,128)(2,1)S(1)} custom-call(s32[2]{0:T(128)S(1)} %pad_add_fusion.meta, bf16[16,64,768]{2,1,0:T(8,128)(2,1)S(1)} %get-tuple-element.62.refs_0_, bf16[16,64,768]{2,1,0:T(8,128)(2,1)S(1)} %get-tuple-element.63.refs_1_, bf16[16,64,768]{2,1,0:T(8,128)(2,1)S(1)} %copy-done.1, bf16[4,2,64,768]{3,2,1,0:T(8,128)(2,1)S(1)} %copy-done.4), custom_call_target="tpu_custom_call" | custom-call | flops 1200000000 | bytes 1000000 | tf_op jit(solution)/shard_map/near_queries/pallas_call | solution.py:467
  29.2 1.0 %broadcast_select_fusion = bf16[256,384]{1,0:T(8,128)(2,1)S(1)} fusion(bf16[256,384]{1,0:T(8,128)(2,1)S(1)} %collective-permute-done.5.rest_3_, bf16[256,384]{1,0:T(8,128)(2,1)} %collective-permute-done.4.rest_1_, pred[]{:T(512)S(6)} %eq.5), kind=kLoop, calls=%fused_computation.1 | loop fusion | flops 98304 | bytes 589825 | tf_op jit(solution)/shard_map/jit(_where)/select_n | solution.py:573
  30.2 0.6 %collective-permute-start.6 = (bf16[256,384]{1,0:T(8,128)(2,1)S(1)}, bf16[256,384]{1,0:T(8,128)(2,1)S(1)}, u32[]{:S(2)}, u32[]{:S(2)}) collective-permute-start(bf16[256,384]{1,0:T(8,128)(2,1)S(1)} %broadcast_select_fusion), channel_id=1, source_target_pairs={{0,8},{1,25},{2,10},{3,27},{4,12},{5,29},{6,14},{7,31},{8,0},{9,17... | collective-permute-start | bytes 589832 | tf_op jit(solution)/shard_map/ppermute | solution.py:535
  30.8 2.6 %near_queries.5.refs_2_ = bf16[16,64,128]{2,1,0:T(8,128)(2,1)S(1)} custom-call(s32[2]{0:T(128)S(1)} %pad_add_fusion.meta, bf16[16,64,768]{2,1,0:T(8,128)(2,1)S(1)} %get-tuple-element.62.refs_0_, bf16[16,64,768]{2,1,0:T(8,128)(2,1)S(1)} %get-tuple-element.63.refs_1_, bf16[16,64,768]{2,1,0:T(8,128)(2,1)S(1)} %copy-done.1, bf16[4,2,64,768]{3,2,1,0:T(8,128)(2,1)S(1)} %copy-done.4), custom_call_target="tpu_custom_call" | custom-call | flops 600000000 | bytes 1000000 | tf_op jit(solution)/shard_map/near_queries/pallas_call | solution.py:467
  33.4 2.6 %collective-permute-done.6.rest_2_ = bf16[256,384]{1,0:T(8,128)(2,1)S(1)} collective-permute-done((bf16[256,384]{1,0:T(8,128)(2,1)S(1)}, bf16[256,384]{1,0:T(8,128)(2,1)S(1)}, u32[]{:S(2)}, u32[]{:S(2)}) %collective-permute-start.6) | collective-permute-done | bytes 196640 | tf_op jit(solution)/shard_map/ppermute | solution.py:535
  36.0 0.5 collective-permute-start.8
  36.5 0.0 collective-permute-start.11
  36.5 0.5 collective-permute-start.9
  37.0 0.7 %collective-permute-done.12.refs_5_ = bf16[2,2,64,768]{3,2,1,0:T(8,128)(2,1)S(1)} collective-permute-done((bf16[2,2,64,768]{3,2,1,0:T(8,128)(2,1)S(1)}, bf16[2,2,64,768]{3,2,1,0:T(8,128)(2,1)S(1)}, u32[]{:S(2)}, u32[]{:S(2)}) %collective-permute-start.12) | collective-permute-done | bytes 393248 | tf_op jit(solution)/shard_map/ppermute | solution.py:535
  37.7 2.0 %wide_queries.2 = (bf16[16,64,256]{2,1,0:T(8,128)(2,1)S(1)}, f32[64,256]{1,0:T(8,128)S(1)}, f32[64,256]{1,0:T(8,128)S(1)}) custom-call(s32[2]{0:T(128)S(1)} %pad_add_fusion.meta, bf16[16,64,768]{2,1,0:T(8,128)(2,1)S(1)} %get-tuple-element.62.refs_0_, bf16[16,64,768]{2,1,0:T(8,128)(2,1)S(1)} %get-tuple-element.63.refs_1_, bf16[16,64,768]{2,1,0:T(8,128)(2,1)S(1)} %copy-done.1, ...), custom_call_target="tpu_custom_call" | custom-call | flops 400000000 | bytes 1000000 | tf_op jit(solution)/shard_map/wide_queries/pallas_call | solution.py:481
  39.7 0.0 copy-start.2
  39.8 3.9 %slide_queries.1 = (bf16[64,256]{1,0:T(8,128)(2,1)S(1)}, bf16[64,256]{1,0:T(8,128)(2,1)S(1)}, bf16[64,256]{1,0:T(8,128)(2,1)S(1)}, bf16[64,256]{1,0:T(8,128)(2,1)S(1)}) custom-call(s32[2]{0:T(128)S(1)} %pad_add_fusion.meta, bf16[64,640]{1,0:T(8,128)(2,1)S(1)} %copy-done.9, bf16[64,640]{1,0:T(8,128)(2,1)S(1)} %copy-done.11, bf16[64,640]{1,0:T(8,128)(2,1)S(1)} %copy-done.13, ...), custom_call_target="tpu_custom_call" | custom-call | flops 800000000 | bytes 2000000 | tf_op jit(solution)/shard_map/slide_queries/pallas_call | solution.py:499
  43.7 1.5 %collective-permute-start.13 = (bf16[64,256]{1,0:T(8,128)(2,1)S(1)}, bf16[64,256]{1,0:T(8,128)(2,1)S(1)}, u32[]{:S(2)}, u32[]{:S(2)}) collective-permute-start(bf16[64,256]{1,0:T(8,128)(2,1)S(1)} %get-tuple-element.108), channel_id=1, source_target_pairs={{0,2},{1,3},{2,0},{3,1},{4,6},{5,7},{6,4},{7,5},{8,10},{9,11},{10,... | collective-permute-start | bytes 98312 | tf_op jit(solution)/shard_map/ppermute | solution.py:535
  45.2 2.5 %collective-permute-start.14 = (bf16[64,256]{1,0:T(8,128)(2,1)S(1)}, bf16[64,256]{1,0:T(8,128)(2,1)S(1)}, u32[]{:S(2)}, u32[]{:S(2)}) collective-permute-start(bf16[64,256]{1,0:T(8,128)(2,1)S(1)} %get-tuple-element.109), channel_id=1, source_target_pairs={{0,4},{1,5},{2,6},{3,7},{4,0},{5,1},{6,2},{7,3},{8,12},{9,13},{10,... | collective-permute-start | bytes 98312 | tf_op jit(solution)/shard_map/ppermute | solution.py:535
  47.7 0.2 collective-permute-start.15
  47.9 3.2 %wide_queries.3 = (bf16[16,64,512]{2,1,0:T(8,128)(2,1)S(1)}, f32[64,512]{1,0:T(8,128)S(1)}, f32[64,512]{1,0:T(8,128)S(1)}) custom-call(s32[2]{0:T(128)S(1)} %pad_add_fusion.meta, bf16[16,64,768]{2,1,0:T(8,128)(2,1)S(1)} %get-tuple-element.62.refs_0_, bf16[16,64,768]{2,1,0:T(8,128)(2,1)S(1)} %get-tuple-element.63.refs_1_, bf16[16,64,768]{2,1,0:T(8,128)(2,1)S(1)} %copy-done.2, ...), custom_call_target="tpu_custom_call" | custom-call | flops 800000000 | bytes 1000000 | tf_op jit(solution)/shard_map/wide_queries/pallas_call | solution.py:481
  51.2 0.6 %collective-permute-done.15.refs_12_ = bf16[64,256]{1,0:T(8,128)(2,1)S(1)} collective-permute-done((bf16[64,256]{1,0:T(8,128)(2,1)S(1)}, bf16[64,256]{1,0:T(8,128)(2,1)S(1)}, u32[]{:S(2)}, u32[]{:S(2)}) %collective-permute-start.15) | collective-permute-done | bytes 32800 | tf_op jit(solution)/shard_map/ppermute | solution.py:535
  51.7 2.5 %merge_rows.1 = bf16[1024,768]{1,0:T(8,128)(2,1)} custom-call(s32[2]{0:T(128)S(1)} %pad_add_fusion.meta, bf16[16,64,384]{2,1,0:T(8,128)(2,1)S(1)} %copy-done.7, bf16[16,64,256]{2,1,0:T(8,128)(2,1)S(1)} %near_queries.4.refs_1_, bf16[16,64,128]{2,1,0:T(8,128)(2,1)S(1)} %near_queries.5.refs_2_, bf16[16,64,256]{2,1,0:T(8,128)(2,1)S(1)} %get-tuple-element.87.refs_3_, ...), custom_call_target="tpu_custom_call" | custom-call | tf_op jit(solution)/shard_map/merge_rows/pallas_call | solution.py:511
  (49 shorter events, 0.1 us)
Async XLA Ops:
  4.8 0.7 %copy-start.16 = (bf16[2,2,64,768]{3,2,1,0:T(8,128)(2,1)}, bf16[2,2,64,768]{3,2,1,0:T(8,128)(2,1)S(1)}, u32[]{:S(2)}) copy-start(bf16[2,2,64,768]{3,2,1,0:T(8,128)(2,1)S(1)} %get-tuple-element.78) | copy-start | bytes 1179652
  5.5 12.5 %copy-start = (bf16[16,64,768]{2,1,0:T(8,128)(2,1)}, bf16[16,64,768]{2,1,0:T(8,128)(2,1)S(1)}, u32[]{:S(2)}) copy-start(bf16[16,64,768]{2,1,0:T(8,128)(2,1)S(1)} %get-tuple-element.64.refs_2_) | copy-start | bytes 4718596
  5.6 13.5 %copy-start.8 = (bf16[64,640]{1,0:T(8,128)(2,1)}, bf16[64,640]{1,0:T(8,128)(2,1)S(1)}, u32[]{:S(2)}) copy-start(bf16[64,640]{1,0:T(8,128)(2,1)S(1)} %get-tuple-element.68.a0) | copy-start | bytes 245764
  5.6 6.5 %collective-permute-start.3 = (bf16[4,2,64,768]{3,2,1,0:T(8,128)(2,1)S(1)}, bf16[4,2,64,768]{3,2,1,0:T(8,128)(2,1)S(1)}, u32[]{:S(2)}, u32[]{:S(2)}) collective-permute-start(bf16[4,2,64,768]{3,2,1,0:T(8,128)(2,1)S(1)} %get-tuple-element.65), channel_id=1, source_target_pairs={{0,1},{1,0},{2,3},{3,2},{4,5},{5,4},{6,7},{7,6},{8,9},{9,8},{10,11... | collective-permute-start | bytes 2359304 | tf_op jit(solution)/shard_map/ppermute | solution.py:535
  7.0 12.0 %collective-permute-start = (bf16[64,640]{1,0:T(8,128)(2,1)S(1)}, bf16[64,640]{1,0:T(8,128)(2,1)S(1)}, u32[]{:S(2)}, u32[]{:S(2)}) collective-permute-start(bf16[64,640]{1,0:T(8,128)(2,1)S(1)} %get-tuple-element.59), channel_id=1, source_target_pairs={{0,2},{1,3},{2,0},{3,1},{4,6},{5,7},{6,4},{7,5},{8,10},{9,11},{10,... | collective-permute-start | bytes 245768 | tf_op jit(solution)/shard_map/ppermute | solution.py:535
  8.7 10.3 %collective-permute-start.1 = (bf16[64,640]{1,0:T(8,128)(2,1)S(1)}, bf16[64,640]{1,0:T(8,128)(2,1)S(1)}, u32[]{:S(2)}, u32[]{:S(2)}) collective-permute-start(bf16[64,640]{1,0:T(8,128)(2,1)S(1)} %get-tuple-element.60), channel_id=1, source_target_pairs={{0,4},{1,5},{2,6},{3,7},{4,0},{5,1},{6,2},{7,3},{8,12},{9,13},{10,... | collective-permute-start | bytes 245768 | tf_op jit(solution)/shard_map/ppermute | solution.py:535
  12.0 7.0 %collective-permute-start.2 = (bf16[64,640]{1,0:T(8,128)(2,1)S(1)}, bf16[64,640]{1,0:T(8,128)(2,1)S(1)}, u32[]{:S(2)}, u32[]{:S(2)}) collective-permute-start(bf16[64,640]{1,0:T(8,128)(2,1)S(1)} %get-tuple-element.61), channel_id=1, source_target_pairs={{0,6},{1,7},{2,4},{3,5},{4,2},{5,3},{6,0},{7,1},{8,14},{9,15},{10,... | collective-permute-start | bytes 245768 | tf_op jit(solution)/shard_map/ppermute | solution.py:535
  12.0 6.1 %copy-start.3 = (bf16[4,2,64,768]{3,2,1,0:T(8,128)(2,1)}, bf16[4,2,64,768]{3,2,1,0:T(8,128)(2,1)S(1)}, u32[]{:S(2)}) copy-start(bf16[4,2,64,768]{3,2,1,0:T(8,128)(2,1)S(1)} %collective-permute-done.3.refs_3_) | copy-start | bytes 2359300
  18.1 0.9 %copy-start.6 = (bf16[16,64,384]{2,1,0:T(8,128)(2,1)}, bf16[16,64,384]{2,1,0:T(8,128)(2,1)S(1)}, u32[]{:S(2)}) copy-start(bf16[16,64,384]{2,1,0:T(8,128)(2,1)S(1)} %near_queries.3.refs_0_) | copy-start | bytes 2359300
  19.0 3.1 %copy-start.12 = (bf16[64,640]{1,0:T(8,128)(2,1)}, bf16[64,640]{1,0:T(8,128)(2,1)S(1)}, u32[]{:S(2)}) copy-start(bf16[64,640]{1,0:T(8,128)(2,1)S(1)} %collective-permute-done.1.a2) | copy-start | bytes 245764
  19.0 3.1 %copy-start.14 = (bf16[64,640]{1,0:T(8,128)(2,1)}, bf16[64,640]{1,0:T(8,128)(2,1)S(1)}, u32[]{:S(2)}) copy-start(bf16[64,640]{1,0:T(8,128)(2,1)S(1)} %collective-permute-done.2.a3) | copy-start | bytes 245764
  19.6 9.6 %collective-permute-start.5 = (bf16[256,384]{1,0:T(8,128)(2,1)S(1)}, bf16[256,384]{1,0:T(8,128)(2,1)S(1)}, u32[]{:S(2)}, u32[]{:S(2)}) collective-permute-start(bf16[256,384]{1,0:T(8,128)(2,1)S(1)} %pad_maximum_fusion.rest_0_), channel_id=1, source_target_pairs={{0,24},{1,25},{2,26},{3,27},{4,28},{5,29},{6,30},{7,31},{8,16},{9,... | collective-permute-start | bytes 589832 | tf_op jit(solution)/shard_map/ppermute | solution.py:535
  22.1 7.1 %collective-permute-start.4 = (bf16[256,384]{1,0:T(8,128)(2,1)S(1)}, bf16[256,384]{1,0:T(8,128)(2,1)}, u32[]{:S(2)}, u32[]{:S(2)}) collective-permute-start(bf16[256,384]{1,0:T(8,128)(2,1)S(1)} %pad_maximum_fusion.rest_0_), channel_id=1, source_target_pairs={{0,8},{1,9},{2,10},{3,11},{4,12},{5,13},{6,14},{7,15},{8,0},{9,1},... | collective-permute-start | bytes 589832 | tf_op jit(solution)/shard_map/ppermute | solution.py:535
  22.1 11.3 %collective-permute-start.7 = (bf16[2,2,64,768]{3,2,1,0:T(8,128)(2,1)}, bf16[2,2,64,768]{3,2,1,0:T(8,128)(2,1)S(1)}, u32[]{:S(2)}, u32[]{:S(2)}) collective-permute-start(bf16[2,2,64,768]{3,2,1,0:T(8,128)(2,1)} %copy-done.16), channel_id=1, source_target_pairs={{0,2},{1,3},{2,0},{3,1},{4,6},{5,7},{6,4},{7,5},{8,10},{9,11},{10,... | collective-permute-start | bytes 1179656 | tf_op jit(solution)/shard_map/ppermute | solution.py:535
  22.4 1.4 %copy-start.1 = (bf16[16,64,768]{2,1,0:T(8,128)(2,1)S(1)}, bf16[16,64,768]{2,1,0:T(8,128)(2,1)}, u32[]{:S(2)}) copy-start(bf16[16,64,768]{2,1,0:T(8,128)(2,1)} %copy-done) | copy-start | bytes 4718596
  23.8 1.1 %copy-start.4 = (bf16[4,2,64,768]{3,2,1,0:T(8,128)(2,1)S(1)}, bf16[4,2,64,768]{3,2,1,0:T(8,128)(2,1)}, u32[]{:S(2)}) copy-start(bf16[4,2,64,768]{3,2,1,0:T(8,128)(2,1)} %copy-done.3) | copy-start | bytes 2359300
  30.2 5.8 %collective-permute-start.6 = (bf16[256,384]{1,0:T(8,128)(2,1)S(1)}, bf16[256,384]{1,0:T(8,128)(2,1)S(1)}, u32[]{:S(2)}, u32[]{:S(2)}) collective-permute-start(bf16[256,384]{1,0:T(8,128)(2,1)S(1)} %broadcast_select_fusion), channel_id=1, source_target_pairs={{0,8},{1,25},{2,10},{3,27},{4,12},{5,29},{6,14},{7,31},{8,0},{9,17... | collective-permute-start | bytes 589832 | tf_op jit(solution)/shard_map/ppermute | solution.py:535
  33.3 6.4 %copy-start.9 = (bf16[64,640]{1,0:T(8,128)(2,1)S(1)}, bf16[64,640]{1,0:T(8,128)(2,1)}, u32[]{:S(2)}) copy-start(bf16[64,640]{1,0:T(8,128)(2,1)} %copy-done.8) | copy-start | bytes 245764
  33.4 6.4 %copy-start.11 = (bf16[64,640]{1,0:T(8,128)(2,1)S(1)}, bf16[64,640]{1,0:T(8,128)(2,1)}, u32[]{:S(2)}) copy-start(bf16[64,640]{1,0:T(8,128)(2,1)} %copy-done.10) | copy-start | bytes 245764
  33.4 6.4 %copy-start.13 = (bf16[64,640]{1,0:T(8,128)(2,1)S(1)}, bf16[64,640]{1,0:T(8,128)(2,1)}, u32[]{:S(2)}) copy-start(bf16[64,640]{1,0:T(8,128)(2,1)} %copy-done.12) | copy-start | bytes 245764
  33.4 6.4 %copy-start.15 = (bf16[64,640]{1,0:T(8,128)(2,1)S(1)}, bf16[64,640]{1,0:T(8,128)(2,1)}, u32[]{:S(2)}) copy-start(bf16[64,640]{1,0:T(8,128)(2,1)} %copy-done.14) | copy-start | bytes 245764
  36.0 1.7 %collective-permute-start.12 = (bf16[2,2,64,768]{3,2,1,0:T(8,128)(2,1)S(1)}, bf16[2,2,64,768]{3,2,1,0:T(8,128)(2,1)S(1)}, u32[]{:S(2)}, u32[]{:S(2)}) collective-permute-start(bf16[2,2,64,768]{3,2,1,0:T(8,128)(2,1)S(1)} %collective-permute-done.7.refs_4_), channel_id=1, source_target_pairs={{0,1},{1,0},{2,3},{3,2},{4,5},{5,4},{6,7},{7,6},{8,9},{9,8},{10,11... | collective-permute-start | bytes 1179656 | tf_op jit(solution)/shard_map/ppermute | solution.py:535
  36.0 3.7 %collective-permute-start.8 = (bf16[256,384]{1,0:T(8,128)(2,1)S(1)}, bf16[256,384]{1,0:T(8,128)(2,1)S(1)}, u32[]{:S(2)}, u32[]{:S(2)}) collective-permute-start(bf16[256,384]{1,0:T(8,128)(2,1)S(1)} %pad_maximum_fusion.rest_0_), channel_id=1, source_target_pairs={{0,1},{1,0},{2,3},{3,2},{4,5},{5,4},{6,7},{7,6},{8,9},{9,8},{10,11... | collective-permute-start | bytes 589832 | tf_op jit(solution)/shard_map/ppermute | solution.py:535
  36.5 3.2 %collective-permute-start.11 = (bf16[256,384]{1,0:T(8,128)(2,1)S(1)}, bf16[256,384]{1,0:T(8,128)(2,1)S(1)}, u32[]{:S(2)}, u32[]{:S(2)}) collective-permute-start(bf16[256,384]{1,0:T(8,128)(2,1)S(1)} %collective-permute-done.5.rest_3_), channel_id=1, source_target_pairs={{0,1},{1,0},{2,3},{3,2},{4,5},{5,4},{6,7},{7,6},{8,9},{9,8},{10,11... | collective-permute-start | bytes 589832 | tf_op jit(solution)/shard_map/ppermute | solution.py:535
  36.5 3.2 %collective-permute-start.9 = (bf16[256,384]{1,0:T(8,128)(2,1)}, bf16[256,384]{1,0:T(8,128)(2,1)S(1)}, u32[]{:S(2)}, u32[]{:S(2)}) collective-permute-start(bf16[256,384]{1,0:T(8,128)(2,1)} %collective-permute-done.4.rest_1_), channel_id=1, source_target_pairs={{0,1},{1,0},{2,3},{3,2},{4,5},{5,4},{6,7},{7,6},{8,9},{9,8},{10,11... | collective-permute-start | bytes 589832 | tf_op jit(solution)/shard_map/ppermute | solution.py:535
  37.0 2.7 %collective-permute-start.10 = (bf16[256,384]{1,0:T(8,128)(2,1)S(1)}, bf16[256,384]{1,0:T(8,128)(2,1)S(1)}, u32[]{:S(2)}, u32[]{:S(2)}) collective-permute-start(bf16[256,384]{1,0:T(8,128)(2,1)S(1)} %collective-permute-done.6.rest_2_), channel_id=1, source_target_pairs={{0,1},{1,0},{2,3},{3,2},{4,5},{5,4},{6,7},{7,6},{8,9},{9,8},{10,11... | collective-permute-start | bytes 589832 | tf_op jit(solution)/shard_map/ppermute | solution.py:535
  39.7 8.2 %copy-start.2 = (bf16[16,64,768]{2,1,0:T(8,128)(2,1)S(1)}, bf16[16,64,768]{2,1,0:T(8,128)(2,1)}, u32[]{:S(2)}) copy-start(bf16[16,64,768]{2,1,0:T(8,128)(2,1)} %copy-done) | copy-start | bytes 4718596
  39.7 8.2 %copy-start.5 = (bf16[4,2,64,768]{3,2,1,0:T(8,128)(2,1)S(1)}, bf16[4,2,64,768]{3,2,1,0:T(8,128)(2,1)}, u32[]{:S(2)}) copy-start(bf16[4,2,64,768]{3,2,1,0:T(8,128)(2,1)} %copy-done.3) | copy-start | bytes 2359300
  43.7 8.0 %copy-start.7 = (bf16[16,64,384]{2,1,0:T(8,128)(2,1)S(1)}, bf16[16,64,384]{2,1,0:T(8,128)(2,1)}, u32[]{:S(2)}) copy-start(bf16[16,64,384]{2,1,0:T(8,128)(2,1)} %copy-done.6) | copy-start | bytes 2359300
  43.7 7.4 %collective-permute-start.13 = (bf16[64,256]{1,0:T(8,128)(2,1)S(1)}, bf16[64,256]{1,0:T(8,128)(2,1)S(1)}, u32[]{:S(2)}, u32[]{:S(2)}) collective-permute-start(bf16[64,256]{1,0:T(8,128)(2,1)S(1)} %get-tuple-element.108), channel_id=1, source_target_pairs={{0,2},{1,3},{2,0},{3,1},{4,6},{5,7},{6,4},{7,5},{8,10},{9,11},{10,... | collective-permute-start | bytes 98312 | tf_op jit(solution)/shard_map/ppermute | solution.py:535
  45.2 5.9 %collective-permute-start.14 = (bf16[64,256]{1,0:T(8,128)(2,1)S(1)}, bf16[64,256]{1,0:T(8,128)(2,1)S(1)}, u32[]{:S(2)}, u32[]{:S(2)}) collective-permute-start(bf16[64,256]{1,0:T(8,128)(2,1)S(1)} %get-tuple-element.109), channel_id=1, source_target_pairs={{0,4},{1,5},{2,6},{3,7},{4,0},{5,1},{6,2},{7,3},{8,12},{9,13},{10,... | collective-permute-start | bytes 98312 | tf_op jit(solution)/shard_map/ppermute | solution.py:535
  47.7 4.0 %collective-permute-start.15 = (bf16[64,256]{1,0:T(8,128)(2,1)S(1)}, bf16[64,256]{1,0:T(8,128)(2,1)S(1)}, u32[]{:S(2)}, u32[]{:S(2)}) collective-permute-start(bf16[64,256]{1,0:T(8,128)(2,1)S(1)} %get-tuple-element.110), channel_id=1, source_target_pairs={{0,6},{1,7},{2,4},{3,5},{4,2},{5,3},{6,0},{7,1},{8,14},{9,15},{10,... | collective-permute-start | bytes 98312 | tf_op jit(solution)/shard_map/ppermute | solution.py:535
  (1 other events, 0.6 us)

commit v9 on v6

--- a/solution.py
+++ b/solution.py
@@ -27,7 +27,7 @@
 CLASS_U = {"A": ODD, "B": [2, 6, 10, 14], "C": [4, 12], "D": [8, 0]}
 PAIR_OF = [0, 2, 3, 5]
 LONE_OF = [2, 3, 8, 9]
-NEAR_PARTS = [(0, 1), (1, 5)]
+NEAR_PARTS = [(0, 2), (2, 4)]
 WIDE_PARTS = [(0, 2), (2, 4)]
 
 
@@ -571,7 +571,7 @@
     blocks += [move(block, other_core) for block in blocks]
     wide = [local_far(*WIDE_PARTS[0], later, *local, near, cross)]
     blocks, wide[0], later = lax.optimization_barrier((blocks, wide[0], later))
-    back = slide_wide(meta, [slab[:, 0:256] for slab in slabs], blocks)
+    back = slide_wide(meta, slabs, blocks)
     back, later = lax.optimization_barrier((back, later))
     back = [back[0]] + [move(back[step], along_z(step)) for step in (1, 2, 3)]
     wide.append(local_far(*WIDE_PARTS[1], later, *local, near, cross))

time: 49.5 us -> 47.9 us (0.968)
  waiting for transfers between devices: 3.98 us -> 2.69 us
    ppermute x16, waiting for transfers between devices: 3.98 us -> 2.69 us  [move(): return lax.ppermute(block, 'seq', route)]
  transfers between devices with their start and end apart: 16 -> 16, of which waited for: 3 -> 3; matrix products, arithmetic and copies ran while one was open for 0% -> 0% of each run, Pallas kernels for 35% -> 36%
where the time goes in v9:
time: 47.9 us; the launch traced here: 47.8 us
  Pallas kernels  27.2 us (57%)
  starting transfers between devices  16.7 us (35%)
  waiting for transfers between devices  2.69 us (6%)
  between operations  1.01 us (2%)
    ppermute x16, starting transfers between devices, move(): return lax.ppermute(block, 'seq', route)  16.7 us
    pallas_call x2, Pallas kernels, local_near(): pl.pallas_call(functools.partial(local_kernel, 'ABC', first, many), in_sp...  12.1 us
    pallas_call x2, Pallas kernels, local_far(): pl.pallas_call(functools.partial(local_kernel, 'D', first, many), in_spec...  5.17 us
    pallas_call x1, Pallas kernels, split(): pl.pallas_call(split_kernel, in_specs=[smem()] + [pl.BlockSpec(memory_spa...  4.07 us
    pallas_call x1, Pallas kernels, slide_wide(): pl.pallas_call(far_kernel, in_specs=[smem()] + [vmem()] * 12, out_specs=[...  3.35 us
    ppermute x16, waiting for transfers between devices, move(): return lax.ppermute(block, 'seq', route)  2.69 us
    pallas_call x1, Pallas kernels, merge(): pl.pallas_call(merge_kernel, in_specs=[smem()] + [vmem()] * (len(NEAR_PAR...  2.48 us
  transfers between devices with their start and end apart: 16, of which 3 were waited for; matrix products, arithmetic and copies ran while one was open for 0% of the time, Pallas kernels for 36%

profile of v9, /device:TPU:1, one launch (start us, length us, event | category | flops | bytes accessed | tf_op | source)
XLA Modules:
  0.0 47.8 jit_solution(4027607301106835844)
XLA Ops:
  0.7 0.1 pad_add_fusion.meta
  0.7 4.1 %split_rows.1 = (bf16[16,64,768]{2,1,0:T(8,128)(2,1)S(1)}, bf16[16,64,768]{2,1,0:T(8,128)(2,1)S(1)}, bf16[16,64,768]{2,1,0:T(8,128)(2,1)S(1)}, bf16[4,2,64,768]{...) custom-call(s32[2]{0:T(128)S(1)} %pad_add_fusion.meta, ...), custom_call_target="tpu_custom_call" | custom-call | tf_op jit(solution)/shard_map/split_rows/pallas_call | solution.py:449
  4.8 1.5 %collective-permute-start.3 = (bf16[4,2,64,768]{3,2,1,0:T(8,128)(2,1)S(1)}, bf16[4,2,64,768]{3,2,1,0:T(8,128)(2,1)S(1)}, u32[]{:S(2)}, u32[]{:S(2)}) collective-permute-start(bf16[4,2,64,768]{3,2,1,0:T(8,128)(2,1)S(1)} %get-tuple-element.63), channel_id=1, source_target_pairs={{0,1},{1,0},{2,3},{3,2},{4,5},{5,4},{6,7},{7,6},{8,9},{9,8},{10,11... | collective-permute-start | bytes 2359304 | tf_op jit(solution)/shard_map/ppermute | solution.py:535
  6.3 1.7 %collective-permute-start = (bf16[64,640]{1,0:T(8,128)(2,1)S(1)}, bf16[64,640]{1,0:T(8,128)(2,1)S(1)}, u32[]{:S(2)}, u32[]{:S(2)}) collective-permute-start(bf16[64,640]{1,0:T(8,128)(2,1)S(1)} %get-tuple-element.57), channel_id=1, source_target_pairs={{0,2},{1,3},{2,0},{3,1},{4,6},{5,7},{6,4},{7,5},{8,10},{9,11},{10,... | collective-permute-start | bytes 245768 | tf_op jit(solution)/shard_map/ppermute | solution.py:535
  8.0 3.3 %collective-permute-start.1 = (bf16[64,640]{1,0:T(8,128)(2,1)S(1)}, bf16[64,640]{1,0:T(8,128)(2,1)S(1)}, u32[]{:S(2)}, u32[]{:S(2)}) collective-permute-start(bf16[64,640]{1,0:T(8,128)(2,1)S(1)} %get-tuple-element.58), channel_id=1, source_target_pairs={{0,4},{1,5},{2,6},{3,7},{4,0},{5,1},{6,2},{7,3},{8,12},{9,13},{10,... | collective-permute-start | bytes 245768 | tf_op jit(solution)/shard_map/ppermute | solution.py:535
  11.4 0.0 collective-permute-start.2
  11.4 0.0 collective-permute-done.3.refs_3_
  11.4 4.3 %near_queries.2.refs_0_ = bf16[16,64,256]{2,1,0:T(8,128)(2,1)S(1)} custom-call(s32[2]{0:T(128)S(1)} %pad_add_fusion.meta, bf16[16,64,768]{2,1,0:T(8,128)(2,1)S(1)} %get-tuple-element.60.refs_0_, bf16[16,64,768]{2,1,0:T(8,128)(2,1)S(1)} %get-tuple-element.61.refs_1_, bf16[16,64,768]{2,1,0:T(8,128)(2,1)S(1)} %get-tuple-element.62.refs_2_, ...), custom_call_target="tpu_custom_call" | custom-call | flops 1200000000 | bytes 1000000 | tf_op jit(solution)/shard_map/near_queries/pallas_call | solution.py:467
  15.6 0.0 collective-permute-done.a1
  15.7 0.0 collective-permute-done.1.a2
  15.7 1.9 %collective-permute-done.2.a3 = bf16[64,640]{1,0:T(8,128)(2,1)S(1)} collective-permute-done((bf16[64,640]{1,0:T(8,128)(2,1)S(1)}, bf16[64,640]{1,0:T(8,128)(2,1)S(1)}, u32[]{:S(2)}, u32[]{:S(2)}) %collective-permute-start.2) | collective-permute-done | bytes 81952 | tf_op jit(solution)/shard_map/ppermute | solution.py:535
  17.6 0.0 collective-permute-start.7
  17.7 2.6 %collective-permute-start.6 = (bf16[256,384]{1,0:T(8,128)(2,1)S(1)}, bf16[256,384]{1,0:T(8,128)(2,1)S(1)}, u32[]{:S(2)}, u32[]{:S(2)}) collective-permute-start(bf16[256,384]{1,0:T(8,128)(2,1)S(1)} %pad_maximum_fusion.rest_0_), channel_id=1, source_target_pairs={{0,24},{1,25},{2,26},{3,27},{4,28},{5,29},{6,30},{7,31},{8,16},{9,... | collective-permute-start | bytes 589832 | tf_op jit(solution)/shard_map/ppermute | solution.py:535
  20.2 0.5 %collective-permute-start.5 = (bf16[256,384]{1,0:T(8,128)(2,1)S(1)}, bf16[256,384]{1,0:T(8,128)(2,1)S(1)}, u32[]{:S(2)}, u32[]{:S(2)}) collective-permute-start(bf16[256,384]{1,0:T(8,128)(2,1)S(1)} %pad_maximum_fusion.rest_0_), channel_id=1, source_target_pairs={{0,16},{1,17},{2,18},{3,19},{4,20},{5,21},{6,22},{7,23},{8,24},{9,... | collective-permute-start | bytes 589832 | tf_op jit(solution)/shard_map/ppermute | solution.py:535
  20.8 0.3 collective-permute-start.4
  21.0 7.9 %near_queries.3.refs_1_ = bf16[16,64,512]{2,1,0:T(8,128)(2,1)S(1)} custom-call(s32[2]{0:T(128)S(1)} %pad_add_fusion.meta, bf16[16,64,768]{2,1,0:T(8,128)(2,1)S(1)} %get-tuple-element.60.refs_0_, bf16[16,64,768]{2,1,0:T(8,128)(2,1)S(1)} %get-tuple-element.61.refs_1_, bf16[16,64,768]{2,1,0:T(8,128)(2,1)S(1)} %get-tuple-element.62.refs_2_, ...), custom_call_target="tpu_custom_call" | custom-call | flops 2400000000 | bytes 1000000 | tf_op jit(solution)/shard_map/near_queries/pallas_call | solution.py:467
  28.9 0.0 collective-permute-done.6.rest_3_
  28.9 0.4 collective-permute-done.4.rest_1_
  29.3 0.0 collective-permute-done.7.refs_4_
  29.3 1.8 %collective-permute-start.12 = (bf16[2,2,64,768]{3,2,1,0:T(8,128)(2,1)S(1)}, bf16[2,2,64,768]{3,2,1,0:T(8,128)(2,1)S(1)}, u32[]{:S(2)}, u32[]{:S(2)}) collective-permute-start(bf16[2,2,64,768]{3,2,1,0:T(8,128)(2,1)S(1)} %collective-permute-done.7.refs_4_), channel_id=1, source_target_pairs={{0,1},{1,0},{2,3},{3,2},{4,5},{5,4},{6,7},{7,6},{8,9},{9,8},{10,11... | collective-permute-start | bytes 1179656 | tf_op jit(solution)/shard_map/ppermute | solution.py:535
  31.1 0.0 collective-permute-start.8
  31.1 0.5 %collective-permute-start.9 = (bf16[256,384]{1,0:T(8,128)(2,1)S(1)}, bf16[256,384]{1,0:T(8,128)(2,1)S(1)}, u32[]{:S(2)}, u32[]{:S(2)}) collective-permute-start(bf16[256,384]{1,0:T(8,128)(2,1)S(1)} %collective-permute-done.4.rest_1_), channel_id=1, source_target_pairs={{0,1},{1,0},{2,3},{3,2},{4,5},{5,4},{6,7},{7,6},{8,9},{9,8},{10,11... | collective-permute-start | bytes 589832 | tf_op jit(solution)/shard_map/ppermute | solution.py:535
  31.6 0.0 collective-permute-start.10
  31.6 0.5 %collective-permute-start.11 = (bf16[256,384]{1,0:T(8,128)(2,1)S(1)}, bf16[256,384]{1,0:T(8,128)(2,1)S(1)}, u32[]{:S(2)}, u32[]{:S(2)}) collective-permute-start(bf16[256,384]{1,0:T(8,128)(2,1)S(1)} %collective-permute-done.6.rest_3_), channel_id=1, source_target_pairs={{0,1},{1,0},{2,3},{3,2},{4,5},{5,4},{6,7},{7,6},{8,9},{9,8},{10,11... | collective-permute-start | bytes 589832 | tf_op jit(solution)/shard_map/ppermute | solution.py:535
  32.2 0.3 collective-permute-done.12.refs_5_
  32.5 2.0 %wide_queries.2 = (bf16[16,64,256]{2,1,0:T(8,128)(2,1)S(1)}, f32[64,256]{1,0:T(8,128)S(1)}, f32[64,256]{1,0:T(8,128)S(1)}) custom-call(s32[2]{0:T(128)S(1)} %pad_add_fusion.meta, bf16[16,64,768]{2,1,0:T(8,128)(2,1)S(1)} %get-tuple-element.60.refs_0_, bf16[16,64,768]{2,1,0:T(8,128)(2,1)S(1)} %get-tuple-element.61.refs_1_, ...), custom_call_target="tpu_custom_call" | custom-call | flops 400000000 | bytes 1000000 | tf_op jit(solution)/shard_map/wide_queries/pallas_call | solution.py:481
  34.5 3.4 %slide_queries.1 = (bf16[64,256]{1,0:T(8,128)(2,1)S(1)}, bf16[64,256]{1,0:T(8,128)(2,1)S(1)}, bf16[64,256]{1,0:T(8,128)(2,1)S(1)}, bf16[64,256]{1,0:T(8,128)(2,1)S(1)}) custom-call(s32[2]{0:T(128)S(1)} %pad_add_fusion.meta, bf16[64,640]{1,0:T(8,128)(2,1)S(1)} %get-tuple-element.66.a0, bf16[64,640]{1,0:T(8,128)(2,1)S(1)} %collective-permute-done.a1, ...), custom_call_target="tpu_custom_call" | custom-call | flops 800000000 | bytes 2000000 | tf_op jit(solution)/shard_map/slide_queries/pallas_call | solution.py:499
  37.9 1.5 %collective-permute-start.13 = (bf16[64,256]{1,0:T(8,128)(2,1)S(1)}, bf16[64,256]{1,0:T(8,128)(2,1)S(1)}, u32[]{:S(2)}, u32[]{:S(2)}) collective-permute-start(bf16[64,256]{1,0:T(8,128)(2,1)S(1)} %get-tuple-element.104), channel_id=1, source_target_pairs={{0,2},{1,3},{2,0},{3,1},{4,6},{5,7},{6,4},{7,5},{8,10},{9,11},{10,... | collective-permute-start | bytes 98312 | tf_op jit(solution)/shard_map/ppermute | solution.py:535
  39.4 0.7 %collective-permute-start.14 = (bf16[64,256]{1,0:T(8,128)(2,1)S(1)}, bf16[64,256]{1,0:T(8,128)(2,1)S(1)}, u32[]{:S(2)}, u32[]{:S(2)}) collective-permute-start(bf16[64,256]{1,0:T(8,128)(2,1)S(1)} %get-tuple-element.105), channel_id=1, source_target_pairs={{0,4},{1,5},{2,6},{3,7},{4,0},{5,1},{6,2},{7,3},{8,12},{9,13},{10,... | collective-permute-start | bytes 98312 | tf_op jit(solution)/shard_map/ppermute | solution.py:535
  40.0 1.8 %collective-permute-start.15 = (bf16[64,256]{1,0:T(8,128)(2,1)S(1)}, bf16[64,256]{1,0:T(8,128)(2,1)S(1)}, u32[]{:S(2)}, u32[]{:S(2)}) collective-permute-start(bf16[64,256]{1,0:T(8,128)(2,1)S(1)} %get-tuple-element.106), channel_id=1, source_target_pairs={{0,6},{1,7},{2,4},{3,5},{4,2},{5,3},{6,0},{7,1},{8,14},{9,15},{10,... | collective-permute-start | bytes 98312 | tf_op jit(solution)/shard_map/ppermute | solution.py:535
  41.9 3.2 %wide_queries.3 = (bf16[16,64,512]{2,1,0:T(8,128)(2,1)S(1)}, f32[64,512]{1,0:T(8,128)S(1)}, f32[64,512]{1,0:T(8,128)S(1)}) custom-call(s32[2]{0:T(128)S(1)} %pad_add_fusion.meta, bf16[16,64,768]{2,1,0:T(8,128)(2,1)S(1)} %get-tuple-element.60.refs_0_, bf16[16,64,768]{2,1,0:T(8,128)(2,1)S(1)} %get-tuple-element.61.refs_1_, ...), custom_call_target="tpu_custom_call" | custom-call | flops 800000000 | bytes 1000000 | tf_op jit(solution)/shard_map/wide_queries/pallas_call | solution.py:481
  45.1 2.5 %merge_rows.1 = bf16[1024,768]{1,0:T(8,128)(2,1)} custom-call(s32[2]{0:T(128)S(1)} %pad_add_fusion.meta, bf16[16,64,256]{2,1,0:T(8,128)(2,1)S(1)} %near_queries.2.refs_0_, bf16[16,64,512]{2,1,0:T(8,128)(2,1)S(1)} %near_queries.3.refs_1_, bf16[16,64,256]{2,1,0:T(8,128)(2,1)S(1)} %get-tuple-element.83.refs_2_, ...), custom_call_target="tpu_custom_call" | custom-call | tf_op jit(solution)/shard_map/merge_rows/pallas_call | solution.py:511
  (13 shorter events, 0.1 us)
Async XLA Ops:
  4.8 6.5 %collective-permute-start.3 = (bf16[4,2,64,768]{3,2,1,0:T(8,128)(2,1)S(1)}, bf16[4,2,64,768]{3,2,1,0:T(8,128)(2,1)S(1)}, u32[]{:S(2)}, u32[]{:S(2)}) collective-permute-start(bf16[4,2,64,768]{3,2,1,0:T(8,128)(2,1)S(1)} %get-tuple-element.63), channel_id=1, source_target_pairs={{0,1},{1,0},{2,3},{3,2},{4,5},{5,4},{6,7},{7,6},{8,9},{9,8},{10,11... | collective-permute-start | bytes 2359304 | tf_op jit(solution)/shard_map/ppermute | solution.py:535
  6.3 9.3 %collective-permute-start = (bf16[64,640]{1,0:T(8,128)(2,1)S(1)}, bf16[64,640]{1,0:T(8,128)(2,1)S(1)}, u32[]{:S(2)}, u32[]{:S(2)}) collective-permute-start(bf16[64,640]{1,0:T(8,128)(2,1)S(1)} %get-tuple-element.57), channel_id=1, source_target_pairs={{0,2},{1,3},{2,0},{3,1},{4,6},{5,7},{6,4},{7,5},{8,10},{9,11},{10,... | collective-permute-start | bytes 245768 | tf_op jit(solution)/shard_map/ppermute | solution.py:535
  8.0 7.6 %collective-permute-start.1 = (bf16[64,640]{1,0:T(8,128)(2,1)S(1)}, bf16[64,640]{1,0:T(8,128)(2,1)S(1)}, u32[]{:S(2)}, u32[]{:S(2)}) collective-permute-start(bf16[64,640]{1,0:T(8,128)(2,1)S(1)} %get-tuple-element.58), channel_id=1, source_target_pairs={{0,4},{1,5},{2,6},{3,7},{4,0},{5,1},{6,2},{7,3},{8,12},{9,13},{10,... | collective-permute-start | bytes 245768 | tf_op jit(solution)/shard_map/ppermute | solution.py:535
  11.4 6.2 %collective-permute-start.2 = (bf16[64,640]{1,0:T(8,128)(2,1)S(1)}, bf16[64,640]{1,0:T(8,128)(2,1)S(1)}, u32[]{:S(2)}, u32[]{:S(2)}) collective-permute-start(bf16[64,640]{1,0:T(8,128)(2,1)S(1)} %get-tuple-element.59), channel_id=1, source_target_pairs={{0,6},{1,7},{2,4},{3,5},{4,2},{5,3},{6,0},{7,1},{8,14},{9,15},{10,... | collective-permute-start | bytes 245768 | tf_op jit(solution)/shard_map/ppermute | solution.py:535
  17.6 11.7 %collective-permute-start.7 = (bf16[2,2,64,768]{3,2,1,0:T(8,128)(2,1)S(1)}, bf16[2,2,64,768]{3,2,1,0:T(8,128)(2,1)S(1)}, u32[]{:S(2)}, u32[]{:S(2)}) collective-permute-start(bf16[2,2,64,768]{3,2,1,0:T(8,128)(2,1)S(1)} %get-tuple-element.72), channel_id=1, source_target_pairs={{0,2},{1,3},{2,0},{3,1},{4,6},{5,7},{6,4},{7,5},{8,10},{9,11},{10,... | collective-permute-start | bytes 1179656 | tf_op jit(solution)/shard_map/ppermute | solution.py:535
  17.7 11.2 %collective-permute-start.6 = (bf16[256,384]{1,0:T(8,128)(2,1)S(1)}, bf16[256,384]{1,0:T(8,128)(2,1)S(1)}, u32[]{:S(2)}, u32[]{:S(2)}) collective-permute-start(bf16[256,384]{1,0:T(8,128)(2,1)S(1)} %pad_maximum_fusion.rest_0_), channel_id=1, source_target_pairs={{0,24},{1,25},{2,26},{3,27},{4,28},{5,29},{6,30},{7,31},{8,16},{9,... | collective-permute-start | bytes 589832 | tf_op jit(solution)/shard_map/ppermute | solution.py:535
  20.2 8.7 %collective-permute-start.5 = (bf16[256,384]{1,0:T(8,128)(2,1)S(1)}, bf16[256,384]{1,0:T(8,128)(2,1)S(1)}, u32[]{:S(2)}, u32[]{:S(2)}) collective-permute-start(bf16[256,384]{1,0:T(8,128)(2,1)S(1)} %pad_maximum_fusion.rest_0_), channel_id=1, source_target_pairs={{0,16},{1,17},{2,18},{3,19},{4,20},{5,21},{6,22},{7,23},{8,24},{9,... | collective-permute-start | bytes 589832 | tf_op jit(solution)/shard_map/ppermute | solution.py:535
  20.8 8.6 %collective-permute-start.4 = (bf16[256,384]{1,0:T(8,128)(2,1)S(1)}, bf16[256,384]{1,0:T(8,128)(2,1)S(1)}, u32[]{:S(2)}, u32[]{:S(2)}) collective-permute-start(bf16[256,384]{1,0:T(8,128)(2,1)S(1)} %pad_maximum_fusion.rest_0_), channel_id=1, source_target_pairs={{0,8},{1,9},{2,10},{3,11},{4,12},{5,13},{6,14},{7,15},{8,0},{9,1},... | collective-permute-start | bytes 589832 | tf_op jit(solution)/shard_map/ppermute | solution.py:535
  29.3 3.2 %collective-permute-start.12 = (bf16[2,2,64,768]{3,2,1,0:T(8,128)(2,1)S(1)}, bf16[2,2,64,768]{3,2,1,0:T(8,128)(2,1)S(1)}, u32[]{:S(2)}, u32[]{:S(2)}) collective-permute-start(bf16[2,2,64,768]{3,2,1,0:T(8,128)(2,1)S(1)} %collective-permute-done.7.refs_4_), channel_id=1, source_target_pairs={{0,1},{1,0},{2,3},{3,2},{4,5},{5,4},{6,7},{7,6},{8,9},{9,8},{10,11... | collective-permute-start | bytes 1179656 | tf_op jit(solution)/shard_map/ppermute | solution.py:535
  31.1 3.3 %collective-permute-start.8 = (bf16[256,384]{1,0:T(8,128)(2,1)S(1)}, bf16[256,384]{1,0:T(8,128)(2,1)S(1)}, u32[]{:S(2)}, u32[]{:S(2)}) collective-permute-start(bf16[256,384]{1,0:T(8,128)(2,1)S(1)} %pad_maximum_fusion.rest_0_), channel_id=1, source_target_pairs={{0,1},{1,0},{2,3},{3,2},{4,5},{5,4},{6,7},{7,6},{8,9},{9,8},{10,11... | collective-permute-start | bytes 589832 | tf_op jit(solution)/shard_map/ppermute | solution.py:535
  31.1 3.3 %collective-permute-start.9 = (bf16[256,384]{1,0:T(8,128)(2,1)S(1)}, bf16[256,384]{1,0:T(8,128)(2,1)S(1)}, u32[]{:S(2)}, u32[]{:S(2)}) collective-permute-start(bf16[256,384]{1,0:T(8,128)(2,1)S(1)} %collective-permute-done.4.rest_1_), channel_id=1, source_target_pairs={{0,1},{1,0},{2,3},{3,2},{4,5},{5,4},{6,7},{7,6},{8,9},{9,8},{10,11... | collective-permute-start | bytes 589832 | tf_op jit(solution)/shard_map/ppermute | solution.py:535
  31.6 2.8 %collective-permute-start.10 = (bf16[256,384]{1,0:T(8,128)(2,1)S(1)}, bf16[256,384]{1,0:T(8,128)(2,1)S(1)}, u32[]{:S(2)}, u32[]{:S(2)}) collective-permute-start(bf16[256,384]{1,0:T(8,128)(2,1)S(1)} %collective-permute-done.5.rest_2_), channel_id=1, source_target_pairs={{0,1},{1,0},{2,3},{3,2},{4,5},{5,4},{6,7},{7,6},{8,9},{9,8},{10,11... | collective-permute-start | bytes 589832 | tf_op jit(solution)/shard_map/ppermute | solution.py:535
  31.6 2.8 %collective-permute-start.11 = (bf16[256,384]{1,0:T(8,128)(2,1)S(1)}, bf16[256,384]{1,0:T(8,128)(2,1)S(1)}, u32[]{:S(2)}, u32[]{:S(2)}) collective-permute-start(bf16[256,384]{1,0:T(8,128)(2,1)S(1)} %collective-permute-done.6.rest_3_), channel_id=1, source_target_pairs={{0,1},{1,0},{2,3},{3,2},{4,5},{5,4},{6,7},{7,6},{8,9},{9,8},{10,11... | collective-permute-start | bytes 589832 | tf_op jit(solution)/shard_map/ppermute | solution.py:535
  37.9 7.2 %collective-permute-start.13 = (bf16[64,256]{1,0:T(8,128)(2,1)S(1)}, bf16[64,256]{1,0:T(8,128)(2,1)S(1)}, u32[]{:S(2)}, u32[]{:S(2)}) collective-permute-start(bf16[64,256]{1,0:T(8,128)(2,1)S(1)} %get-tuple-element.104), channel_id=1, source_target_pairs={{0,2},{1,3},{2,0},{3,1},{4,6},{5,7},{6,4},{7,5},{8,10},{9,11},{10,... | collective-permute-start | bytes 98312 | tf_op jit(solution)/shard_map/ppermute | solution.py:535
  39.4 5.7 %collective-permute-start.14 = (bf16[64,256]{1,0:T(8,128)(2,1)S(1)}, bf16[64,256]{1,0:T(8,128)(2,1)S(1)}, u32[]{:S(2)}, u32[]{:S(2)}) collective-permute-start(bf16[64,256]{1,0:T(8,128)(2,1)S(1)} %get-tuple-element.105), channel_id=1, source_target_pairs={{0,4},{1,5},{2,6},{3,7},{4,0},{5,1},{6,2},{7,3},{8,12},{9,13},{10,... | collective-permute-start | bytes 98312 | tf_op jit(solution)/shard_map/ppermute | solution.py:535
  40.0 5.1 %collective-permute-start.15 = (bf16[64,256]{1,0:T(8,128)(2,1)S(1)}, bf16[64,256]{1,0:T(8,128)(2,1)S(1)}, u32[]{:S(2)}, u32[]{:S(2)}) collective-permute-start(bf16[64,256]{1,0:T(8,128)(2,1)S(1)} %get-tuple-element.106), channel_id=1, source_target_pairs={{0,6},{1,7},{2,4},{3,5},{4,2},{5,3},{6,0},{7,1},{8,14},{9,15},{10,... | collective-permute-start | bytes 98312 | tf_op jit(solution)/shard_map/ppermute | solution.py:535

commit v10 on v9

--- a/solution.py
+++ b/solution.py
@@ -557,13 +557,13 @@
     qt, kt, vt, sel, sel8, z0, z1, z2, z3 = split(meta, query_tiles, key_tiles, value_tiles)
     slabs = [z0] + [move(slab, along_z(step)) for step, slab in ((1, z1), (2, z2), (3, z3))]
     pair = move(sel, other_core)
+    near = move(sel8, next_chip)
     local = (qt, kt, vt, pair)
     close = [local_near(*NEAR_PARTS[0], meta, *local)]
-    slabs, close[0], sel8, later = lax.optimization_barrier((slabs, close[0], sel8, meta))
+    slabs, close[0], later = lax.optimization_barrier((slabs, close[0], meta))
     own = jnp.concatenate([slab[:, 256:640] for slab in slabs], axis=0)
     own, later = lax.optimization_barrier((own, later))
     moved = [move(own, along_x(step)) for step in (1, 2, 3)]
-    near = move(sel8, next_chip)
     close.append(local_near(*NEAR_PARTS[1], later, *local))
     moved, near, close[1], later = lax.optimization_barrier((moved, near, close[1], later))
     cross = move(near, other_core)

time: 47.9 us -> 47.8 us (level)
  no operation moved by 1% of the time
where the time goes in v10:
time: 47.8 us; the launch traced here: 47.7 us
  Pallas kernels  27.2 us (57%)
  starting transfers between devices  16.6 us (35%)
  waiting for transfers between devices  2.66 us (6%)
  between operations  1.02 us (2%)
    ppermute x16, starting transfers between devices, move(): return lax.ppermute(block, 'seq', route)  16.6 us
    pallas_call x2, Pallas kernels, local_near(): pl.pallas_call(functools.partial(local_kernel, 'ABC', first, many), in_sp...  12.2 us
    pallas_call x2, Pallas kernels, local_far(): pl.pallas_call(functools.partial(local_kernel, 'D', first, many), in_spec...  5.17 us
    pallas_call x1, Pallas kernels, split(): pl.pallas_call(split_kernel, in_specs=[smem()] + [pl.BlockSpec(memory_spa...  4.07 us
    pallas_call x1, Pallas kernels, slide_wide(): pl.pallas_call(far_kernel, in_specs=[smem()] + [vmem()] * 12, out_specs=[...  3.35 us
    ppermute x16, waiting for transfers between devices, move(): return lax.ppermute(block, 'seq', route)  2.66 us
    pallas_call x1, Pallas kernels, merge(): pl.pallas_call(merge_kernel, in_specs=[smem()] + [vmem()] * (len(NEAR_PAR...  2.48 us
  transfers between devices with their start and end apart: 16, of which 3 were waited for; matrix products, arithmetic and copies ran while one was open for 0% of the time, Pallas kernels for 36%

profile of v10, /device:TPU:1, one launch (start us, length us, event | category | flops | bytes accessed | tf_op | source)
XLA Modules:
  0.0 47.7 jit_solution(10841355579595573956)
XLA Ops:
  0.7 0.1 pad_add_fusion.meta
  0.7 4.1 %split_rows.1 = (bf16[16,64,768]{2,1,0:T(8,128)(2,1)S(1)}, bf16[16,64,768]{2,1,0:T(8,128)(2,1)S(1)}, bf16[16,64,768]{2,1,0:T(8,128)(2,1)S(1)}, bf16[4,2,64,768]{...) custom-call(s32[2]{0:T(128)S(1)} %pad_add_fusion.meta, ...), custom_call_target="tpu_custom_call" | custom-call | tf_op jit(solution)/shard_map/split_rows/pallas_call | solution.py:449
  4.8 1.5 %collective-permute-start.3 = (bf16[4,2,64,768]{3,2,1,0:T(8,128)(2,1)S(1)}, bf16[4,2,64,768]{3,2,1,0:T(8,128)(2,1)S(1)}, u32[]{:S(2)}, u32[]{:S(2)}) collective-permute-start(bf16[4,2,64,768]{3,2,1,0:T(8,128)(2,1)S(1)} %get-tuple-element.62), channel_id=1, source_target_pairs={{0,1},{1,0},{2,3},{3,2},{4,5},{5,4},{6,7},{7,6},{8,9},{9,8},{10,11... | collective-permute-start | bytes 2359304 | tf_op jit(solution)/shard_map/ppermute | solution.py:535
  6.3 1.7 %collective-permute-start = (bf16[64,640]{1,0:T(8,128)(2,1)S(1)}, bf16[64,640]{1,0:T(8,128)(2,1)S(1)}, u32[]{:S(2)}, u32[]{:S(2)}) collective-permute-start(bf16[64,640]{1,0:T(8,128)(2,1)S(1)} %get-tuple-element.56), channel_id=1, source_target_pairs={{0,2},{1,3},{2,0},{3,1},{4,6},{5,7},{6,4},{7,5},{8,10},{9,11},{10,... | collective-permute-start | bytes 245768 | tf_op jit(solution)/shard_map/ppermute | solution.py:535
  8.0 3.3 %collective-permute-start.1 = (bf16[64,640]{1,0:T(8,128)(2,1)S(1)}, bf16[64,640]{1,0:T(8,128)(2,1)S(1)}, u32[]{:S(2)}, u32[]{:S(2)}) collective-permute-start(bf16[64,640]{1,0:T(8,128)(2,1)S(1)} %get-tuple-element.57), channel_id=1, source_target_pairs={{0,4},{1,5},{2,6},{3,7},{4,0},{5,1},{6,2},{7,3},{8,12},{9,13},{10,... | collective-permute-start | bytes 245768 | tf_op jit(solution)/shard_map/ppermute | solution.py:535
  11.4 0.0 collective-permute-start.2
  11.4 0.0 collective-permute-start.7
  11.4 4.3 %near_queries.2.refs_0_ = bf16[16,64,256]{2,1,0:T(8,128)(2,1)S(1)} custom-call(s32[2]{0:T(128)S(1)} %pad_add_fusion.meta, bf16[16,64,768]{2,1,0:T(8,128)(2,1)S(1)} %get-tuple-element.59.refs_0_, bf16[16,64,768]{2,1,0:T(8,128)(2,1)S(1)} %get-tuple-element.60.refs_1_, bf16[16,64,768]{2,1,0:T(8,128)(2,1)S(1)} %get-tuple-element.61.refs_2_, ...), custom_call_target="tpu_custom_call" | custom-call | flops 1200000000 | bytes 1000000 | tf_op jit(solution)/shard_map/near_queries/pallas_call | solution.py:467
  15.7 0.0 collective-permute-done.a1
  15.7 1.9 %collective-permute-done.2.a3 = bf16[64,640]{1,0:T(8,128)(2,1)S(1)} collective-permute-done((bf16[64,640]{1,0:T(8,128)(2,1)S(1)}, bf16[64,640]{1,0:T(8,128)(2,1)S(1)}, u32[]{:S(2)}, u32[]{:S(2)}) %collective-permute-start.2) | collective-permute-done | bytes 81952 | tf_op jit(solution)/shard_map/ppermute | solution.py:535
  17.7 2.6 %collective-permute-start.6 = (bf16[256,384]{1,0:T(8,128)(2,1)S(1)}, bf16[256,384]{1,0:T(8,128)(2,1)S(1)}, u32[]{:S(2)}, u32[]{:S(2)}) collective-permute-start(bf16[256,384]{1,0:T(8,128)(2,1)S(1)} %pad_maximum_fusion.rest_0_), channel_id=1, source_target_pairs={{0,24},{1,25},{2,26},{3,27},{4,28},{5,29},{6,30},{7,31},{8,16},{9,... | collective-permute-start | bytes 589832 | tf_op jit(solution)/shard_map/ppermute | solution.py:535
  20.2 0.5 %collective-permute-start.5 = (bf16[256,384]{1,0:T(8,128)(2,1)S(1)}, bf16[256,384]{1,0:T(8,128)(2,1)S(1)}, u32[]{:S(2)}, u32[]{:S(2)}) collective-permute-start(bf16[256,384]{1,0:T(8,128)(2,1)S(1)} %pad_maximum_fusion.rest_0_), channel_id=1, source_target_pairs={{0,16},{1,17},{2,18},{3,19},{4,20},{5,21},{6,22},{7,23},{8,24},{9,... | collective-permute-start | bytes 589832 | tf_op jit(solution)/shard_map/ppermute | solution.py:535
  20.7 0.3 collective-permute-start.4
  21.0 7.9 %near_queries.3.refs_1_ = bf16[16,64,512]{2,1,0:T(8,128)(2,1)S(1)} custom-call(s32[2]{0:T(128)S(1)} %pad_add_fusion.meta, bf16[16,64,768]{2,1,0:T(8,128)(2,1)S(1)} %get-tuple-element.59.refs_0_, bf16[16,64,768]{2,1,0:T(8,128)(2,1)S(1)} %get-tuple-element.60.refs_1_, bf16[16,64,768]{2,1,0:T(8,128)(2,1)S(1)} %get-tuple-element.61.refs_2_, ...), custom_call_target="tpu_custom_call" | custom-call | flops 2400000000 | bytes 1000000 | tf_op jit(solution)/shard_map/near_queries/pallas_call | solution.py:467
  28.9 0.0 collective-permute-done.5.rest_2_
  28.9 0.4 collective-permute-done.4.rest_1_
  29.3 1.8 %collective-permute-start.12 = (bf16[2,2,64,768]{3,2,1,0:T(8,128)(2,1)S(1)}, bf16[2,2,64,768]{3,2,1,0:T(8,128)(2,1)S(1)}, u32[]{:S(2)}, u32[]{:S(2)}) collective-permute-start(bf16[2,2,64,768]{3,2,1,0:T(8,128)(2,1)S(1)} %collective-permute-done.7.refs_4_), channel_id=1, source_target_pairs={{0,1},{1,0},{2,3},{3,2},{4,5},{5,4},{6,7},{7,6},{8,9},{9,8},{10,11... | collective-permute-start | bytes 1179656 | tf_op jit(solution)/shard_map/ppermute | solution.py:535
  31.1 0.0 collective-permute-start.8
  31.1 0.5 %collective-permute-start.9 = (bf16[256,384]{1,0:T(8,128)(2,1)S(1)}, bf16[256,384]{1,0:T(8,128)(2,1)S(1)}, u32[]{:S(2)}, u32[]{:S(2)}) collective-permute-start(bf16[256,384]{1,0:T(8,128)(2,1)S(1)} %collective-permute-done.4.rest_1_), channel_id=1, source_target_pairs={{0,1},{1,0},{2,3},{3,2},{4,5},{5,4},{6,7},{7,6},{8,9},{9,8},{10,11... | collective-permute-start | bytes 589832 | tf_op jit(solution)/shard_map/ppermute | solution.py:535
  31.6 0.0 collective-permute-start.10
  31.6 0.5 %collective-permute-start.11 = (bf16[256,384]{1,0:T(8,128)(2,1)S(1)}, bf16[256,384]{1,0:T(8,128)(2,1)S(1)}, u32[]{:S(2)}, u32[]{:S(2)}) collective-permute-start(bf16[256,384]{1,0:T(8,128)(2,1)S(1)} %collective-permute-done.6.rest_3_), channel_id=1, source_target_pairs={{0,1},{1,0},{2,3},{3,2},{4,5},{5,4},{6,7},{7,6},{8,9},{9,8},{10,11... | collective-permute-start | bytes 589832 | tf_op jit(solution)/shard_map/ppermute | solution.py:535
  32.1 0.3 collective-permute-done.12.refs_5_
  32.5 2.0 %wide_queries.2 = (bf16[16,64,256]{2,1,0:T(8,128)(2,1)S(1)}, f32[64,256]{1,0:T(8,128)S(1)}, f32[64,256]{1,0:T(8,128)S(1)}) custom-call(s32[2]{0:T(128)S(1)} %pad_add_fusion.meta, bf16[16,64,768]{2,1,0:T(8,128)(2,1)S(1)} %get-tuple-element.59.refs_0_, bf16[16,64,768]{2,1,0:T(8,128)(2,1)S(1)} %get-tuple-element.60.refs_1_, ...), custom_call_target="tpu_custom_call" | custom-call | flops 400000000 | bytes 1000000 | tf_op jit(solution)/shard_map/wide_queries/pallas_call | solution.py:481
  34.5 0.0 collective-permute-done.10.rest_6_
  34.5 3.4 %slide_queries.1 = (bf16[64,256]{1,0:T(8,128)(2,1)S(1)}, bf16[64,256]{1,0:T(8,128)(2,1)S(1)}, bf16[64,256]{1,0:T(8,128)(2,1)S(1)}, bf16[64,256]{1,0:T(8,128)(2,1)S(1)}) custom-call(s32[2]{0:T(128)S(1)} %pad_add_fusion.meta, bf16[64,640]{1,0:T(8,128)(2,1)S(1)} %get-tuple-element.64.a0, bf16[64,640]{1,0:T(8,128)(2,1)S(1)} %collective-permute-done.a1, ...), custom_call_target="tpu_custom_call" | custom-call | flops 800000000 | bytes 2000000 | tf_op jit(solution)/shard_map/slide_queries/pallas_call | solution.py:499
  37.8 0.1 collective-permute-start.13
  37.9 2.0 %collective-permute-start.14 = (bf16[64,256]{1,0:T(8,128)(2,1)S(1)}, bf16[64,256]{1,0:T(8,128)(2,1)S(1)}, u32[]{:S(2)}, u32[]{:S(2)}) collective-permute-start(bf16[64,256]{1,0:T(8,128)(2,1)S(1)} %get-tuple-element.103), channel_id=1, source_target_pairs={{0,4},{1,5},{2,6},{3,7},{4,0},{5,1},{6,2},{7,3},{8,12},{9,13},{10,... | collective-permute-start | bytes 98312 | tf_op jit(solution)/shard_map/ppermute | solution.py:535
  40.0 1.8 %collective-permute-start.15 = (bf16[64,256]{1,0:T(8,128)(2,1)S(1)}, bf16[64,256]{1,0:T(8,128)(2,1)S(1)}, u32[]{:S(2)}, u32[]{:S(2)}) collective-permute-start(bf16[64,256]{1,0:T(8,128)(2,1)S(1)} %get-tuple-element.104), channel_id=1, source_target_pairs={{0,6},{1,7},{2,4},{3,5},{4,2},{5,3},{6,0},{7,1},{8,14},{9,15},{10,... | collective-permute-start | bytes 98312 | tf_op jit(solution)/shard_map/ppermute | solution.py:535
  41.8 3.2 %wide_queries.3 = (bf16[16,64,512]{2,1,0:T(8,128)(2,1)S(1)}, f32[64,512]{1,0:T(8,128)S(1)}, f32[64,512]{1,0:T(8,128)S(1)}) custom-call(s32[2]{0:T(128)S(1)} %pad_add_fusion.meta, bf16[16,64,768]{2,1,0:T(8,128)(2,1)S(1)} %get-tuple-element.59.refs_0_, bf16[16,64,768]{2,1,0:T(8,128)(2,1)S(1)} %get-tuple-element.60.refs_1_, ...), custom_call_target="tpu_custom_call" | custom-call | flops 800000000 | bytes 1000000 | tf_op jit(solution)/shard_map/wide_queries/pallas_call | solution.py:481
  45.0 0.0 collective-permute-done.13.refs_9_
  45.0 0.0 collective-permute-done.14.refs_10_
  45.0 2.5 %merge_rows.1 = bf16[1024,768]{1,0:T(8,128)(2,1)} custom-call(s32[2]{0:T(128)S(1)} %pad_add_fusion.meta, bf16[16,64,256]{2,1,0:T(8,128)(2,1)S(1)} %near_queries.2.refs_0_, bf16[16,64,512]{2,1,0:T(8,128)(2,1)S(1)} %near_queries.3.refs_1_, bf16[16,64,256]{2,1,0:T(8,128)(2,1)S(1)} %get-tuple-element.81.refs_2_, ...), custom_call_target="tpu_custom_call" | custom-call | tf_op jit(solution)/shard_map/merge_rows/pallas_call | solution.py:511
  (13 shorter events, 0.1 us)
Async XLA Ops:
  4.8 6.6 %collective-permute-start.3 = (bf16[4,2,64,768]{3,2,1,0:T(8,128)(2,1)S(1)}, bf16[4,2,64,768]{3,2,1,0:T(8,128)(2,1)S(1)}, u32[]{:S(2)}, u32[]{:S(2)}) collective-permute-start(bf16[4,2,64,768]{3,2,1,0:T(8,128)(2,1)S(1)} %get-tuple-element.62), channel_id=1, source_target_pairs={{0,1},{1,0},{2,3},{3,2},{4,5},{5,4},{6,7},{7,6},{8,9},{9,8},{10,11... | collective-permute-start | bytes 2359304 | tf_op jit(solution)/shard_map/ppermute | solution.py:535
  6.3 9.3 %collective-permute-start = (bf16[64,640]{1,0:T(8,128)(2,1)S(1)}, bf16[64,640]{1,0:T(8,128)(2,1)S(1)}, u32[]{:S(2)}, u32[]{:S(2)}) collective-permute-start(bf16[64,640]{1,0:T(8,128)(2,1)S(1)} %get-tuple-element.56), channel_id=1, source_target_pairs={{0,2},{1,3},{2,0},{3,1},{4,6},{5,7},{6,4},{7,5},{8,10},{9,11},{10,... | collective-permute-start | bytes 245768 | tf_op jit(solution)/shard_map/ppermute | solution.py:535
  8.0 7.6 %collective-permute-start.1 = (bf16[64,640]{1,0:T(8,128)(2,1)S(1)}, bf16[64,640]{1,0:T(8,128)(2,1)S(1)}, u32[]{:S(2)}, u32[]{:S(2)}) collective-permute-start(bf16[64,640]{1,0:T(8,128)(2,1)S(1)} %get-tuple-element.57), channel_id=1, source_target_pairs={{0,4},{1,5},{2,6},{3,7},{4,0},{5,1},{6,2},{7,3},{8,12},{9,13},{10,... | collective-permute-start | bytes 245768 | tf_op jit(solution)/shard_map/ppermute | solution.py:535
  11.4 6.2 %collective-permute-start.2 = (bf16[64,640]{1,0:T(8,128)(2,1)S(1)}, bf16[64,640]{1,0:T(8,128)(2,1)S(1)}, u32[]{:S(2)}, u32[]{:S(2)}) collective-permute-start(bf16[64,640]{1,0:T(8,128)(2,1)S(1)} %get-tuple-element.58), channel_id=1, source_target_pairs={{0,6},{1,7},{2,4},{3,5},{4,2},{5,3},{6,0},{7,1},{8,14},{9,15},{10,... | collective-permute-start | bytes 245768 | tf_op jit(solution)/shard_map/ppermute | solution.py:535
  11.4 17.5 %collective-permute-start.7 = (bf16[2,2,64,768]{3,2,1,0:T(8,128)(2,1)S(1)}, bf16[2,2,64,768]{3,2,1,0:T(8,128)(2,1)S(1)}, u32[]{:S(2)}, u32[]{:S(2)}) collective-permute-start(bf16[2,2,64,768]{3,2,1,0:T(8,128)(2,1)S(1)} %get-tuple-element.70), channel_id=1, source_target_pairs={{0,2},{1,3},{2,0},{3,1},{4,6},{5,7},{6,4},{7,5},{8,10},{9,11},{10,... | collective-permute-start | bytes 1179656 | tf_op jit(solution)/shard_map/ppermute | solution.py:535
  17.7 11.2 %collective-permute-start.6 = (bf16[256,384]{1,0:T(8,128)(2,1)S(1)}, bf16[256,384]{1,0:T(8,128)(2,1)S(1)}, u32[]{:S(2)}, u32[]{:S(2)}) collective-permute-start(bf16[256,384]{1,0:T(8,128)(2,1)S(1)} %pad_maximum_fusion.rest_0_), channel_id=1, source_target_pairs={{0,24},{1,25},{2,26},{3,27},{4,28},{5,29},{6,30},{7,31},{8,16},{9,... | collective-permute-start | bytes 589832 | tf_op jit(solution)/shard_map/ppermute | solution.py:535
  20.2 8.7 %collective-permute-start.5 = (bf16[256,384]{1,0:T(8,128)(2,1)S(1)}, bf16[256,384]{1,0:T(8,128)(2,1)S(1)}, u32[]{:S(2)}, u32[]{:S(2)}) collective-permute-start(bf16[256,384]{1,0:T(8,128)(2,1)S(1)} %pad_maximum_fusion.rest_0_), channel_id=1, source_target_pairs={{0,16},{1,17},{2,18},{3,19},{4,20},{5,21},{6,22},{7,23},{8,24},{9,... | collective-permute-start | bytes 589832 | tf_op jit(solution)/shard_map/ppermute | solution.py:535
  20.7 8.6 %collective-permute-start.4 = (bf16[256,384]{1,0:T(8,128)(2,1)S(1)}, bf16[256,384]{1,0:T(8,128)(2,1)S(1)}, u32[]{:S(2)}, u32[]{:S(2)}) collective-permute-start(bf16[256,384]{1,0:T(8,128)(2,1)S(1)} %pad_maximum_fusion.rest_0_), channel_id=1, source_target_pairs={{0,8},{1,9},{2,10},{3,11},{4,12},{5,13},{6,14},{7,15},{8,0},{9,1},... | collective-permute-start | bytes 589832 | tf_op jit(solution)/shard_map/ppermute | solution.py:535
  29.3 3.2 %collective-permute-start.12 = (bf16[2,2,64,768]{3,2,1,0:T(8,128)(2,1)S(1)}, bf16[2,2,64,768]{3,2,1,0:T(8,128)(2,1)S(1)}, u32[]{:S(2)}, u32[]{:S(2)}) collective-permute-start(bf16[2,2,64,768]{3,2,1,0:T(8,128)(2,1)S(1)} %collective-permute-done.7.refs_4_), channel_id=1, source_target_pairs={{0,1},{1,0},{2,3},{3,2},{4,5},{5,4},{6,7},{7,6},{8,9},{9,8},{10,11... | collective-permute-start | bytes 1179656 | tf_op jit(solution)/shard_map/ppermute | solution.py:535
  31.1 3.3 %collective-permute-start.8 = (bf16[256,384]{1,0:T(8,128)(2,1)S(1)}, bf16[256,384]{1,0:T(8,128)(2,1)S(1)}, u32[]{:S(2)}, u32[]{:S(2)}) collective-permute-start(bf16[256,384]{1,0:T(8,128)(2,1)S(1)} %pad_maximum_fusion.rest_0_), channel_id=1, source_target_pairs={{0,1},{1,0},{2,3},{3,2},{4,5},{5,4},{6,7},{7,6},{8,9},{9,8},{10,11... | collective-permute-start | bytes 589832 | tf_op jit(solution)/shard_map/ppermute | solution.py:535
  31.1 3.3 %collective-permute-start.9 = (bf16[256,384]{1,0:T(8,128)(2,1)S(1)}, bf16[256,384]{1,0:T(8,128)(2,1)S(1)}, u32[]{:S(2)}, u32[]{:S(2)}) collective-permute-start(bf16[256,384]{1,0:T(8,128)(2,1)S(1)} %collective-permute-done.4.rest_1_), channel_id=1, source_target_pairs={{0,1},{1,0},{2,3},{3,2},{4,5},{5,4},{6,7},{7,6},{8,9},{9,8},{10,11... | collective-permute-start | bytes 589832 | tf_op jit(solution)/shard_map/ppermute | solution.py:535
  31.6 2.8 %collective-permute-start.10 = (bf16[256,384]{1,0:T(8,128)(2,1)S(1)}, bf16[256,384]{1,0:T(8,128)(2,1)S(1)}, u32[]{:S(2)}, u32[]{:S(2)}) collective-permute-start(bf16[256,384]{1,0:T(8,128)(2,1)S(1)} %collective-permute-done.5.rest_2_), channel_id=1, source_target_pairs={{0,1},{1,0},{2,3},{3,2},{4,5},{5,4},{6,7},{7,6},{8,9},{9,8},{10,11... | collective-permute-start | bytes 589832 | tf_op jit(solution)/shard_map/ppermute | solution.py:535
  31.6 2.9 %collective-permute-start.11 = (bf16[256,384]{1,0:T(8,128)(2,1)S(1)}, bf16[256,384]{1,0:T(8,128)(2,1)S(1)}, u32[]{:S(2)}, u32[]{:S(2)}) collective-permute-start(bf16[256,384]{1,0:T(8,128)(2,1)S(1)} %collective-permute-done.6.rest_3_), channel_id=1, source_target_pairs={{0,1},{1,0},{2,3},{3,2},{4,5},{5,4},{6,7},{7,6},{8,9},{9,8},{10,11... | collective-permute-start | bytes 589832 | tf_op jit(solution)/shard_map/ppermute | solution.py:535
  37.8 7.1 %collective-permute-start.13 = (bf16[64,256]{1,0:T(8,128)(2,1)S(1)}, bf16[64,256]{1,0:T(8,128)(2,1)S(1)}, u32[]{:S(2)}, u32[]{:S(2)}) collective-permute-start(bf16[64,256]{1,0:T(8,128)(2,1)S(1)} %get-tuple-element.102), channel_id=1, source_target_pairs={{0,2},{1,3},{2,0},{3,1},{4,6},{5,7},{6,4},{7,5},{8,10},{9,11},{10,... | collective-permute-start | bytes 98312 | tf_op jit(solution)/shard_map/ppermute | solution.py:535
  37.9 7.1 %collective-permute-start.14 = (bf16[64,256]{1,0:T(8,128)(2,1)S(1)}, bf16[64,256]{1,0:T(8,128)(2,1)S(1)}, u32[]{:S(2)}, u32[]{:S(2)}) collective-permute-start(bf16[64,256]{1,0:T(8,128)(2,1)S(1)} %get-tuple-element.103), channel_id=1, source_target_pairs={{0,4},{1,5},{2,6},{3,7},{4,0},{5,1},{6,2},{7,3},{8,12},{9,13},{10,... | collective-permute-start | bytes 98312 | tf_op jit(solution)/shard_map/ppermute | solution.py:535
  40.0 5.0 %collective-permute-start.15 = (bf16[64,256]{1,0:T(8,128)(2,1)S(1)}, bf16[64,256]{1,0:T(8,128)(2,1)S(1)}, u32[]{:S(2)}, u32[]{:S(2)}) collective-permute-start(bf16[64,256]{1,0:T(8,128)(2,1)S(1)} %get-tuple-element.104), channel_id=1, source_target_pairs={{0,6},{1,7},{2,4},{3,5},{4,2},{5,3},{6,0},{7,1},{8,14},{9,15},{10,... | collective-permute-start | bytes 98312 | tf_op jit(solution)/shard_map/ppermute | solution.py:535

commit v11 on v10

--- a/solution.py
+++ b/solution.py
@@ -565,8 +565,8 @@
     own, later = lax.optimization_barrier((own, later))
     moved = [move(own, along_x(step)) for step in (1, 2, 3)]
     close.append(local_near(*NEAR_PARTS[1], later, *local))
-    moved, near, close[1], later = lax.optimization_barrier((moved, near, close[1], later))
     cross = move(near, other_core)
+    moved, close[1], later = lax.optimization_barrier((moved, close[1], later))
     blocks = [own] + moved
     blocks += [move(block, other_core) for block in blocks]
     wide = [local_far(*WIDE_PARTS[0], later, *local, near, cross)]

time: 47.8 us -> 54.6 us (1.14)
  waiting for transfers between devices: 2.66 us -> 7.92 us
  starting transfers between devices: 16.6 us -> 18.2 us
    ppermute x16, waiting for transfers between devices: 2.66 us -> 7.92 us  [move(): return lax.ppermute(block, 'seq', route)]
    ppermute x16, starting transfers between devices: 16.6 us -> 18.2 us  [move(): return lax.ppermute(block, 'seq', route)]
  transfers between devices with their start and end apart: 16 -> 16, of which waited for: 3 -> 4; matrix products, arithmetic and copies ran while one was open for 0% -> 0% of each run, Pallas kernels for 36% -> 32%
where the time goes in v11:
time: 54.6 us; the launch traced here: 54.4 us
  Pallas kernels  27.2 us (50%)
  starting transfers between devices  18.2 us (33%)
  waiting for transfers between devices  7.92 us (15%)
  between operations  1 us (2%)
    ppermute x16, starting transfers between devices, move(): return lax.ppermute(block, 'seq', route)  18.2 us
    pallas_call x2, Pallas kernels, local_near(): pl.pallas_call(functools.partial(local_kernel, 'ABC', first, many), in_sp...  12.2 us
    ppermute x16, waiting for transfers between devices, move(): return lax.ppermute(block, 'seq', route)  7.92 us
    pallas_call x2, Pallas kernels, local_far(): pl.pallas_call(functools.partial(local_kernel, 'D', first, many), in_spec...  5.18 us
    pallas_call x1, Pallas kernels, split(): pl.pallas_call(split_kernel, in_specs=[smem()] + [pl.BlockSpec(memory_spa...  4.07 us
    pallas_call x1, Pallas kernels, slide_wide(): pl.pallas_call(far_kernel, in_specs=[smem()] + [vmem()] * 12, out_specs=[...  3.35 us
    pallas_call x1, Pallas kernels, merge(): pl.pallas_call(merge_kernel, in_specs=[smem()] + [vmem()] * (len(NEAR_PAR...  2.48 us
  transfers between devices with their start and end apart: 16, of which 4 were waited for; matrix products, arithmetic and copies ran while one was open for 0% of the time, Pallas kernels for 32%

profile of v11, /device:TPU:1, one launch (start us, length us, event | category | flops | bytes accessed | tf_op | source)
XLA Modules:
  0.0 54.4 jit_solution(8609960702340766129)
XLA Ops:
  0.7 0.1 pad_add_fusion.meta
  0.7 4.1 %split_rows.1 = (bf16[16,64,768]{2,1,0:T(8,128)(2,1)S(1)}, bf16[16,64,768]{2,1,0:T(8,128)(2,1)S(1)}, bf16[16,64,768]{2,1,0:T(8,128)(2,1)S(1)}, bf16[4,2,64,768]{...) custom-call(s32[2]{0:T(128)S(1)} %pad_add_fusion.meta, ...), custom_call_target="tpu_custom_call" | custom-call | tf_op jit(solution)/shard_map/split_rows/pallas_call | solution.py:449
  4.8 1.5 %collective-permute-start.3 = (bf16[4,2,64,768]{3,2,1,0:T(8,128)(2,1)S(1)}, bf16[4,2,64,768]{3,2,1,0:T(8,128)(2,1)S(1)}, u32[]{:S(2)}, u32[]{:S(2)}) collective-permute-start(bf16[4,2,64,768]{3,2,1,0:T(8,128)(2,1)S(1)} %get-tuple-element.61), channel_id=1, source_target_pairs={{0,1},{1,0},{2,3},{3,2},{4,5},{5,4},{6,7},{7,6},{8,9},{9,8},{10,11... | collective-permute-start | bytes 2359304 | tf_op jit(solution)/shard_map/ppermute | solution.py:535
  6.3 1.7 %collective-permute-start.11 = (bf16[2,2,64,768]{3,2,1,0:T(8,128)(2,1)S(1)}, bf16[2,2,64,768]{3,2,1,0:T(8,128)(2,1)S(1)}, u32[]{:S(2)}, u32[]{:S(2)}) collective-permute-start(bf16[2,2,64,768]{3,2,1,0:T(8,128)(2,1)S(1)} %get-tuple-element.75), channel_id=1, source_target_pairs={{0,2},{1,3},{2,0},{3,1},{4,6},{5,7},{6,4},{7,5},{8,10},{9,11},{10,... | collective-permute-start | bytes 1179656 | tf_op jit(solution)/shard_map/ppermute | solution.py:535
  8.0 0.0 collective-permute-start
  8.1 3.4 %collective-permute-start.1 = (bf16[64,640]{1,0:T(8,128)(2,1)S(1)}, bf16[64,640]{1,0:T(8,128)(2,1)S(1)}, u32[]{:S(2)}, u32[]{:S(2)}) collective-permute-start(bf16[64,640]{1,0:T(8,128)(2,1)S(1)} %get-tuple-element.56), channel_id=1, source_target_pairs={{0,4},{1,5},{2,6},{3,7},{4,0},{5,1},{6,2},{7,3},{8,12},{9,13},{10,... | collective-permute-start | bytes 245768 | tf_op jit(solution)/shard_map/ppermute | solution.py:535
  11.5 0.4 collective-permute-start.2
  11.9 5.5 %collective-permute-done.11.refs_4_ = bf16[2,2,64,768]{3,2,1,0:T(8,128)(2,1)S(1)} collective-permute-done((bf16[2,2,64,768]{3,2,1,0:T(8,128)(2,1)S(1)}, bf16[2,2,64,768]{3,2,1,0:T(8,128)(2,1)S(1)}, u32[]{:S(2)}, u32[]{:S(2)}) %collective-permute-start.11) | collective-permute-done | bytes 393248 | tf_op jit(solution)/shard_map/ppermute | solution.py:535
  17.4 1.0 %collective-permute-start.12 = (bf16[2,2,64,768]{3,2,1,0:T(8,128)(2,1)S(1)}, bf16[2,2,64,768]{3,2,1,0:T(8,128)(2,1)S(1)}, u32[]{:S(2)}, u32[]{:S(2)}) collective-permute-start(bf16[2,2,64,768]{3,2,1,0:T(8,128)(2,1)S(1)} %collective-permute-done.11.refs_4_), channel_id=1, source_target_pairs={{0,1},{1,0},{2,3},{3,2},{4,5},{5,4},{6,7},{7,6},{8,9},{9,8},{10,11... | collective-permute-start | bytes 1179656 | tf_op jit(solution)/shard_map/ppermute | solution.py:535
  18.4 4.3 %near_queries.2.refs_0_ = bf16[16,64,256]{2,1,0:T(8,128)(2,1)S(1)} custom-call(s32[2]{0:T(128)S(1)} %pad_add_fusion.meta, bf16[16,64,768]{2,1,0:T(8,128)(2,1)S(1)} %get-tuple-element.58.refs_0_, bf16[16,64,768]{2,1,0:T(8,128)(2,1)S(1)} %get-tuple-element.59.refs_1_, bf16[16,64,768]{2,1,0:T(8,128)(2,1)S(1)} %get-tuple-element.60.refs_2_, ...), custom_call_target="tpu_custom_call" | custom-call | flops 1200000000 | bytes 1000000 | tf_op jit(solution)/shard_map/near_queries/pallas_call | solution.py:467
  22.7 1.4 %collective-permute-done.1.a2 = bf16[64,640]{1,0:T(8,128)(2,1)S(1)} collective-permute-done((bf16[64,640]{1,0:T(8,128)(2,1)S(1)}, bf16[64,640]{1,0:T(8,128)(2,1)S(1)}, u32[]{:S(2)}, u32[]{:S(2)}) %collective-permute-start.1) | collective-permute-done | bytes 81952 | tf_op jit(solution)/shard_map/ppermute | solution.py:535
  24.1 1.0 %collective-permute-start.7 = (bf16[256,384]{1,0:T(8,128)(2,1)S(1)}, bf16[256,384]{1,0:T(8,128)(2,1)S(1)}, u32[]{:S(2)}, u32[]{:S(2)}) collective-permute-start(bf16[256,384]{1,0:T(8,128)(2,1)S(1)} %pad_maximum_fusion.rest_0_), channel_id=1, source_target_pairs={{0,1},{1,0},{2,3},{3,2},{4,5},{5,4},{6,7},{7,6},{8,9},{9,8},{10,11... | collective-permute-start | bytes 589832 | tf_op jit(solution)/shard_map/ppermute | solution.py:535
  25.1 2.5 %collective-permute-start.6 = (bf16[256,384]{1,0:T(8,128)(2,1)S(1)}, bf16[256,384]{1,0:T(8,128)(2,1)S(1)}, u32[]{:S(2)}, u32[]{:S(2)}) collective-permute-start(bf16[256,384]{1,0:T(8,128)(2,1)S(1)} %pad_maximum_fusion.rest_0_), channel_id=1, source_target_pairs={{0,24},{1,25},{2,26},{3,27},{4,28},{5,29},{6,30},{7,31},{8,16},{9,... | collective-permute-start | bytes 589832 | tf_op jit(solution)/shard_map/ppermute | solution.py:535
  27.6 0.5 collective-permute-start.5
  28.1 0.3 collective-permute-start.4
  28.4 7.9 %near_queries.3.refs_1_ = bf16[16,64,512]{2,1,0:T(8,128)(2,1)S(1)} custom-call(s32[2]{0:T(128)S(1)} %pad_add_fusion.meta, bf16[16,64,768]{2,1,0:T(8,128)(2,1)S(1)} %get-tuple-element.58.refs_0_, bf16[16,64,768]{2,1,0:T(8,128)(2,1)S(1)} %get-tuple-element.59.refs_1_, bf16[16,64,768]{2,1,0:T(8,128)(2,1)S(1)} %get-tuple-element.60.refs_2_, ...), custom_call_target="tpu_custom_call" | custom-call | flops 2400000000 | bytes 1000000 | tf_op jit(solution)/shard_map/near_queries/pallas_call | solution.py:467
  36.2 0.7 %collective-permute-done.6.rest_3_ = bf16[256,384]{1,0:T(8,128)(2,1)S(1)} collective-permute-done((bf16[256,384]{1,0:T(8,128)(2,1)S(1)}, bf16[256,384]{1,0:T(8,128)(2,1)S(1)}, u32[]{:S(2)}, u32[]{:S(2)}) %collective-permute-start.6) | collective-permute-done | bytes 196640 | tf_op jit(solution)/shard_map/ppermute | solution.py:535
  37.0 0.0 collective-permute-done.5.rest_2_
  37.0 0.3 collective-permute-done.4.rest_1_
  37.3 1.2 %collective-permute-start.8 = (bf16[256,384]{1,0:T(8,128)(2,1)S(1)}, bf16[256,384]{1,0:T(8,128)(2,1)S(1)}, u32[]{:S(2)}, u32[]{:S(2)}) collective-permute-start(bf16[256,384]{1,0:T(8,128)(2,1)S(1)} %collective-permute-done.4.rest_1_), channel_id=1, source_target_pairs={{0,1},{1,0},{2,3},{3,2},{4,5},{5,4},{6,7},{7,6},{8,9},{9,8},{10,11... | collective-permute-start | bytes 589832 | tf_op jit(solution)/shard_map/ppermute | solution.py:535
  38.5 0.0 collective-permute-start.9
  38.5 0.5 collective-permute-start.10
  39.0 2.0 %wide_queries.2 = (bf16[16,64,256]{2,1,0:T(8,128)(2,1)S(1)}, f32[64,256]{1,0:T(8,128)S(1)}, f32[64,256]{1,0:T(8,128)S(1)}) custom-call(s32[2]{0:T(128)S(1)} %pad_add_fusion.meta, bf16[16,64,768]{2,1,0:T(8,128)(2,1)S(1)} %get-tuple-element.58.refs_0_, bf16[16,64,768]{2,1,0:T(8,128)(2,1)S(1)} %get-tuple-element.59.refs_1_, ...), custom_call_target="tpu_custom_call" | custom-call | flops 400000000 | bytes 1000000 | tf_op jit(solution)/shard_map/wide_queries/pallas_call | solution.py:481
  41.0 0.0 collective-permute-done.8.rest_5_
  41.0 0.0 collective-permute-done.9.rest_6_
  41.0 3.4 %slide_queries.1 = (bf16[64,256]{1,0:T(8,128)(2,1)S(1)}, bf16[64,256]{1,0:T(8,128)(2,1)S(1)}, bf16[64,256]{1,0:T(8,128)(2,1)S(1)}, bf16[64,256]{1,0:T(8,128)(2,1)S(1)}) custom-call(s32[2]{0:T(128)S(1)} %pad_add_fusion.meta, bf16[64,640]{1,0:T(8,128)(2,1)S(1)} %get-tuple-element.63.a0, bf16[64,640]{1,0:T(8,128)(2,1)S(1)} %collective-permute-done.a1, ...), custom_call_target="tpu_custom_call" | custom-call | flops 800000000 | bytes 2000000 | tf_op jit(solution)/shard_map/slide_queries/pallas_call | solution.py:499
  44.4 0.3 collective-permute-start.13
  44.7 2.8 %collective-permute-start.14 = (bf16[64,256]{1,0:T(8,128)(2,1)S(1)}, bf16[64,256]{1,0:T(8,128)(2,1)S(1)}, u32[]{:S(2)}, u32[]{:S(2)}) collective-permute-start(bf16[64,256]{1,0:T(8,128)(2,1)S(1)} %get-tuple-element.101), channel_id=1, source_target_pairs={{0,4},{1,5},{2,6},{3,7},{4,0},{5,1},{6,2},{7,3},{8,12},{9,13},{10,... | collective-permute-start | bytes 98312 | tf_op jit(solution)/shard_map/ppermute | solution.py:535
  47.5 1.0 %collective-permute-start.15 = (bf16[64,256]{1,0:T(8,128)(2,1)S(1)}, bf16[64,256]{1,0:T(8,128)(2,1)S(1)}, u32[]{:S(2)}, u32[]{:S(2)}) collective-permute-start(bf16[64,256]{1,0:T(8,128)(2,1)S(1)} %get-tuple-element.102), channel_id=1, source_target_pairs={{0,6},{1,7},{2,4},{3,5},{4,2},{5,3},{6,0},{7,1},{8,14},{9,15},{10,... | collective-permute-start | bytes 98312 | tf_op jit(solution)/shard_map/ppermute | solution.py:535
  48.5 3.2 %wide_queries.3 = (bf16[16,64,512]{2,1,0:T(8,128)(2,1)S(1)}, f32[64,512]{1,0:T(8,128)S(1)}, f32[64,512]{1,0:T(8,128)S(1)}) custom-call(s32[2]{0:T(128)S(1)} %pad_add_fusion.meta, bf16[16,64,768]{2,1,0:T(8,128)(2,1)S(1)} %get-tuple-element.58.refs_0_, bf16[16,64,768]{2,1,0:T(8,128)(2,1)S(1)} %get-tuple-element.59.refs_1_, ...), custom_call_target="tpu_custom_call" | custom-call | flops 800000000 | bytes 1000000 | tf_op jit(solution)/shard_map/wide_queries/pallas_call | solution.py:481
  51.7 0.0 collective-permute-done.13.refs_9_
  51.8 2.5 %merge_rows.1 = bf16[1024,768]{1,0:T(8,128)(2,1)} custom-call(s32[2]{0:T(128)S(1)} %pad_add_fusion.meta, bf16[16,64,256]{2,1,0:T(8,128)(2,1)S(1)} %near_queries.2.refs_0_, bf16[16,64,512]{2,1,0:T(8,128)(2,1)S(1)} %near_queries.3.refs_1_, bf16[16,64,256]{2,1,0:T(8,128)(2,1)S(1)} %get-tuple-element.79.refs_2_, ...), custom_call_target="tpu_custom_call" | custom-call | tf_op jit(solution)/shard_map/merge_rows/pallas_call | solution.py:511
  (13 shorter events, 0.1 us)
Async XLA Ops:
  4.8 13.6 %collective-permute-start.3 = (bf16[4,2,64,768]{3,2,1,0:T(8,128)(2,1)S(1)}, bf16[4,2,64,768]{3,2,1,0:T(8,128)(2,1)S(1)}, u32[]{:S(2)}, u32[]{:S(2)}) collective-permute-start(bf16[4,2,64,768]{3,2,1,0:T(8,128)(2,1)S(1)} %get-tuple-element.61), channel_id=1, source_target_pairs={{0,1},{1,0},{2,3},{3,2},{4,5},{5,4},{6,7},{7,6},{8,9},{9,8},{10,11... | collective-permute-start | bytes 2359304 | tf_op jit(solution)/shard_map/ppermute | solution.py:535
  6.3 11.1 %collective-permute-start.11 = (bf16[2,2,64,768]{3,2,1,0:T(8,128)(2,1)S(1)}, bf16[2,2,64,768]{3,2,1,0:T(8,128)(2,1)S(1)}, u32[]{:S(2)}, u32[]{:S(2)}) collective-permute-start(bf16[2,2,64,768]{3,2,1,0:T(8,128)(2,1)S(1)} %get-tuple-element.75), channel_id=1, source_target_pairs={{0,2},{1,3},{2,0},{3,1},{4,6},{5,7},{6,4},{7,5},{8,10},{9,11},{10,... | collective-permute-start | bytes 1179656 | tf_op jit(solution)/shard_map/ppermute | solution.py:535
  8.0 14.6 %collective-permute-start = (bf16[64,640]{1,0:T(8,128)(2,1)S(1)}, bf16[64,640]{1,0:T(8,128)(2,1)S(1)}, u32[]{:S(2)}, u32[]{:S(2)}) collective-permute-start(bf16[64,640]{1,0:T(8,128)(2,1)S(1)} %get-tuple-element.55), channel_id=1, source_target_pairs={{0,2},{1,3},{2,0},{3,1},{4,6},{5,7},{6,4},{7,5},{8,10},{9,11},{10,... | collective-permute-start | bytes 245768 | tf_op jit(solution)/shard_map/ppermute | solution.py:535
  8.1 16.0 %collective-permute-start.1 = (bf16[64,640]{1,0:T(8,128)(2,1)S(1)}, bf16[64,640]{1,0:T(8,128)(2,1)S(1)}, u32[]{:S(2)}, u32[]{:S(2)}) collective-permute-start(bf16[64,640]{1,0:T(8,128)(2,1)S(1)} %get-tuple-element.56), channel_id=1, source_target_pairs={{0,4},{1,5},{2,6},{3,7},{4,0},{5,1},{6,2},{7,3},{8,12},{9,13},{10,... | collective-permute-start | bytes 245768 | tf_op jit(solution)/shard_map/ppermute | solution.py:535
  11.5 12.6 %collective-permute-start.2 = (bf16[64,640]{1,0:T(8,128)(2,1)S(1)}, bf16[64,640]{1,0:T(8,128)(2,1)S(1)}, u32[]{:S(2)}, u32[]{:S(2)}) collective-permute-start(bf16[64,640]{1,0:T(8,128)(2,1)S(1)} %get-tuple-element.57), channel_id=1, source_target_pairs={{0,6},{1,7},{2,4},{3,5},{4,2},{5,3},{6,0},{7,1},{8,14},{9,15},{10,... | collective-permute-start | bytes 245768 | tf_op jit(solution)/shard_map/ppermute | solution.py:535
  17.4 21.6 %collective-permute-start.12 = (bf16[2,2,64,768]{3,2,1,0:T(8,128)(2,1)S(1)}, bf16[2,2,64,768]{3,2,1,0:T(8,128)(2,1)S(1)}, u32[]{:S(2)}, u32[]{:S(2)}) collective-permute-start(bf16[2,2,64,768]{3,2,1,0:T(8,128)(2,1)S(1)} %collective-permute-done.11.refs_4_), channel_id=1, source_target_pairs={{0,1},{1,0},{2,3},{3,2},{4,5},{5,4},{6,7},{7,6},{8,9},{9,8},{10,11... | collective-permute-start | bytes 1179656 | tf_op jit(solution)/shard_map/ppermute | solution.py:535
  24.1 16.8 %collective-permute-start.7 = (bf16[256,384]{1,0:T(8,128)(2,1)S(1)}, bf16[256,384]{1,0:T(8,128)(2,1)S(1)}, u32[]{:S(2)}, u32[]{:S(2)}) collective-permute-start(bf16[256,384]{1,0:T(8,128)(2,1)S(1)} %pad_maximum_fusion.rest_0_), channel_id=1, source_target_pairs={{0,1},{1,0},{2,3},{3,2},{4,5},{5,4},{6,7},{7,6},{8,9},{9,8},{10,11... | collective-permute-start | bytes 589832 | tf_op jit(solution)/shard_map/ppermute | solution.py:535
  25.1 11.9 %collective-permute-start.6 = (bf16[256,384]{1,0:T(8,128)(2,1)S(1)}, bf16[256,384]{1,0:T(8,128)(2,1)S(1)}, u32[]{:S(2)}, u32[]{:S(2)}) collective-permute-start(bf16[256,384]{1,0:T(8,128)(2,1)S(1)} %pad_maximum_fusion.rest_0_), channel_id=1, source_target_pairs={{0,24},{1,25},{2,26},{3,27},{4,28},{5,29},{6,30},{7,31},{8,16},{9,... | collective-permute-start | bytes 589832 | tf_op jit(solution)/shard_map/ppermute | solution.py:535
  27.6 9.4 %collective-permute-start.5 = (bf16[256,384]{1,0:T(8,128)(2,1)S(1)}, bf16[256,384]{1,0:T(8,128)(2,1)S(1)}, u32[]{:S(2)}, u32[]{:S(2)}) collective-permute-start(bf16[256,384]{1,0:T(8,128)(2,1)S(1)} %pad_maximum_fusion.rest_0_), channel_id=1, source_target_pairs={{0,16},{1,17},{2,18},{3,19},{4,20},{5,21},{6,22},{7,23},{8,24},{9,... | collective-permute-start | bytes 589832 | tf_op jit(solution)/shard_map/ppermute | solution.py:535
  28.1 9.2 %collective-permute-start.4 = (bf16[256,384]{1,0:T(8,128)(2,1)S(1)}, bf16[256,384]{1,0:T(8,128)(2,1)S(1)}, u32[]{:S(2)}, u32[]{:S(2)}) collective-permute-start(bf16[256,384]{1,0:T(8,128)(2,1)S(1)} %pad_maximum_fusion.rest_0_), channel_id=1, source_target_pairs={{0,8},{1,9},{2,10},{3,11},{4,12},{5,13},{6,14},{7,15},{8,0},{9,1},... | collective-permute-start | bytes 589832 | tf_op jit(solution)/shard_map/ppermute | solution.py:535
  37.3 3.7 %collective-permute-start.8 = (bf16[256,384]{1,0:T(8,128)(2,1)S(1)}, bf16[256,384]{1,0:T(8,128)(2,1)S(1)}, u32[]{:S(2)}, u32[]{:S(2)}) collective-permute-start(bf16[256,384]{1,0:T(8,128)(2,1)S(1)} %collective-permute-done.4.rest_1_), channel_id=1, source_target_pairs={{0,1},{1,0},{2,3},{3,2},{4,5},{5,4},{6,7},{7,6},{8,9},{9,8},{10,11... | collective-permute-start | bytes 589832 | tf_op jit(solution)/shard_map/ppermute | solution.py:535
  38.5 2.5 %collective-permute-start.9 = (bf16[256,384]{1,0:T(8,128)(2,1)S(1)}, bf16[256,384]{1,0:T(8,128)(2,1)S(1)}, u32[]{:S(2)}, u32[]{:S(2)}) collective-permute-start(bf16[256,384]{1,0:T(8,128)(2,1)S(1)} %collective-permute-done.5.rest_2_), channel_id=1, source_target_pairs={{0,1},{1,0},{2,3},{3,2},{4,5},{5,4},{6,7},{7,6},{8,9},{9,8},{10,11... | collective-permute-start | bytes 589832 | tf_op jit(solution)/shard_map/ppermute | solution.py:535
  38.5 2.5 %collective-permute-start.10 = (bf16[256,384]{1,0:T(8,128)(2,1)S(1)}, bf16[256,384]{1,0:T(8,128)(2,1)S(1)}, u32[]{:S(2)}, u32[]{:S(2)}) collective-permute-start(bf16[256,384]{1,0:T(8,128)(2,1)S(1)} %collective-permute-done.6.rest_3_), channel_id=1, source_target_pairs={{0,1},{1,0},{2,3},{3,2},{4,5},{5,4},{6,7},{7,6},{8,9},{9,8},{10,11... | collective-permute-start | bytes 589832 | tf_op jit(solution)/shard_map/ppermute | solution.py:535
  44.4 7.4 %collective-permute-start.13 = (bf16[64,256]{1,0:T(8,128)(2,1)S(1)}, bf16[64,256]{1,0:T(8,128)(2,1)S(1)}, u32[]{:S(2)}, u32[]{:S(2)}) collective-permute-start(bf16[64,256]{1,0:T(8,128)(2,1)S(1)} %get-tuple-element.100), channel_id=1, source_target_pairs={{0,2},{1,3},{2,0},{3,1},{4,6},{5,7},{6,4},{7,5},{8,10},{9,11},{10,... | collective-permute-start | bytes 98312 | tf_op jit(solution)/shard_map/ppermute | solution.py:535
  44.7 7.1 %collective-permute-start.14 = (bf16[64,256]{1,0:T(8,128)(2,1)S(1)}, bf16[64,256]{1,0:T(8,128)(2,1)S(1)}, u32[]{:S(2)}, u32[]{:S(2)}) collective-permute-start(bf16[64,256]{1,0:T(8,128)(2,1)S(1)} %get-tuple-element.101), channel_id=1, source_target_pairs={{0,4},{1,5},{2,6},{3,7},{4,0},{5,1},{6,2},{7,3},{8,12},{9,13},{10,... | collective-permute-start | bytes 98312 | tf_op jit(solution)/shard_map/ppermute | solution.py:535
  47.5 4.3 %collective-permute-start.15 = (bf16[64,256]{1,0:T(8,128)(2,1)S(1)}, bf16[64,256]{1,0:T(8,128)(2,1)S(1)}, u32[]{:S(2)}, u32[]{:S(2)}) collective-permute-start(bf16[64,256]{1,0:T(8,128)(2,1)S(1)} %get-tuple-element.102), channel_id=1, source_target_pairs={{0,6},{1,7},{2,4},{3,5},{4,2},{5,3},{6,0},{7,1},{8,14},{9,15},{10,... | collective-permute-start | bytes 98312 | tf_op jit(solution)/shard_map/ppermute | solution.py:535
